TPU v7x, 512 devices: a whole 4x8x8 slice. The times are simulated.
512 devices in a mesh: row: 64 (over y, z), col: 8 (over x, core).
Axes of the slice: x: 4, y: 8, z: 8, core: 2. Of those that a mesh axis runs over, the one named last changes fastest.
Arguments:
- right_sides: float32 [8, 4096, 256], P(None, 'row'), may hold values from -6 to 6
- diag_inverse: float32 [4, 4096, 4096], P(None, 'col', 'row'), may hold values from -0.25 to 0.25
- lower_blocks: float32 [6, 4096, 4096], P(None, 'row', 'col'), may hold values from -0.046875 to 0.046875
- trail_panel: float32 [4, 4096, 4, 4096], P(None, 'row', None, 'col'), may hold values from -0.046875 to 0.046875
Outputs:
- solution: float32 [4, 4096, 256], P(None, 'col', 'row')
- trail_rest: float32 [4, 4096, 256], P(None, 'row', 'col')
All inputs are finite; a program needn't handle non-finite values.
Results may differ from a plain program's by a relative error of at most 0.0001.
Values sent between devices are 32-bit elements; how exact they have to be, the bound alone decides.
No kernel may reach another device: no remote copies, remote signals or barrier semaphores. Data moves between devices by JAX's collectives and lax.ppermute only.
A program may use at most 64 MiB of HBM per device.

v0:
```python
import jax
import jax.numpy as jnp
from jax import lax
from jax.sharding import PartitionSpec as P

HIGHEST_PREC = lax.Precision.HIGHEST


def pair_index(block_row, prior_row):
    return block_row * (block_row - 1) // 2 + prior_row


def block_product(matrix, solved_block):
    return jnp.dot(matrix, solved_block, precision=HIGHEST_PREC, preferred_element_type=jnp.float32)


def panel_product(trail_panel, block_row, solved_block):
    return jnp.einsum(
        "mrn,nc->mrc", trail_panel[:, :, block_row, :], solved_block, precision=HIGHEST_PREC
    )


def shards(right_sides, diag_inverse, lower_blocks, trail_panel):
    step_count = diag_inverse.shape[0]
    trail_count = trail_panel.shape[0]
    local_rows = right_sides.shape[1]
    column_count = right_sides.shape[2]
    solved = []
    pending = [None] * step_count
    trail_acc = jnp.zeros((trail_count, local_rows, column_count), jnp.float32)
    for block_row in range(step_count):
        if block_row == 0:
            current = right_sides[0]
        else:
            partial_value = pending[block_row]
            current = right_sides[block_row] - lax.psum(partial_value, "col")
        local_term = block_product(diag_inverse[block_row], current)
        solved_block = lax.psum(local_term, "row")
        solved.append(solved_block)
        for later_row in range(block_row + 1, step_count):
            contrib = block_product(lower_blocks[pair_index(later_row, block_row)], solved_block)
            pending[later_row] = (
                contrib if pending[later_row] is None else pending[later_row] + contrib
            )
        trail_acc = trail_acc + panel_product(trail_panel, block_row, solved_block)
    shared = lax.psum_scatter(trail_acc, "col", scatter_dimension=2, tiled=True)
    own_width = shared.shape[2]
    own_sides = lax.dynamic_slice_in_dim(
        right_sides[step_count:], lax.axis_index("col") * own_width, own_width, 2
    )
    trail_rest = own_sides - shared
    stacked = jnp.stack(solved)
    out_width = column_count // lax.axis_size("row")
    solution = lax.dynamic_slice_in_dim(stacked, lax.axis_index("row") * out_width, out_width, 2)
    return (solution, trail_rest)


def solution(mesh):
    placed = (
        P(None, "row", None),
        P(None, "col", "row"),
        P(None, "row", "col"),
        P(None, "row", None, "col"),
    )
    return jax.shard_map(
        shards,
        mesh=mesh,
        in_specs=placed,
        out_specs=(P(None, "col", "row"), P(None, "row", "col")),
        check_vma=False,
    )
```

profile of v0, /device:TPU:1, one launch (start us, length us, event | category | flops | bytes accessed | tf_op | source)
XLA Modules:
  0.0 931.0 jit_solution(10455983002185645724)
XLA Ops:
  7.2 2.3 fusion.22
  9.6 158.9 %all-reduce.10.cloned.1.call-done = f32[512,256]{1,0:T(8,128)} async-done(((f32[512,256]{1,0:T(8,128)}), f32[512,256]{1,0:T(8,128)}) %all-reduce.10.cloned.1.call-update) | async-done | bytes 524304 | tf_op jit(solution)/shard_map/psum | solution.py:38
  168.5 2.2 convolution_bitcast_fusion.3
  170.7 69.5 %all-reduce.12.cloned.1.call-done = f32[64,256]{1,0:T(8,128)} async-done(((f32[64,256]{1,0:T(8,128)}), f32[64,256]{1,0:T(8,128)}) %all-reduce.12.cloned.1.call-update) | async-done | bytes 65552 | tf_op jit(solution)/shard_map/psum | solution.py:36
  240.2 2.4 convolution_bitcast_fusion.2
  242.7 1.3 fusion.18
  244.0 151.5 %all-reduce.14.cloned.1.call-done = f32[512,256]{1,0:T(8,128)} async-done(((f32[512,256]{1,0:T(8,128)}), f32[512,256]{1,0:T(8,128)}) %all-reduce.14.cloned.1.call-update) | async-done | bytes 524304 | tf_op jit(solution)/shard_map/psum | solution.py:38
  395.5 2.1 fusion.2
  397.7 2.8 fusion.39
  400.5 66.6 %all-reduce.16.cloned.1.call-done = f32[64,256]{1,0:T(8,128)} async-done(((f32[64,256]{1,0:T(8,128)}), f32[64,256]{1,0:T(8,128)}) %all-reduce.16.cloned.1.call-update) | async-done | bytes 65552 | tf_op jit(solution)/shard_map/psum | solution.py:36
  467.1 2.4 convolution_bitcast_fusion.1
  469.5 0.0 all-reduce.20.cloned.1.call-start
  469.6 0.1 constant_dynamic-slice_fusion
  469.7 0.1 copy.30
  469.8 1.3 dynamic-slice
  471.7 1.3 fusion.14
  473.1 1.4 convolution_add_fusion.4
  474.5 147.9 %all-reduce.18.cloned.1.call-done = f32[512,256]{1,0:T(8,128)} async-done(((f32[512,256]{1,0:T(8,128)}), f32[512,256]{1,0:T(8,128)}) %all-reduce.18.cloned.1.call-update) | async-done | bytes 524304 | tf_op jit(solution)/shard_map/psum | solution.py:38
  622.3 2.1 fusion.1
  624.5 0.6 fusion.6
  625.2 68.7 %all-reduce.20.cloned.1.call-done = f32[64,256]{1,0:T(8,128)} async-done(((f32[64,256]{1,0:T(8,128)}), f32[64,256]{1,0:T(8,128)}) %all-reduce.20.cloned.1.call-update) | async-done | bytes 65552 | tf_op jit(solution)/shard_map/psum | solution.py:36
  693.9 2.4 convolution_bitcast_fusion
  696.4 0.6 convolution_add_fusion.2
  697.0 0.6 convolution_add_fusion.1
  697.7 151.6 %all-reduce.22.cloned.1.call-done = f32[512,256]{1,0:T(8,128)} async-done(((f32[512,256]{1,0:T(8,128)}), f32[512,256]{1,0:T(8,128)}) %all-reduce.22.cloned.1.call-update) | async-done | bytes 524304 | tf_op jit(solution)/shard_map/psum | solution.py:38
  849.3 1.7 fusion
  851.0 1.0 copy.23
  852.0 0.3 fusion.5
  852.4 0.9 copy.24
  853.3 69.3 %all-reduce.24.cloned.1.call-done = f32[4,64,256]{1,0,2:T(4,128)} async-done(((f32[4,64,256]{1,0,2:T(4,128)}), f32[4,64,256]{1,0,2:T(4,128)}) %all-reduce.24.cloned.1.call-update) | async-done | bytes 262160
  922.7 0.9 dynamic-slice_subtract_fusion
  923.5 0.6 copy.25
  (35 shorter events, 0.5 us)
Async XLA Ops:
  7.2 161.3 %all-reduce.10.cloned.1.call-start = ((), (), s32[]{:S(2)}) async-start(), calls=%async_computation | async-start | bytes 1048576 | tf_op jit(solution)/shard_map/psum | solution.py:38
  9.5 388.2 %copy-start.3 = (f32[4,64,4,512]{3,2,1,0:T(4,128)S(1)}, f32[4,64,4,512]{3,2,1,0:T(4,128)}, u32[]{:S(2)}) copy-start(f32[4,64,4,512]{3,2,1,0:T(4,128)} %param.7) | copy-start | bytes 6291460
  9.6 230.6 %all-reduce.12.cloned.1.call-start = ((), (), s32[]{:S(2)}) async-start(), calls=%async_computation.1 | async-start | bytes 131072 | tf_op jit(solution)/shard_map/psum | solution.py:36
  168.5 74.2 %copy-start = (f32[512,256]{1,0:T(8,128)S(1)}, f32[512,256]{1,0:T(8,128)}, u32[]{:S(2)}) copy-start(f32[512,256]{1,0:T(8,128)} %all-reduce.10.cloned.1.call-done) | copy-start | bytes 1572868
  170.7 224.8 %all-reduce.14.cloned.1.call-start = ((), (), s32[]{:S(2)}) async-start(), calls=%async_computation.2 | async-start | bytes 1048576 | tf_op jit(solution)/shard_map/psum | solution.py:38
  242.6 224.5 %all-reduce.16.cloned.1.call-start = ((), (), s32[]{:S(2)}) async-start(), calls=%async_computation.3 | async-start | bytes 131072 | tf_op jit(solution)/shard_map/psum | solution.py:36
  397.6 71.9 %slice-start = ((f32[8,64,256]{2,1,0:T(8,128)}), f32[4,64,256]{2,1,0:T(8,128)S(1)}, s32[]{:S(2)}) async-start(f32[8,64,256]{2,1,0:T(8,128)} %param.4), calls=%async_computation.8 | async-start | bytes 524288 | tf_op jit(solution)/shard_map/slice | solution.py:49
  397.7 224.7 %all-reduce.18.cloned.1.call-start = ((), (), s32[]{:S(2)}) async-start(), calls=%async_computation.4 | async-start | bytes 1048576 | tf_op jit(solution)/shard_map/psum | solution.py:38
  400.5 72.6 %copy-start.1 = (f32[512,256]{1,0:T(8,128)S(1)}, f32[512,256]{1,0:T(8,128)}, u32[]{:S(2)}) copy-start(f32[512,256]{1,0:T(8,128)} %all-reduce.14.cloned.1.call-done) | copy-start | bytes 1572868
  400.5 224.0 %copy-start.8 = (f32[4,64,1,512]{3,2,1,0:T(1,128)S(1)}, f32[4,64,1,512]{3,2,1,0:T(1,128)}, u32[]{:S(2)}) copy-start(f32[4,64,1,512]{3,2,1,0:T(1,128)} %get-tuple-element.9) | copy-start | bytes 1572868
  469.5 224.4 %all-reduce.20.cloned.1.call-start = ((), (), s32[]{:S(2)}) async-start(), calls=%async_computation.5 | async-start | bytes 131072 | tf_op jit(solution)/shard_map/psum | solution.py:36
  473.1 223.3 %copy-start.7 = (f32[4,64,1,512]{3,2,1,0:T(1,128)S(1)}, f32[4,64,1,512]{3,2,1,0:T(1,128)}, u32[]{:S(2)}) copy-start(f32[4,64,1,512]{3,2,1,0:T(1,128)} %get-tuple-element.8) | copy-start | bytes 1572868
  624.5 224.8 %all-reduce.22.cloned.1.call-start = ((), (), s32[]{:S(2)}) async-start(), calls=%async_computation.6 | async-start | bytes 1048576 | tf_op jit(solution)/shard_map/psum | solution.py:38
  624.5 72.5 %copy-start.2 = (f32[512,256]{1,0:T(8,128)S(1)}, f32[512,256]{1,0:T(8,128)}, u32[]{:S(2)}) copy-start(f32[512,256]{1,0:T(8,128)} %all-reduce.18.cloned.1.call-done) | copy-start | bytes 1572868
  624.5 72.5 %copy-start.6 = (f32[4,64,1,512]{3,2,1,0:T(1,128)S(1)}, f32[4,64,1,512]{3,2,1,0:T(1,128)}, u32[]{:S(2)}) copy-start(f32[4,64,1,512]{3,2,1,0:T(1,128)} %get-tuple-element.7) | copy-start | bytes 1572868
  625.2 224.1 %copy-start.5 = (f32[4,64,1,512]{3,2,1,0:T(1,128)S(1)}, f32[4,64,1,512]{3,2,1,0:T(1,128)}, u32[]{:S(2)}) copy-start(f32[4,64,1,512]{3,2,1,0:T(1,128)} %get-tuple-element.6) | copy-start | bytes 1572868
  696.3 226.4 %all-reduce.24.cloned.1.call-start = ((), (), s32[]{:S(2)}) async-start(), calls=%async_computation.7 | async-start | bytes 1048576
  849.3 2.8 copy-start.4
Sparse Core Ops, SparseCore 0:
  11.2 157.2 all-reduce.9
  171.5 68.6 all-reduce.11
  243.4 152.0 all-reduce.13
  398.3 68.6 all-reduce.15
  470.1 152.1 all-reduce.17
  625.2 68.6 all-reduce.19
  697.1 152.1 all-reduce.21
  852.1 70.4 all-reduce.23
where the time goes:
time: 932 us; the launch traced here: 931 us
  waiting for transfers between devices  884 us (95%)
  matrix products  23.6 us (3%)
  between operations  15 us (2%)
    psum x4, waiting for transfers between devices, shards(): solved_block = lax.psum(local_term, 'row')  610 us
    psum x3, waiting for transfers between devices, shards(): current = right_sides[block_row] - lax.psum(partial_value, 'col')  205 us
    unnamed x9, waiting for transfers between devices  69.5 us
    dot_general x10, matrix products, block_product(): jnp.dot(matrix, solved_block, precision=HIGHEST_PREC, preferred_element_t...  20 us
  transfers between devices with their start and end apart: 8, of which 8 were waited for; matrix products, arithmetic and copies ran while one was open for 1% of the time, Pallas kernels for 0%

commit v1 on v0

--- a/solution.py
+++ b/solution.py
@@ -14,10 +14,22 @@
     return jnp.dot(matrix, solved_block, precision=HIGHEST_PREC, preferred_element_type=jnp.float32)
 
 
-def panel_product(trail_panel, block_row, solved_block):
-    return jnp.einsum(
-        "mrn,nc->mrc", trail_panel[:, :, block_row, :], solved_block, precision=HIGHEST_PREC
-    )
+def reduce_scatter(value, axis):
+    size = lax.axis_size(axis)
+    pieces = lax.all_to_all(value, axis, 0, 0, tiled=True)
+    return pieces.reshape((size, value.shape[0] // size) + value.shape[1:]).sum(0)
+
+
+def replicate(piece, axis):
+    size = lax.axis_size(axis)
+    copies = jnp.broadcast_to(piece[None], (size,) + piece.shape)
+    copies = copies.reshape((size * piece.shape[0],) + piece.shape[1:])
+    return lax.all_to_all(copies, axis, 0, 0, tiled=True)
+
+
+def sum_over(value, axis):
+    size = lax.axis_size(axis)
+    return replicate(value, axis).reshape((size,) + value.shape).sum(0)
 
 
 def shards(right_sides, diag_inverse, lower_blocks, trail_panel):
@@ -27,24 +39,27 @@
     column_count = right_sides.shape[2]
     solved = []
     pending = [None] * step_count
-    trail_acc = jnp.zeros((trail_count, local_rows, column_count), jnp.float32)
+    trail_acc = None
     for block_row in range(step_count):
         if block_row == 0:
             current = right_sides[0]
         else:
-            partial_value = pending[block_row]
-            current = right_sides[block_row] - lax.psum(partial_value, "col")
+            current = right_sides[block_row] - sum_over(pending[block_row], "col")
         local_term = block_product(diag_inverse[block_row], current)
-        solved_block = lax.psum(local_term, "row")
+        solved_block = replicate(reduce_scatter(local_term, "row"), "row")
         solved.append(solved_block)
         for later_row in range(block_row + 1, step_count):
             contrib = block_product(lower_blocks[pair_index(later_row, block_row)], solved_block)
             pending[later_row] = (
                 contrib if pending[later_row] is None else pending[later_row] + contrib
             )
-        trail_acc = trail_acc + panel_product(trail_panel, block_row, solved_block)
-    shared = lax.psum_scatter(trail_acc, "col", scatter_dimension=2, tiled=True)
-    own_width = shared.shape[2]
+        contrib = jnp.einsum(
+            "nc,mrn->cmr", solved_block, trail_panel[:, :, block_row, :], precision=HIGHEST_PREC
+        )
+        trail_acc = contrib if trail_acc is None else trail_acc + contrib
+    shared = reduce_scatter(trail_acc.reshape(column_count, trail_count * local_rows), "col")
+    own_width = shared.shape[0]
+    shared = shared.reshape(own_width, trail_count, local_rows).transpose(1, 2, 0)
     own_sides = lax.dynamic_slice_in_dim(
         right_sides[step_count:], lax.axis_index("col") * own_width, own_width, 2
     )

time: 932 us -> 272 us (0.29)
  waiting for transfers between devices: 884 us -> 59.2 us
  blocking collectives: 0 us -> 150 us
  starting transfers between devices: 0.33 us -> 35.8 us
  between operations: 15 us -> 0.92 us
  matrix products: 23.6 us -> 10.9 us
    psum x7 -> x0, waiting for transfers between devices: 815 us -> none  [the longest x4 610 us: shards(): solved_block = lax.psum(local_term, 'row')]
    all_to_all x0 -> x7, blocking collectives: none -> 150 us  [the longest x3 75.5 us: reduce_scatter(): pieces = lax.all_to_all(value, axis, 0, 0, tiled=True)]
    unnamed x9 -> x0, waiting for transfers between devices: 69.5 us -> none
    all_to_all x0 -> x5, waiting for transfers between devices: none -> 59.2 us  [the longest x3 38.1 us: replicate(): return lax.all_to_all(copies, axis, 0, 0, tiled=True)]
    all_to_all x0 -> x5, starting transfers between devices: none -> 35.8 us  [the longest x3 22.9 us: replicate(): return lax.all_to_all(copies, axis, 0, 0, tiled=True)]
    dot_general x10, matrix products: 20 us -> 8.42 us  [block_product(): jnp.dot(matrix, solved_block, precision=HIGHEST_PREC, preferred_element_t...]
  transfers between devices with their start and end apart: 8 -> 5, of which waited for: 8 -> 5; matrix products, arithmetic and copies ran while one was open for 1% -> 4% of each run, Pallas kernels for 0% -> 0%
where the time goes in v1:
time: 272 us; the launch traced here: 271 us
  blocking collectives  150 us (55%)
  waiting for transfers between devices  59.2 us (22%)
  starting transfers between devices  35.8 us (13%)
  local copies, waits for them, and re-layouts  14.1 us (5%)
  matrix products  10.9 us (4%)
    all_to_all x3, blocking collectives, reduce_scatter(): pieces = lax.all_to_all(value, axis, 0, 0, tiled=True)  75.5 us
    all_to_all x4, blocking collectives, replicate(): return lax.all_to_all(copies, axis, 0, 0, tiled=True)  74.1 us
    all_to_all x3, waiting for transfers between devices, replicate(): return lax.all_to_all(copies, axis, 0, 0, tiled=True)  38.1 us
    all_to_all x3, starting transfers between devices, replicate(): return lax.all_to_all(copies, axis, 0, 0, tiled=True)  22.9 us
    all_to_all x2, waiting for transfers between devices, reduce_scatter(): pieces = lax.all_to_all(value, axis, 0, 0, tiled=True)  21.1 us
    all_to_all x2, starting transfers between devices, reduce_scatter(): pieces = lax.all_to_all(value, axis, 0, 0, tiled=True)  13 us
    dot_general x10, matrix products, block_product(): jnp.dot(matrix, solved_block, precision=HIGHEST_PREC, preferred_element_t...  8.42 us
    slice x1, local copies, waits for them, and re-layouts, shards(): trail_panel[:, :, block_row, :]  5.87 us
  transfers between devices with their start and end apart: 5, of which 5 were waited for; matrix products, arithmetic and copies ran while one was open for 4% of the time, Pallas kernels for 0%

profile of v1, /device:TPU:1, one launch (start us, length us, event | category | flops | bytes accessed | tf_op | source)
XLA Modules:
  0.0 271.4 jit_solution(2564290526355639726)
XLA Ops:
  0.6 0.9 slice.57
  1.7 1.5 fusion.18
  3.2 33.3 %all_to_all.96 = f32[64,8,256]{2,1,0:T(8,128)S(1)} all-to-all(f32[64,8,256]{2,1,0:T(8,128)S(1)} %fusion.18), channel_id=1, replica_groups=mesh['row'=64,'col'=8] {'row'}, dimensions={0} | all-to-all | bytes 1048576 | tf_op jit(solution)/shard_map/all_to_all | solution.py:19
  36.6 23.8 %all_to_all.97 = f32[64,8,256]{2,1,0:T(8,128)S(1)} all-to-all(f32[64,8,256]{2,1,0:T(8,128)S(1)} %broadcast_in_dim.14), channel_id=1, replica_groups=mesh['row'=64,'col'=8] {'row'}, dimensions={0} | all-to-all | bytes 1048576 | tf_op jit(solution)/shard_map/all_to_all | solution.py:27
  60.9 17.5 %all_to_all.98 = f32[8,64,256]{2,1,0:T(8,128)S(1)} all-to-all(f32[8,64,256]{2,1,0:T(8,128)S(1)} %broadcast_in_dim.15), channel_id=1, replica_groups=mesh['row'=64,'col'=8] {'col'}, dimensions={0} | all-to-all | bytes 1048576 | tf_op jit(solution)/shard_map/all_to_all | solution.py:27
  78.5 1.5 convolution_bitcast_fusion.2
  80.2 21.1 %all_to_all.99 = f32[64,8,256]{2,1,0:T(8,128)S(1)} all-to-all(f32[64,8,256]{2,1,0:T(8,128)S(1)} %bitcast.127), channel_id=1, replica_groups=mesh['row'=64,'col'=8] {'row'}, dimensions={0} | all-to-all | bytes 1048576 | tf_op jit(solution)/shard_map/all_to_all | solution.py:19
  101.3 0.8 broadcast_in_dim.16
  102.2 7.6 %all-to-all-start.4 = ((f32[64,8,256]{2,1,0:T(8,128)}), f32[64,8,256]{2,1,0:T(8,128)S(1)}, u32[]{:S(2)}, u32[]{:S(2)}) async-start(f32[64,8,256]{2,1,0:T(8,128)} %broadcast_in_dim.16), calls=%async_computation.4 | async-start | bytes 1048576 | tf_op jit(solution)/shard_map/all_to_all | solution.py:27
  110.2 15.3 %all-to-all-done.4 = f32[64,8,256]{2,1,0:T(8,128)S(1)} async-done(((f32[64,8,256]{2,1,0:T(8,128)}), f32[64,8,256]{2,1,0:T(8,128)S(1)}, u32[]{:S(2)}, u32[]{:S(2)}) %all-to-all-start.4) | async-done | bytes 524320 | tf_op jit(solution)/shard_map/all_to_all | solution.py:27
  126.0 16.3 %all_to_all.100 = f32[8,64,256]{2,1,0:T(8,128)S(1)} all-to-all(f32[8,64,256]{2,1,0:T(8,128)S(1)} %broadcast_in_dim.17), channel_id=1, replica_groups=mesh['row'=64,'col'=8] {'col'}, dimensions={0} | all-to-all | bytes 1048576 | tf_op jit(solution)/shard_map/all_to_all | solution.py:27
  142.3 1.5 convolution_bitcast_fusion.1
  144.0 21.1 %all_to_all.101 = f32[64,8,256]{2,1,0:T(8,128)S(1)} all-to-all(f32[64,8,256]{2,1,0:T(8,128)S(1)} %bitcast.128), channel_id=1, replica_groups=mesh['row'=64,'col'=8] {'row'}, dimensions={0} | all-to-all | bytes 1048576 | tf_op jit(solution)/shard_map/all_to_all | solution.py:19
  165.2 0.8 broadcast_in_dim.18
  166.0 7.6 %all-to-all-start.7 = ((f32[64,8,256]{2,1,0:T(8,128)}), f32[64,8,256]{2,1,0:T(8,128)S(1)}, u32[]{:S(2)}, u32[]{:S(2)}) async-start(f32[64,8,256]{2,1,0:T(8,128)} %broadcast_in_dim.18), calls=%async_computation.7 | async-start | bytes 1048576 | tf_op jit(solution)/shard_map/all_to_all | solution.py:27
  174.5 14.9 %all-to-all-done.7 = f32[64,8,256]{2,1,0:T(8,128)S(1)} async-done(((f32[64,8,256]{2,1,0:T(8,128)}), f32[64,8,256]{2,1,0:T(8,128)S(1)}, u32[]{:S(2)}, u32[]{:S(2)}) %all-to-all-start.7) | async-done | bytes 524320 | tf_op jit(solution)/shard_map/all_to_all | solution.py:27
  189.8 16.4 %all_to_all.102 = f32[8,64,256]{2,1,0:T(8,128)S(1)} all-to-all(f32[8,64,256]{2,1,0:T(8,128)S(1)} %broadcast_in_dim.19), channel_id=1, replica_groups=mesh['row'=64,'col'=8] {'col'}, dimensions={0} | all-to-all | bytes 1048576 | tf_op jit(solution)/shard_map/all_to_all | solution.py:27
  206.3 1.5 convolution_bitcast_fusion
  207.8 1.0 copy.31
  208.8 5.1 %all-to-all-start.9 = ((f32[64,8,256]{2,1,0:T(8,128)}), f32[64,8,256]{2,1,0:T(8,128)S(1)}, u32[]{:S(2)}, u32[]{:S(2)}) async-start(f32[64,8,256]{2,1,0:T(8,128)} %bitcast.32), calls=%async_computation.9 | async-start | bytes 1048576 | tf_op jit(solution)/shard_map/all_to_all | solution.py:19
  214.0 16.1 %all-to-all-done.9 = f32[64,8,256]{2,1,0:T(8,128)S(1)} async-done(((f32[64,8,256]{2,1,0:T(8,128)}), f32[64,8,256]{2,1,0:T(8,128)S(1)}, u32[]{:S(2)}, u32[]{:S(2)}) %all-to-all-start.9) | async-done | bytes 524320 | tf_op jit(solution)/shard_map/all_to_all | solution.py:19
  230.2 0.8 broadcast_in_dim.20
  231.0 7.6 %all-to-all-start.10 = ((f32[64,8,256]{2,1,0:T(8,128)}), f32[64,8,256]{2,1,0:T(8,128)S(1)}, u32[]{:S(2)}, u32[]{:S(2)}) async-start(f32[64,8,256]{2,1,0:T(8,128)} %broadcast_in_dim.20), calls=%async_computation.10 | async-start | bytes 1048576 | tf_op jit(solution)/shard_map/all_to_all | solution.py:27
  238.6 5.9 %fusion.46 = (f32[4,64,1,512]{3,2,1,0:T(1,128)S(1)}, f32[4,64,1,512]{3,2,1,0:T(1,128)S(1)}, f32[4,64,1,512]{3,2,1,0:T(1,128)S(1)}, f32[4,64,1,512]{3,2,1,0:T(1,128)S(1)}) fusion(f32[4,64,4,512]{3,2,1,0:T(4,128)} %param.7), kind=kLoop, calls=%fused_computation.69 | loop fusion | bytes 4194304 | tf_op jit(solution)/shard_map/slice | solution.py:57
  244.5 0.6 fusion.5
  245.8 0.6 convolution_add_fusion.1
  246.4 7.9 %all-to-all-done.10 = f32[64,8,256]{2,1,0:T(8,128)S(1)} async-done(((f32[64,8,256]{2,1,0:T(8,128)}), f32[64,8,256]{2,1,0:T(8,128)S(1)}, u32[]{:S(2)}, u32[]{:S(2)}) %all-to-all-start.10) | async-done | bytes 524320 | tf_op jit(solution)/shard_map/all_to_all | solution.py:27
  255.2 1.0 all_to_all.82
  256.2 7.8 %all-to-all-start.11 = ((f32[8,32,256]{2,1,0:T(8,128)}), f32[8,32,256]{2,1,0:T(8,128)S(1)}, u32[]{:S(2)}, u32[]{:S(2)}) async-start(f32[8,32,256]{2,1,0:T(8,128)} %all_to_all.82), calls=%async_computation.11 | async-start | bytes 524288 | tf_op jit(solution)/shard_map/all_to_all | solution.py:19
  264.6 0.9 copy.38
  265.6 5.0 %all-to-all-done.11 = f32[8,32,256]{2,1,0:T(8,128)S(1)} async-done(((f32[8,32,256]{2,1,0:T(8,128)}), f32[8,32,256]{2,1,0:T(8,128)S(1)}, u32[]{:S(2)}, u32[]{:S(2)}) %all-to-all-start.11) | async-done | bytes 262176 | tf_op jit(solution)/shard_map/all_to_all | solution.py:19
  270.7 0.6 copy.39
  (36 shorter events, 5.8 us)
Async XLA Ops:
  1.7 58.7 %copy-start = (f32[6,64,512]{2,1,0:T(8,128)S(1)}, f32[6,64,512]{2,1,0:T(8,128)}, u32[]{:S(2)}) copy-start(f32[6,64,512]{2,1,0:T(8,128)} %param.6) | copy-start | bytes 2359300
  36.6 41.9 %copy-start.2 = (f32[4,512,64]{1,2,0:T(8,128)S(1)}, f32[4,512,64]{1,2,0:T(8,128)}, u32[]{:S(2)}) copy-start(f32[4,512,64]{1,2,0:T(8,128)} %param.5) | copy-start | bytes 1572868
  102.2 23.3 %all-to-all-start.4 = ((f32[64,8,256]{2,1,0:T(8,128)}), f32[64,8,256]{2,1,0:T(8,128)S(1)}, u32[]{:S(2)}, u32[]{:S(2)}) async-start(f32[64,8,256]{2,1,0:T(8,128)} %broadcast_in_dim.16), calls=%async_computation.4 | async-start | bytes 1048576 | tf_op jit(solution)/shard_map/all_to_all | solution.py:27
  166.0 23.3 %all-to-all-start.7 = ((f32[64,8,256]{2,1,0:T(8,128)}), f32[64,8,256]{2,1,0:T(8,128)S(1)}, u32[]{:S(2)}, u32[]{:S(2)}) async-start(f32[64,8,256]{2,1,0:T(8,128)} %broadcast_in_dim.18), calls=%async_computation.7 | async-start | bytes 1048576 | tf_op jit(solution)/shard_map/all_to_all | solution.py:27
  189.8 24.1 %copy-start.1 = (f32[8,64,256]{2,1,0:T(8,128)S(1)}, f32[8,64,256]{2,1,0:T(8,128)}, u32[]{:S(2)}) copy-start(f32[8,64,256]{2,1,0:T(8,128)} %param.4) | copy-start | bytes 1572868
  208.8 21.3 %all-to-all-start.9 = ((f32[64,8,256]{2,1,0:T(8,128)}), f32[64,8,256]{2,1,0:T(8,128)S(1)}, u32[]{:S(2)}, u32[]{:S(2)}) async-start(f32[64,8,256]{2,1,0:T(8,128)} %bitcast.32), calls=%async_computation.9 | async-start | bytes 1048576 | tf_op jit(solution)/shard_map/all_to_all | solution.py:19
  231.0 23.4 %all-to-all-start.10 = ((f32[64,8,256]{2,1,0:T(8,128)}), f32[64,8,256]{2,1,0:T(8,128)S(1)}, u32[]{:S(2)}, u32[]{:S(2)}) async-start(f32[64,8,256]{2,1,0:T(8,128)} %broadcast_in_dim.20), calls=%async_computation.10 | async-start | bytes 1048576 | tf_op jit(solution)/shard_map/all_to_all | solution.py:27
  256.2 14.4 %all-to-all-start.11 = ((f32[8,32,256]{2,1,0:T(8,128)}), f32[8,32,256]{2,1,0:T(8,128)S(1)}, u32[]{:S(2)}, u32[]{:S(2)}) async-start(f32[8,32,256]{2,1,0:T(8,128)} %all_to_all.82), calls=%async_computation.11 | async-start | bytes 524288 | tf_op jit(solution)/shard_map/all_to_all | solution.py:19

commit v2 on v0

v2 whole, which is shorter than its diff:
```python
import jax
import jax.numpy as jnp
from jax import lax
from jax.sharding import PartitionSpec as P

HIGHEST_PREC = lax.Precision.HIGHEST
GROUPS = 4
PART_ROWS = 8
PART_COLUMNS = 256


def pair_index(block_row, prior_row):
    return block_row * (block_row - 1) // 2 + prior_row


def times(left, right):
    return jnp.dot(left, right, precision=HIGHEST_PREC, preferred_element_type=jnp.float32)


def times_transposed(left, right):
    return lax.dot_general(
        left,
        right,
        (((1,), (1,)), ((), ())),
        precision=HIGHEST_PREC,
        preferred_element_type=jnp.float32,
    )


def to_parts(value):
    rows, columns = value.shape
    split = value.reshape(rows // PART_ROWS, PART_ROWS, columns // PART_COLUMNS, PART_COLUMNS)
    return split.transpose(0, 2, 1, 3).reshape(-1, PART_ROWS, PART_COLUMNS)


def from_parts(parts, columns):
    split = parts.reshape(-1, columns // PART_COLUMNS, PART_ROWS, PART_COLUMNS)
    return split.transpose(0, 2, 1, 3).reshape(-1, columns)


def swap(parts, axis, groups=None):
    return lax.all_to_all(parts, axis, 0, 0, axis_index_groups=groups, tiled=True)


def copies(part, count):
    return jnp.broadcast_to(part[None], (count,) + part.shape)


def sum_over(value, axis):
    return swap(copies(value, lax.axis_size(axis)), axis).sum(0)


def shards(right_sides, diag_inverse, lower_blocks, trail_panel):
    step_count = diag_inverse.shape[0]
    trail_count = trail_panel.shape[0]
    local_rows = right_sides.shape[1]
    column_count = right_sides.shape[2]
    row_size = lax.axis_size("row")
    col_size = lax.axis_size("col")
    members = row_size // GROUPS
    width = column_count // GROUPS
    row = lax.axis_index("row")
    group = row // members
    groups = [[g * members + m for m in range(members)] for g in range(GROUPS)]
    diag = diag_inverse.transpose(0, 2, 1)
    block_width = diag.shape[2]

    def from_partners(value):
        got = [value]
        for shift in range(1, GROUPS):
            pairs = [(r, (r - shift * members) % row_size) for r in range(row_size)]
            got.append(lax.ppermute(value, "row", pairs))
        return got

    def own_rows(value):
        return lax.dynamic_slice_in_dim(value, group * width, width, 0)

    later_sides = right_sides[1:step_count].reshape(-1, block_width)
    first = jnp.concatenate([lower_blocks[0], diag[1], later_sides], 0)
    second = jnp.concatenate(
        [lower_blocks[1:].reshape(-1, block_width), diag[2:].reshape(-1, block_width)], 0
    )
    first_all = from_partners(first)
    second_all = from_partners(second)

    def block_of(index, is_diag):
        if is_diag:
            source, at = (first_all, 1) if index == 1 else (second_all, 5 + index - 2)
        else:
            source, at = (first_all, 0) if index == 0 else (second_all, index - 1)
        return jnp.concatenate([s[at * local_rows : (at + 1) * local_rows] for s in source], 0)

    def sides_of(block_row):
        parts = []
        for s in first_all:
            sides = s[2 * local_rows :].reshape(step_count - 1, local_rows, column_count)
            parts.append(sides[block_row - 1])
        return own_rows(jnp.concatenate(parts, 0).T)

    trail = [
        trail_panel[:, :, j, :].reshape(trail_count * local_rows, block_width)
        for j in range(step_count)
    ]
    out_width = column_count // row_size
    outs = []
    grouped = []

    partial_value = times(right_sides[0].T, diag[0])
    part = swap(to_parts(partial_value), "row").sum(0)
    whole = from_parts(swap(copies(part, row_size), "row"), block_width)
    outs.append(lax.dynamic_slice_in_dim(whole, row * out_width, out_width, 0))
    trail_acc = times_transposed(whole, trail[0])
    grouped.append(own_rows(whole))

    for block_row in range(1, step_count):
        update = None
        for prior_row in range(block_row):
            block = block_of(pair_index(block_row, prior_row), False)
            term = times_transposed(grouped[prior_row], block)
            update = term if update is None else update + term
        current = sides_of(block_row) - sum_over(update, "col")
        partial_value = times(current, block_of(block_row, True))
        part = swap(to_parts(partial_value), "row", groups).sum(0)
        if block_row < step_count - 1:
            solved = from_parts(swap(copies(part, members), "row", groups), block_width)
            grouped.append(solved)
            place = (row % members) * out_width
            outs.append(lax.dynamic_slice_in_dim(solved, place, out_width, 0))
        else:
            whole = from_parts(swap(copies(part, row_size), "row"), block_width)
            outs.append(lax.dynamic_slice_in_dim(whole, row * out_width, out_width, 0))

    middle = jnp.stack(grouped[1:])
    spread = jnp.concatenate(from_partners(middle) * 2, 1)
    middle = lax.dynamic_slice_in_dim(spread, (GROUPS - group) % GROUPS * width, column_count, 1)
    for j in range(1, step_count - 1):
        trail_acc = trail_acc + times_transposed(middle[j - 1], trail[j])
    trail_acc = trail_acc + times_transposed(whole, trail[step_count - 1])

    own_width = column_count // col_size
    shared = swap(trail_acc.reshape(col_size, own_width, -1), "col").sum(0)
    shared = shared.reshape(own_width, trail_count, local_rows).transpose(1, 2, 0)
    own_sides = lax.dynamic_slice_in_dim(
        right_sides[step_count:], lax.axis_index("col") * own_width, own_width, 2
    )
    trail_rest = own_sides - shared
    return (jnp.stack(outs).transpose(0, 2, 1), trail_rest)


def solution(mesh):
    placed = (
        P(None, "row", None),
        P(None, "col", "row"),
        P(None, "row", "col"),
        P(None, "row", None, "col"),
    )
    return jax.shard_map(
        shards,
        mesh=mesh,
        in_specs=placed,
        out_specs=(P(None, "col", "row"), P(None, "row", "col")),
        check_vma=False,
    )
```

time: 932 us -> 350 us (0.38)
  waiting for transfers between devices: 884 us -> 163 us
  starting transfers between devices: 0.33 us -> 117 us
  local copies, waits for them, and re-layouts: 6.87 us -> 44.5 us
  between operations: 15 us -> 1.35 us
    psum x7 -> x0, waiting for transfers between devices: 815 us -> none  [the longest x4 610 us: shards(): solved_block = lax.psum(local_term, 'row')]
    all_to_all x0 -> x12, waiting for transfers between devices: none -> 107 us  [swap(): lax.all_to_all(parts, axis, 0, 0, axis_index_groups=groups, tiled=True)]
    all_to_all x0 -> x12, starting transfers between devices: none -> 82.3 us  [swap(): lax.all_to_all(parts, axis, 0, 0, axis_index_groups=groups, tiled=True)]
    unnamed x9 -> x0, waiting for transfers between devices: 69.5 us -> none
    ppermute x0 -> x9, waiting for transfers between devices: none -> 56 us  [from_partners(): got.append(lax.ppermute(value, 'row', pairs))]
    ppermute x0 -> x9, starting transfers between devices: none -> 35 us  [from_partners(): got.append(lax.ppermute(value, 'row', pairs))]
    slice x1 -> x18, local copies, waits for them, and re-layouts: 2.77 us -> 20.1 us  [the longest x7 10.1 us: block_of(): s[at * local_rows:(at + 1) * local_rows]]
    squeeze x0 -> x18, local copies, waits for them, and re-layouts: none -> 9.8 us  [sides_of(): parts.append(sides[block_row - 1])]
  transfers between devices with their start and end apart: 8 -> 21, of which waited for: 8 -> 13; matrix products, arithmetic and copies ran while one was open for 1% -> 14% of each run, Pallas kernels for 0% -> 0%
where the time goes in v2:
time: 350 us; the launch traced here: 348 us
  waiting for transfers between devices  163 us (47%)
  starting transfers between devices  117 us (33%)
  local copies, waits for them, and re-layouts  44.5 us (13%)
  matrix products  18.6 us (5%)
  other arithmetic  3.95 us (1%)
    all_to_all x12, waiting for transfers between devices, swap(): lax.all_to_all(parts, axis, 0, 0, axis_index_groups=groups, tiled=True)  107 us
    all_to_all x12, starting transfers between devices, swap(): lax.all_to_all(parts, axis, 0, 0, axis_index_groups=groups, tiled=True)  82.3 us
    ppermute x9, waiting for transfers between devices, from_partners(): got.append(lax.ppermute(value, 'row', pairs))  56 us
    ppermute x9, starting transfers between devices, from_partners(): got.append(lax.ppermute(value, 'row', pairs))  35 us
    dot_general x10, matrix products, times_transposed(): lax.dot_general(left, right, (((1,), (1,)), ((), ())), precision=HIGHEST_...  12.7 us
    slice x7, local copies, waits for them, and re-layouts, block_of(): s[at * local_rows:(at + 1) * local_rows]  10.1 us
    squeeze x18, local copies, waits for them, and re-layouts, sides_of(): parts.append(sides[block_row - 1])  9.8 us
    unnamed x46, local copies, waits for them, and re-layouts  7.97 us
  transfers between devices with their start and end apart: 21, of which 13 were waited for; matrix products, arithmetic and copies ran while one was open for 14% of the time, Pallas kernels for 0%

profile of v2, /device:TPU:1, one launch (start us, length us, event | category | flops | bytes accessed | tf_op | source)
XLA Modules:
  0.0 348.2 jit_solution(1282755489329980992)
XLA Ops:
  5.6 17.3 %all-to-all-start = ((f32[64,8,256]{2,1,0:T(8,128)}), f32[64,8,256]{2,1,0:T(8,128)S(1)}, u32[]{:S(2)}, u32[]{:S(2)}) async-start(f32[64,8,256]{2,1,0:T(8,128)} %bitcast.10), calls=%async_computation | async-start | bytes 1048576 | tf_op jit(solution)/shard_map/all_to_all | solution.py:42
  24.7 3.8 %collective-permute-start.2 = (f32[224,512]{1,0:T(8,128)}, f32[224,512]{1,0:T(8,128)}, u32[]{:S(2)}, u32[]{:S(2)}) collective-permute-start(f32[224,512]{1,0:T(8,128)} %pad_maximum_fusion.1), channel_id=1, source_target_pairs={{0,128},{8,136},{16,144},{24,152},{32,160},{40,168},{48,176},{56,1... | collective-permute-start | bytes 1376264 | tf_op jit(solution)/shard_map/ppermute | solution.py:72
  28.5 5.4 %collective-permute-start.1 = (f32[224,512]{1,0:T(8,128)}, f32[224,512]{1,0:T(8,128)}, u32[]{:S(2)}, u32[]{:S(2)}) collective-permute-start(f32[224,512]{1,0:T(8,128)} %pad_maximum_fusion.1), channel_id=1, source_target_pairs={{0,256},{8,264},{16,272},{24,280},{32,288},{40,296},{48,304},{56,3... | collective-permute-start | bytes 1376264 | tf_op jit(solution)/shard_map/ppermute | solution.py:72
  33.9 5.1 %collective-permute-start = (f32[224,512]{1,0:T(8,128)}, f32[224,512]{1,0:T(8,128)}, u32[]{:S(2)}, u32[]{:S(2)}) collective-permute-start(f32[224,512]{1,0:T(8,128)} %pad_maximum_fusion.1), channel_id=1, source_target_pairs={{0,384},{8,392},{16,400},{24,408},{32,416},{40,424},{48,432},{56,4... | collective-permute-start | bytes 1376264 | tf_op jit(solution)/shard_map/ppermute | solution.py:72
  41.0 4.0 %collective-permute-start.4 = (f32[448,512]{1,0:T(8,128)S(1)}, f32[448,512]{1,0:T(8,128)}, u32[]{:S(2)}, u32[]{:S(2)}) collective-permute-start(f32[448,512]{1,0:T(8,128)S(1)} %pad_maximum_fusion), channel_id=1, source_target_pairs={{0,256},{8,264},{16,272},{24,280},{32,288},{40,296},{48,304},{56,3... | collective-permute-start | bytes 2752520 | tf_op jit(solution)/shard_map/ppermute | solution.py:72
  46.1 10.7 %all-to-all-start.1 = ((f32[64,8,256]{2,1,0:T(8,128)}), f32[64,8,256]{2,1,0:T(8,128)S(1)}, u32[]{:S(2)}, u32[]{:S(2)}) async-start(f32[64,8,256]{2,1,0:T(8,128)} %broadcast_in_dim.14), calls=%async_computation.1 | async-start | bytes 1048576 | tf_op jit(solution)/shard_map/all_to_all | solution.py:42
  56.8 5.2 %collective-permute-start.3 = (f32[448,512]{1,0:T(8,128)S(1)}, f32[448,512]{1,0:T(8,128)}, u32[]{:S(2)}, u32[]{:S(2)}) collective-permute-start(f32[448,512]{1,0:T(8,128)S(1)} %pad_maximum_fusion), channel_id=1, source_target_pairs={{0,384},{8,392},{16,400},{24,408},{32,416},{40,424},{48,432},{56,4... | collective-permute-start | bytes 2752520 | tf_op jit(solution)/shard_map/ppermute | solution.py:72
  63.1 10.5 %collective-permute-done.1 = f32[224,512]{1,0:T(8,128)} collective-permute-done((f32[224,512]{1,0:T(8,128)}, f32[224,512]{1,0:T(8,128)}, u32[]{:S(2)}, u32[]{:S(2)}) %collective-permute-start.1) | collective-permute-done | bytes 458784 | tf_op jit(solution)/shard_map/ppermute | solution.py:72
  76.1 42.4 %collective-permute-done = f32[224,512]{1,0:T(8,128)} collective-permute-done((f32[224,512]{1,0:T(8,128)}, f32[224,512]{1,0:T(8,128)}, u32[]{:S(2)}, u32[]{:S(2)}) %collective-permute-start) | collective-permute-done | bytes 458784 | tf_op jit(solution)/shard_map/ppermute | solution.py:72
  121.2 47.3 %all-to-all-done.1 = f32[64,8,256]{2,1,0:T(8,128)S(1)} async-done(((f32[64,8,256]{2,1,0:T(8,128)}), f32[64,8,256]{2,1,0:T(8,128)S(1)}, u32[]{:S(2)}, u32[]{:S(2)}) %all-to-all-start.1) | async-done | bytes 524320 | tf_op jit(solution)/shard_map/all_to_all | solution.py:42
  170.0 8.1 %all-to-all-start.2 = ((f32[8,64,256]{2,1,0:T(8,128)}), f32[8,64,256]{2,1,0:T(8,128)S(1)}, u32[]{:S(2)}, u32[]{:S(2)}) async-start(f32[8,64,256]{2,1,0:T(8,128)} %broadcast_in_dim.15), calls=%async_computation.2 | async-start | bytes 1048576 | tf_op jit(solution)/shard_map/all_to_all | solution.py:42
  181.8 5.7 %all-to-all-done.2 = f32[8,64,256]{2,1,0:T(8,128)S(1)} async-done(((f32[8,64,256]{2,1,0:T(8,128)}), f32[8,64,256]{2,1,0:T(8,128)S(1)}, u32[]{:S(2)}, u32[]{:S(2)}) %all-to-all-start.2) | async-done | bytes 524320 | tf_op jit(solution)/shard_map/all_to_all | solution.py:42
  188.7 4.0 %all-to-all-start.3 = ((f32[16,8,256]{2,1,0:T(8,128)}), f32[16,8,256]{2,1,0:T(8,128)S(1)}, u32[]{:S(2)}, u32[]{:S(2)}) async-start(f32[16,8,256]{2,1,0:T(8,128)} %bitcast.23), calls=%async_computation.3 | async-start | bytes 262144 | tf_op jit(solution)/shard_map/all_to_all | solution.py:42
  194.9 5.3 %all-to-all-done.3 = f32[16,8,256]{2,1,0:T(8,128)S(1)} async-done(((f32[16,8,256]{2,1,0:T(8,128)}), f32[16,8,256]{2,1,0:T(8,128)S(1)}, u32[]{:S(2)}, u32[]{:S(2)}) %all-to-all-start.3) | async-done | bytes 131104 | tf_op jit(solution)/shard_map/all_to_all | solution.py:42
  200.8 3.5 %all-to-all-start.4 = ((f32[16,8,256]{2,1,0:T(8,128)}), f32[16,8,256]{2,1,0:T(8,128)S(1)}, u32[]{:S(2)}, u32[]{:S(2)}) async-start(f32[16,8,256]{2,1,0:T(8,128)} %broadcast_in_dim.16), calls=%async_computation.4 | async-start | bytes 262144 | tf_op jit(solution)/shard_map/all_to_all | solution.py:42
  206.5 5.3 %all-to-all-done.4 = f32[16,8,256]{2,1,0:T(8,128)S(1)} async-done(((f32[16,8,256]{2,1,0:T(8,128)}), f32[16,8,256]{2,1,0:T(8,128)S(1)}, u32[]{:S(2)}, u32[]{:S(2)}) %all-to-all-start.4) | async-done | bytes 131104 | tf_op jit(solution)/shard_map/all_to_all | solution.py:42
  213.8 6.8 %all-to-all-start.5 = ((f32[8,64,256]{2,1,0:T(8,128)}), f32[8,64,256]{2,1,0:T(8,128)S(1)}, u32[]{:S(2)}, u32[]{:S(2)}) async-start(f32[8,64,256]{2,1,0:T(8,128)} %broadcast_in_dim.17), calls=%async_computation.5 | async-start | bytes 1048576 | tf_op jit(solution)/shard_map/all_to_all | solution.py:42
  221.1 9.0 %all-to-all-done.5 = f32[8,64,256]{2,1,0:T(8,128)S(1)} async-done(((f32[8,64,256]{2,1,0:T(8,128)}), f32[8,64,256]{2,1,0:T(8,128)S(1)}, u32[]{:S(2)}, u32[]{:S(2)}) %all-to-all-start.5) | async-done | bytes 524320 | tf_op jit(solution)/shard_map/all_to_all | solution.py:42
  231.3 3.6 %all-to-all-start.6 = ((f32[16,8,256]{2,1,0:T(8,128)}), f32[16,8,256]{2,1,0:T(8,128)S(1)}, u32[]{:S(2)}, u32[]{:S(2)}) async-start(f32[16,8,256]{2,1,0:T(8,128)} %bitcast.39), calls=%async_computation.6 | async-start | bytes 262144 | tf_op jit(solution)/shard_map/all_to_all | solution.py:42
  235.0 7.4 %all-to-all-done.6 = f32[16,8,256]{2,1,0:T(8,128)S(1)} async-done(((f32[16,8,256]{2,1,0:T(8,128)}), f32[16,8,256]{2,1,0:T(8,128)S(1)}, u32[]{:S(2)}, u32[]{:S(2)}) %all-to-all-start.6) | async-done | bytes 131104 | tf_op jit(solution)/shard_map/all_to_all | solution.py:42
  243.1 4.3 %all-to-all-start.7 = ((f32[16,8,256]{2,1,0:T(8,128)}), f32[16,8,256]{2,1,0:T(8,128)S(1)}, u32[]{:S(2)}, u32[]{:S(2)}) async-start(f32[16,8,256]{2,1,0:T(8,128)} %broadcast_in_dim.18), calls=%async_computation.7 | async-start | bytes 262144 | tf_op jit(solution)/shard_map/all_to_all | solution.py:42
  249.0 2.5 fusion.48
  251.4 3.3 all-to-all-done.7
  258.8 5.8 %all-to-all-start.8 = ((f32[8,64,256]{2,1,0:T(8,128)}), f32[8,64,256]{2,1,0:T(8,128)S(1)}, u32[]{:S(2)}, u32[]{:S(2)}) async-start(f32[8,64,256]{2,1,0:T(8,128)} %broadcast_in_dim.19), calls=%async_computation.8 | async-start | bytes 1048576 | tf_op jit(solution)/shard_map/all_to_all | solution.py:42
  276.6 3.0 collective-permute-start.6
  282.5 3.5 %all-to-all-start.9 = ((f32[16,8,256]{2,1,0:T(8,128)}), f32[16,8,256]{2,1,0:T(8,128)S(1)}, u32[]{:S(2)}, u32[]{:S(2)}) async-start(f32[16,8,256]{2,1,0:T(8,128)} %bitcast.54), calls=%async_computation.9 | async-start | bytes 262144 | tf_op jit(solution)/shard_map/all_to_all | solution.py:42
  286.7 4.5 %collective-permute-start.7 = (f32[2,64,512]{2,1,0:T(8,128)}, f32[2,64,512]{2,1,0:T(8,128)S(1)}, u32[]{:S(2)}, u32[]{:S(2)}) collective-permute-start(f32[2,64,512]{2,1,0:T(8,128)} %get-tuple-element.62), channel_id=1, source_target_pairs={{0,256},{8,264},{16,272},{24,280},{32,288},{40,296},{48,304},{56,3... | collective-permute-start | bytes 786440 | tf_op jit(solution)/shard_map/ppermute | solution.py:72
  296.3 9.1 %all-to-all-start.10 = ((f32[64,8,256]{2,1,0:T(8,128)}), f32[64,8,256]{2,1,0:T(8,128)S(1)}, u32[]{:S(2)}, u32[]{:S(2)}) async-start(f32[64,8,256]{2,1,0:T(8,128)} %broadcast_in_dim.20), calls=%async_computation.10 | async-start | bytes 1048576 | tf_op jit(solution)/shard_map/all_to_all | solution.py:42
  307.9 3.1 collective-permute-done.8
  317.2 15.2 %all-to-all-done.10 = f32[64,8,256]{2,1,0:T(8,128)S(1)} async-done(((f32[64,8,256]{2,1,0:T(8,128)}), f32[64,8,256]{2,1,0:T(8,128)S(1)}, u32[]{:S(2)}, u32[]{:S(2)}) %all-to-all-start.10) | async-done | bytes 524320 | tf_op jit(solution)/shard_map/all_to_all | solution.py:42
  335.4 5.5 %all-to-all-start.11 = ((f32[8,32,256]{2,1,0:T(8,128)}), f32[8,32,256]{2,1,0:T(8,128)S(1)}, u32[]{:S(2)}, u32[]{:S(2)}) async-start(f32[8,32,256]{2,1,0:T(8,128)} %bitcast.70), calls=%async_computation.11 | async-start | bytes 524288 | tf_op jit(solution)/shard_map/all_to_all | solution.py:42
  341.6 5.8 %all-to-all-done.11 = f32[8,32,256]{2,1,0:T(8,128)S(1)} async-done(((f32[8,32,256]{2,1,0:T(8,128)}), f32[8,32,256]{2,1,0:T(8,128)S(1)}, u32[]{:S(2)}, u32[]{:S(2)}) %all-to-all-start.11) | async-done | bytes 262176 | tf_op jit(solution)/shard_map/all_to_all | solution.py:42
  (138 shorter events, 70.8 us)
Async XLA Ops:
  0.6 22.3 %slice-start.1 = ((f32[8,64,256]{2,1,0:T(8,128)}), f32[3,64,256]{2,1,0:T(8,128)S(1)}, s32[]{:S(2)}) async-start(f32[8,64,256]{2,1,0:T(8,128)} %param.4), calls=%async_computation.13 | async-start | bytes 393216 | tf_op jit(solution)/shard_map/slice | solution.py:78
  0.6 22.3 %copy-start = (f32[6,64,512]{2,1,0:T(8,128)S(1)}, f32[6,64,512]{2,1,0:T(8,128)}, u32[]{:S(2)}) copy-start(f32[6,64,512]{2,1,0:T(8,128)} %param.6) | copy-start | bytes 2359300
  5.6 33.4 %copy-start.2 = (f32[4,512,64]{1,2,0:T(8,128)S(1)}, f32[4,512,64]{1,2,0:T(8,128)}, u32[]{:S(2)}) copy-start(f32[4,512,64]{1,2,0:T(8,128)} %param.5) | copy-start | bytes 1572868
  5.6 39.5 %all-to-all-start = ((f32[64,8,256]{2,1,0:T(8,128)}), f32[64,8,256]{2,1,0:T(8,128)S(1)}, u32[]{:S(2)}, u32[]{:S(2)}) async-start(f32[64,8,256]{2,1,0:T(8,128)} %bitcast.10), calls=%async_computation | async-start | bytes 1048576 | tf_op jit(solution)/shard_map/all_to_all | solution.py:42
  24.7 32.2 %collective-permute-start.2 = (f32[224,512]{1,0:T(8,128)}, f32[224,512]{1,0:T(8,128)}, u32[]{:S(2)}, u32[]{:S(2)}) collective-permute-start(f32[224,512]{1,0:T(8,128)} %pad_maximum_fusion.1), channel_id=1, source_target_pairs={{0,128},{8,136},{16,144},{24,152},{32,160},{40,168},{48,176},{56,1... | collective-permute-start | bytes 1376264 | tf_op jit(solution)/shard_map/ppermute | solution.py:72
  28.5 45.1 %collective-permute-start.1 = (f32[224,512]{1,0:T(8,128)}, f32[224,512]{1,0:T(8,128)}, u32[]{:S(2)}, u32[]{:S(2)}) collective-permute-start(f32[224,512]{1,0:T(8,128)} %pad_maximum_fusion.1), channel_id=1, source_target_pairs={{0,256},{8,264},{16,272},{24,280},{32,288},{40,296},{48,304},{56,3... | collective-permute-start | bytes 1376264 | tf_op jit(solution)/shard_map/ppermute | solution.py:72
  33.9 84.6 %collective-permute-start = (f32[224,512]{1,0:T(8,128)}, f32[224,512]{1,0:T(8,128)}, u32[]{:S(2)}, u32[]{:S(2)}) collective-permute-start(f32[224,512]{1,0:T(8,128)} %pad_maximum_fusion.1), channel_id=1, source_target_pairs={{0,384},{8,392},{16,400},{24,408},{32,416},{40,424},{48,432},{56,4... | collective-permute-start | bytes 1376264 | tf_op jit(solution)/shard_map/ppermute | solution.py:72
  39.1 140.6 %collective-permute-start.5 = (f32[448,512]{1,0:T(8,128)S(1)}, f32[448,512]{1,0:T(8,128)}, u32[]{:S(2)}, u32[]{:S(2)}) collective-permute-start(f32[448,512]{1,0:T(8,128)S(1)} %pad_maximum_fusion), channel_id=1, source_target_pairs={{0,128},{8,136},{16,144},{24,152},{32,160},{40,168},{48,176},{56,1... | collective-permute-start | bytes 2752520 | tf_op jit(solution)/shard_map/ppermute | solution.py:72
  41.0 151.7 %collective-permute-start.4 = (f32[448,512]{1,0:T(8,128)S(1)}, f32[448,512]{1,0:T(8,128)}, u32[]{:S(2)}, u32[]{:S(2)}) collective-permute-start(f32[448,512]{1,0:T(8,128)S(1)} %pad_maximum_fusion), channel_id=1, source_target_pairs={{0,256},{8,264},{16,272},{24,280},{32,288},{40,296},{48,304},{56,3... | collective-permute-start | bytes 2752520 | tf_op jit(solution)/shard_map/ppermute | solution.py:72
  46.1 122.5 %all-to-all-start.1 = ((f32[64,8,256]{2,1,0:T(8,128)}), f32[64,8,256]{2,1,0:T(8,128)S(1)}, u32[]{:S(2)}, u32[]{:S(2)}) async-start(f32[64,8,256]{2,1,0:T(8,128)} %broadcast_in_dim.14), calls=%async_computation.1 | async-start | bytes 1048576 | tf_op jit(solution)/shard_map/all_to_all | solution.py:42
  56.8 147.5 %collective-permute-start.3 = (f32[448,512]{1,0:T(8,128)S(1)}, f32[448,512]{1,0:T(8,128)}, u32[]{:S(2)}, u32[]{:S(2)}) collective-permute-start(f32[448,512]{1,0:T(8,128)S(1)} %pad_maximum_fusion), channel_id=1, source_target_pairs={{0,384},{8,392},{16,400},{24,408},{32,416},{40,424},{48,432},{56,4... | collective-permute-start | bytes 2752520 | tf_op jit(solution)/shard_map/ppermute | solution.py:72
  170.0 17.6 %all-to-all-start.2 = ((f32[8,64,256]{2,1,0:T(8,128)}), f32[8,64,256]{2,1,0:T(8,128)S(1)}, u32[]{:S(2)}, u32[]{:S(2)}) async-start(f32[8,64,256]{2,1,0:T(8,128)} %broadcast_in_dim.15), calls=%async_computation.2 | async-start | bytes 1048576 | tf_op jit(solution)/shard_map/all_to_all | solution.py:42
  188.7 11.5 %all-to-all-start.3 = ((f32[16,8,256]{2,1,0:T(8,128)}), f32[16,8,256]{2,1,0:T(8,128)S(1)}, u32[]{:S(2)}, u32[]{:S(2)}) async-start(f32[16,8,256]{2,1,0:T(8,128)} %bitcast.23), calls=%async_computation.3 | async-start | bytes 262144 | tf_op jit(solution)/shard_map/all_to_all | solution.py:42
  192.7 19.0 %copy-start.13 = (f32[64,512]{1,0:T(8,128)S(1)}, f32[64,512]{1,0:T(8,128)}, u32[]{:S(2)}) copy-start(f32[64,512]{1,0:T(8,128)} %get-tuple-element.31) | copy-start | bytes 393220
  200.8 10.9 %all-to-all-start.4 = ((f32[16,8,256]{2,1,0:T(8,128)}), f32[16,8,256]{2,1,0:T(8,128)S(1)}, u32[]{:S(2)}, u32[]{:S(2)}) async-start(f32[16,8,256]{2,1,0:T(8,128)} %broadcast_in_dim.16), calls=%async_computation.4 | async-start | bytes 262144 | tf_op jit(solution)/shard_map/all_to_all | solution.py:42
  213.8 16.3 %all-to-all-start.5 = ((f32[8,64,256]{2,1,0:T(8,128)}), f32[8,64,256]{2,1,0:T(8,128)S(1)}, u32[]{:S(2)}, u32[]{:S(2)}) async-start(f32[8,64,256]{2,1,0:T(8,128)} %broadcast_in_dim.17), calls=%async_computation.5 | async-start | bytes 1048576 | tf_op jit(solution)/shard_map/all_to_all | solution.py:42
  220.8 26.6 %slice-start.2 = ((f32[8,64,256]{2,1,0:T(8,128)}), f32[4,64,256]{2,1,0:T(8,128)S(1)}, s32[]{:S(2)}) async-start(f32[8,64,256]{2,1,0:T(8,128)} %param.4), calls=%async_computation.14 | async-start | bytes 524288 | tf_op jit(solution)/shard_map/slice | solution.py:144
  220.9 27.3 %copy-start.6 = (f32[1,64,256]{2,1,0:T(8,128)S(1)}, f32[1,64,256]{2,1,0:T(8,128)}, u32[]{:S(2)}) copy-start(f32[1,64,256]{2,1,0:T(8,128)} %get-tuple-element.39) | copy-start | bytes 196612
  230.2 24.6 %copy-start.9 = (f32[64,512]{1,0:T(8,128)S(1)}, f32[64,512]{1,0:T(8,128)}, u32[]{:S(2)}) copy-start(f32[64,512]{1,0:T(8,128)} %get-tuple-element.28) | copy-start | bytes 393220
  231.3 23.4 %copy-start.11 = (f32[64,512]{1,0:T(8,128)S(1)}, f32[64,512]{1,0:T(8,128)}, u32[]{:S(2)}) copy-start(f32[64,512]{1,0:T(8,128)} %get-tuple-element.21) | copy-start | bytes 393220
  231.3 25.0 %copy-start.8 = (f32[64,512]{1,0:T(8,128)S(1)}, f32[64,512]{1,0:T(8,128)}, u32[]{:S(2)}) copy-start(f32[64,512]{1,0:T(8,128)} %get-tuple-element.26) | copy-start | bytes 393220
  231.3 25.0 %copy-start.10 = (f32[64,512]{1,0:T(8,128)S(1)}, f32[64,512]{1,0:T(8,128)}, u32[]{:S(2)}) copy-start(f32[64,512]{1,0:T(8,128)} %get-tuple-element.19) | copy-start | bytes 393220
  231.3 11.0 %all-to-all-start.6 = ((f32[16,8,256]{2,1,0:T(8,128)}), f32[16,8,256]{2,1,0:T(8,128)S(1)}, u32[]{:S(2)}, u32[]{:S(2)}) async-start(f32[16,8,256]{2,1,0:T(8,128)} %bitcast.39), calls=%async_computation.6 | async-start | bytes 262144 | tf_op jit(solution)/shard_map/all_to_all | solution.py:42
  243.1 11.7 %all-to-all-start.7 = ((f32[16,8,256]{2,1,0:T(8,128)}), f32[16,8,256]{2,1,0:T(8,128)S(1)}, u32[]{:S(2)}, u32[]{:S(2)}) async-start(f32[16,8,256]{2,1,0:T(8,128)} %broadcast_in_dim.18), calls=%async_computation.7 | async-start | bytes 262144 | tf_op jit(solution)/shard_map/all_to_all | solution.py:42
  258.8 20.8 %all-to-all-start.8 = ((f32[8,64,256]{2,1,0:T(8,128)}), f32[8,64,256]{2,1,0:T(8,128)S(1)}, u32[]{:S(2)}, u32[]{:S(2)}) async-start(f32[8,64,256]{2,1,0:T(8,128)} %broadcast_in_dim.19), calls=%async_computation.8 | async-start | bytes 1048576 | tf_op jit(solution)/shard_map/all_to_all | solution.py:42
  276.6 28.9 %collective-permute-start.6 = (f32[2,64,512]{2,1,0:T(8,128)}, f32[2,64,512]{2,1,0:T(8,128)}, u32[]{:S(2)}, u32[]{:S(2)}) collective-permute-start(f32[2,64,512]{2,1,0:T(8,128)} %get-tuple-element.62), channel_id=1, source_target_pairs={{0,384},{8,392},{16,400},{24,408},{32,416},{40,424},{48,432},{56,4... | collective-permute-start | bytes 786440 | tf_op jit(solution)/shard_map/ppermute | solution.py:72
  282.5 13.0 %all-to-all-start.9 = ((f32[16,8,256]{2,1,0:T(8,128)}), f32[16,8,256]{2,1,0:T(8,128)S(1)}, u32[]{:S(2)}, u32[]{:S(2)}) async-start(f32[16,8,256]{2,1,0:T(8,128)} %bitcast.54), calls=%async_computation.9 | async-start | bytes 262144 | tf_op jit(solution)/shard_map/all_to_all | solution.py:42
  286.7 20.5 %collective-permute-start.7 = (f32[2,64,512]{2,1,0:T(8,128)}, f32[2,64,512]{2,1,0:T(8,128)S(1)}, u32[]{:S(2)}, u32[]{:S(2)}) collective-permute-start(f32[2,64,512]{2,1,0:T(8,128)} %get-tuple-element.62), channel_id=1, source_target_pairs={{0,256},{8,264},{16,272},{24,280},{32,288},{40,296},{48,304},{56,3... | collective-permute-start | bytes 786440 | tf_op jit(solution)/shard_map/ppermute | solution.py:72
  291.1 19.8 %collective-permute-start.8 = (f32[2,64,512]{2,1,0:T(8,128)}, f32[2,64,512]{2,1,0:T(8,128)S(1)}, u32[]{:S(2)}, u32[]{:S(2)}) collective-permute-start(f32[2,64,512]{2,1,0:T(8,128)} %get-tuple-element.62), channel_id=1, source_target_pairs={{0,128},{8,136},{16,144},{24,152},{32,160},{40,168},{48,176},{56,1... | collective-permute-start | bytes 786440 | tf_op jit(solution)/shard_map/ppermute | solution.py:72
  296.3 36.1 %all-to-all-start.10 = ((f32[64,8,256]{2,1,0:T(8,128)}), f32[64,8,256]{2,1,0:T(8,128)S(1)}, u32[]{:S(2)}, u32[]{:S(2)}) async-start(f32[64,8,256]{2,1,0:T(8,128)} %broadcast_in_dim.20), calls=%async_computation.10 | async-start | bytes 1048576 | tf_op jit(solution)/shard_map/all_to_all | solution.py:42
  317.1 30.4 %copy-start.4 = (f32[4,64,32]{1,0,2:T(4,128)S(1)}, f32[4,64,32]{1,0,2:T(4,128)}, u32[]{:S(2)}) copy-start(f32[4,64,32]{1,0,2:T(4,128)} %copy.52) | copy-start | bytes 98308
  335.4 12.1 %all-to-all-start.11 = ((f32[8,32,256]{2,1,0:T(8,128)}), f32[8,32,256]{2,1,0:T(8,128)S(1)}, u32[]{:S(2)}, u32[]{:S(2)}) async-start(f32[8,32,256]{2,1,0:T(8,128)} %bitcast.70), calls=%async_computation.11 | async-start | bytes 524288 | tf_op jit(solution)/shard_map/all_to_all | solution.py:42
  (8 other events, 126.8 us)

commit v3 on v1

v3 whole, which is shorter than its diff:
```python
import jax
import jax.numpy as jnp
from jax import lax
from jax.sharding import PartitionSpec as P

HIGHEST_PREC = lax.Precision.HIGHEST
Z_SIZE = 8


def pair_index(block_row, prior_row):
    return block_row * (block_row - 1) // 2 + prior_row


def times(left, right):
    return jnp.dot(left, right, precision=HIGHEST_PREC, preferred_element_type=jnp.float32)


def swap(parts, axis, groups=None):
    return lax.all_to_all(parts, axis, 0, 0, axis_index_groups=groups, tiled=True)


def copies(part, count):
    return jnp.broadcast_to(part[None], (count,) + part.shape)


def reduce_scatter(value, axis, count, groups=None):
    parts = value.reshape((count, value.shape[0] // count) + value.shape[1:])
    return swap(parts, axis, groups).sum(0)


def replicate(part, axis, count, groups=None):
    parts = swap(copies(part, count), axis, groups)
    return parts.reshape((-1,) + part.shape[1:])


def shards(right_sides, diag_inverse, lower_blocks, trail_panel):
    step_count = diag_inverse.shape[0]
    trail_count = trail_panel.shape[0]
    local_rows = right_sides.shape[1]
    column_count = right_sides.shape[2]
    row_size = lax.axis_size("row")
    col_size = lax.axis_size("col")
    members = row_size // 2
    half = column_count // 2
    row = lax.axis_index("row")
    group = row // Z_SIZE % 2
    groups = [[r for r in range(row_size) if r // Z_SIZE % 2 == g] for g in range(2)]
    partners = [(r, r + Z_SIZE if r // Z_SIZE % 2 == 0 else r - Z_SIZE) for r in range(row_size)]

    def from_partner(value):
        return lax.ppermute(value, "row", partners)

    def half_of(value, which):
        return lax.dynamic_slice_in_dim(value, which * half, half, value.ndim - 1)

    own_diag = diag_inverse.transpose(0, 2, 1)
    later_sides = right_sides[1:step_count]
    got_sides = from_partner(half_of(later_sides, 1 - group))
    first = from_partner(jnp.stack([lower_blocks[0], own_diag[1]]))
    second = from_partner(jnp.concatenate([lower_blocks[1:], own_diag[2:]]))
    got_lower = [first[0]] + [second[i] for i in range(lower_blocks.shape[0] - 1)]
    got_diag = [None, first[1]] + [
        second[lower_blocks.shape[0] - 1 + i] for i in range(step_count - 2)
    ]
    own_sides_half = half_of(later_sides, group)

    part = reduce_scatter(times(diag_inverse[0], right_sides[0]), "row", row_size)
    whole = replicate(part, "row", row_size)
    solved = [whole]
    halves = [half_of(whole, group)]

    for block_row in range(1, step_count):
        update = None
        for prior_row in range(block_row):
            index = pair_index(block_row, prior_row)
            term = jnp.stack(
                [
                    times(lower_blocks[index], halves[prior_row]),
                    times(got_lower[index], halves[prior_row]),
                ]
            )
            update = term if update is None else update + term
        total = swap(copies(update, col_size), "col").sum(0)
        current = own_sides_half[block_row - 1] - total[0]
        partner_current = got_sides[block_row - 1] - total[1]
        partial_value = times(diag_inverse[block_row], current) + times(
            got_diag[block_row].T, partner_current
        )
        part = reduce_scatter(partial_value, "row", members, groups)
        if block_row < step_count - 1:
            solved_half = replicate(part, "row", members, groups)
            halves.append(solved_half)
            other = from_partner(solved_half)
            solved.append(
                jnp.concatenate(
                    [
                        jnp.where(group == 0, solved_half, other),
                        jnp.where(group == 0, other, solved_half),
                    ],
                    1,
                )
            )
        else:
            parts = swap(copies(part, row_size), "row")
            parts = parts.reshape((-1, 2, Z_SIZE) + part.shape)
            solved.append(parts.transpose(0, 2, 3, 1, 4).reshape(-1, column_count))

    trail_acc = None
    for block_row in range(step_count):
        contrib = jnp.einsum(
            "nc,mrn->cmr",
            solved[block_row],
            trail_panel[:, :, block_row, :],
            precision=HIGHEST_PREC,
        )
        trail_acc = contrib if trail_acc is None else trail_acc + contrib
    shared = reduce_scatter(trail_acc.reshape(column_count, -1), "col", col_size)
    own_width = shared.shape[0]
    shared = shared.reshape(own_width, trail_count, local_rows).transpose(1, 2, 0)
    own_sides = lax.dynamic_slice_in_dim(
        right_sides[step_count:], lax.axis_index("col") * own_width, own_width, 2
    )
    trail_rest = own_sides - shared
    out_width = column_count // row_size
    outs = [lax.dynamic_slice_in_dim(s, row * out_width, out_width, 1) for s in solved]
    return (jnp.stack(outs), trail_rest)


def solution(mesh):
    placed = (
        P(None, "row", None),
        P(None, "col", "row"),
        P(None, "row", "col"),
        P(None, "row", None, "col"),
    )
    return jax.shard_map(
        shards,
        mesh=mesh,
        in_specs=placed,
        out_specs=(P(None, "col", "row"), P(None, "row", "col")),
        check_vma=False,
    )
```

time: 272 us -> 272 us (level)
  blocking collectives: 150 us -> 75.2 us
  starting transfers between devices: 35.8 us -> 79.1 us
  waiting for transfers between devices: 59.2 us -> 75.1 us
  matrix products: 10.9 us -> 19.2 us
  other arithmetic: 0.77 us -> 4.49 us
    all_to_all x7 -> x3, blocking collectives: 150 us -> 75.2 us  [swap(): lax.all_to_all(parts, axis, 0, 0, axis_index_groups=groups, tiled=True)]
    all_to_all x5 -> x9, starting transfers between devices: 35.8 us -> 65.6 us  [swap(): lax.all_to_all(parts, axis, 0, 0, axis_index_groups=groups, tiled=True)]
    all_to_all x5 -> x9, waiting for transfers between devices: 59.2 us -> 73.8 us  [swap(): lax.all_to_all(parts, axis, 0, 0, axis_index_groups=groups, tiled=True)]
    ppermute x0 -> x5, starting transfers between devices: none -> 13.5 us  [from_partner(): return lax.ppermute(value, 'row', partners)]
    dot_general x14 -> x23, matrix products: 10.9 us -> 19.2 us  [the longest x19 15.6 us: times(): jnp.dot(left, right, precision=HIGHEST_PREC, preferred_element_type=jnp.f...]
    broadcast_in_dim x7, local copies, waits for them, and re-layouts: 2.63 us -> 5.73 us  [copies(): return jnp.broadcast_to(part[None], (count,) + part.shape)]
    slice x1, local copies, waits for them, and re-layouts: 5.87 us -> 2.79 us  [shards(): trail_panel[:, :, block_row, :]]
  transfers between devices with their start and end apart: 5 -> 14, of which waited for: 5 -> 10; matrix products, arithmetic and copies ran while one was open for 4% -> 7% of each run, Pallas kernels for 0% -> 0%
where the time goes in v3:
time: 272 us; the launch traced here: 271 us
  starting transfers between devices  79.1 us (29%)
  blocking collectives  75.2 us (28%)
  waiting for transfers between devices  75.1 us (28%)
  matrix products  19.2 us (7%)
  local copies, waits for them, and re-layouts  16.4 us (6%)
  other arithmetic  4.49 us (2%)
    all_to_all x3, blocking collectives, swap(): lax.all_to_all(parts, axis, 0, 0, axis_index_groups=groups, tiled=True)  75.2 us
    all_to_all x9, waiting for transfers between devices, swap(): lax.all_to_all(parts, axis, 0, 0, axis_index_groups=groups, tiled=True)  73.8 us
    all_to_all x9, starting transfers between devices, swap(): lax.all_to_all(parts, axis, 0, 0, axis_index_groups=groups, tiled=True)  65.6 us
    dot_general x19, matrix products, times(): jnp.dot(left, right, precision=HIGHEST_PREC, preferred_element_type=jnp.f...  15.6 us
    ppermute x5, starting transfers between devices, from_partner(): return lax.ppermute(value, 'row', partners)  13.5 us
    broadcast_in_dim x7, local copies, waits for them, and re-layouts, copies(): return jnp.broadcast_to(part[None], (count,) + part.shape)  5.73 us
  transfers between devices with their start and end apart: 14, of which 10 were waited for; matrix products, arithmetic and copies ran while one was open for 7% of the time, Pallas kernels for 0%

profile of v3, /device:TPU:1, one launch (start us, length us, event | category | flops | bytes accessed | tf_op | source)
XLA Modules:
  0.0 270.8 jit_solution(7756852707912165655)
XLA Ops:
  1.7 1.5 fusion.8
  3.2 33.4 %all_to_all.60 = f32[64,8,256]{2,1,0:T(8,128)S(1)} all-to-all(f32[64,8,256]{2,1,0:T(8,128)S(1)} %fusion.8), channel_id=1, replica_groups=mesh['row'=64,'col'=8] {'row'}, dimensions={0} | all-to-all | bytes 1048576 | tf_op jit(solution)/shard_map/all_to_all | solution.py:19
  37.5 7.8 %all-to-all-start.1 = ((f32[64,8,256]{2,1,0:T(8,128)}), f32[64,8,256]{2,1,0:T(8,128)S(1)}, u32[]{:S(2)}, u32[]{:S(2)}) async-start(f32[64,8,256]{2,1,0:T(8,128)} %broadcast_in_dim.14), calls=%async_computation.1 | async-start | bytes 1048576 | tf_op jit(solution)/shard_map/all_to_all | solution.py:19
  45.4 2.9 %collective-permute-start = (f32[2,64,512]{2,1,0:T(8,128)S(1)}, f32[2,64,512]{2,1,0:T(8,128)S(1)}, u32[]{:S(2)}, u32[]{:S(2)}) collective-permute-start(f32[2,64,512]{2,1,0:T(8,128)S(1)} %pad_maximum_fusion.3), channel_id=1, source_target_pairs={{0,64},{8,72},{16,80},{24,88},{32,96},{40,104},{48,112},{56,120},{... | collective-permute-start | bytes 786440 | tf_op jit(solution)/shard_map/ppermute | solution.py:51
  48.3 12.9 %all-to-all-done.1 = f32[64,8,256]{2,1,0:T(8,128)S(1)} async-done(((f32[64,8,256]{2,1,0:T(8,128)}), f32[64,8,256]{2,1,0:T(8,128)S(1)}, u32[]{:S(2)}, u32[]{:S(2)}) %all-to-all-start.1) | async-done | bytes 524320 | tf_op jit(solution)/shard_map/all_to_all | solution.py:19
  64.0 8.2 %all-to-all-start.2 = ((f32[8,2,64,128]{3,2,1,0:T(8,128)}), f32[8,2,64,128]{3,2,1,0:T(8,128)S(1)}, u32[]{:S(2)}, u32[]{:S(2)}) async-start(f32[8,2,64,128]{3,2,1,0:T(8,128)} %broadcast_in_dim.15), calls=%async_computation.2 | async-start | bytes 1048576 | tf_op jit(solution)/shard_map/all_to_all | solution.py:19
  73.2 2.8 %collective-permute-start.1 = (f32[3,64,128]{2,1,0:T(8,128)S(1)}, f32[3,64,128]{2,1,0:T(8,128)S(1)}, u32[]{:S(2)}, u32[]{:S(2)}) collective-permute-start(f32[3,64,128]{2,1,0:T(8,128)S(1)} %constant_dynamic-slice_fusion.2), channel_id=1, source_target_pairs={{0,64},{8,72},{16,80},{24,88},{32,96},{40,104},{48,112},{56,120},{... | collective-permute-start | bytes 294920 | tf_op jit(solution)/shard_map/ppermute | solution.py:51
  77.0 2.5 collective-permute-start.3
  79.5 2.1 all-to-all-done.2
  82.2 1.4 convolution_add_fusion.2
  83.7 26.0 %all_to_all.61 = f32[32,16,128]{2,1,0:T(8,128)S(1)} all-to-all(f32[32,16,128]{2,1,0:T(8,128)S(1)} %bitcast.196), channel_id=1, replica_groups={{0,8,16,24,32,40,48,56,128,136,144,152,160,168,176,184,256,264,272,280,..., dimensions={0} | all-to-all | bytes 524288 | tf_op jit(solution)/shard_map/all_to_all | solution.py:19
  110.5 5.9 %all-to-all-start.4 = ((f32[32,16,128]{2,1,0:T(8,128)}), f32[32,16,128]{2,1,0:T(8,128)S(1)}, u32[]{:S(2)}, u32[]{:S(2)}) async-start(f32[32,16,128]{2,1,0:T(8,128)} %broadcast_in_dim.16), calls=%async_computation.4 | async-start | bytes 524288 | tf_op jit(solution)/shard_map/all_to_all | solution.py:19
  117.9 10.7 %all-to-all-done.4 = f32[32,16,128]{2,1,0:T(8,128)S(1)} async-done(((f32[32,16,128]{2,1,0:T(8,128)}), f32[32,16,128]{2,1,0:T(8,128)S(1)}, u32[]{:S(2)}, u32[]{:S(2)}) %all-to-all-start.4) | async-done | bytes 262176 | tf_op jit(solution)/shard_map/all_to_all | solution.py:19
  131.0 7.9 %all-to-all-start.5 = ((f32[8,2,64,128]{3,2,1,0:T(8,128)}), f32[8,2,64,128]{3,2,1,0:T(8,128)S(1)}, u32[]{:S(2)}, u32[]{:S(2)}) async-start(f32[8,2,64,128]{3,2,1,0:T(8,128)} %broadcast_in_dim.17), calls=%async_computation.5 | async-start | bytes 1048576 | tf_op jit(solution)/shard_map/all_to_all | solution.py:19
  138.9 9.5 %all-to-all-done.5 = f32[8,2,64,128]{3,2,1,0:T(8,128)S(1)} async-done(((f32[8,2,64,128]{3,2,1,0:T(8,128)}), f32[8,2,64,128]{3,2,1,0:T(8,128)S(1)}, u32[]{:S(2)}, u32[]{:S(2)}) %all-to-all-start.5) | async-done | bytes 524320 | tf_op jit(solution)/shard_map/all_to_all | solution.py:19
  150.3 15.8 %all_to_all.62 = f32[32,16,128]{2,1,0:T(8,128)S(1)} all-to-all(f32[32,16,128]{2,1,0:T(8,128)S(1)} %bitcast.197), channel_id=1, replica_groups={{0,8,16,24,32,40,48,56,128,136,144,152,160,168,176,184,256,264,272,280,..., dimensions={0} | all-to-all | bytes 524288 | tf_op jit(solution)/shard_map/all_to_all | solution.py:19
  166.9 6.0 %all-to-all-start.7 = ((f32[32,16,128]{2,1,0:T(8,128)}), f32[32,16,128]{2,1,0:T(8,128)S(1)}, u32[]{:S(2)}, u32[]{:S(2)}) async-start(f32[32,16,128]{2,1,0:T(8,128)} %broadcast_in_dim.18), calls=%async_computation.7 | async-start | bytes 524288 | tf_op jit(solution)/shard_map/all_to_all | solution.py:19
  175.9 9.7 %all-to-all-done.7 = f32[32,16,128]{2,1,0:T(8,128)S(1)} async-done(((f32[32,16,128]{2,1,0:T(8,128)}), f32[32,16,128]{2,1,0:T(8,128)S(1)}, u32[]{:S(2)}, u32[]{:S(2)}) %all-to-all-start.7) | async-done | bytes 262176 | tf_op jit(solution)/shard_map/all_to_all | solution.py:19
  187.9 6.4 %all-to-all-start.8 = ((f32[8,2,64,128]{3,2,1,0:T(8,128)}), f32[8,2,64,128]{3,2,1,0:T(8,128)}, u32[]{:S(2)}, u32[]{:S(2)}) async-start(f32[8,2,64,128]{3,2,1,0:T(8,128)} %broadcast_in_dim.19), calls=%async_computation.8 | async-start | bytes 1048576 | tf_op jit(solution)/shard_map/all_to_all | solution.py:19
  194.3 9.6 %all-to-all-done.8 = f32[8,2,64,128]{3,2,1,0:T(8,128)} async-done(((f32[8,2,64,128]{3,2,1,0:T(8,128)}), f32[8,2,64,128]{3,2,1,0:T(8,128)}, u32[]{:S(2)}, u32[]{:S(2)}) %all-to-all-start.8) | async-done | bytes 524320 | tf_op jit(solution)/shard_map/all_to_all | solution.py:19
  205.0 1.3 convolution_bitcast_fusion
  206.3 1.3 convolution_add_fusion
  208.5 4.4 %all-to-all-start.9 = ((f32[32,16,128]{2,1,0:T(8,128)}), f32[32,16,128]{2,1,0:T(8,128)S(1)}, u32[]{:S(2)}, u32[]{:S(2)}) async-start(f32[32,16,128]{2,1,0:T(8,128)} %bitcast.195), calls=%async_computation.9 | async-start | bytes 524288 | tf_op jit(solution)/shard_map/all_to_all | solution.py:19
  213.0 2.8 %fusion.66 = (f32[4,64,1,512]{3,2,1,0:T(1,128)}, f32[4,64,1,512]{3,2,1,0:T(1,128)}, f32[4,64,1,512]{3,2,1,0:T(1,128)}, f32[4,64,1,512]{3,2,1,0:T(1,128)}) fusion(f32[4,64,4,512]{3,2,1,0:T(4,128)S(1)} %copy-done.1), kind=kLoop, calls=%fused_computation.120 | loop fusion | bytes 4194304 | tf_op jit(solution)/shard_map/slice | solution.py:113
  216.7 2.9 %collective-permute-start.2 = (f32[512,128]{1,0:T(8,128)S(1)}, f32[512,128]{1,0:T(8,128)S(1)}, u32[]{:S(2)}, u32[]{:S(2)}) collective-permute-start(f32[512,128]{1,0:T(8,128)S(1)} %bitcast.186), channel_id=1, source_target_pairs={{0,64},{8,72},{16,80},{24,88},{32,96},{40,104},{48,112},{56,120},{... | collective-permute-start | bytes 786440 | tf_op jit(solution)/shard_map/ppermute | solution.py:51
  219.9 1.7 fusion.4
  221.6 2.3 collective-permute-start.4
  224.0 1.4 all-to-all-done.9
  226.2 10.7 %all-to-all-start.10 = ((f32[64,16,128]{2,1,0:T(8,128)}), f32[64,16,128]{2,1,0:T(8,128)S(1)}, u32[]{:S(2)}, u32[]{:S(2)}) async-start(f32[64,16,128]{2,1,0:T(8,128)} %broadcast_in_dim.20), calls=%async_computation.10 | async-start | bytes 1048576 | tf_op jit(solution)/shard_map/all_to_all | solution.py:19
  239.9 12.5 %all-to-all-done.10 = f32[64,16,128]{2,1,0:T(8,128)S(1)} async-done(((f32[64,16,128]{2,1,0:T(8,128)}), f32[64,16,128]{2,1,0:T(8,128)S(1)}, u32[]{:S(2)}, u32[]{:S(2)}) %all-to-all-start.10) | async-done | bytes 524320 | tf_op jit(solution)/shard_map/all_to_all | solution.py:19
  255.2 8.3 %all-to-all-start.11 = ((f32[8,32,256]{2,1,0:T(8,128)}), f32[8,32,256]{2,1,0:T(8,128)S(1)}, u32[]{:S(2)}, u32[]{:S(2)}) async-start(f32[8,32,256]{2,1,0:T(8,128)} %reshape_reshape.3), calls=%async_computation.11 | async-start | bytes 524288 | tf_op jit(solution)/shard_map/all_to_all | solution.py:19
  264.6 5.5 %all-to-all-done.11 = f32[8,32,256]{2,1,0:T(8,128)S(1)} async-done(((f32[8,32,256]{2,1,0:T(8,128)}), f32[8,32,256]{2,1,0:T(8,128)S(1)}, u32[]{:S(2)}, u32[]{:S(2)}) %all-to-all-start.11) | async-done | bytes 262176 | tf_op jit(solution)/shard_map/all_to_all | solution.py:19
  (92 shorter events, 31.4 us)
Async XLA Ops:
  1.7 43.6 %copy-start.5 = (f32[4,512,64]{1,2,0:T(8,128)S(1)}, f32[4,512,64]{1,2,0:T(8,128)}, u32[]{:S(2)}) copy-start(f32[4,512,64]{1,2,0:T(8,128)} %param.5) | copy-start | bytes 1572868
  1.7 43.7 %slice-start = ((f32[6,64,512]{2,1,0:T(8,128)}), f32[1,64,512]{2,1,0:T(8,128)S(1)}, s32[]{:S(2)}) async-start(f32[6,64,512]{2,1,0:T(8,128)} %param.6), calls=%async_computation.12 | async-start | bytes 262144 | tf_op jit(solution)/shard_map/slice | solution.py:78
  3.2 58.1 %copy-start = (f32[6,64,512]{2,1,0:T(8,128)S(1)}, f32[6,64,512]{2,1,0:T(8,128)}, u32[]{:S(2)}) copy-start(f32[6,64,512]{2,1,0:T(8,128)} %param.6) | copy-start | bytes 2359300
  37.5 23.8 %all-to-all-start.1 = ((f32[64,8,256]{2,1,0:T(8,128)}), f32[64,8,256]{2,1,0:T(8,128)S(1)}, u32[]{:S(2)}, u32[]{:S(2)}) async-start(f32[64,8,256]{2,1,0:T(8,128)} %broadcast_in_dim.14), calls=%async_computation.1 | async-start | bytes 1048576 | tf_op jit(solution)/shard_map/all_to_all | solution.py:19
  45.4 17.5 %collective-permute-start = (f32[2,64,512]{2,1,0:T(8,128)S(1)}, f32[2,64,512]{2,1,0:T(8,128)S(1)}, u32[]{:S(2)}, u32[]{:S(2)}) collective-permute-start(f32[2,64,512]{2,1,0:T(8,128)S(1)} %pad_maximum_fusion.3), channel_id=1, source_target_pairs={{0,64},{8,72},{16,80},{24,88},{32,96},{40,104},{48,112},{56,120},{... | collective-permute-start | bytes 786440 | tf_op jit(solution)/shard_map/ppermute | solution.py:51
  62.9 1.2 copy-start.6
  63.1 12.8 %slice-start.1 = ((f32[6,64,512]{2,1,0:T(8,128)}), f32[5,64,512]{2,1,0:T(8,128)S(1)}, s32[]{:S(2)}) async-start(f32[6,64,512]{2,1,0:T(8,128)} %param.6), calls=%async_computation.13 | async-start | bytes 1310720 | tf_op jit(solution)/shard_map/slice | solution.py:60
  64.0 17.6 %all-to-all-start.2 = ((f32[8,2,64,128]{3,2,1,0:T(8,128)}), f32[8,2,64,128]{3,2,1,0:T(8,128)S(1)}, u32[]{:S(2)}, u32[]{:S(2)}) async-start(f32[8,2,64,128]{3,2,1,0:T(8,128)} %broadcast_in_dim.15), calls=%async_computation.2 | async-start | bytes 1048576 | tf_op jit(solution)/shard_map/all_to_all | solution.py:19
  73.2 9.0 %collective-permute-start.1 = (f32[3,64,128]{2,1,0:T(8,128)S(1)}, f32[3,64,128]{2,1,0:T(8,128)S(1)}, u32[]{:S(2)}, u32[]{:S(2)}) collective-permute-start(f32[3,64,128]{2,1,0:T(8,128)S(1)} %constant_dynamic-slice_fusion.2), channel_id=1, source_target_pairs={{0,64},{8,72},{16,80},{24,88},{32,96},{40,104},{48,112},{56,120},{... | collective-permute-start | bytes 294920 | tf_op jit(solution)/shard_map/ppermute | solution.py:51
  77.0 39.7 %collective-permute-start.3 = (f32[7,64,512]{2,1,0:T(8,128)}, f32[7,64,512]{2,1,0:T(8,128)}, u32[]{:S(2)}, u32[]{:S(2)}) collective-permute-start(f32[7,64,512]{2,1,0:T(8,128)} %pad_maximum_fusion), channel_id=1, source_target_pairs={{0,64},{8,72},{16,80},{24,88},{32,96},{40,104},{48,112},{56,120},{... | collective-permute-start | bytes 2752520 | tf_op jit(solution)/shard_map/ppermute | solution.py:51
  82.1 66.7 %copy-start.7 = (f32[3,64,128]{2,1,0:T(8,128)}, f32[3,64,128]{2,1,0:T(8,128)S(1)}, u32[]{:S(2)}) copy-start(f32[3,64,128]{2,1,0:T(8,128)S(1)} %collective-permute-done.1) | copy-start | bytes 294916
  110.5 18.2 %all-to-all-start.4 = ((f32[32,16,128]{2,1,0:T(8,128)}), f32[32,16,128]{2,1,0:T(8,128)S(1)}, u32[]{:S(2)}, u32[]{:S(2)}) async-start(f32[32,16,128]{2,1,0:T(8,128)} %broadcast_in_dim.16), calls=%async_computation.4 | async-start | bytes 524288 | tf_op jit(solution)/shard_map/all_to_all | solution.py:19
  131.0 17.4 %all-to-all-start.5 = ((f32[8,2,64,128]{3,2,1,0:T(8,128)}), f32[8,2,64,128]{3,2,1,0:T(8,128)S(1)}, u32[]{:S(2)}, u32[]{:S(2)}) async-start(f32[8,2,64,128]{3,2,1,0:T(8,128)} %broadcast_in_dim.17), calls=%async_computation.5 | async-start | bytes 1048576 | tf_op jit(solution)/shard_map/all_to_all | solution.py:19
  166.9 18.6 %all-to-all-start.7 = ((f32[32,16,128]{2,1,0:T(8,128)}), f32[32,16,128]{2,1,0:T(8,128)S(1)}, u32[]{:S(2)}, u32[]{:S(2)}) async-start(f32[32,16,128]{2,1,0:T(8,128)} %broadcast_in_dim.18), calls=%async_computation.7 | async-start | bytes 524288 | tf_op jit(solution)/shard_map/all_to_all | solution.py:19
  187.1 25.9 %copy-start.1 = (f32[4,64,4,512]{3,2,1,0:T(4,128)S(1)}, f32[4,64,4,512]{3,2,1,0:T(4,128)}, u32[]{:S(2)}) copy-start(f32[4,64,4,512]{3,2,1,0:T(4,128)} %param.7) | copy-start | bytes 6291460
  187.9 16.0 %all-to-all-start.8 = ((f32[8,2,64,128]{3,2,1,0:T(8,128)}), f32[8,2,64,128]{3,2,1,0:T(8,128)}, u32[]{:S(2)}, u32[]{:S(2)}) async-start(f32[8,2,64,128]{3,2,1,0:T(8,128)} %broadcast_in_dim.19), calls=%async_computation.8 | async-start | bytes 1048576 | tf_op jit(solution)/shard_map/all_to_all | solution.py:19
  208.5 16.8 %all-to-all-start.9 = ((f32[32,16,128]{2,1,0:T(8,128)}), f32[32,16,128]{2,1,0:T(8,128)S(1)}, u32[]{:S(2)}, u32[]{:S(2)}) async-start(f32[32,16,128]{2,1,0:T(8,128)} %bitcast.195), calls=%async_computation.9 | async-start | bytes 524288 | tf_op jit(solution)/shard_map/all_to_all | solution.py:19
  216.7 20.3 %collective-permute-start.2 = (f32[512,128]{1,0:T(8,128)S(1)}, f32[512,128]{1,0:T(8,128)S(1)}, u32[]{:S(2)}, u32[]{:S(2)}) collective-permute-start(f32[512,128]{1,0:T(8,128)S(1)} %bitcast.186), channel_id=1, source_target_pairs={{0,64},{8,72},{16,80},{24,88},{32,96},{40,104},{48,112},{56,120},{... | collective-permute-start | bytes 786440 | tf_op jit(solution)/shard_map/ppermute | solution.py:51
  219.9 17.1 %copy-start.4 = (f32[4,64,1,512]{3,2,1,0:T(1,128)S(1)}, f32[4,64,1,512]{3,2,1,0:T(1,128)}, u32[]{:S(2)}) copy-start(f32[4,64,1,512]{3,2,1,0:T(1,128)} %get-tuple-element.8) | copy-start | bytes 1572868
  221.6 16.1 %collective-permute-start.4 = (f32[512,128]{1,0:T(8,128)S(1)}, f32[512,128]{1,0:T(8,128)}, u32[]{:S(2)}, u32[]{:S(2)}) collective-permute-start(f32[512,128]{1,0:T(8,128)S(1)} %bitcast.190), channel_id=1, source_target_pairs={{0,64},{8,72},{16,80},{24,88},{32,96},{40,104},{48,112},{56,120},{... | collective-permute-start | bytes 786440 | tf_op jit(solution)/shard_map/ppermute | solution.py:51
  226.2 26.2 %all-to-all-start.10 = ((f32[64,16,128]{2,1,0:T(8,128)}), f32[64,16,128]{2,1,0:T(8,128)S(1)}, u32[]{:S(2)}, u32[]{:S(2)}) async-start(f32[64,16,128]{2,1,0:T(8,128)} %broadcast_in_dim.20), calls=%async_computation.10 | async-start | bytes 1048576 | tf_op jit(solution)/shard_map/all_to_all | solution.py:19
  237.0 2.2 copy-start.3
  239.3 14.0 %copy-start.2 = (f32[4,64,1,512]{3,2,1,0:T(1,128)S(1)}, f32[4,64,1,512]{3,2,1,0:T(1,128)}, u32[]{:S(2)}) copy-start(f32[4,64,1,512]{3,2,1,0:T(1,128)} %get-tuple-element.6) | copy-start | bytes 1572868
  255.2 14.8 %all-to-all-start.11 = ((f32[8,32,256]{2,1,0:T(8,128)}), f32[8,32,256]{2,1,0:T(8,128)S(1)}, u32[]{:S(2)}, u32[]{:S(2)}) async-start(f32[8,32,256]{2,1,0:T(8,128)} %reshape_reshape.3), calls=%async_computation.11 | async-start | bytes 524288 | tf_op jit(solution)/shard_map/all_to_all | solution.py:19

commit v4 on v0

v4 whole, which is shorter than its diff:
```python
import jax
import jax.numpy as jnp
from jax import lax
from jax.sharding import PartitionSpec as P

HIGHEST_PREC = lax.Precision.HIGHEST
CORES = 2


def pair_index(block_row, prior_row):
    return block_row * (block_row - 1) // 2 + prior_row


def contract(left, right, axes):
    return lax.dot_general(
        left,
        right,
        (((axes[0],), (axes[1],)), ((), ())),
        precision=HIGHEST_PREC,
        preferred_element_type=jnp.float32,
    )


def swap(parts, axis, groups=None):
    return lax.all_to_all(parts, axis, 0, 0, axis_index_groups=groups, tiled=True)


def copies(part, count):
    return jnp.broadcast_to(part[None], (count,) + part.shape)


def halves_swapped(value):
    return jnp.roll(value, value.shape[-1] // 2, value.ndim - 1)


def shards(right_sides, diag_inverse, lower_blocks, trail_panel):
    step_count = diag_inverse.shape[0]
    pair_count = lower_blocks.shape[0]
    trail_count = trail_panel.shape[0]
    local_rows = right_sides.shape[1]
    column_count = right_sides.shape[2]
    block_width = lower_blocks.shape[2]
    row_size = lax.axis_size("row")
    col_size = lax.axis_size("col")
    members = row_size // 2
    chips = col_size // CORES
    half = column_count // 2
    quarter = half // 2
    row = lax.axis_index("row")
    col = lax.axis_index("col")
    parity = row % 2
    core = col % CORES
    row_groups = [[r for r in range(row_size) if r % 2 == g] for g in range(2)]
    chip_groups = [[c for c in range(col_size) if c % CORES == g] for g in range(CORES)]
    row_pairs = [(r, r ^ 1) for r in range(row_size)]
    core_pairs = [(c, c ^ 1) for c in range(col_size)]
    low = lax.broadcasted_iota(jnp.int32, (1, half), 1) < quarter

    def from_row(value):
        return lax.ppermute(value, "row", row_pairs)

    def from_core(value):
        return lax.ppermute(value, "col", core_pairs)

    def gathered(own):
        by_row = from_row(own)
        return own, by_row, from_core(own), from_core(by_row)

    own_diag = diag_inverse.transpose(0, 2, 1)

    own_sides = lax.dynamic_slice_in_dim(right_sides[1:step_count], core * half, half, 2)
    sides = jnp.concatenate([own_sides, from_row(own_sides)], 1)
    sides = jnp.where(low == (parity == 0), sides, halves_swapped(sides))
    batches = []
    for block_row in range(1, step_count):
        start = pair_index(block_row, 0)
        own = [lower_blocks[start : start + block_row], own_diag[block_row : block_row + 1]]
        batches.append(gathered(jnp.concatenate(own)))

    def lower_of(block_row, prior_row):
        return jnp.concatenate([b[prior_row] for b in batches[block_row - 1]])

    def diag_of(block_row):
        return jnp.concatenate([b[block_row] for b in batches[block_row - 1]])

    def update_of(block_row, prior_row):
        both = contract(lower_of(block_row, prior_row), solved[prior_row], (1, 0))
        rows = 2 * local_rows
        return jnp.where(low, both[:rows], both[rows:])

    def by_core(value):
        other = from_core(value)
        straight = jnp.where(low, value, other)
        turned = halves_swapped(jnp.where(low, value, other))
        return jnp.where(core == 0, straight, turned)

    local_term = contract(own_diag[0], right_sides[0], (0, 0))
    parts = local_term.reshape(row_size, block_width // row_size, column_count)
    part = swap(parts, "row").sum(0)
    mine = lax.dynamic_slice_in_dim(part, core * half, half, 1)
    other = from_core(lax.dynamic_slice_in_dim(part, (1 - core) * half, half, 1))
    for_even = jnp.where(low, mine, halves_swapped(other))
    for_odd = jnp.where(low, halves_swapped(mine), other)
    parts = copies(jnp.stack([for_even, for_odd]), members).reshape(row_size, -1, half)
    solved = [swap(parts, "row").reshape(block_width, half)]

    for block_row in range(1, step_count):
        update = None
        for prior_row in range(block_row):
            term = update_of(block_row, prior_row)
            update = term if update is None else update + term
        total = swap(copies(update, chips), "col", chip_groups).sum(0)
        current = sides[block_row - 1] - (total + halves_swapped(total))
        zero = jnp.zeros_like(current)
        spread = jnp.concatenate([jnp.where(low, current, zero), jnp.where(low, zero, current)])
        local_term = contract(diag_of(block_row), spread, (0, 0))
        parts = local_term.reshape(members, block_width // members, half)
        part = swap(parts, "row", row_groups).sum(0)
        if block_row < step_count - 1:
            parts = swap(copies(part, members), "row", row_groups)
            solved.append(parts.reshape(block_width, half))

    wholes = []
    for value in solved:
        straight = by_core(value)
        other = from_row(straight)
        wholes.append(
            (
                jnp.where(parity == 0, straight, other),
                jnp.where(parity == 0, other, straight),
            )
        )
    parts = swap(copies(by_core(part), row_size), "row")
    parts = parts.reshape(members, 2, -1, half)
    wholes.append(tuple(parts[:, g].reshape(block_width, half) for g in range(2)))

    shared_parts = []
    for g in range(2):
        acc = None
        for block_row in range(step_count):
            contrib = jnp.einsum(
                "nc,mrn->cmr",
                wholes[block_row][g],
                trail_panel[:, :, block_row, :],
                precision=HIGHEST_PREC,
            )
            acc = contrib if acc is None else acc + contrib
        shared_parts.append(acc.reshape(CORES, chips // 2, -1, trail_count * local_rows))
    shared = jnp.stack(shared_parts, 1).reshape(col_size, -1, trail_count * local_rows)
    shared = swap(shared, "col").sum(0)
    own_width = shared.shape[0]
    shared = shared.reshape(own_width, trail_count, local_rows).transpose(1, 2, 0)
    below = lax.dynamic_slice_in_dim(right_sides[step_count:], col * own_width, own_width, 2)
    trail_rest = below - shared

    out_width = column_count // row_size
    first = row * out_width
    place = first % quarter + first // half * quarter
    odd = first // quarter % 2 == 1
    outs = []
    for even_part, odd_part in wholes:
        picked = [lax.dynamic_slice_in_dim(v, place, out_width, 1) for v in (even_part, odd_part)]
        outs.append(jnp.where(odd, picked[1], picked[0]))
    return (jnp.stack(outs), trail_rest)


def solution(mesh):
    placed = (
        P(None, "row", None),
        P(None, "col", "row"),
        P(None, "row", "col"),
        P(None, "row", None, "col"),
    )
    return jax.shard_map(
        shards,
        mesh=mesh,
        in_specs=placed,
        out_specs=(P(None, "col", "row"), P(None, "row", "col")),
        check_vma=False,
    )
```

time: 932 us -> 283 us (0.30)
  waiting for transfers between devices: 884 us -> 77.6 us
  starting transfers between devices: 0.33 us -> 144 us
  local copies, waits for them, and re-layouts: 6.87 us -> 28.8 us
  between operations: 15 us -> 1.61 us
    psum x7 -> x0, waiting for transfers between devices: 815 us -> none  [the longest x4 610 us: shards(): solved_block = lax.psum(local_term, 'row')]
    all_to_all x0 -> x12, starting transfers between devices: none -> 90 us  [swap(): lax.all_to_all(parts, axis, 0, 0, axis_index_groups=groups, tiled=True)]
    unnamed x9 -> x0, waiting for transfers between devices: 69.5 us -> none
    all_to_all x0 -> x12, waiting for transfers between devices: none -> 66.8 us  [swap(): lax.all_to_all(parts, axis, 0, 0, axis_index_groups=groups, tiled=True)]
    ppermute x0 -> x18, starting transfers between devices: none -> 54.4 us  [the longest x11 35.4 us: from_core(): return lax.ppermute(value, 'col', core_pairs)]
    ppermute x0 -> x18, waiting for transfers between devices: none -> 10.8 us  [the longest x7 10.5 us: from_row(): return lax.ppermute(value, 'row', row_pairs)]
    dot_general x14 -> x18, matrix products: 23.6 us -> 21.3 us  [the longest x10 16.6 us: contract(): lax.dot_general(left, right, (((axes[0],), (axes[1],)), ((), ())), precis...]
  transfers between devices with their start and end apart: 8 -> 30, of which waited for: 8 -> 13; matrix products, arithmetic and copies ran while one was open for 1% -> 16% of each run, Pallas kernels for 0% -> 0%
where the time goes in v4:
time: 283 us; the launch traced here: 281 us
  starting transfers between devices  144 us (51%)
  waiting for transfers between devices  77.6 us (27%)
  local copies, waits for them, and re-layouts  28.8 us (10%)
  matrix products  21.3 us (8%)
  other arithmetic  7.48 us (3%)
    all_to_all x12, starting transfers between devices, swap(): lax.all_to_all(parts, axis, 0, 0, axis_index_groups=groups, tiled=True)  90 us
    all_to_all x12, waiting for transfers between devices, swap(): lax.all_to_all(parts, axis, 0, 0, axis_index_groups=groups, tiled=True)  66.8 us
    ppermute x11, starting transfers between devices, from_core(): return lax.ppermute(value, 'col', core_pairs)  35.4 us
    ppermute x7, starting transfers between devices, from_row(): return lax.ppermute(value, 'row', row_pairs)  19.1 us
    dot_general x10, matrix products, contract(): lax.dot_general(left, right, (((axes[0],), (axes[1],)), ((), ())), precis...  16.6 us
    ppermute x7, waiting for transfers between devices, from_row(): return lax.ppermute(value, 'row', row_pairs)  10.5 us
    squeeze x10, local copies, waits for them, and re-layouts, lower_of(): return jnp.concatenate([b[prior_row] for b in batches[block_row - 1]])  6.82 us
    slice x1, local copies, waits for them, and re-layouts, shards(): trail_panel[:, :, block_row, :]  5.83 us
  transfers between devices with their start and end apart: 30, of which 13 were waited for; matrix products, arithmetic and copies ran while one was open for 16% of the time, Pallas kernels for 0%

profile of v4, /device:TPU:1, one launch (start us, length us, event | category | flops | bytes accessed | tf_op | source)
XLA Modules:
  0.0 281.2 jit_solution(16291145206830600749)
XLA Ops:
  5.0 17.3 %all-to-all-start = ((f32[64,8,256]{2,1,0:T(8,128)}), f32[64,8,256]{2,1,0:T(8,128)S(1)}, u32[]{:S(2)}, u32[]{:S(2)}) async-start(f32[64,8,256]{2,1,0:T(8,128)} %fusion.88), calls=%async_computation | async-start | bytes 1048576 | tf_op jit(solution)/shard_map/all_to_all | solution.py:25
  23.3 2.9 %collective-permute-start.4 = (f32[2,64,512]{2,1,0:T(8,128)S(1)}, f32[2,64,512]{2,1,0:T(8,128)S(1)}, u32[]{:S(2)}, u32[]{:S(2)}) collective-permute-start(f32[2,64,512]{2,1,0:T(8,128)S(1)} %pad_maximum_fusion.3), channel_id=1, source_target_pairs={{0,1},{1,0},{2,3},{3,2},{4,5},{5,4},{6,7},{7,6},{8,9},{9,8},{10,11... | collective-permute-start | bytes 786440 | tf_op jit(solution)/shard_map/ppermute | solution.py:63
  26.1 3.2 %collective-permute-start.3 = (f32[2,64,512]{2,1,0:T(8,128)S(1)}, f32[2,64,512]{2,1,0:T(8,128)S(1)}, u32[]{:S(2)}, u32[]{:S(2)}) collective-permute-start(f32[2,64,512]{2,1,0:T(8,128)S(1)} %pad_maximum_fusion.3), channel_id=1, source_target_pairs={{0,8},{8,0},{16,24},{24,16},{32,40},{40,32},{48,56},{56,48},{64,72... | collective-permute-start | bytes 786440 | tf_op jit(solution)/shard_map/ppermute | solution.py:60
  32.3 3.2 %collective-permute-start.9 = (f32[3,64,512]{2,1,0:T(8,128)}, f32[3,64,512]{2,1,0:T(8,128)}, u32[]{:S(2)}, u32[]{:S(2)}) collective-permute-start(f32[3,64,512]{2,1,0:T(8,128)} %pad_maximum_fusion.1), channel_id=1, source_target_pairs={{0,8},{8,0},{16,24},{24,16},{32,40},{40,32},{48,56},{56,48},{64,72... | collective-permute-start | bytes 1179656 | tf_op jit(solution)/shard_map/ppermute | solution.py:60
  35.6 3.1 %all-to-all-done = f32[64,8,256]{2,1,0:T(8,128)S(1)} async-done(((f32[64,8,256]{2,1,0:T(8,128)}), f32[64,8,256]{2,1,0:T(8,128)S(1)}, u32[]{:S(2)}, u32[]{:S(2)}) %all-to-all-start) | async-done | bytes 524320 | tf_op jit(solution)/shard_map/all_to_all | solution.py:25
  38.7 5.8 %collective-permute-start = (f32[8,128]{1,0:T(8,128)S(1)}, f32[8,128]{1,0:T(8,128)S(1)}, u32[]{:S(2)}, u32[]{:S(2)}) collective-permute-start(f32[8,128]{1,0:T(8,128)S(1)} %constant_dynamic-slice_fusion.2), channel_id=1, source_target_pairs={{0,1},{1,0},{2,3},{3,2},{4,5},{5,4},{6,7},{7,6},{8,9},{9,8},{10,11... | collective-permute-start | bytes 12296 | tf_op jit(solution)/shard_map/ppermute | solution.py:63
  48.4 10.1 %all-to-all-start.1 = ((f32[64,8,128]{2,1,0:T(8,128)}), f32[64,8,128]{2,1,0:T(8,128)S(1)}, u32[]{:S(2)}, u32[]{:S(2)}) async-start(f32[64,8,128]{2,1,0:T(8,128)} %bitcast.8), calls=%async_computation.1 | async-start | bytes 524288 | tf_op jit(solution)/shard_map/all_to_all | solution.py:25
  58.6 13.4 %all-to-all-done.1 = f32[64,8,128]{2,1,0:T(8,128)S(1)} async-done(((f32[64,8,128]{2,1,0:T(8,128)}), f32[64,8,128]{2,1,0:T(8,128)S(1)}, u32[]{:S(2)}, u32[]{:S(2)}) %all-to-all-start.1) | async-done | bytes 262176 | tf_op jit(solution)/shard_map/all_to_all | solution.py:25
  74.2 4.0 %all-to-all-start.2 = ((f32[4,128,128]{2,1,0:T(8,128)}), f32[4,128,128]{2,1,0:T(8,128)S(1)}, u32[]{:S(2)}, u32[]{:S(2)}) async-start(f32[4,128,128]{2,1,0:T(8,128)} %broadcast_in_dim.169), calls=%async_computation.2 | async-start | bytes 524288 | tf_op jit(solution)/shard_map/all_to_all | solution.py:25
  78.3 5.4 %all-to-all-done.2 = f32[4,128,128]{2,1,0:T(8,128)S(1)} async-done(((f32[4,128,128]{2,1,0:T(8,128)}), f32[4,128,128]{2,1,0:T(8,128)S(1)}, u32[]{:S(2)}, u32[]{:S(2)}) %all-to-all-start.2) | async-done | bytes 262176 | tf_op jit(solution)/shard_map/all_to_all | solution.py:25
  85.7 4.7 %all-to-all-start.3 = ((f32[32,16,128]{2,1,0:T(8,128)}), f32[32,16,128]{2,1,0:T(8,128)S(1)}, u32[]{:S(2)}, u32[]{:S(2)}) async-start(f32[32,16,128]{2,1,0:T(8,128)} %bitcast.20), calls=%async_computation.3 | async-start | bytes 524288 | tf_op jit(solution)/shard_map/all_to_all | solution.py:25
  90.4 4.6 %collective-permute-start.10 = (f32[3,64,512]{2,1,0:T(8,128)}, f32[3,64,512]{2,1,0:T(8,128)}, u32[]{:S(2)}, u32[]{:S(2)}) collective-permute-start(f32[3,64,512]{2,1,0:T(8,128)} %pad_maximum_fusion.1), channel_id=1, source_target_pairs={{0,1},{1,0},{2,3},{3,2},{4,5},{5,4},{6,7},{7,6},{8,9},{9,8},{10,11... | collective-permute-start | bytes 1179656 | tf_op jit(solution)/shard_map/ppermute | solution.py:63
  95.0 3.0 %collective-permute-start.14 = (f32[4,64,512]{2,1,0:T(8,128)S(1)}, f32[4,64,512]{2,1,0:T(8,128)S(1)}, u32[]{:S(2)}, u32[]{:S(2)}) collective-permute-start(f32[4,64,512]{2,1,0:T(8,128)S(1)} %pad_maximum_fusion), channel_id=1, source_target_pairs={{0,8},{8,0},{16,24},{24,16},{32,40},{40,32},{48,56},{56,48},{64,72... | collective-permute-start | bytes 1572872 | tf_op jit(solution)/shard_map/ppermute | solution.py:60
  102.7 11.2 %all-to-all-start.4 = ((f32[32,16,128]{2,1,0:T(8,128)}), f32[32,16,128]{2,1,0:T(8,128)S(1)}, u32[]{:S(2)}, u32[]{:S(2)}) async-start(f32[32,16,128]{2,1,0:T(8,128)} %broadcast_in_dim.170), calls=%async_computation.4 | async-start | bytes 524288 | tf_op jit(solution)/shard_map/all_to_all | solution.py:25
  117.9 9.1 %all-to-all-done.4 = f32[32,16,128]{2,1,0:T(8,128)S(1)} async-done(((f32[32,16,128]{2,1,0:T(8,128)}), f32[32,16,128]{2,1,0:T(8,128)S(1)}, u32[]{:S(2)}, u32[]{:S(2)}) %all-to-all-start.4) | async-done | bytes 262176 | tf_op jit(solution)/shard_map/all_to_all | solution.py:25
  129.2 3.4 %all-to-all-start.5 = ((f32[4,128,128]{2,1,0:T(8,128)}), f32[4,128,128]{2,1,0:T(8,128)S(1)}, u32[]{:S(2)}, u32[]{:S(2)}) async-start(f32[4,128,128]{2,1,0:T(8,128)} %broadcast_in_dim.171), calls=%async_computation.5 | async-start | bytes 524288 | tf_op jit(solution)/shard_map/all_to_all | solution.py:25
  132.6 3.8 %collective-permute-start.15 = (f32[4,64,512]{2,1,0:T(8,128)S(1)}, f32[4,64,512]{2,1,0:T(8,128)S(1)}, u32[]{:S(2)}, u32[]{:S(2)}) collective-permute-start(f32[4,64,512]{2,1,0:T(8,128)S(1)} %pad_maximum_fusion), channel_id=1, source_target_pairs={{0,1},{1,0},{2,3},{3,2},{4,5},{5,4},{6,7},{7,6},{8,9},{9,8},{10,11... | collective-permute-start | bytes 1572872 | tf_op jit(solution)/shard_map/ppermute | solution.py:63
  141.3 5.6 %all-to-all-start.6 = ((f32[32,16,128]{2,1,0:T(8,128)}), f32[32,16,128]{2,1,0:T(8,128)S(1)}, u32[]{:S(2)}, u32[]{:S(2)}) async-start(f32[32,16,128]{2,1,0:T(8,128)} %bitcast.187), calls=%async_computation.6 | async-start | bytes 524288 | tf_op jit(solution)/shard_map/all_to_all | solution.py:25
  148.6 9.9 %all-to-all-done.6 = f32[32,16,128]{2,1,0:T(8,128)S(1)} async-done(((f32[32,16,128]{2,1,0:T(8,128)}), f32[32,16,128]{2,1,0:T(8,128)S(1)}, u32[]{:S(2)}, u32[]{:S(2)}) %all-to-all-start.6) | async-done | bytes 262176 | tf_op jit(solution)/shard_map/all_to_all | solution.py:25
  159.3 5.2 %all-to-all-start.7 = ((f32[32,16,128]{2,1,0:T(8,128)}), f32[32,16,128]{2,1,0:T(8,128)S(1)}, u32[]{:S(2)}, u32[]{:S(2)}) async-start(f32[32,16,128]{2,1,0:T(8,128)} %broadcast_in_dim.172), calls=%async_computation.7 | async-start | bytes 524288 | tf_op jit(solution)/shard_map/all_to_all | solution.py:25
  167.4 8.5 %all-to-all-done.7 = f32[32,16,128]{2,1,0:T(8,128)S(1)} async-done(((f32[32,16,128]{2,1,0:T(8,128)}), f32[32,16,128]{2,1,0:T(8,128)S(1)}, u32[]{:S(2)}, u32[]{:S(2)}) %all-to-all-start.7) | async-done | bytes 262176 | tf_op jit(solution)/shard_map/all_to_all | solution.py:25
  177.3 5.5 %all-to-all-start.8 = ((f32[4,128,128]{2,1,0:T(8,128)}), f32[4,128,128]{2,1,0:T(8,128)S(1)}, u32[]{:S(2)}, u32[]{:S(2)}) async-start(f32[4,128,128]{2,1,0:T(8,128)} %broadcast_in_dim.174), calls=%async_computation.8 | async-start | bytes 524288 | tf_op jit(solution)/shard_map/all_to_all | solution.py:25
  182.7 5.8 %fusion.127 = (f32[4,64,1,512]{3,2,1,0:T(1,128)S(1)}, f32[4,64,1,512]{3,2,1,0:T(1,128)S(1)}, f32[4,64,1,512]{3,2,1,0:T(1,128)S(1)}, f32[4,64,1,512]{3,2,1,0:T(1,128)S(1)}) fusion(f32[4,64,4,512]{3,2,1,0:T(4,128)} %param.7), kind=kLoop, calls=%fused_computation.223 | loop fusion | bytes 4194304 | tf_op jit(solution)/shard_map/slice | solution.py:144
  192.1 5.0 %collective-permute-start.1 = (f32[512,128]{1,0:T(8,128)S(1)}, f32[512,128]{1,0:T(8,128)}, u32[]{:S(2)}, u32[]{:S(2)}) collective-permute-start(f32[512,128]{1,0:T(8,128)S(1)} %bitcast.180), channel_id=1, source_target_pairs={{0,1},{1,0},{2,3},{3,2},{4,5},{5,4},{6,7},{7,6},{8,9},{9,8},{10,11... | collective-permute-start | bytes 786440 | tf_op jit(solution)/shard_map/ppermute | solution.py:63
  204.5 4.7 %all-to-all-start.9 = ((f32[32,16,128]{2,1,0:T(8,128)}), f32[32,16,128]{2,1,0:T(8,128)S(1)}, u32[]{:S(2)}, u32[]{:S(2)}) async-start(f32[32,16,128]{2,1,0:T(8,128)} %bitcast.56), calls=%async_computation.9 | async-start | bytes 524288 | tf_op jit(solution)/shard_map/all_to_all | solution.py:25
  213.2 3.0 %collective-permute-start.8 = (f32[512,128]{1,0:T(8,128)S(1)}, f32[512,128]{1,0:T(8,128)S(1)}, u32[]{:S(2)}, u32[]{:S(2)}) collective-permute-start(f32[512,128]{1,0:T(8,128)S(1)} %maximum_select_fusion.1), channel_id=1, source_target_pairs={{0,8},{8,0},{16,24},{24,16},{32,40},{40,32},{48,56},{56,48},{64,72... | collective-permute-start | bytes 786440 | tf_op jit(solution)/shard_map/ppermute | solution.py:60
  219.5 4.7 %collective-permute-done.2 = f32[512,128]{1,0:T(8,128)S(1)} collective-permute-done((f32[512,128]{1,0:T(8,128)S(1)}, f32[512,128]{1,0:T(8,128)S(1)}, u32[]{:S(2)}, u32[]{:S(2)}) %collective-permute-start.2) | collective-permute-done | bytes 262176 | tf_op jit(solution)/shard_map/ppermute | solution.py:60
  224.3 5.6 %collective-permute-done.8 = f32[512,128]{1,0:T(8,128)S(1)} collective-permute-done((f32[512,128]{1,0:T(8,128)S(1)}, f32[512,128]{1,0:T(8,128)S(1)}, u32[]{:S(2)}, u32[]{:S(2)}) %collective-permute-start.8) | collective-permute-done | bytes 262176 | tf_op jit(solution)/shard_map/ppermute | solution.py:60
  234.2 10.5 %all-to-all-start.10 = ((f32[64,16,128]{2,1,0:T(8,128)}), f32[64,16,128]{2,1,0:T(8,128)}, u32[]{:S(2)}, u32[]{:S(2)}) async-start(f32[64,16,128]{2,1,0:T(8,128)} %broadcast_in_dim.175), calls=%async_computation.10 | async-start | bytes 1048576 | tf_op jit(solution)/shard_map/all_to_all | solution.py:25
  249.7 11.4 %all-to-all-done.10 = f32[64,16,128]{2,1,0:T(8,128)} async-done(((f32[64,16,128]{2,1,0:T(8,128)}), f32[64,16,128]{2,1,0:T(8,128)}, u32[]{:S(2)}, u32[]{:S(2)}) %all-to-all-start.10) | async-done | bytes 524320 | tf_op jit(solution)/shard_map/all_to_all | solution.py:25
  266.0 7.9 %all-to-all-start.11 = ((f32[8,32,256]{2,1,0:T(8,128)}), f32[8,32,256]{2,1,0:T(8,128)S(1)}, u32[]{:S(2)}, u32[]{:S(2)}) async-start(f32[8,32,256]{2,1,0:T(8,128)} %bitcast.73), calls=%async_computation.11 | async-start | bytes 524288 | tf_op jit(solution)/shard_map/all_to_all | solution.py:25
  275.1 5.3 %all-to-all-done.11 = f32[8,32,256]{2,1,0:T(8,128)S(1)} async-done(((f32[8,32,256]{2,1,0:T(8,128)}), f32[8,32,256]{2,1,0:T(8,128)S(1)}, u32[]{:S(2)}, u32[]{:S(2)}) %all-to-all-start.11) | async-done | bytes 262176 | tf_op jit(solution)/shard_map/all_to_all | solution.py:25
  (159 shorter events, 73.0 us)
Async XLA Ops:
  5.0 33.6 %all-to-all-start = ((f32[64,8,256]{2,1,0:T(8,128)}), f32[64,8,256]{2,1,0:T(8,128)S(1)}, u32[]{:S(2)}, u32[]{:S(2)}) async-start(f32[64,8,256]{2,1,0:T(8,128)} %fusion.88), calls=%async_computation | async-start | bytes 1048576 | tf_op jit(solution)/shard_map/all_to_all | solution.py:25
  23.3 35.2 %collective-permute-start.4 = (f32[2,64,512]{2,1,0:T(8,128)S(1)}, f32[2,64,512]{2,1,0:T(8,128)S(1)}, u32[]{:S(2)}, u32[]{:S(2)}) collective-permute-start(f32[2,64,512]{2,1,0:T(8,128)S(1)} %pad_maximum_fusion.3), channel_id=1, source_target_pairs={{0,1},{1,0},{2,3},{3,2},{4,5},{5,4},{6,7},{7,6},{8,9},{9,8},{10,11... | collective-permute-start | bytes 786440 | tf_op jit(solution)/shard_map/ppermute | solution.py:63
  26.1 18.7 %collective-permute-start.3 = (f32[2,64,512]{2,1,0:T(8,128)S(1)}, f32[2,64,512]{2,1,0:T(8,128)S(1)}, u32[]{:S(2)}, u32[]{:S(2)}) collective-permute-start(f32[2,64,512]{2,1,0:T(8,128)S(1)} %pad_maximum_fusion.3), channel_id=1, source_target_pairs={{0,8},{8,0},{16,24},{24,16},{32,40},{40,32},{48,56},{56,48},{64,72... | collective-permute-start | bytes 786440 | tf_op jit(solution)/shard_map/ppermute | solution.py:60
  29.4 15.4 %collective-permute-start.6 = (f32[3,64,128]{2,1,0:T(8,128)S(1)}, f32[3,64,128]{2,1,0:T(8,128)S(1)}, u32[]{:S(2)}, u32[]{:S(2)}) collective-permute-start(f32[3,64,128]{2,1,0:T(8,128)S(1)} %constant_dynamic-slice_fusion), channel_id=1, source_target_pairs={{0,8},{8,0},{16,24},{24,16},{32,40},{40,32},{48,56},{56,48},{64,72... | collective-permute-start | bytes 294920 | tf_op jit(solution)/shard_map/ppermute | solution.py:60
  32.3 65.7 %collective-permute-start.9 = (f32[3,64,512]{2,1,0:T(8,128)}, f32[3,64,512]{2,1,0:T(8,128)}, u32[]{:S(2)}, u32[]{:S(2)}) collective-permute-start(f32[3,64,512]{2,1,0:T(8,128)} %pad_maximum_fusion.1), channel_id=1, source_target_pairs={{0,8},{8,0},{16,24},{24,16},{32,40},{40,32},{48,56},{56,48},{64,72... | collective-permute-start | bytes 1179656 | tf_op jit(solution)/shard_map/ppermute | solution.py:60
  38.7 8.6 %collective-permute-start = (f32[8,128]{1,0:T(8,128)S(1)}, f32[8,128]{1,0:T(8,128)S(1)}, u32[]{:S(2)}, u32[]{:S(2)}) collective-permute-start(f32[8,128]{1,0:T(8,128)S(1)} %constant_dynamic-slice_fusion.2), channel_id=1, source_target_pairs={{0,1},{1,0},{2,3},{3,2},{4,5},{5,4},{6,7},{7,6},{8,9},{9,8},{10,11... | collective-permute-start | bytes 12296 | tf_op jit(solution)/shard_map/ppermute | solution.py:63
  44.9 13.7 %collective-permute-start.5 = (f32[2,64,512]{2,1,0:T(8,128)S(1)}, f32[2,64,512]{2,1,0:T(8,128)S(1)}, u32[]{:S(2)}, u32[]{:S(2)}) collective-permute-start(f32[2,64,512]{2,1,0:T(8,128)S(1)} %collective-permute-done.3), channel_id=1, source_target_pairs={{0,1},{1,0},{2,3},{3,2},{4,5},{5,4},{6,7},{7,6},{8,9},{9,8},{10,11... | collective-permute-start | bytes 786440 | tf_op jit(solution)/shard_map/ppermute | solution.py:63
  48.4 23.6 %all-to-all-start.1 = ((f32[64,8,128]{2,1,0:T(8,128)}), f32[64,8,128]{2,1,0:T(8,128)S(1)}, u32[]{:S(2)}, u32[]{:S(2)}) async-start(f32[64,8,128]{2,1,0:T(8,128)} %bitcast.8), calls=%async_computation.1 | async-start | bytes 524288 | tf_op jit(solution)/shard_map/all_to_all | solution.py:25
  74.2 9.5 %all-to-all-start.2 = ((f32[4,128,128]{2,1,0:T(8,128)}), f32[4,128,128]{2,1,0:T(8,128)S(1)}, u32[]{:S(2)}, u32[]{:S(2)}) async-start(f32[4,128,128]{2,1,0:T(8,128)} %broadcast_in_dim.169), calls=%async_computation.2 | async-start | bytes 524288 | tf_op jit(solution)/shard_map/all_to_all | solution.py:25
  85.7 16.3 %all-to-all-start.3 = ((f32[32,16,128]{2,1,0:T(8,128)}), f32[32,16,128]{2,1,0:T(8,128)S(1)}, u32[]{:S(2)}, u32[]{:S(2)}) async-start(f32[32,16,128]{2,1,0:T(8,128)} %bitcast.20), calls=%async_computation.3 | async-start | bytes 524288 | tf_op jit(solution)/shard_map/all_to_all | solution.py:25
  90.4 23.6 %collective-permute-start.10 = (f32[3,64,512]{2,1,0:T(8,128)}, f32[3,64,512]{2,1,0:T(8,128)}, u32[]{:S(2)}, u32[]{:S(2)}) collective-permute-start(f32[3,64,512]{2,1,0:T(8,128)} %pad_maximum_fusion.1), channel_id=1, source_target_pairs={{0,1},{1,0},{2,3},{3,2},{4,5},{5,4},{6,7},{7,6},{8,9},{9,8},{10,11... | collective-permute-start | bytes 1179656 | tf_op jit(solution)/shard_map/ppermute | solution.py:63
  95.0 41.4 %collective-permute-start.14 = (f32[4,64,512]{2,1,0:T(8,128)S(1)}, f32[4,64,512]{2,1,0:T(8,128)S(1)}, u32[]{:S(2)}, u32[]{:S(2)}) collective-permute-start(f32[4,64,512]{2,1,0:T(8,128)S(1)} %pad_maximum_fusion), channel_id=1, source_target_pairs={{0,8},{8,0},{16,24},{24,16},{32,40},{40,32},{48,56},{56,48},{64,72... | collective-permute-start | bytes 1572872 | tf_op jit(solution)/shard_map/ppermute | solution.py:60
  98.0 17.7 %collective-permute-start.11 = (f32[3,64,512]{2,1,0:T(8,128)}, f32[3,64,512]{2,1,0:T(8,128)S(1)}, u32[]{:S(2)}, u32[]{:S(2)}) collective-permute-start(f32[3,64,512]{2,1,0:T(8,128)} %collective-permute-done.9), channel_id=1, source_target_pairs={{0,1},{1,0},{2,3},{3,2},{4,5},{5,4},{6,7},{7,6},{8,9},{9,8},{10,11... | collective-permute-start | bytes 1179656 | tf_op jit(solution)/shard_map/ppermute | solution.py:63
  102.7 24.2 %all-to-all-start.4 = ((f32[32,16,128]{2,1,0:T(8,128)}), f32[32,16,128]{2,1,0:T(8,128)S(1)}, u32[]{:S(2)}, u32[]{:S(2)}) async-start(f32[32,16,128]{2,1,0:T(8,128)} %broadcast_in_dim.170), calls=%async_computation.4 | async-start | bytes 524288 | tf_op jit(solution)/shard_map/all_to_all | solution.py:25
  129.2 9.2 %all-to-all-start.5 = ((f32[4,128,128]{2,1,0:T(8,128)}), f32[4,128,128]{2,1,0:T(8,128)S(1)}, u32[]{:S(2)}, u32[]{:S(2)}) async-start(f32[4,128,128]{2,1,0:T(8,128)} %broadcast_in_dim.171), calls=%async_computation.5 | async-start | bytes 524288 | tf_op jit(solution)/shard_map/all_to_all | solution.py:25
  132.6 15.1 %collective-permute-start.15 = (f32[4,64,512]{2,1,0:T(8,128)S(1)}, f32[4,64,512]{2,1,0:T(8,128)S(1)}, u32[]{:S(2)}, u32[]{:S(2)}) collective-permute-start(f32[4,64,512]{2,1,0:T(8,128)S(1)} %pad_maximum_fusion), channel_id=1, source_target_pairs={{0,1},{1,0},{2,3},{3,2},{4,5},{5,4},{6,7},{7,6},{8,9},{9,8},{10,11... | collective-permute-start | bytes 1572872 | tf_op jit(solution)/shard_map/ppermute | solution.py:63
  136.4 28.1 %collective-permute-start.16 = (f32[4,64,512]{2,1,0:T(8,128)S(1)}, f32[4,64,512]{2,1,0:T(8,128)S(1)}, u32[]{:S(2)}, u32[]{:S(2)}) collective-permute-start(f32[4,64,512]{2,1,0:T(8,128)S(1)} %collective-permute-done.14), channel_id=1, source_target_pairs={{0,1},{1,0},{2,3},{3,2},{4,5},{5,4},{6,7},{7,6},{8,9},{9,8},{10,11... | collective-permute-start | bytes 1572872 | tf_op jit(solution)/shard_map/ppermute | solution.py:63
  141.3 17.2 %all-to-all-start.6 = ((f32[32,16,128]{2,1,0:T(8,128)}), f32[32,16,128]{2,1,0:T(8,128)S(1)}, u32[]{:S(2)}, u32[]{:S(2)}) async-start(f32[32,16,128]{2,1,0:T(8,128)} %bitcast.187), calls=%async_computation.6 | async-start | bytes 524288 | tf_op jit(solution)/shard_map/all_to_all | solution.py:25
  148.6 27.3 %copy-start.2 = (f32[64,512]{1,0:T(8,128)S(1)}, f32[64,512]{1,0:T(8,128)}, u32[]{:S(2)}) copy-start(f32[64,512]{1,0:T(8,128)} %get-tuple-element.27) | copy-start | bytes 393220
  148.6 27.3 %copy-start.5 = (f32[64,512]{1,0:T(8,128)S(1)}, f32[64,512]{1,0:T(8,128)}, u32[]{:S(2)}) copy-start(f32[64,512]{1,0:T(8,128)} %get-tuple-element.38) | copy-start | bytes 393220
  159.3 16.6 %all-to-all-start.7 = ((f32[32,16,128]{2,1,0:T(8,128)}), f32[32,16,128]{2,1,0:T(8,128)S(1)}, u32[]{:S(2)}, u32[]{:S(2)}) async-start(f32[32,16,128]{2,1,0:T(8,128)} %broadcast_in_dim.172), calls=%async_computation.7 | async-start | bytes 524288 | tf_op jit(solution)/shard_map/all_to_all | solution.py:25
  177.3 24.2 %all-to-all-start.8 = ((f32[4,128,128]{2,1,0:T(8,128)}), f32[4,128,128]{2,1,0:T(8,128)S(1)}, u32[]{:S(2)}, u32[]{:S(2)}) async-start(f32[4,128,128]{2,1,0:T(8,128)} %broadcast_in_dim.174), calls=%async_computation.8 | async-start | bytes 524288 | tf_op jit(solution)/shard_map/all_to_all | solution.py:25
  192.1 17.1 %collective-permute-start.1 = (f32[512,128]{1,0:T(8,128)S(1)}, f32[512,128]{1,0:T(8,128)}, u32[]{:S(2)}, u32[]{:S(2)}) collective-permute-start(f32[512,128]{1,0:T(8,128)S(1)} %bitcast.180), channel_id=1, source_target_pairs={{0,1},{1,0},{2,3},{3,2},{4,5},{5,4},{6,7},{7,6},{8,9},{9,8},{10,11... | collective-permute-start | bytes 786440 | tf_op jit(solution)/shard_map/ppermute | solution.py:63
  197.1 12.0 %collective-permute-start.7 = (f32[512,128]{1,0:T(8,128)S(1)}, f32[512,128]{1,0:T(8,128)}, u32[]{:S(2)}, u32[]{:S(2)}) collective-permute-start(f32[512,128]{1,0:T(8,128)S(1)} %bitcast.183), channel_id=1, source_target_pairs={{0,1},{1,0},{2,3},{3,2},{4,5},{5,4},{6,7},{7,6},{8,9},{9,8},{10,11... | collective-permute-start | bytes 786440 | tf_op jit(solution)/shard_map/ppermute | solution.py:63
  199.0 10.1 %collective-permute-start.12 = (f32[512,128]{1,0:T(8,128)S(1)}, f32[512,128]{1,0:T(8,128)}, u32[]{:S(2)}, u32[]{:S(2)}) collective-permute-start(f32[512,128]{1,0:T(8,128)S(1)} %bitcast.185), channel_id=1, source_target_pairs={{0,1},{1,0},{2,3},{3,2},{4,5},{5,4},{6,7},{7,6},{8,9},{9,8},{10,11... | collective-permute-start | bytes 786440 | tf_op jit(solution)/shard_map/ppermute | solution.py:63
  204.5 25.4 %all-to-all-start.9 = ((f32[32,16,128]{2,1,0:T(8,128)}), f32[32,16,128]{2,1,0:T(8,128)S(1)}, u32[]{:S(2)}, u32[]{:S(2)}) async-start(f32[32,16,128]{2,1,0:T(8,128)} %bitcast.56), calls=%async_computation.9 | async-start | bytes 524288 | tf_op jit(solution)/shard_map/all_to_all | solution.py:25
  210.6 13.6 %collective-permute-start.2 = (f32[512,128]{1,0:T(8,128)S(1)}, f32[512,128]{1,0:T(8,128)S(1)}, u32[]{:S(2)}, u32[]{:S(2)}) collective-permute-start(f32[512,128]{1,0:T(8,128)S(1)} %maximum_select_fusion), channel_id=1, source_target_pairs={{0,8},{8,0},{16,24},{24,16},{32,40},{40,32},{48,56},{56,48},{64,72... | collective-permute-start | bytes 786440 | tf_op jit(solution)/shard_map/ppermute | solution.py:60
  213.2 16.6 %collective-permute-start.8 = (f32[512,128]{1,0:T(8,128)S(1)}, f32[512,128]{1,0:T(8,128)S(1)}, u32[]{:S(2)}, u32[]{:S(2)}) collective-permute-start(f32[512,128]{1,0:T(8,128)S(1)} %maximum_select_fusion.1), channel_id=1, source_target_pairs={{0,8},{8,0},{16,24},{24,16},{32,40},{40,32},{48,56},{56,48},{64,72... | collective-permute-start | bytes 786440 | tf_op jit(solution)/shard_map/ppermute | solution.py:60
  217.2 30.3 %collective-permute-start.13 = (f32[512,128]{1,0:T(8,128)}, f32[512,128]{1,0:T(8,128)}, u32[]{:S(2)}, u32[]{:S(2)}) collective-permute-start(f32[512,128]{1,0:T(8,128)} %maximum_select_fusion.2), channel_id=1, source_target_pairs={{0,8},{8,0},{16,24},{24,16},{32,40},{40,32},{48,56},{56,48},{64,72... | collective-permute-start | bytes 786440 | tf_op jit(solution)/shard_map/ppermute | solution.py:60
  229.9 3.3 %collective-permute-start.17 = (f32[16,128]{1,0:T(8,128)S(1)}, f32[16,128]{1,0:T(8,128)S(1)}, u32[]{:S(2)}, u32[]{:S(2)}) collective-permute-start(f32[16,128]{1,0:T(8,128)S(1)} %reduce_sum.78), channel_id=1, source_target_pairs={{0,1},{1,0},{2,3},{3,2},{4,5},{5,4},{6,7},{7,6},{8,9},{9,8},{10,11... | collective-permute-start | bytes 24584 | tf_op jit(solution)/shard_map/ppermute | solution.py:63
  234.2 26.9 %all-to-all-start.10 = ((f32[64,16,128]{2,1,0:T(8,128)}), f32[64,16,128]{2,1,0:T(8,128)}, u32[]{:S(2)}, u32[]{:S(2)}) async-start(f32[64,16,128]{2,1,0:T(8,128)} %broadcast_in_dim.175), calls=%async_computation.10 | async-start | bytes 1048576 | tf_op jit(solution)/shard_map/all_to_all | solution.py:25
  266.0 14.4 %all-to-all-start.11 = ((f32[8,32,256]{2,1,0:T(8,128)}), f32[8,32,256]{2,1,0:T(8,128)S(1)}, u32[]{:S(2)}, u32[]{:S(2)}) async-start(f32[8,32,256]{2,1,0:T(8,128)} %bitcast.73), calls=%async_computation.11 | async-start | bytes 524288 | tf_op jit(solution)/shard_map/all_to_all | solution.py:25
  (11 other events, 232.3 us)

commit v5 on v0

v5 whole, which is shorter than its diff:
```python
import jax
import jax.numpy as jnp
from jax import lax
from jax.sharding import PartitionSpec as P

PRECISION = lax.Precision.HIGHEST
CORES = 2


def pair_index(block_row, prior_row):
    return block_row * (block_row - 1) // 2 + prior_row


def contract(left, right, axes):
    return lax.dot_general(
        left,
        right,
        (((axes[0],), (axes[1],)), ((), ())),
        precision=PRECISION,
        preferred_element_type=jnp.float32,
    )


def swap(parts, axis, groups=None):
    return lax.all_to_all(parts, axis, 0, 0, axis_index_groups=groups, tiled=True)


def copies(part, count):
    return jnp.broadcast_to(part[None], (count,) + part.shape)


def halves_swapped(value):
    return jnp.roll(value, value.shape[-1] // 2, value.ndim - 1)


def tie(*values):
    return lax.optimization_barrier(values)


def shards(right_sides, diag_inverse, lower_blocks, trail_panel):
    step_count = diag_inverse.shape[0]
    trail_count = trail_panel.shape[0]
    local_rows = right_sides.shape[1]
    column_count = right_sides.shape[2]
    width = lower_blocks.shape[2]
    row_size = lax.axis_size("row")
    col_size = lax.axis_size("col")
    members = row_size // 2
    chips = col_size // CORES
    half = column_count // 2
    quarter = half // 2
    row = lax.axis_index("row")
    col = lax.axis_index("col")
    parity = row % 2
    core = col % CORES
    row_groups = [[r for r in range(row_size) if r % 2 == g] for g in range(2)]
    chip_groups = [[c for c in range(col_size) if c % CORES == g] for g in range(CORES)]
    row_pairs = [(r, r ^ 1) for r in range(row_size)]
    core_pairs = [(c, c ^ 1) for c in range(col_size)]
    low = lax.broadcasted_iota(jnp.int32, (1, half), 1) < quarter

    def from_row(value):
        return lax.ppermute(value, "row", row_pairs)

    def from_core(value):
        return lax.ppermute(value, "col", core_pairs)

    own_diag = diag_inverse.transpose(0, 2, 1)
    own_sides = lax.dynamic_slice_in_dim(right_sides[:step_count], parity * half, half, 2)
    sent_sides = lax.dynamic_slice_in_dim(right_sides[:step_count], (1 - parity) * half, half, 2)

    def side_of(block_row, received):
        value = jnp.concatenate([own_sides[block_row], received])
        return jnp.where(low == (core == 0), value, halves_swapped(value))

    def matrix(pieces, index):
        return jnp.concatenate([p[:, index * width : (index + 1) * width] for p in pieces])

    def update_of(matrices, solved_block):
        both = contract(matrices, solved_block, (1, 0))
        rows = 2 * local_rows
        return jnp.where(low, both[:rows], both[rows:])

    def partial_of(matrices, current):
        zero = jnp.zeros_like(current)
        spread = jnp.concatenate([jnp.where(low, current, zero), jnp.where(low, zero, current)])
        return contract(matrices, spread, (0, 0))

    def scattered(value):
        parts = value.reshape(members, width // members, half)
        return swap(parts, "row", row_groups)

    def gathered(part):
        return swap(copies(part, members), "row", row_groups)

    def summed(update):
        return swap(copies(update, chips), "col", chip_groups)

    def current_of(side, parts):
        total = parts.sum(0)
        return side - (total + halves_swapped(total))

    def by_core(value, other):
        straight = jnp.where(low, value, other)
        return jnp.where(core == 0, straight, halves_swapped(straight))

    def by_parity(value, other):
        return jnp.concatenate(
            [jnp.where(parity == 0, value, other), jnp.where(parity == 0, other, value)], 1
        )

    trail = [trail_panel[:, :, j, :] for j in range(step_count)]

    def below_of(whole, block_row):
        return jnp.einsum("nc,mrn->cmr", whole, trail[block_row], precision=PRECISION)

    front = jnp.concatenate([own_diag[0], sent_sides[0]], 1)
    front_row = from_row(front)
    front_core = from_core(own_diag[0])
    front_both = from_core(front_row)
    pieces = [own_diag[0], front_row, front_core, front_both]
    current = side_of(0, front_row[:, width:])
    local_term = partial_of(matrix(pieces, 0), current)
    parts = scattered(local_term)

    first = jnp.concatenate(
        [lower_blocks[0], own_diag[1]] + [sent_sides[i] for i in range(1, step_count)], 1
    )
    first, _ = tie(first, front_both)
    first_row, first_core = from_row(first), from_core(first[:, : 2 * width])
    parts, first_row, first_core = tie(parts, first_row, first_core)
    part = parts.sum(0)

    second = jnp.concatenate([lower_blocks[1], lower_blocks[2], own_diag[2]], 1)
    second, _ = tie(second, first_row)
    first_both = from_core(first_row)
    second_row, second_core = from_row(second), from_core(second)
    parts = gathered(part)
    parts, first_both, second_row, second_core = tie(parts, first_both, second_row, second_core)
    solved_0 = parts.reshape(width, half)
    firsts = [first, first_row, first_core, first_both]

    sides = [
        side_of(i, first_row[:, 2 * width + (i - 1) * half : 2 * width + i * half])
        for i in range(1, step_count)
    ]
    parts = summed(update_of(matrix(firsts, 0), solved_0))
    third = jnp.concatenate([lower_blocks[3], lower_blocks[4], lower_blocks[5], own_diag[3]], 1)
    third, _ = tie(third, solved_0)
    third_row, third_core = from_row(third), from_core(third)
    second_both = from_core(second_row)
    current = current_of(sides[0], parts)
    parts = scattered(partial_of(matrix(firsts, 1), current))
    core_0 = from_core(solved_0)
    parts, second_both, third_row, third_core, core_0 = tie(
        parts, second_both, third_row, third_core, core_0
    )
    part = parts.sum(0)
    seconds = [second, second_row, second_core, second_both]
    pending_2 = update_of(matrix(seconds, 0), solved_0)
    straight_0 = by_core(solved_0, core_0)
    whole_0 = by_parity(straight_0, from_row(straight_0))
    third_both = from_core(third_row)
    parts = gathered(part)
    parts, whole_0, third_both, pending_2 = tie(parts, whole_0, third_both, pending_2)
    solved_1 = parts.reshape(width, half)
    thirds = [third, third_row, third_core, third_both]

    parts = summed(pending_2 + update_of(matrix(seconds, 1), solved_1))
    current = current_of(sides[1], parts)
    parts = scattered(partial_of(matrix(seconds, 2), current))
    below = below_of(whole_0, 0)
    core_1 = from_core(solved_1)
    parts, below, core_1 = tie(parts, below, core_1)
    part = parts.sum(0)
    straight_1 = by_core(solved_1, core_1)
    whole_1 = by_parity(straight_1, from_row(straight_1))
    pending_3 = update_of(matrix(thirds, 0), solved_0) + update_of(matrix(thirds, 1), solved_1)
    parts = gathered(part)
    parts, whole_1, pending_3 = tie(parts, whole_1, pending_3)
    solved_2 = parts.reshape(width, half)

    parts = summed(pending_3 + update_of(matrix(thirds, 2), solved_2))
    core_2 = from_core(solved_2)
    current = current_of(sides[2], parts)
    parts = scattered(partial_of(matrix(thirds, 3), current))
    straight_2 = by_core(solved_2, core_2)
    row_2 = from_row(straight_2)
    below = below + below_of(whole_1, 1)
    parts, below, row_2 = tie(parts, below, row_2)
    part = parts.sum(0)
    part = by_core(part, from_core(part))
    parts = swap(copies(part, row_size), "row")
    whole_2 = by_parity(straight_2, row_2)
    below = below + below_of(whole_2, 2)
    parts, below = tie(parts, below)
    parts = parts.reshape(members, 2, width // members, half)
    whole_3 = parts.transpose(0, 2, 1, 3).reshape(width, column_count)

    below = below + below_of(whole_3, 3)
    shared = swap(below.reshape(column_count, -1), "col")
    own_width = column_count // col_size
    shared = shared.reshape(col_size, own_width, -1).sum(0)
    shared = shared.reshape(own_width, trail_count, local_rows).transpose(1, 2, 0)
    own_below = lax.dynamic_slice_in_dim(right_sides[step_count:], col * own_width, own_width, 2)
    trail_rest = own_below - shared

    out_width = column_count // row_size
    outs = [
        lax.dynamic_slice_in_dim(whole, row * out_width, out_width, 1)
        for whole in (whole_0, whole_1, whole_2, whole_3)
    ]
    return (jnp.stack(outs), trail_rest)


def solution(mesh):
    placed = (
        P(None, "row", None),
        P(None, "col", "row"),
        P(None, "row", "col"),
        P(None, "row", None, "col"),
    )
    return jax.shard_map(
        shards,
        mesh=mesh,
        in_specs=placed,
        out_specs=(P(None, "col", "row"), P(None, "row", "col")),
        check_vma=False,
    )
```

time: 932 us -> 293 us (0.31)
  waiting for transfers between devices: 884 us -> 87.7 us
  starting transfers between devices: 0.33 us -> 146 us
  local copies, waits for them, and re-layouts: 6.87 us -> 28.2 us
  between operations: 15 us -> 1.83 us
    psum x7 -> x0, waiting for transfers between devices: 815 us -> none  [the longest x4 610 us: shards(): solved_block = lax.psum(local_term, 'row')]
    all_to_all x0 -> x12, starting transfers between devices: none -> 78 us  [swap(): lax.all_to_all(parts, axis, 0, 0, axis_index_groups=groups, tiled=True)]
    unnamed x9 -> x0, waiting for transfers between devices: 69.5 us -> none
    ppermute x0 -> x19, starting transfers between devices: none -> 68.1 us  [the longest x12 49.7 us: from_core(): return lax.ppermute(value, 'col', core_pairs)]
    all_to_all x0 -> x12, waiting for transfers between devices: none -> 56.1 us  [swap(): lax.all_to_all(parts, axis, 0, 0, axis_index_groups=groups, tiled=True)]
    ppermute x0 -> x19, waiting for transfers between devices: none -> 31.6 us  [the longest x7 28.8 us: from_row(): return lax.ppermute(value, 'row', row_pairs)]
    slice x1 -> x23, local copies, waits for them, and re-layouts: 2.77 us -> 13.5 us  [the longest x12 8.67 us: matrix(): p[:, index * width:(index + 1) * width]]
  transfers between devices with their start and end apart: 8 -> 31, of which waited for: 8 -> 15; matrix products, arithmetic and copies ran while one was open for 1% -> 12% of each run, Pallas kernels for 0% -> 0%
where the time goes in v5:
time: 293 us; the launch traced here: 291 us
  starting transfers between devices  146 us (50%)
  waiting for transfers between devices  87.7 us (30%)
  local copies, waits for them, and re-layouts  28.2 us (10%)
  matrix products  18.9 us (6%)
  other arithmetic  7.93 us (3%)
    all_to_all x12, starting transfers between devices, swap(): lax.all_to_all(parts, axis, 0, 0, axis_index_groups=groups, tiled=True)  78 us
    all_to_all x12, waiting for transfers between devices, swap(): lax.all_to_all(parts, axis, 0, 0, axis_index_groups=groups, tiled=True)  56.1 us
    ppermute x12, starting transfers between devices, from_core(): return lax.ppermute(value, 'col', core_pairs)  49.7 us
    ppermute x7, waiting for transfers between devices, from_row(): return lax.ppermute(value, 'row', row_pairs)  28.8 us
    ppermute x7, starting transfers between devices, from_row(): return lax.ppermute(value, 'row', row_pairs)  18.5 us
    dot_general x10, matrix products, contract(): lax.dot_general(left, right, (((axes[0],), (axes[1],)), ((), ())), precis...  16.3 us
    slice x12, local copies, waits for them, and re-layouts, matrix(): p[:, index * width:(index + 1) * width]  8.67 us
  transfers between devices with their start and end apart: 31, of which 15 were waited for; matrix products, arithmetic and copies ran while one was open for 12% of the time, Pallas kernels for 0%

profile of v5, /device:TPU:1, one launch (start us, length us, event | category | flops | bytes accessed | tf_op | source)
XLA Modules:
  0.0 290.6 jit_solution(11906074944396615897)
XLA Ops:
  1.8 8.8 %collective-permute-start.2 = (f32[64,512]{1,0:T(8,128)S(1)}, f32[64,512]{1,0:T(8,128)S(1)}, u32[]{:S(2)}, u32[]{:S(2)}) collective-permute-start(f32[64,512]{1,0:T(8,128)S(1)} %get-tuple-element.111), channel_id=1, source_target_pairs={{0,1},{1,0},{2,3},{3,2},{4,5},{5,4},{6,7},{7,6},{8,9},{9,8},{10,11... | collective-permute-start | bytes 393224 | tf_op jit(solution)/shard_map/ppermute | solution.py:66
  15.4 4.8 %collective-permute-done = f32[64,640]{1,0:T(8,128)S(1)} collective-permute-done((f32[64,640]{1,0:T(8,128)S(1)}, f32[64,640]{1,0:T(8,128)S(1)}, u32[]{:S(2)}, u32[]{:S(2)}) %collective-permute-start) | collective-permute-done | bytes 163872 | tf_op jit(solution)/shard_map/ppermute | solution.py:63
  25.8 10.3 %all-to-all-start = ((f32[32,16,128]{2,1,0:T(8,128)}), f32[32,16,128]{2,1,0:T(8,128)S(1)}, u32[]{:S(2)}, u32[]{:S(2)}) async-start(f32[32,16,128]{2,1,0:T(8,128)} %bitcast.9), calls=%async_computation | async-start | bytes 524288 | tf_op jit(solution)/shard_map/all_to_all | solution.py:25
  36.1 3.1 %collective-permute-start.3 = (f32[64,1408]{1,0:T(8,128)S(1)}, f32[64,1408]{1,0:T(8,128)}, u32[]{:S(2)}, u32[]{:S(2)}) collective-permute-start(f32[64,1408]{1,0:T(8,128)S(1)} %fusion.119), channel_id=1, source_target_pairs={{0,8},{8,0},{16,24},{24,16},{32,40},{40,32},{48,56},{56,48},{64,72... | collective-permute-start | bytes 1081352 | tf_op jit(solution)/shard_map/ppermute | solution.py:63
  39.2 2.8 collective-permute-start.4
  43.2 9.9 %collective-permute-done.3 = f32[64,1408]{1,0:T(8,128)} collective-permute-done((f32[64,1408]{1,0:T(8,128)S(1)}, f32[64,1408]{1,0:T(8,128)}, u32[]{:S(2)}, u32[]{:S(2)}) %collective-permute-start.3) | collective-permute-done | bytes 360480 | tf_op jit(solution)/shard_map/ppermute | solution.py:63
  53.8 10.0 %all-to-all-start.1 = ((f32[32,16,128]{2,1,0:T(8,128)}), f32[32,16,128]{2,1,0:T(8,128)S(1)}, u32[]{:S(2)}, u32[]{:S(2)}) async-start(f32[32,16,128]{2,1,0:T(8,128)} %broadcast_in_dim.157), calls=%async_computation.1 | async-start | bytes 524288 | tf_op jit(solution)/shard_map/all_to_all | solution.py:25
  66.5 3.0 %collective-permute-start.7 = (f32[64,1536]{1,0:T(8,128)S(1)}, f32[64,1536]{1,0:T(8,128)S(1)}, u32[]{:S(2)}, u32[]{:S(2)}) collective-permute-start(f32[64,1536]{1,0:T(8,128)S(1)} %pad_maximum_fusion.4), channel_id=1, source_target_pairs={{0,1},{1,0},{2,3},{3,2},{4,5},{5,4},{6,7},{7,6},{8,9},{9,8},{10,11... | collective-permute-start | bytes 1179656 | tf_op jit(solution)/shard_map/ppermute | solution.py:66
  73.8 7.2 %collective-permute-done.6 = f32[64,1536]{1,0:T(8,128)S(1)} collective-permute-done((f32[64,1536]{1,0:T(8,128)S(1)}, f32[64,1536]{1,0:T(8,128)S(1)}, u32[]{:S(2)}, u32[]{:S(2)}) %collective-permute-start.6) | collective-permute-done | bytes 393248 | tf_op jit(solution)/shard_map/ppermute | solution.py:63
  83.1 4.0 %all-to-all-start.2 = ((f32[4,128,128]{2,1,0:T(8,128)}), f32[4,128,128]{2,1,0:T(8,128)S(1)}, u32[]{:S(2)}, u32[]{:S(2)}) async-start(f32[4,128,128]{2,1,0:T(8,128)} %broadcast_in_dim.158), calls=%async_computation.2 | async-start | bytes 524288 | tf_op jit(solution)/shard_map/all_to_all | solution.py:25
  89.2 3.1 %collective-permute-start.10 = (f32[64,2048]{1,0:T(8,128)S(1)}, f32[64,2048]{1,0:T(8,128)S(1)}, u32[]{:S(2)}, u32[]{:S(2)}) collective-permute-start(f32[64,2048]{1,0:T(8,128)S(1)} %pad_maximum_fusion.1), channel_id=1, source_target_pairs={{0,1},{1,0},{2,3},{3,2},{4,5},{5,4},{6,7},{7,6},{8,9},{9,8},{10,11... | collective-permute-start | bytes 1572872 | tf_op jit(solution)/shard_map/ppermute | solution.py:66
  92.3 2.8 collective-permute-start.9
  99.1 9.6 %all-to-all-start.3 = ((f32[32,16,128]{2,1,0:T(8,128)}), f32[32,16,128]{2,1,0:T(8,128)S(1)}, u32[]{:S(2)}, u32[]{:S(2)}) async-start(f32[32,16,128]{2,1,0:T(8,128)} %bitcast.108), calls=%async_computation.3 | async-start | bytes 524288 | tf_op jit(solution)/shard_map/all_to_all | solution.py:25
  116.3 5.3 %all-to-all-done.3 = f32[32,16,128]{2,1,0:T(8,128)S(1)} async-done(((f32[32,16,128]{2,1,0:T(8,128)}), f32[32,16,128]{2,1,0:T(8,128)S(1)}, u32[]{:S(2)}, u32[]{:S(2)}) %all-to-all-start.3) | async-done | bytes 262176 | tf_op jit(solution)/shard_map/all_to_all | solution.py:25
  121.6 3.8 %collective-permute-start.13 = (f32[64,2048]{1,0:T(8,128)S(1)}, f32[64,2048]{1,0:T(8,128)S(1)}, u32[]{:S(2)}, u32[]{:S(2)}) collective-permute-start(f32[64,2048]{1,0:T(8,128)S(1)} %collective-permute-done.9), channel_id=1, source_target_pairs={{0,1},{1,0},{2,3},{3,2},{4,5},{5,4},{6,7},{7,6},{8,9},{9,8},{10,11... | collective-permute-start | bytes 1572872 | tf_op jit(solution)/shard_map/ppermute | solution.py:66
  131.7 5.3 %all-to-all-start.4 = ((f32[32,16,128]{2,1,0:T(8,128)}), f32[32,16,128]{2,1,0:T(8,128)}, u32[]{:S(2)}, u32[]{:S(2)}) async-start(f32[32,16,128]{2,1,0:T(8,128)} %broadcast_in_dim.159), calls=%async_computation.4 | async-start | bytes 524288 | tf_op jit(solution)/shard_map/all_to_all | solution.py:25
  139.7 10.2 %all-to-all-done.4 = f32[32,16,128]{2,1,0:T(8,128)} async-done(((f32[32,16,128]{2,1,0:T(8,128)}), f32[32,16,128]{2,1,0:T(8,128)}, u32[]{:S(2)}, u32[]{:S(2)}) %all-to-all-start.4) | async-done | bytes 262176 | tf_op jit(solution)/shard_map/all_to_all | solution.py:25
  156.7 4.5 %all-to-all-start.5 = ((f32[4,128,128]{2,1,0:T(8,128)}), f32[4,128,128]{2,1,0:T(8,128)S(1)}, u32[]{:S(2)}, u32[]{:S(2)}) async-start(f32[4,128,128]{2,1,0:T(8,128)} %broadcast_in_dim.161), calls=%async_computation.5 | async-start | bytes 524288 | tf_op jit(solution)/shard_map/all_to_all | solution.py:25
  161.3 4.1 %collective-permute-start.14 = (f32[512,128]{1,0:T(8,128)}, f32[512,128]{1,0:T(8,128)}, u32[]{:S(2)}, u32[]{:S(2)}) collective-permute-start(f32[512,128]{1,0:T(8,128)} %bitcast.22), channel_id=1, source_target_pairs={{0,1},{1,0},{2,3},{3,2},{4,5},{5,4},{6,7},{7,6},{8,9},{9,8},{10,11... | collective-permute-start | bytes 786440 | tf_op jit(solution)/shard_map/ppermute | solution.py:66
  169.7 5.9 %all-to-all-start.6 = ((f32[32,16,128]{2,1,0:T(8,128)}), f32[32,16,128]{2,1,0:T(8,128)S(1)}, u32[]{:S(2)}, u32[]{:S(2)}) async-start(f32[32,16,128]{2,1,0:T(8,128)} %bitcast.23), calls=%async_computation.6 | async-start | bytes 524288 | tf_op jit(solution)/shard_map/all_to_all | solution.py:25
  179.0 8.1 %all-to-all-done.6 = f32[32,16,128]{2,1,0:T(8,128)S(1)} async-done(((f32[32,16,128]{2,1,0:T(8,128)}), f32[32,16,128]{2,1,0:T(8,128)S(1)}, u32[]{:S(2)}, u32[]{:S(2)}) %all-to-all-start.6) | async-done | bytes 262176 | tf_op jit(solution)/shard_map/all_to_all | solution.py:25
  192.0 4.5 %all-to-all-start.7 = ((f32[32,16,128]{2,1,0:T(8,128)}), f32[32,16,128]{2,1,0:T(8,128)S(1)}, u32[]{:S(2)}, u32[]{:S(2)}) async-start(f32[32,16,128]{2,1,0:T(8,128)} %broadcast_in_dim.162), calls=%async_computation.7 | async-start | bytes 524288 | tf_op jit(solution)/shard_map/all_to_all | solution.py:25
  196.6 11.5 %all-to-all-done.7 = f32[32,16,128]{2,1,0:T(8,128)S(1)} async-done(((f32[32,16,128]{2,1,0:T(8,128)}), f32[32,16,128]{2,1,0:T(8,128)S(1)}, u32[]{:S(2)}, u32[]{:S(2)}) %all-to-all-start.7) | async-done | bytes 262176 | tf_op jit(solution)/shard_map/all_to_all | solution.py:25
  209.4 3.4 %all-to-all-start.8 = ((f32[4,128,128]{2,1,0:T(8,128)}), f32[4,128,128]{2,1,0:T(8,128)S(1)}, u32[]{:S(2)}, u32[]{:S(2)}) async-start(f32[4,128,128]{2,1,0:T(8,128)} %broadcast_in_dim.163), calls=%async_computation.8 | async-start | bytes 524288 | tf_op jit(solution)/shard_map/all_to_all | solution.py:25
  212.9 7.0 %collective-permute-start.16 = (f32[512,128]{1,0:T(8,128)S(1)}, f32[512,128]{1,0:T(8,128)S(1)}, u32[]{:S(2)}, u32[]{:S(2)}) collective-permute-start(f32[512,128]{1,0:T(8,128)S(1)} %bitcast.105), channel_id=1, source_target_pairs={{0,1},{1,0},{2,3},{3,2},{4,5},{5,4},{6,7},{7,6},{8,9},{9,8},{10,11... | collective-permute-start | bytes 786440 | tf_op jit(solution)/shard_map/ppermute | solution.py:66
  222.0 4.4 %all-to-all-start.9 = ((f32[32,16,128]{2,1,0:T(8,128)}), f32[32,16,128]{2,1,0:T(8,128)S(1)}, u32[]{:S(2)}, u32[]{:S(2)}) async-start(f32[32,16,128]{2,1,0:T(8,128)} %bitcast.29), calls=%async_computation.9 | async-start | bytes 524288 | tf_op jit(solution)/shard_map/all_to_all | solution.py:25
  230.0 6.9 %collective-permute-done.17 = f32[512,128]{1,0:T(8,128)} collective-permute-done((f32[512,128]{1,0:T(8,128)S(1)}, f32[512,128]{1,0:T(8,128)}, u32[]{:S(2)}, u32[]{:S(2)}) %collective-permute-start.17) | collective-permute-done | bytes 262176 | tf_op jit(solution)/shard_map/ppermute | solution.py:63
  238.0 8.0 %collective-permute-start.18 = (f32[16,128]{1,0:T(8,128)S(1)}, f32[16,128]{1,0:T(8,128)S(1)}, u32[]{:S(2)}, u32[]{:S(2)}) collective-permute-start(f32[16,128]{1,0:T(8,128)S(1)} %reduce_sum.78), channel_id=1, source_target_pairs={{0,1},{1,0},{2,3},{3,2},{4,5},{5,4},{6,7},{7,6},{8,9},{9,8},{10,11... | collective-permute-start | bytes 24584 | tf_op jit(solution)/shard_map/ppermute | solution.py:66
  247.8 8.5 %all-to-all-start.10 = ((f32[64,16,128]{2,1,0:T(8,128)}), f32[64,16,128]{2,1,0:T(8,128)S(1)}, u32[]{:S(2)}, u32[]{:S(2)}) async-start(f32[64,16,128]{2,1,0:T(8,128)} %broadcast_in_dim.165), calls=%async_computation.10 | async-start | bytes 1048576 | tf_op jit(solution)/shard_map/all_to_all | solution.py:25
  260.0 13.1 %all-to-all-done.10 = f32[64,16,128]{2,1,0:T(8,128)S(1)} async-done(((f32[64,16,128]{2,1,0:T(8,128)}), f32[64,16,128]{2,1,0:T(8,128)S(1)}, u32[]{:S(2)}, u32[]{:S(2)}) %all-to-all-start.10) | async-done | bytes 524320 | tf_op jit(solution)/shard_map/all_to_all | solution.py:25
  275.7 7.6 %all-to-all-start.11 = ((f32[8,32,256]{2,1,0:T(8,128)}), f32[8,32,256]{2,1,0:T(8,128)S(1)}, u32[]{:S(2)}, u32[]{:S(2)}) async-start(f32[8,32,256]{2,1,0:T(8,128)} %all_to_all.50), calls=%async_computation.11 | async-start | bytes 524288 | tf_op jit(solution)/shard_map/all_to_all | solution.py:25
  284.3 5.6 %all-to-all-done.11 = f32[8,32,256]{2,1,0:T(8,128)S(1)} async-done(((f32[8,32,256]{2,1,0:T(8,128)}), f32[8,32,256]{2,1,0:T(8,128)S(1)}, u32[]{:S(2)}, u32[]{:S(2)}) %all-to-all-start.11) | async-done | bytes 262176 | tf_op jit(solution)/shard_map/all_to_all | solution.py:25
  (200 shorter events, 81.7 us)
Async XLA Ops:
  1.8 22.3 %collective-permute-start.2 = (f32[64,512]{1,0:T(8,128)S(1)}, f32[64,512]{1,0:T(8,128)S(1)}, u32[]{:S(2)}, u32[]{:S(2)}) collective-permute-start(f32[64,512]{1,0:T(8,128)S(1)} %get-tuple-element.111), channel_id=1, source_target_pairs={{0,1},{1,0},{2,3},{3,2},{4,5},{5,4},{6,7},{7,6},{8,9},{9,8},{10,11... | collective-permute-start | bytes 393224 | tf_op jit(solution)/shard_map/ppermute | solution.py:66
  12.4 7.7 %collective-permute-start = (f32[64,640]{1,0:T(8,128)S(1)}, f32[64,640]{1,0:T(8,128)S(1)}, u32[]{:S(2)}, u32[]{:S(2)}) collective-permute-start(f32[64,640]{1,0:T(8,128)S(1)} %pad_maximum_fusion.5), channel_id=1, source_target_pairs={{0,8},{8,0},{16,24},{24,16},{32,40},{40,32},{48,56},{56,48},{64,72... | collective-permute-start | bytes 491528 | tf_op jit(solution)/shard_map/ppermute | solution.py:63
  20.3 3.7 %collective-permute-start.1 = (f32[64,640]{1,0:T(8,128)S(1)}, f32[64,640]{1,0:T(8,128)S(1)}, u32[]{:S(2)}, u32[]{:S(2)}) collective-permute-start(f32[64,640]{1,0:T(8,128)S(1)} %collective-permute-done), channel_id=1, source_target_pairs={{0,1},{1,0},{2,3},{3,2},{4,5},{5,4},{6,7},{7,6},{8,9},{9,8},{10,11... | collective-permute-start | bytes 491528 | tf_op jit(solution)/shard_map/ppermute | solution.py:66
  25.8 27.3 %all-to-all-start = ((f32[32,16,128]{2,1,0:T(8,128)}), f32[32,16,128]{2,1,0:T(8,128)S(1)}, u32[]{:S(2)}, u32[]{:S(2)}) async-start(f32[32,16,128]{2,1,0:T(8,128)} %bitcast.9), calls=%async_computation | async-start | bytes 524288 | tf_op jit(solution)/shard_map/all_to_all | solution.py:25
  36.1 17.0 %collective-permute-start.3 = (f32[64,1408]{1,0:T(8,128)S(1)}, f32[64,1408]{1,0:T(8,128)}, u32[]{:S(2)}, u32[]{:S(2)}) collective-permute-start(f32[64,1408]{1,0:T(8,128)S(1)} %fusion.119), channel_id=1, source_target_pairs={{0,8},{8,0},{16,24},{24,16},{32,40},{40,32},{48,56},{56,48},{64,72... | collective-permute-start | bytes 1081352 | tf_op jit(solution)/shard_map/ppermute | solution.py:63
  39.2 4.0 %collective-permute-start.4 = (f32[64,1024]{1,0:T(8,128)S(1)}, f32[64,1024]{1,0:T(8,128)S(1)}, u32[]{:S(2)}, u32[]{:S(2)}) collective-permute-start(f32[64,1024]{1,0:T(8,128)S(1)} %slice.327), channel_id=1, source_target_pairs={{0,1},{1,0},{2,3},{3,2},{4,5},{5,4},{6,7},{7,6},{8,9},{9,8},{10,11... | collective-permute-start | bytes 786440 | tf_op jit(solution)/shard_map/ppermute | solution.py:66
  53.8 27.3 %all-to-all-start.1 = ((f32[32,16,128]{2,1,0:T(8,128)}), f32[32,16,128]{2,1,0:T(8,128)S(1)}, u32[]{:S(2)}, u32[]{:S(2)}) async-start(f32[32,16,128]{2,1,0:T(8,128)} %broadcast_in_dim.157), calls=%async_computation.1 | async-start | bytes 524288 | tf_op jit(solution)/shard_map/all_to_all | solution.py:25
  63.9 17.2 %collective-permute-start.6 = (f32[64,1536]{1,0:T(8,128)S(1)}, f32[64,1536]{1,0:T(8,128)S(1)}, u32[]{:S(2)}, u32[]{:S(2)}) collective-permute-start(f32[64,1536]{1,0:T(8,128)S(1)} %pad_maximum_fusion.4), channel_id=1, source_target_pairs={{0,8},{8,0},{16,24},{24,16},{32,40},{40,32},{48,56},{56,48},{64,72... | collective-permute-start | bytes 1179656 | tf_op jit(solution)/shard_map/ppermute | solution.py:63
  66.5 14.6 %collective-permute-start.7 = (f32[64,1536]{1,0:T(8,128)S(1)}, f32[64,1536]{1,0:T(8,128)S(1)}, u32[]{:S(2)}, u32[]{:S(2)}) collective-permute-start(f32[64,1536]{1,0:T(8,128)S(1)} %pad_maximum_fusion.4), channel_id=1, source_target_pairs={{0,1},{1,0},{2,3},{3,2},{4,5},{5,4},{6,7},{7,6},{8,9},{9,8},{10,11... | collective-permute-start | bytes 1179656 | tf_op jit(solution)/shard_map/ppermute | solution.py:66
  69.5 4.3 %collective-permute-start.5 = (f32[64,1408]{1,0:T(8,128)}, f32[64,1408]{1,0:T(8,128)S(1)}, u32[]{:S(2)}, u32[]{:S(2)}) collective-permute-start(f32[64,1408]{1,0:T(8,128)} %collective-permute-done.3), channel_id=1, source_target_pairs={{0,1},{1,0},{2,3},{3,2},{4,5},{5,4},{6,7},{7,6},{8,9},{9,8},{10,11... | collective-permute-start | bytes 1081352 | tf_op jit(solution)/shard_map/ppermute | solution.py:66
  83.1 12.1 %all-to-all-start.2 = ((f32[4,128,128]{2,1,0:T(8,128)}), f32[4,128,128]{2,1,0:T(8,128)S(1)}, u32[]{:S(2)}, u32[]{:S(2)}) async-start(f32[4,128,128]{2,1,0:T(8,128)} %broadcast_in_dim.158), calls=%async_computation.2 | async-start | bytes 524288 | tf_op jit(solution)/shard_map/all_to_all | solution.py:25
  89.2 26.4 %collective-permute-start.10 = (f32[64,2048]{1,0:T(8,128)S(1)}, f32[64,2048]{1,0:T(8,128)S(1)}, u32[]{:S(2)}, u32[]{:S(2)}) collective-permute-start(f32[64,2048]{1,0:T(8,128)S(1)} %pad_maximum_fusion.1), channel_id=1, source_target_pairs={{0,1},{1,0},{2,3},{3,2},{4,5},{5,4},{6,7},{7,6},{8,9},{9,8},{10,11... | collective-permute-start | bytes 1572872 | tf_op jit(solution)/shard_map/ppermute | solution.py:66
  92.3 23.9 %collective-permute-start.9 = (f32[64,2048]{1,0:T(8,128)S(1)}, f32[64,2048]{1,0:T(8,128)S(1)}, u32[]{:S(2)}, u32[]{:S(2)}) collective-permute-start(f32[64,2048]{1,0:T(8,128)S(1)} %pad_maximum_fusion.1), channel_id=1, source_target_pairs={{0,8},{8,0},{16,24},{24,16},{32,40},{40,32},{48,56},{56,48},{64,72... | collective-permute-start | bytes 1572872 | tf_op jit(solution)/shard_map/ppermute | solution.py:63
  99.1 22.5 %all-to-all-start.3 = ((f32[32,16,128]{2,1,0:T(8,128)}), f32[32,16,128]{2,1,0:T(8,128)S(1)}, u32[]{:S(2)}, u32[]{:S(2)}) async-start(f32[32,16,128]{2,1,0:T(8,128)} %bitcast.108), calls=%async_computation.3 | async-start | bytes 524288 | tf_op jit(solution)/shard_map/all_to_all | solution.py:25
  109.4 6.1 %collective-permute-start.11 = (f32[512,128]{1,0:T(8,128)S(1)}, f32[512,128]{1,0:T(8,128)S(1)}, u32[]{:S(2)}, u32[]{:S(2)}) collective-permute-start(f32[512,128]{1,0:T(8,128)S(1)} %bitcast.101), channel_id=1, source_target_pairs={{0,1},{1,0},{2,3},{3,2},{4,5},{5,4},{6,7},{7,6},{8,9},{9,8},{10,11... | collective-permute-start | bytes 786440 | tf_op jit(solution)/shard_map/ppermute | solution.py:66
  111.9 3.7 %collective-permute-start.8 = (f32[64,1536]{1,0:T(8,128)S(1)}, f32[64,1536]{1,0:T(8,128)S(1)}, u32[]{:S(2)}, u32[]{:S(2)}) collective-permute-start(f32[64,1536]{1,0:T(8,128)S(1)} %collective-permute-done.6), channel_id=1, source_target_pairs={{0,1},{1,0},{2,3},{3,2},{4,5},{5,4},{6,7},{7,6},{8,9},{9,8},{10,11... | collective-permute-start | bytes 1179656 | tf_op jit(solution)/shard_map/ppermute | solution.py:66
  121.6 28.3 %collective-permute-start.13 = (f32[64,2048]{1,0:T(8,128)S(1)}, f32[64,2048]{1,0:T(8,128)S(1)}, u32[]{:S(2)}, u32[]{:S(2)}) collective-permute-start(f32[64,2048]{1,0:T(8,128)S(1)} %collective-permute-done.9), channel_id=1, source_target_pairs={{0,1},{1,0},{2,3},{3,2},{4,5},{5,4},{6,7},{7,6},{8,9},{9,8},{10,11... | collective-permute-start | bytes 1572872 | tf_op jit(solution)/shard_map/ppermute | solution.py:66
  128.2 11.3 %collective-permute-start.12 = (f32[512,128]{1,0:T(8,128)S(1)}, f32[512,128]{1,0:T(8,128)S(1)}, u32[]{:S(2)}, u32[]{:S(2)}) collective-permute-start(f32[512,128]{1,0:T(8,128)S(1)} %maximum_select_fusion), channel_id=1, source_target_pairs={{0,8},{8,0},{16,24},{24,16},{32,40},{40,32},{48,56},{56,48},{64,72... | collective-permute-start | bytes 786440 | tf_op jit(solution)/shard_map/ppermute | solution.py:63
  131.7 18.2 %all-to-all-start.4 = ((f32[32,16,128]{2,1,0:T(8,128)}), f32[32,16,128]{2,1,0:T(8,128)}, u32[]{:S(2)}, u32[]{:S(2)}) async-start(f32[32,16,128]{2,1,0:T(8,128)} %broadcast_in_dim.159), calls=%async_computation.4 | async-start | bytes 524288 | tf_op jit(solution)/shard_map/all_to_all | solution.py:25
  156.7 10.1 %all-to-all-start.5 = ((f32[4,128,128]{2,1,0:T(8,128)}), f32[4,128,128]{2,1,0:T(8,128)S(1)}, u32[]{:S(2)}, u32[]{:S(2)}) async-start(f32[4,128,128]{2,1,0:T(8,128)} %broadcast_in_dim.161), calls=%async_computation.5 | async-start | bytes 524288 | tf_op jit(solution)/shard_map/all_to_all | solution.py:25
  161.3 17.6 %collective-permute-start.14 = (f32[512,128]{1,0:T(8,128)}, f32[512,128]{1,0:T(8,128)}, u32[]{:S(2)}, u32[]{:S(2)}) collective-permute-start(f32[512,128]{1,0:T(8,128)} %bitcast.22), channel_id=1, source_target_pairs={{0,1},{1,0},{2,3},{3,2},{4,5},{5,4},{6,7},{7,6},{8,9},{9,8},{10,11... | collective-permute-start | bytes 786440 | tf_op jit(solution)/shard_map/ppermute | solution.py:66
  169.7 17.4 %all-to-all-start.6 = ((f32[32,16,128]{2,1,0:T(8,128)}), f32[32,16,128]{2,1,0:T(8,128)S(1)}, u32[]{:S(2)}, u32[]{:S(2)}) async-start(f32[32,16,128]{2,1,0:T(8,128)} %bitcast.23), calls=%async_computation.6 | async-start | bytes 524288 | tf_op jit(solution)/shard_map/all_to_all | solution.py:25
  188.5 8.0 %collective-permute-start.15 = (f32[512,128]{1,0:T(8,128)S(1)}, f32[512,128]{1,0:T(8,128)S(1)}, u32[]{:S(2)}, u32[]{:S(2)}) collective-permute-start(f32[512,128]{1,0:T(8,128)S(1)} %maximum_select_fusion.1), channel_id=1, source_target_pairs={{0,8},{8,0},{16,24},{24,16},{32,40},{40,32},{48,56},{56,48},{64,72... | collective-permute-start | bytes 786440 | tf_op jit(solution)/shard_map/ppermute | solution.py:63
  192.0 16.1 %all-to-all-start.7 = ((f32[32,16,128]{2,1,0:T(8,128)}), f32[32,16,128]{2,1,0:T(8,128)S(1)}, u32[]{:S(2)}, u32[]{:S(2)}) async-start(f32[32,16,128]{2,1,0:T(8,128)} %broadcast_in_dim.162), calls=%async_computation.7 | async-start | bytes 524288 | tf_op jit(solution)/shard_map/all_to_all | solution.py:25
  196.5 23.7 %copy-start.14 = (f32[64,512]{1,0:T(8,128)S(1)}, f32[64,512]{1,0:T(8,128)}, u32[]{:S(2)}) copy-start(f32[64,512]{1,0:T(8,128)} %get-tuple-element.90) | copy-start | bytes 393220
  209.4 10.5 %all-to-all-start.8 = ((f32[4,128,128]{2,1,0:T(8,128)}), f32[4,128,128]{2,1,0:T(8,128)S(1)}, u32[]{:S(2)}, u32[]{:S(2)}) async-start(f32[4,128,128]{2,1,0:T(8,128)} %broadcast_in_dim.163), calls=%async_computation.8 | async-start | bytes 524288 | tf_op jit(solution)/shard_map/all_to_all | solution.py:25
  212.9 13.4 %collective-permute-start.16 = (f32[512,128]{1,0:T(8,128)S(1)}, f32[512,128]{1,0:T(8,128)S(1)}, u32[]{:S(2)}, u32[]{:S(2)}) collective-permute-start(f32[512,128]{1,0:T(8,128)S(1)} %bitcast.105), channel_id=1, source_target_pairs={{0,1},{1,0},{2,3},{3,2},{4,5},{5,4},{6,7},{7,6},{8,9},{9,8},{10,11... | collective-permute-start | bytes 786440 | tf_op jit(solution)/shard_map/ppermute | solution.py:66
  222.0 16.0 %all-to-all-start.9 = ((f32[32,16,128]{2,1,0:T(8,128)}), f32[32,16,128]{2,1,0:T(8,128)S(1)}, u32[]{:S(2)}, u32[]{:S(2)}) async-start(f32[32,16,128]{2,1,0:T(8,128)} %bitcast.29), calls=%async_computation.9 | async-start | bytes 524288 | tf_op jit(solution)/shard_map/all_to_all | solution.py:25
  226.7 10.3 %collective-permute-start.17 = (f32[512,128]{1,0:T(8,128)S(1)}, f32[512,128]{1,0:T(8,128)}, u32[]{:S(2)}, u32[]{:S(2)}) collective-permute-start(f32[512,128]{1,0:T(8,128)S(1)} %maximum_select_fusion.2), channel_id=1, source_target_pairs={{0,8},{8,0},{16,24},{24,16},{32,40},{40,32},{48,56},{56,48},{64,72... | collective-permute-start | bytes 786440 | tf_op jit(solution)/shard_map/ppermute | solution.py:63
  238.0 8.8 %collective-permute-start.18 = (f32[16,128]{1,0:T(8,128)S(1)}, f32[16,128]{1,0:T(8,128)S(1)}, u32[]{:S(2)}, u32[]{:S(2)}) collective-permute-start(f32[16,128]{1,0:T(8,128)S(1)} %reduce_sum.78), channel_id=1, source_target_pairs={{0,1},{1,0},{2,3},{3,2},{4,5},{5,4},{6,7},{7,6},{8,9},{9,8},{10,11... | collective-permute-start | bytes 24584 | tf_op jit(solution)/shard_map/ppermute | solution.py:66
  247.8 25.3 %all-to-all-start.10 = ((f32[64,16,128]{2,1,0:T(8,128)}), f32[64,16,128]{2,1,0:T(8,128)S(1)}, u32[]{:S(2)}, u32[]{:S(2)}) async-start(f32[64,16,128]{2,1,0:T(8,128)} %broadcast_in_dim.165), calls=%async_computation.10 | async-start | bytes 1048576 | tf_op jit(solution)/shard_map/all_to_all | solution.py:25
  275.7 14.1 %all-to-all-start.11 = ((f32[8,32,256]{2,1,0:T(8,128)}), f32[8,32,256]{2,1,0:T(8,128)S(1)}, u32[]{:S(2)}, u32[]{:S(2)}) async-start(f32[8,32,256]{2,1,0:T(8,128)} %all_to_all.50), calls=%async_computation.11 | async-start | bytes 524288 | tf_op jit(solution)/shard_map/all_to_all | solution.py:25
  (26 other events, 382.7 us)

commit v6 on v5

v6 whole, which is shorter than its diff:
```python
import jax
import jax.numpy as jnp
from jax import lax
from jax.sharding import PartitionSpec as P

PRECISION = lax.Precision.HIGHEST
CORES = 2


def pair_index(block_row, prior_row):
    return block_row * (block_row - 1) // 2 + prior_row


def contract(left, right, axes):
    return lax.dot_general(
        left,
        right,
        (((axes[0],), (axes[1],)), ((), ())),
        precision=PRECISION,
        preferred_element_type=jnp.float32,
    )


def swap(parts, axis, groups=None):
    return lax.all_to_all(parts, axis, 0, 0, axis_index_groups=groups, tiled=True)


def copies(part, count):
    return jnp.broadcast_to(part[None], (count,) + part.shape)


def halves_swapped(value):
    return jnp.roll(value, value.shape[-1] // 2, value.ndim - 1)


def window(parts, axis, groups=None, inputs=(), work=None):
    if work is None:
        return swap(parts, axis, groups), ()
    parts, inputs = lax.optimization_barrier((parts, inputs))
    return lax.optimization_barrier((swap(parts, axis, groups), work(*inputs)))


def shards(right_sides, diag_inverse, lower_blocks, trail_panel):
    step_count = diag_inverse.shape[0]
    trail_count = trail_panel.shape[0]
    local_rows = right_sides.shape[1]
    column_count = right_sides.shape[2]
    width = lower_blocks.shape[2]
    row_size = lax.axis_size("row")
    col_size = lax.axis_size("col")
    members = row_size // 2
    chips = col_size // CORES
    half = column_count // 2
    quarter = half // 2
    row = lax.axis_index("row")
    col = lax.axis_index("col")
    parity = row % 2
    core = col % CORES
    row_groups = [[r for r in range(row_size) if r % 2 == g] for g in range(2)]
    chip_groups = [[c for c in range(col_size) if c % CORES == g] for g in range(CORES)]
    row_pairs = [(r, r ^ 1) for r in range(row_size)]
    core_pairs = [(c, c ^ 1) for c in range(col_size)]
    low = lax.broadcasted_iota(jnp.int32, (1, half), 1) < quarter

    def from_row(value):
        return lax.ppermute(value, "row", row_pairs)

    def from_core(value):
        return lax.ppermute(value, "col", core_pairs)

    own_diag = diag_inverse.transpose(0, 2, 1)
    own_sides = lax.dynamic_slice_in_dim(right_sides[:step_count], parity * half, half, 2)
    sent_sides = lax.dynamic_slice_in_dim(right_sides[:step_count], (1 - parity) * half, half, 2)

    def side_of(block_row, received):
        value = jnp.concatenate([own_sides[block_row], received])
        return jnp.where(low == (core == 0), value, halves_swapped(value))

    def matrix(pieces, index):
        return jnp.concatenate([p[:, index * width : (index + 1) * width] for p in pieces])

    def update_of(matrices, solved_block):
        both = contract(matrices, solved_block, (1, 0))
        rows = 2 * local_rows
        return jnp.where(low, both[:rows], both[rows:])

    def partial_of(matrices, current):
        zero = jnp.zeros_like(current)
        spread = jnp.concatenate([jnp.where(low, current, zero), jnp.where(low, zero, current)])
        return contract(matrices, spread, (0, 0))

    def scattered(value, inputs=(), work=None):
        parts = value.reshape(members, width // members, half)
        got, done = window(parts, "row", row_groups, inputs, work)
        return got.sum(0), done

    def gathered(part, inputs=(), work=None):
        got, done = window(copies(part, members), "row", row_groups, inputs, work)
        return got.reshape(width, half), done

    def summed(update, inputs=(), work=None):
        return window(copies(update, chips), "col", chip_groups, inputs, work)

    def current_of(side, parts):
        total = parts.sum(0)
        return side - (total + halves_swapped(total))

    def by_core(value, other):
        straight = jnp.where(low, value, other)
        return jnp.where(core == 0, straight, halves_swapped(straight))

    def by_parity(value, other):
        return jnp.concatenate(
            [jnp.where(parity == 0, value, other), jnp.where(parity == 0, other, value)], 1
        )

    def below_of(whole, trail_block):
        return jnp.einsum("nc,mrn->cmr", whole, trail_block, precision=PRECISION)

    front = jnp.concatenate([own_diag[0], sent_sides[0]], 1)
    front_row = from_row(front)
    front_core = from_core(own_diag[0])
    first = jnp.concatenate(
        [lower_blocks[0], own_diag[1]] + [sent_sides[i] for i in range(1, step_count)], 1
    )
    first, _ = lax.optimization_barrier((first, front))
    first_row = from_row(first)
    front_both = from_core(front_row)

    current = side_of(0, front_row[:, width:])
    diag_0 = matrix([own_diag[0], front_row, front_core, front_both], 0)
    part, firsts = scattered(
        partial_of(diag_0, current),
        (first, first_row),
        lambda own, by_row: (own, by_row, from_core(own[:, : 2 * width]), from_core(by_row)),
    )
    solved_0, (lower_10, diag_1, sides, trail) = gathered(
        part,
        (firsts, trail_panel),
        lambda pieces, panel: (
            matrix(pieces, 0),
            matrix(pieces, 1),
            [
                side_of(i, pieces[1][:, 2 * width + (i - 1) * half : 2 * width + i * half])
                for i in range(1, step_count)
            ],
            [panel[:, :, j, :] for j in range(step_count)],
        ),
    )

    second = jnp.concatenate([lower_blocks[1], lower_blocks[2], lower_blocks[3], own_diag[2]], 1)
    parts, (second_row, core_0) = summed(
        update_of(lower_10, solved_0),
        (second, solved_0),
        lambda own, block: (from_row(own), from_core(block)),
    )
    current = current_of(sides[0], parts)
    part, seconds = scattered(
        partial_of(diag_1, current),
        (second, second_row),
        lambda own, by_row: (own, by_row, from_core(own), from_core(by_row)),
    )
    solved_1, (lower_21, diag_2, pending_2, lower_30, straight_0) = gathered(
        part,
        (seconds, solved_0, core_0),
        lambda pieces, block, other: (
            matrix(pieces, 1),
            matrix(pieces, 3),
            update_of(matrix(pieces, 0), block),
            matrix(pieces, 2),
            by_core(block, other),
        ),
    )

    third = jnp.concatenate([lower_blocks[4], lower_blocks[5], own_diag[3]], 1)
    parts, (third_row, core_1, row_0) = summed(
        pending_2 + update_of(lower_21, solved_1),
        (third, solved_1, straight_0),
        lambda own, block, other: (from_row(own), from_core(block), from_row(other)),
    )
    current = current_of(sides[1], parts)
    part, (thirds, pending_3, straight_1) = scattered(
        partial_of(diag_2, current),
        (third, third_row, lower_30, solved_0, solved_1, core_1),
        lambda own, by_row, lower, block, last, other: (
            (own, by_row, from_core(own), from_core(by_row)),
            update_of(lower, block),
            by_core(last, other),
        ),
    )
    solved_2, (lower_32, diag_3, pending_3, whole_0, below) = gathered(
        part,
        (thirds, pending_3, solved_1, straight_0, row_0, trail[0]),
        lambda pieces, pending, block, straight, other, trail_block: (
            matrix(pieces, 1),
            matrix(pieces, 2),
            pending + update_of(matrix(pieces, 0), block),
            by_parity(straight, other),
            below_of(by_parity(straight, other), trail_block),
        ),
    )

    parts, (row_1, core_2) = summed(
        pending_3 + update_of(lower_32, solved_2),
        (straight_1, solved_2),
        lambda straight, block: (from_row(straight), from_core(block)),
    )
    current = current_of(sides[2], parts)
    part, (row_2, straight_2, whole_1, below) = scattered(
        partial_of(diag_3, current),
        (solved_2, core_2, straight_1, row_1, trail[1], below),
        lambda block, other, straight, by_row, trail_block, total: (
            from_row(by_core(block, other)),
            by_core(block, other),
            by_parity(straight, by_row),
            total + below_of(by_parity(straight, by_row), trail_block),
        ),
    )
    part = by_core(part, from_core(part))
    parts, (whole_2, below) = window(
        copies(part, row_size),
        "row",
        None,
        (straight_2, row_2, trail[2], below),
        lambda straight, other, trail_block, total: (
            by_parity(straight, other),
            total + below_of(by_parity(straight, other), trail_block),
        ),
    )
    parts = parts.reshape(members, 2, width // members, half)
    whole_3 = parts.transpose(0, 2, 1, 3).reshape(width, column_count)

    below = below + below_of(whole_3, trail[3])
    shared = swap(below.reshape(column_count, -1), "col")
    own_width = column_count // col_size
    shared = shared.reshape(col_size, own_width, -1).sum(0)
    shared = shared.reshape(own_width, trail_count, local_rows).transpose(1, 2, 0)
    own_below = lax.dynamic_slice_in_dim(right_sides[step_count:], col * own_width, own_width, 2)
    trail_rest = own_below - shared

    out_width = column_count // row_size
    outs = [
        lax.dynamic_slice_in_dim(whole, row * out_width, out_width, 1)
        for whole in (whole_0, whole_1, whole_2, whole_3)
    ]
    return (jnp.stack(outs), trail_rest)


def solution(mesh):
    placed = (
        P(None, "row", None),
        P(None, "col", "row"),
        P(None, "row", "col"),
        P(None, "row", None, "col"),
    )
    return jax.shard_map(
        shards,
        mesh=mesh,
        in_specs=placed,
        out_specs=(P(None, "col", "row"), P(None, "row", "col")),
        check_vma=False,
    )
```

time: 293 us -> 285 us (0.973)
  blocking collectives: 0 us -> 19.2 us
  starting transfers between devices: 146 us -> 131 us
  waiting for transfers between devices: 87.7 us -> 81.2 us
  matrix products: 18.9 us -> 13.5 us
  local copies, waits for them, and re-layouts: 28.2 us -> 24.5 us
  other arithmetic: 7.93 us -> 11.5 us
    all_to_all x0 -> x2, blocking collectives: none -> 19.2 us  [swap(): lax.all_to_all(parts, axis, 0, 0, axis_index_groups=groups, tiled=True)]
    ppermute x7, waiting for transfers between devices: 28.8 us -> 12.8 us  [from_row(): return lax.ppermute(value, 'row', row_pairs)]
    all_to_all x12 -> x10, waiting for transfers between devices: 56.1 us -> 66.6 us  [swap(): lax.all_to_all(parts, axis, 0, 0, axis_index_groups=groups, tiled=True)]
    all_to_all x12 -> x10, starting transfers between devices: 78 us -> 69.3 us  [swap(): lax.all_to_all(parts, axis, 0, 0, axis_index_groups=groups, tiled=True)]
    dot_general x10, matrix products: 16.3 us -> 10.3 us  [contract(): lax.dot_general(left, right, (((axes[0],), (axes[1],)), ((), ())), precis...]
    ppermute x12, starting transfers between devices: 49.7 us -> 43.7 us  [from_core(): return lax.ppermute(value, 'col', core_pairs)]
    slice x12, local copies, waits for them, and re-layouts: 8.67 us -> 3.33 us  [matrix(): p[:, index * width:(index + 1) * width]]
    squeeze x2 -> x3, local copies, waits for them, and re-layouts: 1.19 us -> 4.88 us  [the longest x2 3.66 us: shards(): third = jnp.concatenate([lower_blocks[4], lower_blocks[5], own_diag[3]], 1)]
  transfers between devices with their start and end apart: 31 -> 29, of which waited for: 15 -> 14; matrix products, arithmetic and copies ran while one was open for 12% -> 11% of each run, Pallas kernels for 0% -> 0%
where the time goes in v6:
time: 285 us; the launch traced here: 283 us
  starting transfers between devices  131 us (46%)
  waiting for transfers between devices  81.2 us (28%)
  local copies, waits for them, and re-layouts  24.5 us (9%)
  blocking collectives  19.2 us (7%)
  matrix products  13.5 us (5%)
  other arithmetic  11.5 us (4%)
    all_to_all x10, starting transfers between devices, swap(): lax.all_to_all(parts, axis, 0, 0, axis_index_groups=groups, tiled=True)  69.3 us
    all_to_all x10, waiting for transfers between devices, swap(): lax.all_to_all(parts, axis, 0, 0, axis_index_groups=groups, tiled=True)  66.6 us
    ppermute x12, starting transfers between devices, from_core(): return lax.ppermute(value, 'col', core_pairs)  43.7 us
    all_to_all x2, blocking collectives, swap(): lax.all_to_all(parts, axis, 0, 0, axis_index_groups=groups, tiled=True)  19.2 us
    ppermute x7, starting transfers between devices, from_row(): return lax.ppermute(value, 'row', row_pairs)  18.2 us
    ppermute x7, waiting for transfers between devices, from_row(): return lax.ppermute(value, 'row', row_pairs)  12.8 us
    dot_general x10, matrix products, contract(): lax.dot_general(left, right, (((axes[0],), (axes[1],)), ((), ())), precis...  10.3 us
  transfers between devices with their start and end apart: 29, of which 14 were waited for; matrix products, arithmetic and copies ran while one was open for 11% of the time, Pallas kernels for 0%

profile of v6, /device:TPU:1, one launch (start us, length us, event | category | flops | bytes accessed | tf_op | source)
XLA Modules:
  0.0 282.9 jit_solution(16924511801585741807)
XLA Ops:
  2.4 8.8 %collective-permute-start.1 = (f32[64,512]{1,0:T(8,128)S(1)}, f32[64,512]{1,0:T(8,128)S(1)}, u32[]{:S(2)}, u32[]{:S(2)}) collective-permute-start(f32[64,512]{1,0:T(8,128)S(1)} %get-tuple-element.265), channel_id=1, source_target_pairs={{0,1},{1,0},{2,3},{3,2},{4,5},{5,4},{6,7},{7,6},{8,9},{9,8},{10,11... | collective-permute-start | bytes 393224 | tf_op jit(solution)/shard_map/ppermute | solution.py:69
  17.5 3.4 %collective-permute-start.3 = (f32[64,1408]{1,0:T(8,128)S(1)}, f32[64,1408]{1,0:T(8,128)}, u32[]{:S(2)}, u32[]{:S(2)}) collective-permute-start(f32[64,1408]{1,0:T(8,128)S(1)} %fusion.62), channel_id=1, source_target_pairs={{0,8},{8,0},{16,24},{24,16},{32,40},{40,32},{48,56},{56,48},{64,72... | collective-permute-start | bytes 1081352 | tf_op jit(solution)/shard_map/ppermute | solution.py:66
  29.5 11.2 %all-to-all-start = ((f32[32,16,128]{2,1,0:T(8,128)}), f32[32,16,128]{2,1,0:T(8,128)S(1)}, u32[]{:S(2)}, u32[]{:S(2)}) async-start(f32[32,16,128]{2,1,0:T(8,128)} %bitcast.4), calls=%async_computation | async-start | bytes 524288 | tf_op jit(solution)/shard_map/all_to_all | solution.py:25
  40.7 3.4 %collective-permute-start.4 = (f32[64,1024]{1,0:T(8,128)S(1)}, f32[64,1024]{1,0:T(8,128)S(1)}, u32[]{:S(2)}, u32[]{:S(2)}) collective-permute-start(f32[64,1024]{1,0:T(8,128)S(1)} %slice.328), channel_id=1, source_target_pairs={{0,1},{1,0},{2,3},{3,2},{4,5},{5,4},{6,7},{7,6},{8,9},{9,8},{10,11... | collective-permute-start | bytes 786440 | tf_op jit(solution)/shard_map/ppermute | solution.py:69
  53.1 9.3 %all-to-all-start.1 = ((f32[32,16,128]{2,1,0:T(8,128)}), f32[32,16,128]{2,1,0:T(8,128)S(1)}, u32[]{:S(2)}, u32[]{:S(2)}) async-start(f32[32,16,128]{2,1,0:T(8,128)} %broadcast_in_dim.160), calls=%async_computation.1 | async-start | bytes 524288 | tf_op jit(solution)/shard_map/all_to_all | solution.py:25
  68.4 6.6 %all-to-all-done.1 = f32[32,16,128]{2,1,0:T(8,128)S(1)} async-done(((f32[32,16,128]{2,1,0:T(8,128)}), f32[32,16,128]{2,1,0:T(8,128)S(1)}, u32[]{:S(2)}, u32[]{:S(2)}) %all-to-all-start.1) | async-done | bytes 262176 | tf_op jit(solution)/shard_map/all_to_all | solution.py:25
  77.8 4.2 %collective-permute-start.7 = (f32[512,128]{1,0:T(8,128)S(1)}, f32[512,128]{1,0:T(8,128)S(1)}, u32[]{:S(2)}, u32[]{:S(2)}) collective-permute-start(f32[512,128]{1,0:T(8,128)S(1)} %bitcast.103), channel_id=1, source_target_pairs={{0,1},{1,0},{2,3},{3,2},{4,5},{5,4},{6,7},{7,6},{8,9},{9,8},{10,11... | collective-permute-start | bytes 786440 | tf_op jit(solution)/shard_map/ppermute | solution.py:69
  82.0 10.3 %all_to_all.64 = f32[4,128,128]{2,1,0:T(8,128)S(1)} all-to-all(f32[4,128,128]{2,1,0:T(8,128)S(1)} %broadcast_in_dim.161), channel_id=1, replica_groups={{0,2,4,6},{1,3,5,7},{8,10,12,14},{9,11,13,15},{16,18,20,22},{17,19,21,2..., dimensions={0} | all-to-all | bytes 524288 | tf_op jit(solution)/shard_map/all_to_all | solution.py:25
  94.3 3.0 %collective-permute-start.8 = (f32[64,2048]{1,0:T(8,128)S(1)}, f32[64,2048]{1,0:T(8,128)S(1)}, u32[]{:S(2)}, u32[]{:S(2)}) collective-permute-start(f32[64,2048]{1,0:T(8,128)S(1)} %pad_maximum_fusion.2), channel_id=1, source_target_pairs={{0,1},{1,0},{2,3},{3,2},{4,5},{5,4},{6,7},{7,6},{8,9},{9,8},{10,11... | collective-permute-start | bytes 1572872 | tf_op jit(solution)/shard_map/ppermute | solution.py:69
  99.2 4.8 %all-to-all-start.3 = ((f32[32,16,128]{2,1,0:T(8,128)}), f32[32,16,128]{2,1,0:T(8,128)S(1)}, u32[]{:S(2)}, u32[]{:S(2)}) async-start(f32[32,16,128]{2,1,0:T(8,128)} %bitcast.22), calls=%async_computation.3 | async-start | bytes 524288 | tf_op jit(solution)/shard_map/all_to_all | solution.py:25
  105.8 10.9 %all-to-all-done.3 = f32[32,16,128]{2,1,0:T(8,128)S(1)} async-done(((f32[32,16,128]{2,1,0:T(8,128)}), f32[32,16,128]{2,1,0:T(8,128)S(1)}, u32[]{:S(2)}, u32[]{:S(2)}) %all-to-all-start.3) | async-done | bytes 262176 | tf_op jit(solution)/shard_map/all_to_all | solution.py:25
  117.4 5.9 %all-to-all-start.4 = ((f32[32,16,128]{2,1,0:T(8,128)}), f32[32,16,128]{2,1,0:T(8,128)S(1)}, u32[]{:S(2)}, u32[]{:S(2)}) async-start(f32[32,16,128]{2,1,0:T(8,128)} %broadcast_in_dim.162), calls=%async_computation.4 | async-start | bytes 524288 | tf_op jit(solution)/shard_map/all_to_all | solution.py:25
  125.5 9.9 %all-to-all-done.4 = f32[32,16,128]{2,1,0:T(8,128)S(1)} async-done(((f32[32,16,128]{2,1,0:T(8,128)}), f32[32,16,128]{2,1,0:T(8,128)S(1)}, u32[]{:S(2)}, u32[]{:S(2)}) %all-to-all-start.4) | async-done | bytes 262176 | tf_op jit(solution)/shard_map/all_to_all | solution.py:25
  136.7 2.8 collective-permute-start.10
  139.5 4.9 %collective-permute-start.11 = (f32[512,128]{1,0:T(8,128)S(1)}, f32[512,128]{1,0:T(8,128)}, u32[]{:S(2)}, u32[]{:S(2)}) collective-permute-start(f32[512,128]{1,0:T(8,128)S(1)} %bitcast.108), channel_id=1, source_target_pairs={{0,1},{1,0},{2,3},{3,2},{4,5},{5,4},{6,7},{7,6},{8,9},{9,8},{10,11... | collective-permute-start | bytes 786440 | tf_op jit(solution)/shard_map/ppermute | solution.py:69
  146.8 3.5 %all-to-all-start.5 = ((f32[4,128,128]{2,1,0:T(8,128)}), f32[4,128,128]{2,1,0:T(8,128)S(1)}, u32[]{:S(2)}, u32[]{:S(2)}) async-start(f32[4,128,128]{2,1,0:T(8,128)} %broadcast_in_dim.164), calls=%async_computation.5 | async-start | bytes 524288 | tf_op jit(solution)/shard_map/all_to_all | solution.py:25
  150.3 5.9 %all-to-all-done.5 = f32[4,128,128]{2,1,0:T(8,128)S(1)} async-done(((f32[4,128,128]{2,1,0:T(8,128)}), f32[4,128,128]{2,1,0:T(8,128)S(1)}, u32[]{:S(2)}, u32[]{:S(2)}) %all-to-all-start.5) | async-done | bytes 262176 | tf_op jit(solution)/shard_map/all_to_all | solution.py:25
  158.1 4.9 %all-to-all-start.6 = ((f32[32,16,128]{2,1,0:T(8,128)}), f32[32,16,128]{2,1,0:T(8,128)S(1)}, u32[]{:S(2)}, u32[]{:S(2)}) async-start(f32[32,16,128]{2,1,0:T(8,128)} %bitcast.27), calls=%async_computation.6 | async-start | bytes 524288 | tf_op jit(solution)/shard_map/all_to_all | solution.py:25
  163.0 3.7 %collective-permute-start.13 = (f32[64,1536]{1,0:T(8,128)S(1)}, f32[64,1536]{1,0:T(8,128)S(1)}, u32[]{:S(2)}, u32[]{:S(2)}) collective-permute-start(f32[64,1536]{1,0:T(8,128)S(1)} %copy-done.4), channel_id=1, source_target_pairs={{0,1},{1,0},{2,3},{3,2},{4,5},{5,4},{6,7},{7,6},{8,9},{9,8},{10,11... | collective-permute-start | bytes 1179656 | tf_op jit(solution)/shard_map/ppermute | solution.py:69
  171.4 3.3 %all-to-all-done.6 = f32[32,16,128]{2,1,0:T(8,128)S(1)} async-done(((f32[32,16,128]{2,1,0:T(8,128)}), f32[32,16,128]{2,1,0:T(8,128)S(1)}, u32[]{:S(2)}, u32[]{:S(2)}) %all-to-all-start.6) | async-done | bytes 262176 | tf_op jit(solution)/shard_map/all_to_all | solution.py:25
  175.5 8.6 %all-to-all-start.7 = ((f32[32,16,128]{2,1,0:T(8,128)}), f32[32,16,128]{2,1,0:T(8,128)S(1)}, u32[]{:S(2)}, u32[]{:S(2)}) async-start(f32[32,16,128]{2,1,0:T(8,128)} %broadcast_in_dim.165), calls=%async_computation.7 | async-start | bytes 524288 | tf_op jit(solution)/shard_map/all_to_all | solution.py:25
  188.7 8.0 %all-to-all-done.7 = f32[32,16,128]{2,1,0:T(8,128)S(1)} async-done(((f32[32,16,128]{2,1,0:T(8,128)}), f32[32,16,128]{2,1,0:T(8,128)S(1)}, u32[]{:S(2)}, u32[]{:S(2)}) %all-to-all-start.7) | async-done | bytes 262176 | tf_op jit(solution)/shard_map/all_to_all | solution.py:25
  197.4 2.9 %collective-permute-start.15 = (f32[512,128]{1,0:T(8,128)}, f32[512,128]{1,0:T(8,128)S(1)}, u32[]{:S(2)}, u32[]{:S(2)}) collective-permute-start(f32[512,128]{1,0:T(8,128)} %maximum_select_fusion.1), channel_id=1, source_target_pairs={{0,8},{8,0},{16,24},{24,16},{32,40},{40,32},{48,56},{56,48},{64,72... | collective-permute-start | bytes 786440 | tf_op jit(solution)/shard_map/ppermute | solution.py:66
  200.2 4.2 %collective-permute-start.16 = (f32[512,128]{1,0:T(8,128)S(1)}, f32[512,128]{1,0:T(8,128)S(1)}, u32[]{:S(2)}, u32[]{:S(2)}) collective-permute-start(f32[512,128]{1,0:T(8,128)S(1)} %bitcast.112), channel_id=1, source_target_pairs={{0,1},{1,0},{2,3},{3,2},{4,5},{5,4},{6,7},{7,6},{8,9},{9,8},{10,11... | collective-permute-start | bytes 786440 | tf_op jit(solution)/shard_map/ppermute | solution.py:69
  204.4 8.9 %all_to_all.65 = f32[4,128,128]{2,1,0:T(8,128)S(1)} all-to-all(f32[4,128,128]{2,1,0:T(8,128)S(1)} %broadcast_in_dim.166), channel_id=1, replica_groups={{0,2,4,6},{1,3,5,7},{8,10,12,14},{9,11,13,15},{16,18,20,22},{17,19,21,2..., dimensions={0} | all-to-all | bytes 524288 | tf_op jit(solution)/shard_map/all_to_all | solution.py:25
  215.3 4.6 %all-to-all-start.9 = ((f32[32,16,128]{2,1,0:T(8,128)}), f32[32,16,128]{2,1,0:T(8,128)S(1)}, u32[]{:S(2)}, u32[]{:S(2)}) async-start(f32[32,16,128]{2,1,0:T(8,128)} %bitcast.31), calls=%async_computation.9 | async-start | bytes 524288 | tf_op jit(solution)/shard_map/all_to_all | solution.py:25
  224.7 9.8 %collective-permute-done.17 = f32[512,128]{1,0:T(8,128)S(1)} collective-permute-done((f32[512,128]{1,0:T(8,128)S(1)}, f32[512,128]{1,0:T(8,128)S(1)}, u32[]{:S(2)}, u32[]{:S(2)}) %collective-permute-start.17) | collective-permute-done | bytes 262176 | tf_op jit(solution)/shard_map/ppermute | solution.py:66
  234.5 2.9 %collective-permute-start.18 = (f32[16,128]{1,0:T(8,128)S(1)}, f32[16,128]{1,0:T(8,128)S(1)}, u32[]{:S(2)}, u32[]{:S(2)}) collective-permute-start(f32[16,128]{1,0:T(8,128)S(1)} %reduce_sum.78), channel_id=1, source_target_pairs={{0,1},{1,0},{2,3},{3,2},{4,5},{5,4},{6,7},{7,6},{8,9},{9,8},{10,11... | collective-permute-start | bytes 24584 | tf_op jit(solution)/shard_map/ppermute | solution.py:69
  239.2 10.2 %all-to-all-start.10 = ((f32[64,16,128]{2,1,0:T(8,128)}), f32[64,16,128]{2,1,0:T(8,128)S(1)}, u32[]{:S(2)}, u32[]{:S(2)}) async-start(f32[64,16,128]{2,1,0:T(8,128)} %broadcast_in_dim.168), calls=%async_computation.10 | async-start | bytes 1048576 | tf_op jit(solution)/shard_map/all_to_all | solution.py:25
  252.5 13.7 %all-to-all-done.10 = f32[64,16,128]{2,1,0:T(8,128)S(1)} async-done(((f32[64,16,128]{2,1,0:T(8,128)}), f32[64,16,128]{2,1,0:T(8,128)S(1)}, u32[]{:S(2)}, u32[]{:S(2)}) %all-to-all-start.10) | async-done | bytes 524320 | tf_op jit(solution)/shard_map/all_to_all | solution.py:25
  269.2 6.4 %all-to-all-start.11 = ((f32[8,32,256]{2,1,0:T(8,128)}), f32[8,32,256]{2,1,0:T(8,128)S(1)}, u32[]{:S(2)}, u32[]{:S(2)}) async-start(f32[8,32,256]{2,1,0:T(8,128)} %all_to_all.50), calls=%async_computation.11 | async-start | bytes 524288 | tf_op jit(solution)/shard_map/all_to_all | solution.py:25
  276.5 5.6 %all-to-all-done.11 = f32[8,32,256]{2,1,0:T(8,128)S(1)} async-done(((f32[8,32,256]{2,1,0:T(8,128)}), f32[8,32,256]{2,1,0:T(8,128)S(1)}, u32[]{:S(2)}, u32[]{:S(2)}) %all-to-all-start.11) | async-done | bytes 262176 | tf_op jit(solution)/shard_map/all_to_all | solution.py:25
  (187 shorter events, 74.7 us)
Async XLA Ops:
  2.4 22.9 %collective-permute-start.1 = (f32[64,512]{1,0:T(8,128)S(1)}, f32[64,512]{1,0:T(8,128)S(1)}, u32[]{:S(2)}, u32[]{:S(2)}) collective-permute-start(f32[64,512]{1,0:T(8,128)S(1)} %get-tuple-element.265), channel_id=1, source_target_pairs={{0,1},{1,0},{2,3},{3,2},{4,5},{5,4},{6,7},{7,6},{8,9},{9,8},{10,11... | collective-permute-start | bytes 393224 | tf_op jit(solution)/shard_map/ppermute | solution.py:69
  13.7 7.7 %collective-permute-start = (f32[64,640]{1,0:T(8,128)S(1)}, f32[64,640]{1,0:T(8,128)S(1)}, u32[]{:S(2)}, u32[]{:S(2)}) collective-permute-start(f32[64,640]{1,0:T(8,128)S(1)} %pad_maximum_fusion.12), channel_id=1, source_target_pairs={{0,8},{8,0},{16,24},{24,16},{32,40},{40,32},{48,56},{56,48},{64,72... | collective-permute-start | bytes 491528 | tf_op jit(solution)/shard_map/ppermute | solution.py:66
  17.5 12.0 %collective-permute-start.3 = (f32[64,1408]{1,0:T(8,128)S(1)}, f32[64,1408]{1,0:T(8,128)}, u32[]{:S(2)}, u32[]{:S(2)}) collective-permute-start(f32[64,1408]{1,0:T(8,128)S(1)} %fusion.62), channel_id=1, source_target_pairs={{0,8},{8,0},{16,24},{24,16},{32,40},{40,32},{48,56},{56,48},{64,72... | collective-permute-start | bytes 1081352 | tf_op jit(solution)/shard_map/ppermute | solution.py:66
  21.5 3.7 %collective-permute-start.2 = (f32[64,640]{1,0:T(8,128)S(1)}, f32[64,640]{1,0:T(8,128)S(1)}, u32[]{:S(2)}, u32[]{:S(2)}) collective-permute-start(f32[64,640]{1,0:T(8,128)S(1)} %collective-permute-done), channel_id=1, source_target_pairs={{0,1},{1,0},{2,3},{3,2},{4,5},{5,4},{6,7},{7,6},{8,9},{9,8},{10,11... | collective-permute-start | bytes 491528 | tf_op jit(solution)/shard_map/ppermute | solution.py:69
  29.5 22.8 %all-to-all-start = ((f32[32,16,128]{2,1,0:T(8,128)}), f32[32,16,128]{2,1,0:T(8,128)S(1)}, u32[]{:S(2)}, u32[]{:S(2)}) async-start(f32[32,16,128]{2,1,0:T(8,128)} %bitcast.4), calls=%async_computation | async-start | bytes 524288 | tf_op jit(solution)/shard_map/all_to_all | solution.py:25
  40.7 8.2 %collective-permute-start.4 = (f32[64,1024]{1,0:T(8,128)S(1)}, f32[64,1024]{1,0:T(8,128)S(1)}, u32[]{:S(2)}, u32[]{:S(2)}) collective-permute-start(f32[64,1024]{1,0:T(8,128)S(1)} %slice.328), channel_id=1, source_target_pairs={{0,1},{1,0},{2,3},{3,2},{4,5},{5,4},{6,7},{7,6},{8,9},{9,8},{10,11... | collective-permute-start | bytes 786440 | tf_op jit(solution)/shard_map/ppermute | solution.py:69
  44.2 5.5 %collective-permute-start.5 = (f32[64,1408]{1,0:T(8,128)}, f32[64,1408]{1,0:T(8,128)}, u32[]{:S(2)}, u32[]{:S(2)}) collective-permute-start(f32[64,1408]{1,0:T(8,128)} %collective-permute-done.3), channel_id=1, source_target_pairs={{0,1},{1,0},{2,3},{3,2},{4,5},{5,4},{6,7},{7,6},{8,9},{9,8},{10,11... | collective-permute-start | bytes 1081352 | tf_op jit(solution)/shard_map/ppermute | solution.py:69
  53.1 21.9 %all-to-all-start.1 = ((f32[32,16,128]{2,1,0:T(8,128)}), f32[32,16,128]{2,1,0:T(8,128)S(1)}, u32[]{:S(2)}, u32[]{:S(2)}) async-start(f32[32,16,128]{2,1,0:T(8,128)} %broadcast_in_dim.160), calls=%async_computation.1 | async-start | bytes 524288 | tf_op jit(solution)/shard_map/all_to_all | solution.py:25
  75.6 16.7 %collective-permute-start.6 = (f32[64,2048]{1,0:T(8,128)S(1)}, f32[64,2048]{1,0:T(8,128)S(1)}, u32[]{:S(2)}, u32[]{:S(2)}) collective-permute-start(f32[64,2048]{1,0:T(8,128)S(1)} %pad_maximum_fusion.2), channel_id=1, source_target_pairs={{0,8},{8,0},{16,24},{24,16},{32,40},{40,32},{48,56},{56,48},{64,72... | collective-permute-start | bytes 1572872 | tf_op jit(solution)/shard_map/ppermute | solution.py:66
  77.8 14.5 %collective-permute-start.7 = (f32[512,128]{1,0:T(8,128)S(1)}, f32[512,128]{1,0:T(8,128)S(1)}, u32[]{:S(2)}, u32[]{:S(2)}) collective-permute-start(f32[512,128]{1,0:T(8,128)S(1)} %bitcast.103), channel_id=1, source_target_pairs={{0,1},{1,0},{2,3},{3,2},{4,5},{5,4},{6,7},{7,6},{8,9},{9,8},{10,11... | collective-permute-start | bytes 786440 | tf_op jit(solution)/shard_map/ppermute | solution.py:69
  94.3 22.4 %collective-permute-start.8 = (f32[64,2048]{1,0:T(8,128)S(1)}, f32[64,2048]{1,0:T(8,128)S(1)}, u32[]{:S(2)}, u32[]{:S(2)}) collective-permute-start(f32[64,2048]{1,0:T(8,128)S(1)} %pad_maximum_fusion.2), channel_id=1, source_target_pairs={{0,1},{1,0},{2,3},{3,2},{4,5},{5,4},{6,7},{7,6},{8,9},{9,8},{10,11... | collective-permute-start | bytes 1572872 | tf_op jit(solution)/shard_map/ppermute | solution.py:69
  97.3 19.4 %collective-permute-start.9 = (f32[64,2048]{1,0:T(8,128)S(1)}, f32[64,2048]{1,0:T(8,128)S(1)}, u32[]{:S(2)}, u32[]{:S(2)}) collective-permute-start(f32[64,2048]{1,0:T(8,128)S(1)} %collective-permute-done.6), channel_id=1, source_target_pairs={{0,1},{1,0},{2,3},{3,2},{4,5},{5,4},{6,7},{7,6},{8,9},{9,8},{10,11... | collective-permute-start | bytes 1572872 | tf_op jit(solution)/shard_map/ppermute | solution.py:69
  99.2 17.4 %all-to-all-start.3 = ((f32[32,16,128]{2,1,0:T(8,128)}), f32[32,16,128]{2,1,0:T(8,128)S(1)}, u32[]{:S(2)}, u32[]{:S(2)}) async-start(f32[32,16,128]{2,1,0:T(8,128)} %bitcast.22), calls=%async_computation.3 | async-start | bytes 524288 | tf_op jit(solution)/shard_map/all_to_all | solution.py:25
  117.4 18.0 %all-to-all-start.4 = ((f32[32,16,128]{2,1,0:T(8,128)}), f32[32,16,128]{2,1,0:T(8,128)S(1)}, u32[]{:S(2)}, u32[]{:S(2)}) async-start(f32[32,16,128]{2,1,0:T(8,128)} %broadcast_in_dim.162), calls=%async_computation.4 | async-start | bytes 524288 | tf_op jit(solution)/shard_map/all_to_all | solution.py:25
  124.7 31.6 %copy-start.16 = (f32[128,128]{1,0:T(8,128)S(1)}, f32[128,128]{1,0:T(8,128)}, u32[]{:S(2)}) copy-start(f32[128,128]{1,0:T(8,128)} %get-tuple-element.159) | copy-start | bytes 196612
  136.7 19.4 %collective-permute-start.10 = (f32[64,1536]{1,0:T(8,128)S(1)}, f32[64,1536]{1,0:T(8,128)S(1)}, u32[]{:S(2)}, u32[]{:S(2)}) collective-permute-start(f32[64,1536]{1,0:T(8,128)S(1)} %copy-done.4), channel_id=1, source_target_pairs={{0,8},{8,0},{16,24},{24,16},{32,40},{40,32},{48,56},{56,48},{64,72... | collective-permute-start | bytes 1179656 | tf_op jit(solution)/shard_map/ppermute | solution.py:66
  139.5 16.6 %collective-permute-start.11 = (f32[512,128]{1,0:T(8,128)S(1)}, f32[512,128]{1,0:T(8,128)}, u32[]{:S(2)}, u32[]{:S(2)}) collective-permute-start(f32[512,128]{1,0:T(8,128)S(1)} %bitcast.108), channel_id=1, source_target_pairs={{0,1},{1,0},{2,3},{3,2},{4,5},{5,4},{6,7},{7,6},{8,9},{9,8},{10,11... | collective-permute-start | bytes 786440 | tf_op jit(solution)/shard_map/ppermute | solution.py:69
  144.4 11.8 %collective-permute-start.12 = (f32[512,128]{1,0:T(8,128)}, f32[512,128]{1,0:T(8,128)}, u32[]{:S(2)}, u32[]{:S(2)}) collective-permute-start(f32[512,128]{1,0:T(8,128)} %maximum_select_fusion), channel_id=1, source_target_pairs={{0,8},{8,0},{16,24},{24,16},{32,40},{40,32},{48,56},{56,48},{64,72... | collective-permute-start | bytes 786440 | tf_op jit(solution)/shard_map/ppermute | solution.py:66
  146.8 9.4 %all-to-all-start.5 = ((f32[4,128,128]{2,1,0:T(8,128)}), f32[4,128,128]{2,1,0:T(8,128)S(1)}, u32[]{:S(2)}, u32[]{:S(2)}) async-start(f32[4,128,128]{2,1,0:T(8,128)} %broadcast_in_dim.164), calls=%async_computation.5 | async-start | bytes 524288 | tf_op jit(solution)/shard_map/all_to_all | solution.py:25
  158.1 16.6 %all-to-all-start.6 = ((f32[32,16,128]{2,1,0:T(8,128)}), f32[32,16,128]{2,1,0:T(8,128)S(1)}, u32[]{:S(2)}, u32[]{:S(2)}) async-start(f32[32,16,128]{2,1,0:T(8,128)} %bitcast.27), calls=%async_computation.6 | async-start | bytes 524288 | tf_op jit(solution)/shard_map/all_to_all | solution.py:25
  163.0 8.4 %collective-permute-start.13 = (f32[64,1536]{1,0:T(8,128)S(1)}, f32[64,1536]{1,0:T(8,128)S(1)}, u32[]{:S(2)}, u32[]{:S(2)}) collective-permute-start(f32[64,1536]{1,0:T(8,128)S(1)} %copy-done.4), channel_id=1, source_target_pairs={{0,1},{1,0},{2,3},{3,2},{4,5},{5,4},{6,7},{7,6},{8,9},{9,8},{10,11... | collective-permute-start | bytes 1179656 | tf_op jit(solution)/shard_map/ppermute | solution.py:69
  166.7 4.7 %collective-permute-start.14 = (f32[64,1536]{1,0:T(8,128)S(1)}, f32[64,1536]{1,0:T(8,128)}, u32[]{:S(2)}, u32[]{:S(2)}) collective-permute-start(f32[64,1536]{1,0:T(8,128)S(1)} %collective-permute-done.10), channel_id=1, source_target_pairs={{0,1},{1,0},{2,3},{3,2},{4,5},{5,4},{6,7},{7,6},{8,9},{9,8},{10,11... | collective-permute-start | bytes 1179656 | tf_op jit(solution)/shard_map/ppermute | solution.py:69
  175.5 21.3 %all-to-all-start.7 = ((f32[32,16,128]{2,1,0:T(8,128)}), f32[32,16,128]{2,1,0:T(8,128)S(1)}, u32[]{:S(2)}, u32[]{:S(2)}) async-start(f32[32,16,128]{2,1,0:T(8,128)} %broadcast_in_dim.165), calls=%async_computation.7 | async-start | bytes 524288 | tf_op jit(solution)/shard_map/all_to_all | solution.py:25
  187.0 26.4 %copy-start.15 = (f32[128,128]{1,0:T(8,128)S(1)}, f32[128,128]{1,0:T(8,128)}, u32[]{:S(2)}) copy-start(f32[128,128]{1,0:T(8,128)} %get-tuple-element.199) | copy-start | bytes 196612
  197.4 16.0 %collective-permute-start.15 = (f32[512,128]{1,0:T(8,128)}, f32[512,128]{1,0:T(8,128)S(1)}, u32[]{:S(2)}, u32[]{:S(2)}) collective-permute-start(f32[512,128]{1,0:T(8,128)} %maximum_select_fusion.1), channel_id=1, source_target_pairs={{0,8},{8,0},{16,24},{24,16},{32,40},{40,32},{48,56},{56,48},{64,72... | collective-permute-start | bytes 786440 | tf_op jit(solution)/shard_map/ppermute | solution.py:66
  200.2 13.1 %collective-permute-start.16 = (f32[512,128]{1,0:T(8,128)S(1)}, f32[512,128]{1,0:T(8,128)S(1)}, u32[]{:S(2)}, u32[]{:S(2)}) collective-permute-start(f32[512,128]{1,0:T(8,128)S(1)} %bitcast.112), channel_id=1, source_target_pairs={{0,1},{1,0},{2,3},{3,2},{4,5},{5,4},{6,7},{7,6},{8,9},{9,8},{10,11... | collective-permute-start | bytes 786440 | tf_op jit(solution)/shard_map/ppermute | solution.py:69
  215.3 19.2 %all-to-all-start.9 = ((f32[32,16,128]{2,1,0:T(8,128)}), f32[32,16,128]{2,1,0:T(8,128)S(1)}, u32[]{:S(2)}, u32[]{:S(2)}) async-start(f32[32,16,128]{2,1,0:T(8,128)} %bitcast.31), calls=%async_computation.9 | async-start | bytes 524288 | tf_op jit(solution)/shard_map/all_to_all | solution.py:25
  220.2 14.3 %collective-permute-start.17 = (f32[512,128]{1,0:T(8,128)S(1)}, f32[512,128]{1,0:T(8,128)S(1)}, u32[]{:S(2)}, u32[]{:S(2)}) collective-permute-start(f32[512,128]{1,0:T(8,128)S(1)} %maximum_select_fusion.2), channel_id=1, source_target_pairs={{0,8},{8,0},{16,24},{24,16},{32,40},{40,32},{48,56},{56,48},{64,72... | collective-permute-start | bytes 786440 | tf_op jit(solution)/shard_map/ppermute | solution.py:66
  224.0 25.5 %copy-start.6 = (f32[4,64,256]{2,1,0:T(8,128)S(1)}, f32[4,64,256]{2,1,0:T(8,128)}, u32[]{:S(2)}) copy-start(f32[4,64,256]{2,1,0:T(8,128)} %get-tuple-element.255) | copy-start | bytes 786436
  234.5 3.7 %collective-permute-start.18 = (f32[16,128]{1,0:T(8,128)S(1)}, f32[16,128]{1,0:T(8,128)S(1)}, u32[]{:S(2)}, u32[]{:S(2)}) collective-permute-start(f32[16,128]{1,0:T(8,128)S(1)} %reduce_sum.78), channel_id=1, source_target_pairs={{0,1},{1,0},{2,3},{3,2},{4,5},{5,4},{6,7},{7,6},{8,9},{9,8},{10,11... | collective-permute-start | bytes 24584 | tf_op jit(solution)/shard_map/ppermute | solution.py:69
  239.2 27.0 %all-to-all-start.10 = ((f32[64,16,128]{2,1,0:T(8,128)}), f32[64,16,128]{2,1,0:T(8,128)S(1)}, u32[]{:S(2)}, u32[]{:S(2)}) async-start(f32[64,16,128]{2,1,0:T(8,128)} %broadcast_in_dim.168), calls=%async_computation.10 | async-start | bytes 1048576 | tf_op jit(solution)/shard_map/all_to_all | solution.py:25
  269.2 12.9 %all-to-all-start.11 = ((f32[8,32,256]{2,1,0:T(8,128)}), f32[8,32,256]{2,1,0:T(8,128)S(1)}, u32[]{:S(2)}, u32[]{:S(2)}) async-start(f32[8,32,256]{2,1,0:T(8,128)} %all_to_all.50), calls=%async_computation.11 | async-start | bytes 524288 | tf_op jit(solution)/shard_map/all_to_all | solution.py:25
  (14 other events, 74.8 us)

commit v7 on v0

v7 whole, which is shorter than its diff:
```python
import jax
import jax.numpy as jnp
from jax import lax
from jax.sharding import PartitionSpec as P

PRECISION = lax.Precision.HIGHEST


def contract(left, right, axes):
    return lax.dot_general(
        left,
        right,
        (((axes[0],), (axes[1],)), ((), ())),
        precision=PRECISION,
        preferred_element_type=jnp.float32,
    )


def swap(parts, axis, groups=None):
    return lax.all_to_all(parts, axis, 0, 0, axis_index_groups=groups, tiled=True)


def copies(part, count):
    return jnp.broadcast_to(part[None], (count,) + part.shape)


def by_deadline(*values):
    return lax.optimization_barrier(values)


def shards(right_sides, diag_inverse, lower_blocks, trail_panel):
    step_count = diag_inverse.shape[0]
    trail_count = trail_panel.shape[0]
    local_rows = right_sides.shape[1]
    column_count = right_sides.shape[2]
    width = lower_blocks.shape[2]
    row_size = lax.axis_size("row")
    col_size = lax.axis_size("col")
    members = row_size // 2
    half = column_count // 2
    row = lax.axis_index("row")
    col = lax.axis_index("col")
    parity = row % 2
    row_groups = [[r for r in range(row_size) if r % 2 == g] for g in range(2)]
    row_pairs = [(r, r ^ 1) for r in range(row_size)]

    def from_partner(value):
        return lax.ppermute(value, "row", row_pairs)

    def half_of(value, which):
        return lax.dynamic_slice_in_dim(value, which * half, half, value.ndim - 1)

    def both(own, received, index):
        return jnp.concatenate([v[:, index * width : (index + 1) * width] for v in (own, received)])

    def by_parity(value, other):
        return jnp.concatenate(
            [jnp.where(parity == 0, value, other), jnp.where(parity == 0, other, value)], 1
        )

    def scattered(value):
        parts = value.reshape(members, width // members, half)
        return swap(parts, "row", row_groups)

    def gathered(part):
        return swap(copies(part, members), "row", row_groups)

    def summed(update):
        return swap(copies(update, col_size), "col")

    def below_of(whole, trail_block):
        return jnp.einsum("nc,mrn->cmr", whole, trail_block, precision=PRECISION)

    own_diag = diag_inverse.transpose(0, 2, 1)
    later = right_sides[1:step_count]
    own_sides = half_of(later, parity)
    sent_sides = half_of(later, 1 - parity)
    trail = [trail_panel[:, :, j, :] for j in range(step_count)]

    first = jnp.concatenate(
        [lower_blocks[0], own_diag[1]] + [sent_sides[i] for i in range(step_count - 1)], 1
    )
    first_got = from_partner(first)
    second = jnp.concatenate(
        [lower_blocks[1], lower_blocks[2], lower_blocks[3], lower_blocks[4], own_diag[2]], 1
    )
    second_got = from_partner(second)
    third = jnp.concatenate([lower_blocks[5], own_diag[3]], 1)
    third_got = from_partner(third)

    local_term = contract(own_diag[0], right_sides[0], (0, 0))
    parts = swap(local_term.reshape(row_size, width // row_size, column_count), "row")
    parts, first_got = by_deadline(parts, first_got)
    lower_10, diag_1 = both(first, first_got, 0), both(first, first_got, 1)
    sides = [
        jnp.concatenate(
            [own_sides[i], first_got[:, 2 * width + i * half : 2 * width + (i + 1) * half]]
        )
        for i in range(step_count - 1)
    ]
    parts = swap(copies(parts.sum(0), row_size), "row")
    parts, lower_10, diag_1, sides = by_deadline(parts, lower_10, diag_1, sides)
    whole_0 = parts.reshape(width, column_count)
    solved_0 = half_of(whole_0, parity)

    parts = summed(contract(lower_10, solved_0, (1, 0)))
    parts, second_got = by_deadline(parts, second_got)
    current = sides[0] - parts.sum(0)
    below = below_of(whole_0, trail[0])
    parts = scattered(contract(diag_1, current, (0, 0)))
    lower_20, lower_21 = both(second, second_got, 0), both(second, second_got, 1)
    lower_30, lower_31 = both(second, second_got, 2), both(second, second_got, 3)
    diag_2 = both(second, second_got, 4)
    parts, lower_21, lower_31, diag_2 = by_deadline(parts, lower_21, lower_31, diag_2)
    pending_2 = contract(lower_20, solved_0, (1, 0))
    pending_3 = contract(lower_30, solved_0, (1, 0))
    parts = gathered(parts.sum(0))
    parts, pending_2, pending_3, below, trail = by_deadline(
        parts, pending_2, pending_3, below, trail
    )
    solved_1 = parts.reshape(width, half)

    parts = summed(pending_2 + contract(lower_21, solved_1, (1, 0)))
    other_1 = from_partner(solved_1)
    parts, third_got, other_1 = by_deadline(parts, third_got, other_1)
    current = sides[1] - parts.sum(0)
    parts = scattered(contract(diag_2, current, (0, 0)))
    lower_32, diag_3 = both(third, third_got, 0), both(third, third_got, 1)
    pending_3 = pending_3 + contract(lower_31, solved_1, (1, 0))
    parts, lower_32, diag_3, pending_3 = by_deadline(parts, lower_32, diag_3, pending_3)
    parts = gathered(parts.sum(0))
    whole_1 = by_parity(solved_1, other_1)
    below = below + below_of(whole_1, trail[1])
    parts, below = by_deadline(parts, below)
    solved_2 = parts.reshape(width, half)

    parts = summed(pending_3 + contract(lower_32, solved_2, (1, 0)))
    other_2 = from_partner(solved_2)
    current = sides[2] - parts.sum(0)
    parts = scattered(contract(diag_3, current, (0, 0)))
    parts, other_2 = by_deadline(parts, other_2)
    parts = swap(copies(parts.sum(0), row_size), "row")
    whole_2 = by_parity(solved_2, other_2)
    below = below + below_of(whole_2, trail[2])
    parts, below = by_deadline(parts, below)
    parts = parts.reshape(members, 2, width // members, half)
    whole_3 = parts.transpose(0, 2, 1, 3).reshape(width, column_count)

    below = below + below_of(whole_3, trail[3])
    shared = swap(below.reshape(column_count, -1), "col")
    own_width = column_count // col_size
    shared = shared.reshape(col_size, own_width, -1).sum(0)
    shared = shared.reshape(own_width, trail_count, local_rows).transpose(1, 2, 0)
    own_below = lax.dynamic_slice_in_dim(right_sides[step_count:], col * own_width, own_width, 2)
    trail_rest = own_below - shared

    out_width = column_count // row_size
    outs = [
        lax.dynamic_slice_in_dim(whole, row * out_width, out_width, 1)
        for whole in (whole_0, whole_1, whole_2, whole_3)
    ]
    return (jnp.stack(outs), trail_rest)


def solution(mesh):
    placed = (
        P(None, "row", None),
        P(None, "col", "row"),
        P(None, "row", "col"),
        P(None, "row", None, "col"),
    )
    return jax.shard_map(
        shards,
        mesh=mesh,
        in_specs=placed,
        out_specs=(P(None, "col", "row"), P(None, "row", "col")),
        check_vma=False,
    )
```

time: 932 us -> 275 us (0.30)
  waiting for transfers between devices: 884 us -> 105 us
  starting transfers between devices: 0.33 us -> 99.1 us
  blocking collectives: 0 us -> 16.8 us
  local copies, waits for them, and re-layouts: 6.87 us -> 23.5 us
  between operations: 15 us -> 1.26 us
    psum x7 -> x0, waiting for transfers between devices: 815 us -> none  [the longest x4 610 us: shards(): solved_block = lax.psum(local_term, 'row')]
    all_to_all x0 -> x11, starting transfers between devices: none -> 85.7 us  [swap(): lax.all_to_all(parts, axis, 0, 0, axis_index_groups=groups, tiled=True)]
    all_to_all x0 -> x11, waiting for transfers between devices: none -> 70.4 us  [swap(): lax.all_to_all(parts, axis, 0, 0, axis_index_groups=groups, tiled=True)]
    unnamed x9 -> x0, waiting for transfers between devices: 69.5 us -> none
    ppermute x0 -> x5, waiting for transfers between devices: none -> 34.5 us  [from_partner(): return lax.ppermute(value, 'row', row_pairs)]
    all_to_all x0 -> x1, blocking collectives: none -> 16.8 us  [swap(): lax.all_to_all(parts, axis, 0, 0, axis_index_groups=groups, tiled=True)]
    ppermute x0 -> x5, starting transfers between devices: none -> 13.3 us  [from_partner(): return lax.ppermute(value, 'row', row_pairs)]
  transfers between devices with their start and end apart: 8 -> 16, of which waited for: 8 -> 12; matrix products, arithmetic and copies ran while one was open for 1% -> 11% of each run, Pallas kernels for 0% -> 0%
where the time goes in v7:
time: 275 us; the launch traced here: 273 us
  waiting for transfers between devices  105 us (38%)
  starting transfers between devices  99.1 us (36%)
  local copies, waits for them, and re-layouts  23.5 us (9%)
  matrix products  17.4 us (6%)
  blocking collectives  16.8 us (6%)
  other arithmetic  10.4 us (4%)
    all_to_all x11, starting transfers between devices, swap(): lax.all_to_all(parts, axis, 0, 0, axis_index_groups=groups, tiled=True)  85.7 us
    all_to_all x11, waiting for transfers between devices, swap(): lax.all_to_all(parts, axis, 0, 0, axis_index_groups=groups, tiled=True)  70.4 us
    ppermute x5, waiting for transfers between devices, from_partner(): return lax.ppermute(value, 'row', row_pairs)  34.5 us
    all_to_all x1, blocking collectives, swap(): lax.all_to_all(parts, axis, 0, 0, axis_index_groups=groups, tiled=True)  16.8 us
    dot_general x10, matrix products, contract(): lax.dot_general(left, right, (((axes[0],), (axes[1],)), ((), ())), precis...  13.5 us
    ppermute x5, starting transfers between devices, from_partner(): return lax.ppermute(value, 'row', row_pairs)  13.3 us
  transfers between devices with their start and end apart: 16, of which 12 were waited for; matrix products, arithmetic and copies ran while one was open for 11% of the time, Pallas kernels for 0%

profile of v7, /device:TPU:1, one launch (start us, length us, event | category | flops | bytes accessed | tf_op | source)
XLA Modules:
  0.0 273.4 jit_solution(9016427632124568691)
XLA Ops:
  2.7 2.2 fusion.16
  5.0 17.1 %all-to-all-start = ((f32[64,8,256]{2,1,0:T(8,128)}), f32[64,8,256]{2,1,0:T(8,128)S(1)}, u32[]{:S(2)}, u32[]{:S(2)}) async-start(f32[64,8,256]{2,1,0:T(8,128)} %fusion.16), calls=%async_computation | async-start | bytes 1048576 | tf_op jit(solution)/shard_map/all_to_all | solution.py:20
  25.5 2.9 %collective-permute-start = (f32[64,1408]{1,0:T(8,128)}, f32[64,1408]{1,0:T(8,128)S(1)}, u32[]{:S(2)}, u32[]{:S(2)}) collective-permute-start(f32[64,1408]{1,0:T(8,128)} %fusion.30), channel_id=1, source_target_pairs={{0,8},{8,0},{16,24},{24,16},{32,40},{40,32},{48,56},{56,48},{64,72... | collective-permute-start | bytes 1081352 | tf_op jit(solution)/shard_map/ppermute | solution.py:48
  28.4 2.4 collective-permute-start.1
  30.8 13.6 %collective-permute-done = f32[64,1408]{1,0:T(8,128)S(1)} collective-permute-done((f32[64,1408]{1,0:T(8,128)}, f32[64,1408]{1,0:T(8,128)S(1)}, u32[]{:S(2)}, u32[]{:S(2)}) %collective-permute-start) | collective-permute-done | bytes 360480 | tf_op jit(solution)/shard_map/ppermute | solution.py:48
  45.4 10.0 %all-to-all-start.1 = ((f32[64,8,256]{2,1,0:T(8,128)}), f32[64,8,256]{2,1,0:T(8,128)S(1)}, u32[]{:S(2)}, u32[]{:S(2)}) async-start(f32[64,8,256]{2,1,0:T(8,128)} %broadcast_in_dim.14), calls=%async_computation.1 | async-start | bytes 1048576 | tf_op jit(solution)/shard_map/all_to_all | solution.py:20
  59.6 12.3 %all-to-all-done.1 = f32[64,8,256]{2,1,0:T(8,128)S(1)} async-done(((f32[64,8,256]{2,1,0:T(8,128)}), f32[64,8,256]{2,1,0:T(8,128)S(1)}, u32[]{:S(2)}, u32[]{:S(2)}) %all-to-all-start.1) | async-done | bytes 524320 | tf_op jit(solution)/shard_map/all_to_all | solution.py:20
  73.1 8.1 %all-to-all-start.2 = ((f32[8,128,128]{2,1,0:T(8,128)}), f32[8,128,128]{2,1,0:T(8,128)S(1)}, u32[]{:S(2)}, u32[]{:S(2)}) async-start(f32[8,128,128]{2,1,0:T(8,128)} %broadcast_in_dim.15), calls=%async_computation.2 | async-start | bytes 1048576 | tf_op jit(solution)/shard_map/all_to_all | solution.py:20
  81.2 2.8 %fusion.40 = (f32[4,64,1,512]{3,2,1,0:T(1,128)}, f32[4,64,1,512]{3,2,1,0:T(1,128)}, f32[4,64,1,512]{3,2,1,0:T(1,128)}, f32[4,64,1,512]{3,2,1,0:T(1,128)}) fusion(f32[4,64,4,512]{3,2,1,0:T(4,128)S(1)} %copy-done.1), kind=kLoop, calls=%fused_computation.98 | loop fusion | bytes 4194304 | tf_op jit(solution)/shard_map/slice | solution.py:78
  84.0 6.7 %all-to-all-done.2 = f32[8,128,128]{2,1,0:T(8,128)S(1)} async-done(((f32[8,128,128]{2,1,0:T(8,128)}), f32[8,128,128]{2,1,0:T(8,128)S(1)}, u32[]{:S(2)}, u32[]{:S(2)}) %all-to-all-start.2) | async-done | bytes 524320 | tf_op jit(solution)/shard_map/all_to_all | solution.py:20
  90.7 2.2 fusion.27
  92.8 4.4 %all-to-all-start.3 = ((f32[32,16,128]{2,1,0:T(8,128)}), f32[32,16,128]{2,1,0:T(8,128)S(1)}, u32[]{:S(2)}, u32[]{:S(2)}) async-start(f32[32,16,128]{2,1,0:T(8,128)} %bitcast.21), calls=%async_computation.3 | async-start | bytes 524288 | tf_op jit(solution)/shard_map/all_to_all | solution.py:20
  101.5 7.7 %all-to-all-done.3 = f32[32,16,128]{2,1,0:T(8,128)S(1)} async-done(((f32[32,16,128]{2,1,0:T(8,128)}), f32[32,16,128]{2,1,0:T(8,128)S(1)}, u32[]{:S(2)}, u32[]{:S(2)}) %all-to-all-start.3) | async-done | bytes 262176 | tf_op jit(solution)/shard_map/all_to_all | solution.py:20
  110.0 6.6 %all-to-all-start.4 = ((f32[32,16,128]{2,1,0:T(8,128)}), f32[32,16,128]{2,1,0:T(8,128)S(1)}, u32[]{:S(2)}, u32[]{:S(2)}) async-start(f32[32,16,128]{2,1,0:T(8,128)} %broadcast_in_dim.16), calls=%async_computation.4 | async-start | bytes 524288 | tf_op jit(solution)/shard_map/all_to_all | solution.py:20
  120.7 7.8 %all-to-all-done.4 = f32[32,16,128]{2,1,0:T(8,128)S(1)} async-done(((f32[32,16,128]{2,1,0:T(8,128)}), f32[32,16,128]{2,1,0:T(8,128)S(1)}, u32[]{:S(2)}, u32[]{:S(2)}) %all-to-all-start.4) | async-done | bytes 262176 | tf_op jit(solution)/shard_map/all_to_all | solution.py:20
  130.6 6.3 %all-to-all-start.5 = ((f32[8,128,128]{2,1,0:T(8,128)}), f32[8,128,128]{2,1,0:T(8,128)S(1)}, u32[]{:S(2)}, u32[]{:S(2)}) async-start(f32[8,128,128]{2,1,0:T(8,128)} %broadcast_in_dim.17), calls=%async_computation.5 | async-start | bytes 1048576 | tf_op jit(solution)/shard_map/all_to_all | solution.py:20
  137.0 2.9 %collective-permute-start.2 = (f32[64,1024]{1,0:T(8,128)S(1)}, f32[64,1024]{1,0:T(8,128)S(1)}, u32[]{:S(2)}, u32[]{:S(2)}) collective-permute-start(f32[64,1024]{1,0:T(8,128)S(1)} %pad_maximum_fusion.7), channel_id=1, source_target_pairs={{0,8},{8,0},{16,24},{24,16},{32,40},{40,32},{48,56},{56,48},{64,72... | collective-permute-start | bytes 786440 | tf_op jit(solution)/shard_map/ppermute | solution.py:48
  139.9 2.3 collective-permute-start.3
  142.3 4.4 %collective-permute-done.2 = f32[64,1024]{1,0:T(8,128)S(1)} collective-permute-done((f32[64,1024]{1,0:T(8,128)S(1)}, f32[64,1024]{1,0:T(8,128)S(1)}, u32[]{:S(2)}, u32[]{:S(2)}) %collective-permute-start.2) | collective-permute-done | bytes 262176 | tf_op jit(solution)/shard_map/ppermute | solution.py:48
  147.3 5.0 %collective-permute-done.3 = f32[512,128]{1,0:T(8,128)} collective-permute-done((f32[512,128]{1,0:T(8,128)S(1)}, f32[512,128]{1,0:T(8,128)}, u32[]{:S(2)}, u32[]{:S(2)}) %collective-permute-start.3) | collective-permute-done | bytes 262176 | tf_op jit(solution)/shard_map/ppermute | solution.py:48
  153.7 4.6 %all-to-all-start.6 = ((f32[32,16,128]{2,1,0:T(8,128)}), f32[32,16,128]{2,1,0:T(8,128)S(1)}, u32[]{:S(2)}, u32[]{:S(2)}) async-start(f32[32,16,128]{2,1,0:T(8,128)} %bitcast.31), calls=%async_computation.6 | async-start | bytes 524288 | tf_op jit(solution)/shard_map/all_to_all | solution.py:20
  162.8 7.4 %all-to-all-done.6 = f32[32,16,128]{2,1,0:T(8,128)S(1)} async-done(((f32[32,16,128]{2,1,0:T(8,128)}), f32[32,16,128]{2,1,0:T(8,128)S(1)}, u32[]{:S(2)}, u32[]{:S(2)}) %all-to-all-start.6) | async-done | bytes 262176 | tf_op jit(solution)/shard_map/all_to_all | solution.py:20
  171.0 6.4 %all-to-all-start.7 = ((f32[32,16,128]{2,1,0:T(8,128)}), f32[32,16,128]{2,1,0:T(8,128)S(1)}, u32[]{:S(2)}, u32[]{:S(2)}) async-start(f32[32,16,128]{2,1,0:T(8,128)} %broadcast_in_dim.18), calls=%async_computation.7 | async-start | bytes 524288 | tf_op jit(solution)/shard_map/all_to_all | solution.py:20
  179.7 9.2 %all-to-all-done.7 = f32[32,16,128]{2,1,0:T(8,128)S(1)} async-done(((f32[32,16,128]{2,1,0:T(8,128)}), f32[32,16,128]{2,1,0:T(8,128)S(1)}, u32[]{:S(2)}, u32[]{:S(2)}) %all-to-all-start.7) | async-done | bytes 262176 | tf_op jit(solution)/shard_map/all_to_all | solution.py:20
  190.3 16.8 %all_to_all.64 = f32[8,128,128]{2,1,0:T(8,128)} all-to-all(f32[8,128,128]{2,1,0:T(8,128)S(1)} %broadcast_in_dim.19), channel_id=1, replica_groups=mesh['row'=64,'col'=8] {'col'}, dimensions={0} | all-to-all | bytes 1048576 | tf_op jit(solution)/shard_map/all_to_all | solution.py:20
  209.6 4.3 %all-to-all-start.9 = ((f32[32,16,128]{2,1,0:T(8,128)}), f32[32,16,128]{2,1,0:T(8,128)S(1)}, u32[]{:S(2)}, u32[]{:S(2)}) async-start(f32[32,16,128]{2,1,0:T(8,128)} %bitcast.34), calls=%async_computation.9 | async-start | bytes 524288 | tf_op jit(solution)/shard_map/all_to_all | solution.py:20
  213.9 2.8 %collective-permute-start.4 = (f32[512,128]{1,0:T(8,128)S(1)}, f32[512,128]{1,0:T(8,128)S(1)}, u32[]{:S(2)}, u32[]{:S(2)}) collective-permute-start(f32[512,128]{1,0:T(8,128)S(1)} %bitcast.129), channel_id=1, source_target_pairs={{0,8},{8,0},{16,24},{24,16},{32,40},{40,32},{48,56},{56,48},{64,72... | collective-permute-start | bytes 786440 | tf_op jit(solution)/shard_map/ppermute | solution.py:48
  216.7 11.5 %collective-permute-done.4 = f32[512,128]{1,0:T(8,128)S(1)} collective-permute-done((f32[512,128]{1,0:T(8,128)S(1)}, f32[512,128]{1,0:T(8,128)S(1)}, u32[]{:S(2)}, u32[]{:S(2)}) %collective-permute-start.4) | collective-permute-done | bytes 262176 | tf_op jit(solution)/shard_map/ppermute | solution.py:48
  229.1 11.0 %all-to-all-start.10 = ((f32[64,16,128]{2,1,0:T(8,128)}), f32[64,16,128]{2,1,0:T(8,128)S(1)}, u32[]{:S(2)}, u32[]{:S(2)}) async-start(f32[64,16,128]{2,1,0:T(8,128)} %broadcast_in_dim.20), calls=%async_computation.10 | async-start | bytes 1048576 | tf_op jit(solution)/shard_map/all_to_all | solution.py:20
  242.8 13.7 %all-to-all-done.10 = f32[64,16,128]{2,1,0:T(8,128)S(1)} async-done(((f32[64,16,128]{2,1,0:T(8,128)}), f32[64,16,128]{2,1,0:T(8,128)S(1)}, u32[]{:S(2)}, u32[]{:S(2)}) %all-to-all-start.10) | async-done | bytes 524320 | tf_op jit(solution)/shard_map/all_to_all | solution.py:20
  259.3 6.8 %all-to-all-start.11 = ((f32[8,32,256]{2,1,0:T(8,128)}), f32[8,32,256]{2,1,0:T(8,128)S(1)}, u32[]{:S(2)}, u32[]{:S(2)}) async-start(f32[8,32,256]{2,1,0:T(8,128)} %all_to_all.50), calls=%async_computation.11 | async-start | bytes 524288 | tf_op jit(solution)/shard_map/all_to_all | solution.py:20
  266.9 5.6 %all-to-all-done.11 = f32[8,32,256]{2,1,0:T(8,128)S(1)} async-done(((f32[8,32,256]{2,1,0:T(8,128)}), f32[8,32,256]{2,1,0:T(8,128)S(1)}, u32[]{:S(2)}, u32[]{:S(2)}) %all-to-all-start.11) | async-done | bytes 262176 | tf_op jit(solution)/shard_map/all_to_all | solution.py:20
  (134 shorter events, 44.2 us)
Async XLA Ops:
  0.6 21.5 %copy-start = (f32[6,64,512]{2,1,0:T(8,128)S(1)}, f32[6,64,512]{2,1,0:T(8,128)}, u32[]{:S(2)}) copy-start(f32[6,64,512]{2,1,0:T(8,128)} %param.6) | copy-start | bytes 2359300
  0.6 22.2 %copy-start.11 = (f32[8,64,256]{2,1,0:T(8,128)S(1)}, f32[8,64,256]{2,1,0:T(8,128)}, u32[]{:S(2)}) copy-start(f32[8,64,256]{2,1,0:T(8,128)} %param.4) | copy-start | bytes 1572868
  2.6 20.3 %copy-start.5 = (f32[4,512,64]{1,2,0:T(8,128)S(1)}, f32[4,512,64]{1,2,0:T(8,128)}, u32[]{:S(2)}) copy-start(f32[4,512,64]{1,2,0:T(8,128)} %param.5) | copy-start | bytes 1572868
  5.0 39.5 %all-to-all-start = ((f32[64,8,256]{2,1,0:T(8,128)}), f32[64,8,256]{2,1,0:T(8,128)S(1)}, u32[]{:S(2)}, u32[]{:S(2)}) async-start(f32[64,8,256]{2,1,0:T(8,128)} %fusion.16), calls=%async_computation | async-start | bytes 1048576 | tf_op jit(solution)/shard_map/all_to_all | solution.py:20
  25.5 19.0 %collective-permute-start = (f32[64,1408]{1,0:T(8,128)}, f32[64,1408]{1,0:T(8,128)S(1)}, u32[]{:S(2)}, u32[]{:S(2)}) collective-permute-start(f32[64,1408]{1,0:T(8,128)} %fusion.30), channel_id=1, source_target_pairs={{0,8},{8,0},{16,24},{24,16},{32,40},{40,32},{48,56},{56,48},{64,72... | collective-permute-start | bytes 1081352 | tf_op jit(solution)/shard_map/ppermute | solution.py:48
  28.4 55.6 %collective-permute-start.1 = (f32[64,2560]{1,0:T(8,128)}, f32[64,2560]{1,0:T(8,128)}, u32[]{:S(2)}, u32[]{:S(2)}) collective-permute-start(f32[64,2560]{1,0:T(8,128)} %copy-done.25), channel_id=1, source_target_pairs={{0,8},{8,0},{16,24},{24,16},{32,40},{40,32},{48,56},{56,48},{64,72... | collective-permute-start | bytes 1966088 | tf_op jit(solution)/shard_map/ppermute | solution.py:48
  45.4 26.4 %all-to-all-start.1 = ((f32[64,8,256]{2,1,0:T(8,128)}), f32[64,8,256]{2,1,0:T(8,128)S(1)}, u32[]{:S(2)}, u32[]{:S(2)}) async-start(f32[64,8,256]{2,1,0:T(8,128)} %broadcast_in_dim.14), calls=%async_computation.1 | async-start | bytes 1048576 | tf_op jit(solution)/shard_map/all_to_all | solution.py:20
  56.3 24.9 %copy-start.1 = (f32[4,64,4,512]{3,2,1,0:T(4,128)S(1)}, f32[4,64,4,512]{3,2,1,0:T(4,128)}, u32[]{:S(2)}) copy-start(f32[4,64,4,512]{3,2,1,0:T(4,128)} %param.7) | copy-start | bytes 6291460
  73.1 17.6 %all-to-all-start.2 = ((f32[8,128,128]{2,1,0:T(8,128)}), f32[8,128,128]{2,1,0:T(8,128)S(1)}, u32[]{:S(2)}, u32[]{:S(2)}) async-start(f32[8,128,128]{2,1,0:T(8,128)} %broadcast_in_dim.15), calls=%async_computation.2 | async-start | bytes 1048576 | tf_op jit(solution)/shard_map/all_to_all | solution.py:20
  84.0 16.8 %copy-start.14 = (f32[64,512]{1,0:T(8,128)S(1)}, f32[64,512]{1,0:T(8,128)}, u32[]{:S(2)}) copy-start(f32[64,512]{1,0:T(8,128)} %get-tuple-element.82) | copy-start | bytes 393220
  92.8 16.4 %all-to-all-start.3 = ((f32[32,16,128]{2,1,0:T(8,128)}), f32[32,16,128]{2,1,0:T(8,128)S(1)}, u32[]{:S(2)}, u32[]{:S(2)}) async-start(f32[32,16,128]{2,1,0:T(8,128)} %bitcast.21), calls=%async_computation.3 | async-start | bytes 524288 | tf_op jit(solution)/shard_map/all_to_all | solution.py:20
  97.3 19.3 %copy-start.4 = (f32[4,64,1,512]{3,2,1,0:T(1,128)S(1)}, f32[4,64,1,512]{3,2,1,0:T(1,128)}, u32[]{:S(2)}) copy-start(f32[4,64,1,512]{3,2,1,0:T(1,128)} %get-tuple-element.76) | copy-start | bytes 1572868
  100.0 17.8 %copy-start.3 = (f32[4,64,1,512]{3,2,1,0:T(1,128)S(1)}, f32[4,64,1,512]{3,2,1,0:T(1,128)}, u32[]{:S(2)}) copy-start(f32[4,64,1,512]{3,2,1,0:T(1,128)} %get-tuple-element.78) | copy-start | bytes 1572868
  101.5 16.4 %copy-start.2 = (f32[4,64,1,512]{3,2,1,0:T(1,128)S(1)}, f32[4,64,1,512]{3,2,1,0:T(1,128)}, u32[]{:S(2)}) copy-start(f32[4,64,1,512]{3,2,1,0:T(1,128)} %get-tuple-element.79) | copy-start | bytes 1572868
  110.0 18.5 %all-to-all-start.4 = ((f32[32,16,128]{2,1,0:T(8,128)}), f32[32,16,128]{2,1,0:T(8,128)S(1)}, u32[]{:S(2)}, u32[]{:S(2)}) async-start(f32[32,16,128]{2,1,0:T(8,128)} %broadcast_in_dim.16), calls=%async_computation.4 | async-start | bytes 524288 | tf_op jit(solution)/shard_map/all_to_all | solution.py:20
  119.2 17.7 %copy-start.6 = (f32[64,512]{1,0:T(8,128)S(1)}, f32[64,512]{1,0:T(8,128)}, u32[]{:S(2)}) copy-start(f32[64,512]{1,0:T(8,128)} %get-tuple-element.97) | copy-start | bytes 393220
  119.6 32.8 %copy-start.8 = (f32[128,512]{1,0:T(8,128)S(1)}, f32[128,512]{1,0:T(8,128)}, u32[]{:S(2)}) copy-start(f32[128,512]{1,0:T(8,128)} %pad_maximum_fusion.6) | copy-start | bytes 786436
  119.6 32.8 %copy-start.23 = (f32[128,128]{1,0:T(8,128)S(1)}, f32[128,128]{1,0:T(8,128)}, u32[]{:S(2)}) copy-start(f32[128,128]{1,0:T(8,128)} %get-tuple-element.50) | copy-start | bytes 196612
  130.6 21.7 %all-to-all-start.5 = ((f32[8,128,128]{2,1,0:T(8,128)}), f32[8,128,128]{2,1,0:T(8,128)S(1)}, u32[]{:S(2)}, u32[]{:S(2)}) async-start(f32[8,128,128]{2,1,0:T(8,128)} %broadcast_in_dim.17), calls=%async_computation.5 | async-start | bytes 1048576 | tf_op jit(solution)/shard_map/all_to_all | solution.py:20
  137.0 9.7 %collective-permute-start.2 = (f32[64,1024]{1,0:T(8,128)S(1)}, f32[64,1024]{1,0:T(8,128)S(1)}, u32[]{:S(2)}, u32[]{:S(2)}) collective-permute-start(f32[64,1024]{1,0:T(8,128)S(1)} %pad_maximum_fusion.7), channel_id=1, source_target_pairs={{0,8},{8,0},{16,24},{24,16},{32,40},{40,32},{48,56},{56,48},{64,72... | collective-permute-start | bytes 786440 | tf_op jit(solution)/shard_map/ppermute | solution.py:48
  139.9 12.4 %collective-permute-start.3 = (f32[512,128]{1,0:T(8,128)S(1)}, f32[512,128]{1,0:T(8,128)}, u32[]{:S(2)}, u32[]{:S(2)}) collective-permute-start(f32[512,128]{1,0:T(8,128)S(1)} %bitcast.126), channel_id=1, source_target_pairs={{0,8},{8,0},{16,24},{24,16},{32,40},{40,32},{48,56},{56,48},{64,72... | collective-permute-start | bytes 786440 | tf_op jit(solution)/shard_map/ppermute | solution.py:48
  153.7 16.5 %all-to-all-start.6 = ((f32[32,16,128]{2,1,0:T(8,128)}), f32[32,16,128]{2,1,0:T(8,128)S(1)}, u32[]{:S(2)}, u32[]{:S(2)}) async-start(f32[32,16,128]{2,1,0:T(8,128)} %bitcast.31), calls=%async_computation.6 | async-start | bytes 524288 | tf_op jit(solution)/shard_map/all_to_all | solution.py:20
  158.3 20.0 %copy-start.7 = (f32[256,4,64]{0,2,1:T(8,128)S(1)}, f32[256,4,64]{0,2,1:T(8,128)}, u32[]{:S(2)}) copy-start(f32[256,4,64]{0,2,1:T(8,128)} %fusion.4) | copy-start | bytes 786436
  162.8 26.1 %copy-start.20 = (f32[128,128]{1,0:T(8,128)S(1)}, f32[128,128]{1,0:T(8,128)}, u32[]{:S(2)}) copy-start(f32[128,128]{1,0:T(8,128)} %convolution_add_fusion.4) | copy-start | bytes 196612
  171.0 18.0 %all-to-all-start.7 = ((f32[32,16,128]{2,1,0:T(8,128)}), f32[32,16,128]{2,1,0:T(8,128)S(1)}, u32[]{:S(2)}, u32[]{:S(2)}) async-start(f32[32,16,128]{2,1,0:T(8,128)} %broadcast_in_dim.18), calls=%async_computation.7 | async-start | bytes 524288 | tf_op jit(solution)/shard_map/all_to_all | solution.py:20
  178.4 29.9 %copy-start.21 = (f32[128,128]{1,0:T(8,128)S(1)}, f32[128,128]{1,0:T(8,128)}, u32[]{:S(2)}) copy-start(f32[128,128]{1,0:T(8,128)} %pad_maximum_fusion.12) | copy-start | bytes 196612
  179.7 28.5 %copy-start.9 = (f32[128,512]{1,0:T(8,128)S(1)}, f32[128,512]{1,0:T(8,128)}, u32[]{:S(2)}) copy-start(f32[128,512]{1,0:T(8,128)} %pad_maximum_fusion.9) | copy-start | bytes 786436
  207.1 32.9 %slice-start = ((f32[8,64,256]{2,1,0:T(8,128)}), f32[4,64,256]{2,1,0:T(8,128)S(1)}, s32[]{:S(2)}) async-start(f32[8,64,256]{2,1,0:T(8,128)} %param.4), calls=%async_computation.12 | async-start | bytes 524288 | tf_op jit(solution)/shard_map/slice | solution.py:154
  209.6 18.6 %all-to-all-start.9 = ((f32[32,16,128]{2,1,0:T(8,128)}), f32[32,16,128]{2,1,0:T(8,128)S(1)}, u32[]{:S(2)}, u32[]{:S(2)}) async-start(f32[32,16,128]{2,1,0:T(8,128)} %bitcast.34), calls=%async_computation.9 | async-start | bytes 524288 | tf_op jit(solution)/shard_map/all_to_all | solution.py:20
  213.9 14.2 %collective-permute-start.4 = (f32[512,128]{1,0:T(8,128)S(1)}, f32[512,128]{1,0:T(8,128)S(1)}, u32[]{:S(2)}, u32[]{:S(2)}) collective-permute-start(f32[512,128]{1,0:T(8,128)S(1)} %bitcast.129), channel_id=1, source_target_pairs={{0,8},{8,0},{16,24},{24,16},{32,40},{40,32},{48,56},{56,48},{64,72... | collective-permute-start | bytes 786440 | tf_op jit(solution)/shard_map/ppermute | solution.py:48
  229.1 27.5 %all-to-all-start.10 = ((f32[64,16,128]{2,1,0:T(8,128)}), f32[64,16,128]{2,1,0:T(8,128)S(1)}, u32[]{:S(2)}, u32[]{:S(2)}) async-start(f32[64,16,128]{2,1,0:T(8,128)} %broadcast_in_dim.20), calls=%async_computation.10 | async-start | bytes 1048576 | tf_op jit(solution)/shard_map/all_to_all | solution.py:20
  259.3 13.3 %all-to-all-start.11 = ((f32[8,32,256]{2,1,0:T(8,128)}), f32[8,32,256]{2,1,0:T(8,128)S(1)}, u32[]{:S(2)}, u32[]{:S(2)}) async-start(f32[8,32,256]{2,1,0:T(8,128)} %all_to_all.50), calls=%async_computation.11 | async-start | bytes 524288 | tf_op jit(solution)/shard_map/all_to_all | solution.py:20
  (11 other events, 60.1 us)

commit v8 on v0

v8 whole, which is shorter than its diff:
```python
import jax
import jax.numpy as jnp
from jax import lax
from jax.sharding import PartitionSpec as P

PRECISION = lax.Precision.HIGHEST


def pair_index(block_row, prior_row):
    return block_row * (block_row - 1) // 2 + prior_row


def contract(left, right, axes):
    return lax.dot_general(
        left,
        right,
        (((axes[0],), (axes[1],)), ((), ())),
        precision=PRECISION,
        preferred_element_type=jnp.float32,
    )


def swap(parts, axis, groups=None):
    return lax.all_to_all(parts, axis, 0, 0, axis_index_groups=groups, tiled=True)


def copies(part, count):
    return jnp.broadcast_to(part[None], (count,) + part.shape)


def shards(right_sides, diag_inverse, lower_blocks, trail_panel):
    step_count = diag_inverse.shape[0]
    trail_count = trail_panel.shape[0]
    local_rows = right_sides.shape[1]
    column_count = right_sides.shape[2]
    width = lower_blocks.shape[2]
    row_size = lax.axis_size("row")
    col_size = lax.axis_size("col")
    members = row_size // 2
    half = column_count // 2
    row = lax.axis_index("row")
    col = lax.axis_index("col")
    parity = row % 2
    row_groups = [[r for r in range(row_size) if r % 2 == g] for g in range(2)]
    pair_groups = [
        [(r + g) * col_size + c for g in range(2) for c in range(col_size)]
        for r in range(0, row_size, 2)
    ]

    own_diag = diag_inverse.transpose(0, 2, 1)
    got_diag = lax.ppermute(own_diag[1:], "row", [(r, r ^ 1) for r in range(row_size)])
    diag = [own_diag[0]]
    for block_row in range(1, step_count):
        own, got = own_diag[block_row], got_diag[block_row - 1]
        diag.append(
            jnp.concatenate([jnp.where(parity == 0, own, got), jnp.where(parity == 0, got, own)])
        )

    solved = []
    below = None
    for block_row in range(step_count):
        if block_row == 0:
            local_term = contract(diag[0], right_sides[0], (0, 0))
            parts = local_term.reshape(row_size, width // row_size, column_count)
            part = swap(parts, "row").sum(0)
            whole = swap(copies(part, row_size), "row").reshape(width, column_count)
        else:
            term = jnp.where(col == 0, right_sides[block_row], 0.0)
            for prior_row in range(block_row):
                block = lower_blocks[pair_index(block_row, prior_row)]
                term = term - contract(block, solved[prior_row], (1, 0))
            halves = jnp.stack([term[:, :half], term[:, half:]])[:, None]
            parts = jnp.broadcast_to(halves, (2, col_size, local_rows, half))
            parts = parts.reshape(2 * col_size, local_rows, half)
            parts = swap(parts, ("row", "col"), pair_groups)
            current = parts.reshape(2, col_size, local_rows, half).sum(1)
            local_term = contract(diag[block_row], current.reshape(2 * local_rows, half), (0, 0))
            parts = local_term.reshape(members, width // members, half)
            part = swap(parts, "row", row_groups).sum(0)
            parts = swap(copies(part, row_size), "row").reshape(members, 2, -1, half)
            whole = parts.transpose(0, 2, 1, 3).reshape(width, column_count)
        solved.append(whole)
        contrib = jnp.einsum(
            "nc,mrn->cmr", whole, trail_panel[:, :, block_row, :], precision=PRECISION
        )
        below = contrib if below is None else below + contrib

    own_width = column_count // col_size
    shared = swap(below.reshape(column_count, -1), "col")
    shared = shared.reshape(col_size, own_width, -1).sum(0)
    shared = shared.reshape(own_width, trail_count, local_rows).transpose(1, 2, 0)
    own_below = lax.dynamic_slice_in_dim(right_sides[step_count:], col * own_width, own_width, 2)
    trail_rest = own_below - shared

    out_width = column_count // row_size
    outs = [lax.dynamic_slice_in_dim(whole, row * out_width, out_width, 1) for whole in solved]
    return (jnp.stack(outs), trail_rest)


def solution(mesh):
    placed = (
        P(None, "row", None),
        P(None, "col", "row"),
        P(None, "row", "col"),
        P(None, "row", None, "col"),
    )
    return jax.shard_map(
        shards,
        mesh=mesh,
        in_specs=placed,
        out_specs=(P(None, "col", "row"), P(None, "row", "col")),
        check_vma=False,
    )
```

time: 932 us -> 276 us (0.30)
  waiting for transfers between devices: 884 us -> 98.6 us
  starting transfers between devices: 0.33 us -> 74.4 us
  blocking collectives: 0 us -> 67.3 us
  matrix products: 23.6 us -> 9.53 us
  between operations: 15 us -> 1.06 us
  local copies, waits for them, and re-layouts: 6.87 us -> 20.6 us
    psum x7 -> x0, waiting for transfers between devices: 815 us -> none  [the longest x4 610 us: shards(): solved_block = lax.psum(local_term, 'row')]
    all_to_all x0 -> x9, waiting for transfers between devices: none -> 93.4 us  [swap(): lax.all_to_all(parts, axis, 0, 0, axis_index_groups=groups, tiled=True)]
    all_to_all x0 -> x9, starting transfers between devices: none -> 69.6 us  [swap(): lax.all_to_all(parts, axis, 0, 0, axis_index_groups=groups, tiled=True)]
    unnamed x9 -> x0, waiting for transfers between devices: 69.5 us -> none
    all_to_all x0 -> x3, blocking collectives: none -> 67.3 us  [swap(): lax.all_to_all(parts, axis, 0, 0, axis_index_groups=groups, tiled=True)]
    dot_general x14, matrix products: 23.6 us -> 9.53 us  [the longest x10 4.93 us: contract(): lax.dot_general(left, right, (((axes[0],), (axes[1],)), ((), ())), precis...]
  transfers between devices with their start and end apart: 8 -> 10, of which waited for: 8 -> 10; matrix products, arithmetic and copies ran while one was open for 1% -> 6% of each run, Pallas kernels for 0% -> 0%
where the time goes in v8:
time: 276 us; the launch traced here: 274 us
  waiting for transfers between devices  98.6 us (36%)
  starting transfers between devices  74.4 us (27%)
  blocking collectives  67.3 us (24%)
  local copies, waits for them, and re-layouts  20.6 us (7%)
  matrix products  9.53 us (3%)
  other arithmetic  2.86 us (1%)
    all_to_all x9, waiting for transfers between devices, swap(): lax.all_to_all(parts, axis, 0, 0, axis_index_groups=groups, tiled=True)  93.4 us
    all_to_all x9, starting transfers between devices, swap(): lax.all_to_all(parts, axis, 0, 0, axis_index_groups=groups, tiled=True)  69.6 us
    all_to_all x3, blocking collectives, swap(): lax.all_to_all(parts, axis, 0, 0, axis_index_groups=groups, tiled=True)  67.3 us
    slice x1, local copies, waits for them, and re-layouts, shards(): trail_panel[:, :, block_row, :]  6.84 us
  transfers between devices with their start and end apart: 10, of which 10 were waited for; matrix products, arithmetic and copies ran while one was open for 6% of the time, Pallas kernels for 0%

profile of v8, /device:TPU:1, one launch (start us, length us, event | category | flops | bytes accessed | tf_op | source)
XLA Modules:
  0.0 274.3 jit_solution(14881141747081686368)
XLA Ops:
  0.6 1.1 slice.118
  1.7 4.8 %collective-permute-start = (f32[3,64,512]{2,1,0:T(8,128)S(1)}, f32[3,64,512]{2,1,0:T(8,128)S(1)}, u32[]{:S(2)}, u32[]{:S(2)}) collective-permute-start(f32[3,64,512]{2,1,0:T(8,128)S(1)} %slice.118), channel_id=1, source_target_pairs={{0,8},{8,0},{16,24},{24,16},{32,40},{40,32},{48,56},{56,48},{64,72... | collective-permute-start | bytes 1179656 | tf_op jit(solution)/shard_map/ppermute | solution.py:51
  6.6 5.1 %collective-permute-done = f32[3,64,512]{2,1,0:T(8,128)S(1)} collective-permute-done((f32[3,64,512]{2,1,0:T(8,128)S(1)}, f32[3,64,512]{2,1,0:T(8,128)S(1)}, u32[]{:S(2)}, u32[]{:S(2)}) %collective-permute-start) | collective-permute-done | bytes 393248 | tf_op jit(solution)/shard_map/ppermute | solution.py:51
  11.7 1.9 select_bitcast_fusion.3
  14.3 34.5 %all_to_all.64 = f32[64,8,256]{2,1,0:T(8,128)S(1)} all-to-all(f32[64,8,256]{2,1,0:T(8,128)S(1)} %fusion.8), channel_id=1, replica_groups=mesh['row'=64,'col'=8] {'row'}, dimensions={0} | all-to-all | bytes 1048576 | tf_op jit(solution)/shard_map/all_to_all | solution.py:24
  49.7 7.7 %all-to-all-start.1 = ((f32[64,8,256]{2,1,0:T(8,128)}), f32[64,8,256]{2,1,0:T(8,128)S(1)}, u32[]{:S(2)}, u32[]{:S(2)}) async-start(f32[64,8,256]{2,1,0:T(8,128)} %broadcast_in_dim.20), calls=%async_computation.1 | async-start | bytes 1048576 | tf_op jit(solution)/shard_map/all_to_all | solution.py:24
  57.4 15.4 %all-to-all-done.1 = f32[64,8,256]{2,1,0:T(8,128)S(1)} async-done(((f32[64,8,256]{2,1,0:T(8,128)}), f32[64,8,256]{2,1,0:T(8,128)S(1)}, u32[]{:S(2)}, u32[]{:S(2)}) %all-to-all-start.1) | async-done | bytes 524320 | tf_op jit(solution)/shard_map/all_to_all | solution.py:24
  74.1 9.7 %all-to-all-start.2 = ((f32[16,64,128]{2,1,0:T(8,128)}), f32[16,64,128]{2,1,0:T(8,128)S(1)}, u32[]{:S(2)}, u32[]{:S(2)}) async-start(f32[16,64,128]{2,1,0:T(8,128)} %bitcast.17), calls=%async_computation.2 | async-start | bytes 1048576 | tf_op jit(solution)/shard_map/all_to_all | solution.py:24
  84.0 9.6 %all-to-all-done.2 = f32[16,64,128]{2,1,0:T(8,128)S(1)} async-done(((f32[16,64,128]{2,1,0:T(8,128)}), f32[16,64,128]{2,1,0:T(8,128)S(1)}, u32[]{:S(2)}, u32[]{:S(2)}) %all-to-all-start.2) | async-done | bytes 524320 | tf_op jit(solution)/shard_map/all_to_all | solution.py:24
  94.1 16.2 %all_to_all.65 = f32[32,16,128]{2,1,0:T(8,128)S(1)} all-to-all(f32[32,16,128]{2,1,0:T(8,128)S(1)} %fusion.28), channel_id=1, replica_groups={{0,16,32,48,64,80,96,112,128,144,160,176,192,208,224,240,256,272,288,30..., dimensions={0} | all-to-all | bytes 524288 | tf_op jit(solution)/shard_map/all_to_all | solution.py:24
  111.2 7.0 %all-to-all-start.4 = ((f32[64,16,128]{2,1,0:T(8,128)}), f32[64,16,128]{2,1,0:T(8,128)S(1)}, u32[]{:S(2)}, u32[]{:S(2)}) async-start(f32[64,16,128]{2,1,0:T(8,128)} %broadcast_in_dim.23), calls=%async_computation.4 | async-start | bytes 1048576 | tf_op jit(solution)/shard_map/all_to_all | solution.py:24
  118.6 15.3 %all-to-all-done.4 = f32[64,16,128]{2,1,0:T(8,128)S(1)} async-done(((f32[64,16,128]{2,1,0:T(8,128)}), f32[64,16,128]{2,1,0:T(8,128)S(1)}, u32[]{:S(2)}, u32[]{:S(2)}) %all-to-all-start.4) | async-done | bytes 524320 | tf_op jit(solution)/shard_map/all_to_all | solution.py:24
  134.6 0.8 broadcast_in_dim.24
  135.5 8.6 %all-to-all-start.5 = ((f32[16,64,128]{2,1,0:T(8,128)}), f32[16,64,128]{2,1,0:T(8,128)S(1)}, u32[]{:S(2)}, u32[]{:S(2)}) async-start(f32[16,64,128]{2,1,0:T(8,128)} %bitcast.35), calls=%async_computation.5 | async-start | bytes 1048576 | tf_op jit(solution)/shard_map/all_to_all | solution.py:24
  144.2 9.7 %all-to-all-done.5 = f32[16,64,128]{2,1,0:T(8,128)S(1)} async-done(((f32[16,64,128]{2,1,0:T(8,128)}), f32[16,64,128]{2,1,0:T(8,128)S(1)}, u32[]{:S(2)}, u32[]{:S(2)}) %all-to-all-start.5) | async-done | bytes 524320 | tf_op jit(solution)/shard_map/all_to_all | solution.py:24
  154.2 16.5 %all_to_all.66 = f32[32,16,128]{2,1,0:T(8,128)S(1)} all-to-all(f32[32,16,128]{2,1,0:T(8,128)S(1)} %fusion.29), channel_id=1, replica_groups={{0,16,32,48,64,80,96,112,128,144,160,176,192,208,224,240,256,272,288,30..., dimensions={0} | all-to-all | bytes 524288 | tf_op jit(solution)/shard_map/all_to_all | solution.py:24
  171.6 7.0 %all-to-all-start.7 = ((f32[64,16,128]{2,1,0:T(8,128)}), f32[64,16,128]{2,1,0:T(8,128)S(1)}, u32[]{:S(2)}, u32[]{:S(2)}) async-start(f32[64,16,128]{2,1,0:T(8,128)} %broadcast_in_dim.25), calls=%async_computation.7 | async-start | bytes 1048576 | tf_op jit(solution)/shard_map/all_to_all | solution.py:24
  179.5 14.9 %all-to-all-done.7 = f32[64,16,128]{2,1,0:T(8,128)S(1)} async-done(((f32[64,16,128]{2,1,0:T(8,128)}), f32[64,16,128]{2,1,0:T(8,128)S(1)}, u32[]{:S(2)}, u32[]{:S(2)}) %all-to-all-start.7) | async-done | bytes 524320 | tf_op jit(solution)/shard_map/all_to_all | solution.py:24
  196.0 8.6 %all-to-all-start.8 = ((f32[16,64,128]{2,1,0:T(8,128)}), f32[16,64,128]{2,1,0:T(8,128)S(1)}, u32[]{:S(2)}, u32[]{:S(2)}) async-start(f32[16,64,128]{2,1,0:T(8,128)} %bitcast.55), calls=%async_computation.8 | async-start | bytes 1048576 | tf_op jit(solution)/shard_map/all_to_all | solution.py:24
  204.5 1.0 slice.111
  205.7 8.7 %all-to-all-done.8 = f32[16,64,128]{2,1,0:T(8,128)S(1)} async-done(((f32[16,64,128]{2,1,0:T(8,128)}), f32[16,64,128]{2,1,0:T(8,128)S(1)}, u32[]{:S(2)}, u32[]{:S(2)}) %all-to-all-start.8) | async-done | bytes 524320 | tf_op jit(solution)/shard_map/all_to_all | solution.py:24
  214.4 1.1 fusion.30
  215.4 5.2 %all-to-all-start.9 = ((f32[32,16,128]{2,1,0:T(8,128)}), f32[32,16,128]{2,1,0:T(8,128)S(1)}, u32[]{:S(2)}, u32[]{:S(2)}) async-start(f32[32,16,128]{2,1,0:T(8,128)} %fusion.30), calls=%async_computation.9 | async-start | bytes 524288 | tf_op jit(solution)/shard_map/all_to_all | solution.py:24
  220.8 6.8 %fusion.27 = (f32[4,64,1,512]{3,2,1,0:T(1,128)S(1)}, f32[4,64,1,512]{3,2,1,0:T(1,128)S(1)}, f32[4,64,1,512]{3,2,1,0:T(1,128)}, f32[4,64,1,512]{3,2,1,0:T(1,128)}) fusion(f32[4,64,4,512]{3,2,1,0:T(4,128)} %param.7), kind=kLoop, calls=%fused_computation.72 | loop fusion | bytes 4194304 | tf_op jit(solution)/shard_map/slice | solution.py:84
  227.7 4.5 %all-to-all-done.9 = f32[32,16,128]{2,1,0:T(8,128)S(1)} async-done(((f32[32,16,128]{2,1,0:T(8,128)}), f32[32,16,128]{2,1,0:T(8,128)S(1)}, u32[]{:S(2)}, u32[]{:S(2)}) %all-to-all-start.9) | async-done | bytes 262176 | tf_op jit(solution)/shard_map/all_to_all | solution.py:24
  233.1 7.6 %all-to-all-start.10 = ((f32[64,16,128]{2,1,0:T(8,128)}), f32[64,16,128]{2,1,0:T(8,128)S(1)}, u32[]{:S(2)}, u32[]{:S(2)}) async-start(f32[64,16,128]{2,1,0:T(8,128)} %broadcast_in_dim.27), calls=%async_computation.10 | async-start | bytes 1048576 | tf_op jit(solution)/shard_map/all_to_all | solution.py:24
  240.9 1.7 fusion.6
  243.3 1.7 convolution_add_fusion.2
  246.3 9.8 %all-to-all-done.10 = f32[64,16,128]{2,1,0:T(8,128)S(1)} async-done(((f32[64,16,128]{2,1,0:T(8,128)}), f32[64,16,128]{2,1,0:T(8,128)S(1)}, u32[]{:S(2)}, u32[]{:S(2)}) %all-to-all-start.10) | async-done | bytes 524320 | tf_op jit(solution)/shard_map/all_to_all | solution.py:24
  257.7 1.0 all_to_all.50
  258.8 8.3 %all-to-all-start.11 = ((f32[8,32,256]{2,1,0:T(8,128)}), f32[8,32,256]{2,1,0:T(8,128)S(1)}, u32[]{:S(2)}, u32[]{:S(2)}) async-start(f32[8,32,256]{2,1,0:T(8,128)} %all_to_all.50), calls=%async_computation.11 | async-start | bytes 524288 | tf_op jit(solution)/shard_map/all_to_all | solution.py:24
  267.9 5.6 %all-to-all-done.11 = f32[8,32,256]{2,1,0:T(8,128)S(1)} async-done(((f32[8,32,256]{2,1,0:T(8,128)}), f32[8,32,256]{2,1,0:T(8,128)S(1)}, u32[]{:S(2)}, u32[]{:S(2)}) %all-to-all-start.11) | async-done | bytes 262176 | tf_op jit(solution)/shard_map/all_to_all | solution.py:24
  (67 shorter events, 16.0 us)
Async XLA Ops:
  0.6 13.1 %copy-start.1 = (f32[8,64,256]{2,1,0:T(8,128)S(1)}, f32[8,64,256]{2,1,0:T(8,128)}, u32[]{:S(2)}) copy-start(f32[8,64,256]{2,1,0:T(8,128)} %param.4) | copy-start | bytes 1572868
  1.7 10.0 %collective-permute-start = (f32[3,64,512]{2,1,0:T(8,128)S(1)}, f32[3,64,512]{2,1,0:T(8,128)S(1)}, u32[]{:S(2)}, u32[]{:S(2)}) collective-permute-start(f32[3,64,512]{2,1,0:T(8,128)S(1)} %slice.118), channel_id=1, source_target_pairs={{0,8},{8,0},{16,24},{24,16},{32,40},{40,32},{48,56},{56,48},{64,72... | collective-permute-start | bytes 1179656 | tf_op jit(solution)/shard_map/ppermute | solution.py:51
  13.7 59.1 %copy-start = (f32[6,64,512]{2,1,0:T(8,128)S(1)}, f32[6,64,512]{2,1,0:T(8,128)}, u32[]{:S(2)}) copy-start(f32[6,64,512]{2,1,0:T(8,128)} %param.6) | copy-start | bytes 2359300
  49.7 23.1 %all-to-all-start.1 = ((f32[64,8,256]{2,1,0:T(8,128)}), f32[64,8,256]{2,1,0:T(8,128)S(1)}, u32[]{:S(2)}, u32[]{:S(2)}) async-start(f32[64,8,256]{2,1,0:T(8,128)} %broadcast_in_dim.20), calls=%async_computation.1 | async-start | bytes 1048576 | tf_op jit(solution)/shard_map/all_to_all | solution.py:24
  74.1 19.5 %all-to-all-start.2 = ((f32[16,64,128]{2,1,0:T(8,128)}), f32[16,64,128]{2,1,0:T(8,128)S(1)}, u32[]{:S(2)}, u32[]{:S(2)}) async-start(f32[16,64,128]{2,1,0:T(8,128)} %bitcast.17), calls=%async_computation.2 | async-start | bytes 1048576 | tf_op jit(solution)/shard_map/all_to_all | solution.py:24
  111.2 22.7 %all-to-all-start.4 = ((f32[64,16,128]{2,1,0:T(8,128)}), f32[64,16,128]{2,1,0:T(8,128)S(1)}, u32[]{:S(2)}, u32[]{:S(2)}) async-start(f32[64,16,128]{2,1,0:T(8,128)} %broadcast_in_dim.23), calls=%async_computation.4 | async-start | bytes 1048576 | tf_op jit(solution)/shard_map/all_to_all | solution.py:24
  135.5 18.4 %all-to-all-start.5 = ((f32[16,64,128]{2,1,0:T(8,128)}), f32[16,64,128]{2,1,0:T(8,128)S(1)}, u32[]{:S(2)}, u32[]{:S(2)}) async-start(f32[16,64,128]{2,1,0:T(8,128)} %bitcast.35), calls=%async_computation.5 | async-start | bytes 1048576 | tf_op jit(solution)/shard_map/all_to_all | solution.py:24
  171.6 22.7 %all-to-all-start.7 = ((f32[64,16,128]{2,1,0:T(8,128)}), f32[64,16,128]{2,1,0:T(8,128)S(1)}, u32[]{:S(2)}, u32[]{:S(2)}) async-start(f32[64,16,128]{2,1,0:T(8,128)} %broadcast_in_dim.25), calls=%async_computation.7 | async-start | bytes 1048576 | tf_op jit(solution)/shard_map/all_to_all | solution.py:24
  194.4 11.1 %copy-start.2 = (f32[64,512]{1,0:T(8,128)S(1)}, f32[64,512]{1,0:T(8,128)}, u32[]{:S(2)}) copy-start(f32[64,512]{1,0:T(8,128)} %get-tuple-element.14) | copy-start | bytes 393220
  196.0 18.4 %all-to-all-start.8 = ((f32[16,64,128]{2,1,0:T(8,128)}), f32[16,64,128]{2,1,0:T(8,128)S(1)}, u32[]{:S(2)}, u32[]{:S(2)}) async-start(f32[16,64,128]{2,1,0:T(8,128)} %bitcast.55), calls=%async_computation.8 | async-start | bytes 1048576 | tf_op jit(solution)/shard_map/all_to_all | solution.py:24
  215.4 16.8 %all-to-all-start.9 = ((f32[32,16,128]{2,1,0:T(8,128)}), f32[32,16,128]{2,1,0:T(8,128)S(1)}, u32[]{:S(2)}, u32[]{:S(2)}) async-start(f32[32,16,128]{2,1,0:T(8,128)} %fusion.30), calls=%async_computation.9 | async-start | bytes 524288 | tf_op jit(solution)/shard_map/all_to_all | solution.py:24
  233.1 23.1 %all-to-all-start.10 = ((f32[64,16,128]{2,1,0:T(8,128)}), f32[64,16,128]{2,1,0:T(8,128)S(1)}, u32[]{:S(2)}, u32[]{:S(2)}) async-start(f32[64,16,128]{2,1,0:T(8,128)} %broadcast_in_dim.27), calls=%async_computation.10 | async-start | bytes 1048576 | tf_op jit(solution)/shard_map/all_to_all | solution.py:24
  258.8 14.8 %all-to-all-start.11 = ((f32[8,32,256]{2,1,0:T(8,128)}), f32[8,32,256]{2,1,0:T(8,128)S(1)}, u32[]{:S(2)}, u32[]{:S(2)}) async-start(f32[8,32,256]{2,1,0:T(8,128)} %all_to_all.50), calls=%async_computation.11 | async-start | bytes 524288 | tf_op jit(solution)/shard_map/all_to_all | solution.py:24

commit v9 on v8

--- a/solution.py
+++ b/solution.py
@@ -48,21 +48,25 @@
     ]
 
     own_diag = diag_inverse.transpose(0, 2, 1)
-    got_diag = lax.ppermute(own_diag[1:], "row", [(r, r ^ 1) for r in range(row_size)])
-    diag = [own_diag[0]]
-    for block_row in range(1, step_count):
-        own, got = own_diag[block_row], got_diag[block_row - 1]
-        diag.append(
-            jnp.concatenate([jnp.where(parity == 0, own, got), jnp.where(parity == 0, got, own)])
-        )
 
+    def pair_diag(own_later):
+        got = lax.ppermute(own_later, "row", [(r, r ^ 1) for r in range(row_size)])
+        even = jnp.where(parity == 0, own_later, got)
+        odd = jnp.where(parity == 0, got, own_later)
+        return jnp.concatenate([even, odd], 1)
+
+    trail = [
+        trail_panel[:, :, j, :].reshape(trail_count * local_rows, width) for j in range(step_count)
+    ]
     solved = []
     below = None
     for block_row in range(step_count):
         if block_row == 0:
-            local_term = contract(diag[0], right_sides[0], (0, 0))
+            local_term = contract(own_diag[0], right_sides[0], (0, 0))
             parts = local_term.reshape(row_size, width // row_size, column_count)
             part = swap(parts, "row").sum(0)
+            part, own_later = lax.optimization_barrier((part, own_diag[1:]))
+            diag = pair_diag(own_later)
             whole = swap(copies(part, row_size), "row").reshape(width, column_count)
         else:
             term = jnp.where(col == 0, right_sides[block_row], 0.0)
@@ -74,19 +78,17 @@
             parts = parts.reshape(2 * col_size, local_rows, half)
             parts = swap(parts, ("row", "col"), pair_groups)
             current = parts.reshape(2, col_size, local_rows, half).sum(1)
-            local_term = contract(diag[block_row], current.reshape(2 * local_rows, half), (0, 0))
+            local_term = contract(diag[block_row - 1], current.reshape(2 * local_rows, half), (0, 0))
             parts = local_term.reshape(members, width // members, half)
             part = swap(parts, "row", row_groups).sum(0)
             parts = swap(copies(part, row_size), "row").reshape(members, 2, -1, half)
             whole = parts.transpose(0, 2, 1, 3).reshape(width, column_count)
         solved.append(whole)
-        contrib = jnp.einsum(
-            "nc,mrn->cmr", whole, trail_panel[:, :, block_row, :], precision=PRECISION
-        )
+        contrib = contract(whole, trail[block_row], (0, 1))
         below = contrib if below is None else below + contrib
 
     own_width = column_count // col_size
-    shared = swap(below.reshape(column_count, -1), "col")
+    shared = swap(below, "col")
     shared = shared.reshape(col_size, own_width, -1).sum(0)
     shared = shared.reshape(own_width, trail_count, local_rows).transpose(1, 2, 0)
     own_below = lax.dynamic_slice_in_dim(right_sides[step_count:], col * own_width, own_width, 2)

time: 276 us -> 272 us (0.986)
  blocking collectives: 67.3 us -> 49.6 us
  starting transfers between devices: 74.4 us -> 83.5 us
  matrix products: 9.53 us -> 13.3 us
    all_to_all x3, blocking collectives: 67.3 us -> 49.6 us  [swap(): lax.all_to_all(parts, axis, 0, 0, axis_index_groups=groups, tiled=True)]
    all_to_all x9, starting transfers between devices: 69.6 us -> 80.3 us  [swap(): lax.all_to_all(parts, axis, 0, 0, axis_index_groups=groups, tiled=True)]
    dot_general x10 -> x14, matrix products: 4.93 us -> 13.3 us  [contract(): lax.dot_general(left, right, (((axes[0],), (axes[1],)), ((), ())), precis...]
    ppermute x1, waiting for transfers between devices: 5.14 us -> 13.1 us  [pair_diag(): got = lax.ppermute(own_later, 'row', [(r, r ^ 1) for r in range(row_size)])]
    all_to_all x9, waiting for transfers between devices: 93.4 us -> 86.1 us  [swap(): lax.all_to_all(parts, axis, 0, 0, axis_index_groups=groups, tiled=True)]
    dot_general x4 -> x0, matrix products: 4.6 us -> none  [shards(): jnp.einsum('nc,mrn->cmr', whole, trail_panel[:, :, block_row, :], precisi...]
  transfers between devices with their start and end apart: 10 -> 10, of which waited for: 10 -> 8; matrix products, arithmetic and copies ran while one was open for 6% -> 8% of each run, Pallas kernels for 0% -> 0%
where the time goes in v9:
time: 272 us; the launch traced here: 270 us
  waiting for transfers between devices  99.2 us (36%)
  starting transfers between devices  83.5 us (31%)
  blocking collectives  49.6 us (18%)
  local copies, waits for them, and re-layouts  22.4 us (8%)
  matrix products  13.3 us (5%)
    all_to_all x9, waiting for transfers between devices, swap(): lax.all_to_all(parts, axis, 0, 0, axis_index_groups=groups, tiled=True)  86.1 us
    all_to_all x9, starting transfers between devices, swap(): lax.all_to_all(parts, axis, 0, 0, axis_index_groups=groups, tiled=True)  80.3 us
    all_to_all x3, blocking collectives, swap(): lax.all_to_all(parts, axis, 0, 0, axis_index_groups=groups, tiled=True)  49.6 us
    dot_general x14, matrix products, contract(): lax.dot_general(left, right, (((axes[0],), (axes[1],)), ((), ())), precis...  13.3 us
    ppermute x1, waiting for transfers between devices, pair_diag(): got = lax.ppermute(own_later, 'row', [(r, r ^ 1) for r in range(row_size)])  13.1 us
    slice x1, local copies, waits for them, and re-layouts, shards(): trail_panel[:, :, j, :].reshape(trail_count * local_rows, width)  6.69 us
  transfers between devices with their start and end apart: 10, of which 8 were waited for; matrix products, arithmetic and copies ran while one was open for 8% of the time, Pallas kernels for 0%

profile of v9, /device:TPU:1, one launch (start us, length us, event | category | flops | bytes accessed | tf_op | source)
XLA Modules:
  0.0 270.1 jit_solution(5487047050580165552)
XLA Ops:
  1.7 2.2 fusion.11
  4.0 17.3 %all-to-all-start = ((f32[64,8,256]{2,1,0:T(8,128)}), f32[64,8,256]{2,1,0:T(8,128)S(1)}, u32[]{:S(2)}, u32[]{:S(2)}) async-start(f32[64,8,256]{2,1,0:T(8,128)} %fusion.11), calls=%async_computation | async-start | bytes 1048576 | tf_op jit(solution)/shard_map/all_to_all | solution.py:24
  21.3 16.3 %all-to-all-done = f32[64,8,256]{2,1,0:T(8,128)S(1)} async-done(((f32[64,8,256]{2,1,0:T(8,128)}), f32[64,8,256]{2,1,0:T(8,128)S(1)}, u32[]{:S(2)}, u32[]{:S(2)}) %all-to-all-start) | async-done | bytes 524320 | tf_op jit(solution)/shard_map/all_to_all | solution.py:24
  38.5 7.8 %all-to-all-start.1 = ((f32[64,8,256]{2,1,0:T(8,128)}), f32[64,8,256]{2,1,0:T(8,128)S(1)}, u32[]{:S(2)}, u32[]{:S(2)}) async-start(f32[64,8,256]{2,1,0:T(8,128)} %broadcast_in_dim.20), calls=%async_computation.1 | async-start | bytes 1048576 | tf_op jit(solution)/shard_map/all_to_all | solution.py:24
  46.3 16.1 %all-to-all-done.1 = f32[64,8,256]{2,1,0:T(8,128)S(1)} async-done(((f32[64,8,256]{2,1,0:T(8,128)}), f32[64,8,256]{2,1,0:T(8,128)S(1)}, u32[]{:S(2)}, u32[]{:S(2)}) %all-to-all-start.1) | async-done | bytes 524320 | tf_op jit(solution)/shard_map/all_to_all | solution.py:24
  63.7 8.9 %all-to-all-start.2 = ((f32[16,64,128]{2,1,0:T(8,128)}), f32[16,64,128]{2,1,0:T(8,128)S(1)}, u32[]{:S(2)}, u32[]{:S(2)}) async-start(f32[16,64,128]{2,1,0:T(8,128)} %bitcast.16), calls=%async_computation.2 | async-start | bytes 1048576 | tf_op jit(solution)/shard_map/all_to_all | solution.py:24
  72.6 3.3 %collective-permute-start = (f32[3,64,512]{2,1,0:T(8,128)S(1)}, f32[3,64,512]{2,1,0:T(8,128)S(1)}, u32[]{:S(2)}, u32[]{:S(2)}) collective-permute-start(f32[3,64,512]{2,1,0:T(8,128)S(1)} %slice.105), channel_id=1, source_target_pairs={{0,8},{8,0},{16,24},{24,16},{32,40},{40,32},{48,56},{56,48},{64,72... | collective-permute-start | bytes 1179656 | tf_op jit(solution)/shard_map/ppermute | solution.py:53
  75.9 13.1 %collective-permute-done = f32[3,64,512]{2,1,0:T(8,128)S(1)} collective-permute-done((f32[3,64,512]{2,1,0:T(8,128)S(1)}, f32[3,64,512]{2,1,0:T(8,128)S(1)}, u32[]{:S(2)}, u32[]{:S(2)}) %collective-permute-start) | collective-permute-done | bytes 393248 | tf_op jit(solution)/shard_map/ppermute | solution.py:53
  89.7 16.6 %all_to_all.64 = f32[32,16,128]{2,1,0:T(8,128)S(1)} all-to-all(f32[32,16,128]{2,1,0:T(8,128)S(1)} %fusion.33), channel_id=1, replica_groups={{0,16,32,48,64,80,96,112,128,144,160,176,192,208,224,240,256,272,288,30..., dimensions={0} | all-to-all | bytes 524288 | tf_op jit(solution)/shard_map/all_to_all | solution.py:24
  107.2 7.0 %all-to-all-start.4 = ((f32[64,16,128]{2,1,0:T(8,128)}), f32[64,16,128]{2,1,0:T(8,128)S(1)}, u32[]{:S(2)}, u32[]{:S(2)}) async-start(f32[64,16,128]{2,1,0:T(8,128)} %broadcast_in_dim.23), calls=%async_computation.4 | async-start | bytes 1048576 | tf_op jit(solution)/shard_map/all_to_all | solution.py:24
  114.2 1.3 fusion.4
  115.5 14.9 %all-to-all-done.4 = f32[64,16,128]{2,1,0:T(8,128)S(1)} async-done(((f32[64,16,128]{2,1,0:T(8,128)}), f32[64,16,128]{2,1,0:T(8,128)S(1)}, u32[]{:S(2)}, u32[]{:S(2)}) %all-to-all-start.4) | async-done | bytes 524320 | tf_op jit(solution)/shard_map/all_to_all | solution.py:24
  131.9 8.8 %all-to-all-start.5 = ((f32[16,64,128]{2,1,0:T(8,128)}), f32[16,64,128]{2,1,0:T(8,128)S(1)}, u32[]{:S(2)}, u32[]{:S(2)}) async-start(f32[16,64,128]{2,1,0:T(8,128)} %bitcast.33), calls=%async_computation.5 | async-start | bytes 1048576 | tf_op jit(solution)/shard_map/all_to_all | solution.py:24
  140.8 9.7 %all-to-all-done.5 = f32[16,64,128]{2,1,0:T(8,128)S(1)} async-done(((f32[16,64,128]{2,1,0:T(8,128)}), f32[16,64,128]{2,1,0:T(8,128)S(1)}, u32[]{:S(2)}, u32[]{:S(2)}) %all-to-all-start.5) | async-done | bytes 524320 | tf_op jit(solution)/shard_map/all_to_all | solution.py:24
  150.9 16.4 %all_to_all.65 = f32[32,16,128]{2,1,0:T(8,128)S(1)} all-to-all(f32[32,16,128]{2,1,0:T(8,128)S(1)} %fusion.34), channel_id=1, replica_groups={{0,16,32,48,64,80,96,112,128,144,160,176,192,208,224,240,256,272,288,30..., dimensions={0} | all-to-all | bytes 524288 | tf_op jit(solution)/shard_map/all_to_all | solution.py:24
  168.2 7.0 %all-to-all-start.7 = ((f32[64,16,128]{2,1,0:T(8,128)}), f32[64,16,128]{2,1,0:T(8,128)S(1)}, u32[]{:S(2)}, u32[]{:S(2)}) async-start(f32[64,16,128]{2,1,0:T(8,128)} %broadcast_in_dim.25), calls=%async_computation.7 | async-start | bytes 1048576 | tf_op jit(solution)/shard_map/all_to_all | solution.py:24
  175.2 1.3 fusion.2
  176.9 14.0 %all-to-all-done.7 = f32[64,16,128]{2,1,0:T(8,128)S(1)} async-done(((f32[64,16,128]{2,1,0:T(8,128)}), f32[64,16,128]{2,1,0:T(8,128)S(1)}, u32[]{:S(2)}, u32[]{:S(2)}) %all-to-all-start.7) | async-done | bytes 524320 | tf_op jit(solution)/shard_map/all_to_all | solution.py:24
  192.5 8.5 %all-to-all-start.8 = ((f32[16,64,128]{2,1,0:T(8,128)}), f32[16,64,128]{2,1,0:T(8,128)S(1)}, u32[]{:S(2)}, u32[]{:S(2)}) async-start(f32[16,64,128]{2,1,0:T(8,128)} %bitcast.52), calls=%async_computation.8 | async-start | bytes 1048576 | tf_op jit(solution)/shard_map/all_to_all | solution.py:24
  201.2 9.7 %all-to-all-done.8 = f32[16,64,128]{2,1,0:T(8,128)S(1)} async-done(((f32[16,64,128]{2,1,0:T(8,128)}), f32[16,64,128]{2,1,0:T(8,128)S(1)}, u32[]{:S(2)}, u32[]{:S(2)}) %all-to-all-start.8) | async-done | bytes 524320 | tf_op jit(solution)/shard_map/all_to_all | solution.py:24
  211.3 16.5 %all_to_all.66 = f32[32,16,128]{2,1,0:T(8,128)S(1)} all-to-all(f32[32,16,128]{2,1,0:T(8,128)S(1)} %fusion.35), channel_id=1, replica_groups={{0,16,32,48,64,80,96,112,128,144,160,176,192,208,224,240,256,272,288,30..., dimensions={0} | all-to-all | bytes 524288 | tf_op jit(solution)/shard_map/all_to_all | solution.py:24
  228.7 7.3 %all-to-all-start.10 = ((f32[64,16,128]{2,1,0:T(8,128)}), f32[64,16,128]{2,1,0:T(8,128)}, u32[]{:S(2)}, u32[]{:S(2)}) async-start(f32[64,16,128]{2,1,0:T(8,128)} %broadcast_in_dim.27), calls=%async_computation.10 | async-start | bytes 1048576 | tf_op jit(solution)/shard_map/all_to_all | solution.py:24
  236.0 6.7 %fusion.32 = (f32[4,64,1,512]{3,2,1,0:T(1,128)}, f32[4,64,1,512]{3,2,1,0:T(1,128)S(1)}, f32[4,64,1,512]{3,2,1,0:T(1,128)S(1)}, f32[4,64,1,512]{3,2,1,0:T(1,128)S(1)}) fusion(f32[4,64,4,512]{3,2,1,0:T(4,128)} %param.7), kind=kLoop, calls=%fused_computation.71 | loop fusion | bytes 4194304 | tf_op jit(solution)/shard_map/slice | solution.py:59
  244.8 2.0 fusion.27
  246.9 1.0 constant_dynamic-slice_fusion.3
  247.9 1.1 copy.45
  249.0 1.1 copy.42
  250.0 1.0 convolution_add_fusion.2
  252.1 1.3 copy.50
  253.5 1.7 convolution_add_fusion
  255.2 7.6 %all-to-all-start.11 = ((f32[8,32,256]{2,1,0:T(8,128)}), f32[8,32,256]{2,1,0:T(8,128)S(1)}, u32[]{:S(2)}, u32[]{:S(2)}) async-start(f32[8,32,256]{2,1,0:T(8,128)} %bitcast.63), calls=%async_computation.11 | async-start | bytes 524288 | tf_op jit(solution)/shard_map/all_to_all | solution.py:24
  263.9 5.4 %all-to-all-done.11 = f32[8,32,256]{2,1,0:T(8,128)S(1)} async-done(((f32[8,32,256]{2,1,0:T(8,128)}), f32[8,32,256]{2,1,0:T(8,128)S(1)}, u32[]{:S(2)}, u32[]{:S(2)}) %all-to-all-start.11) | async-done | bytes 262176 | tf_op jit(solution)/shard_map/all_to_all | solution.py:24
  (69 shorter events, 16.2 us)
Async XLA Ops:
  0.6 20.6 %copy-start.3 = (f32[4,512,64]{1,2,0:T(8,128)S(1)}, f32[4,512,64]{1,2,0:T(8,128)}, u32[]{:S(2)}) copy-start(f32[4,512,64]{1,2,0:T(8,128)} %param.5) | copy-start | bytes 1572868
  3.9 58.4 %copy-start.1 = (f32[6,64,512]{2,1,0:T(8,128)S(1)}, f32[6,64,512]{2,1,0:T(8,128)}, u32[]{:S(2)}) copy-start(f32[6,64,512]{2,1,0:T(8,128)} %param.6) | copy-start | bytes 2359300
  3.9 58.4 %copy-start.2 = (f32[8,64,256]{2,1,0:T(8,128)S(1)}, f32[8,64,256]{2,1,0:T(8,128)}, u32[]{:S(2)}) copy-start(f32[8,64,256]{2,1,0:T(8,128)} %param.4) | copy-start | bytes 1572868
  4.0 33.6 %all-to-all-start = ((f32[64,8,256]{2,1,0:T(8,128)}), f32[64,8,256]{2,1,0:T(8,128)S(1)}, u32[]{:S(2)}, u32[]{:S(2)}) async-start(f32[64,8,256]{2,1,0:T(8,128)} %fusion.11), calls=%async_computation | async-start | bytes 1048576 | tf_op jit(solution)/shard_map/all_to_all | solution.py:24
  38.5 23.9 %all-to-all-start.1 = ((f32[64,8,256]{2,1,0:T(8,128)}), f32[64,8,256]{2,1,0:T(8,128)S(1)}, u32[]{:S(2)}, u32[]{:S(2)}) async-start(f32[64,8,256]{2,1,0:T(8,128)} %broadcast_in_dim.20), calls=%async_computation.1 | async-start | bytes 1048576 | tf_op jit(solution)/shard_map/all_to_all | solution.py:24
  63.7 25.6 %all-to-all-start.2 = ((f32[16,64,128]{2,1,0:T(8,128)}), f32[16,64,128]{2,1,0:T(8,128)S(1)}, u32[]{:S(2)}, u32[]{:S(2)}) async-start(f32[16,64,128]{2,1,0:T(8,128)} %bitcast.16), calls=%async_computation.2 | async-start | bytes 1048576 | tf_op jit(solution)/shard_map/all_to_all | solution.py:24
  72.6 16.4 %collective-permute-start = (f32[3,64,512]{2,1,0:T(8,128)S(1)}, f32[3,64,512]{2,1,0:T(8,128)S(1)}, u32[]{:S(2)}, u32[]{:S(2)}) collective-permute-start(f32[3,64,512]{2,1,0:T(8,128)S(1)} %slice.105), channel_id=1, source_target_pairs={{0,8},{8,0},{16,24},{24,16},{32,40},{40,32},{48,56},{56,48},{64,72... | collective-permute-start | bytes 1179656 | tf_op jit(solution)/shard_map/ppermute | solution.py:53
  107.2 23.1 %all-to-all-start.4 = ((f32[64,16,128]{2,1,0:T(8,128)}), f32[64,16,128]{2,1,0:T(8,128)S(1)}, u32[]{:S(2)}, u32[]{:S(2)}) async-start(f32[64,16,128]{2,1,0:T(8,128)} %broadcast_in_dim.23), calls=%async_computation.4 | async-start | bytes 1048576 | tf_op jit(solution)/shard_map/all_to_all | solution.py:24
  131.9 18.6 %all-to-all-start.5 = ((f32[16,64,128]{2,1,0:T(8,128)}), f32[16,64,128]{2,1,0:T(8,128)S(1)}, u32[]{:S(2)}, u32[]{:S(2)}) async-start(f32[16,64,128]{2,1,0:T(8,128)} %bitcast.33), calls=%async_computation.5 | async-start | bytes 1048576 | tf_op jit(solution)/shard_map/all_to_all | solution.py:24
  168.2 22.7 %all-to-all-start.7 = ((f32[64,16,128]{2,1,0:T(8,128)}), f32[64,16,128]{2,1,0:T(8,128)S(1)}, u32[]{:S(2)}, u32[]{:S(2)}) async-start(f32[64,16,128]{2,1,0:T(8,128)} %broadcast_in_dim.25), calls=%async_computation.7 | async-start | bytes 1048576 | tf_op jit(solution)/shard_map/all_to_all | solution.py:24
  192.5 18.3 %all-to-all-start.8 = ((f32[16,64,128]{2,1,0:T(8,128)}), f32[16,64,128]{2,1,0:T(8,128)S(1)}, u32[]{:S(2)}, u32[]{:S(2)}) async-start(f32[16,64,128]{2,1,0:T(8,128)} %bitcast.52), calls=%async_computation.8 | async-start | bytes 1048576 | tf_op jit(solution)/shard_map/all_to_all | solution.py:24
  228.7 23.4 %all-to-all-start.10 = ((f32[64,16,128]{2,1,0:T(8,128)}), f32[64,16,128]{2,1,0:T(8,128)}, u32[]{:S(2)}, u32[]{:S(2)}) async-start(f32[64,16,128]{2,1,0:T(8,128)} %broadcast_in_dim.27), calls=%async_computation.10 | async-start | bytes 1048576 | tf_op jit(solution)/shard_map/all_to_all | solution.py:24
  242.7 1.2 copy-start
  242.7 1.3 slice-start
  253.5 16.0 %copy-start.4 = (f32[4,64,32]{1,0,2:T(4,128)S(1)}, f32[4,64,32]{1,0,2:T(4,128)}, u32[]{:S(2)}) copy-start(f32[4,64,32]{1,0,2:T(4,128)} %copy.59) | copy-start | bytes 98308
  255.2 14.1 %all-to-all-start.11 = ((f32[8,32,256]{2,1,0:T(8,128)}), f32[8,32,256]{2,1,0:T(8,128)S(1)}, u32[]{:S(2)}, u32[]{:S(2)}) async-start(f32[8,32,256]{2,1,0:T(8,128)} %bitcast.63), calls=%async_computation.11 | async-start | bytes 524288 | tf_op jit(solution)/shard_map/all_to_all | solution.py:24

commit v10 on v9

v10 whole, which is shorter than its diff:
```python
import jax
import jax.numpy as jnp
from jax import lax
from jax.sharding import PartitionSpec as P

PRECISION = lax.Precision.HIGHEST


def contract(left, right, axes):
    return lax.dot_general(
        left,
        right,
        (((axes[0],), (axes[1],)), ((), ())),
        precision=PRECISION,
        preferred_element_type=jnp.float32,
    )


def swap(parts, axis, groups=None):
    return lax.all_to_all(parts, axis, 0, 0, axis_index_groups=groups, tiled=True)


def copies(part, count):
    return jnp.broadcast_to(part[None], (count,) + part.shape)


def by_deadline(*values):
    return lax.optimization_barrier(values)


def shards(right_sides, diag_inverse, lower_blocks, trail_panel):
    step_count = diag_inverse.shape[0]
    trail_count = trail_panel.shape[0]
    local_rows = right_sides.shape[1]
    column_count = right_sides.shape[2]
    width = lower_blocks.shape[2]
    row_size = lax.axis_size("row")
    col_size = lax.axis_size("col")
    members = row_size // 2
    half = column_count // 2
    row = lax.axis_index("row")
    col = lax.axis_index("col")
    even = row % 2 == 0
    row_groups = [[r for r in range(row_size) if r % 2 == g] for g in range(2)]
    pair_groups = [
        [(r + g) * col_size + c for g in range(2) for c in range(col_size)]
        for r in range(0, row_size, 2)
    ]

    def from_partner(value):
        return lax.ppermute(value, "row", [(r, r ^ 1) for r in range(row_size)])

    def ordered(own, got, axis):
        return jnp.concatenate([jnp.where(even, own, got), jnp.where(even, got, own)], axis)

    def half_of(value, which):
        return lax.dynamic_slice_in_dim(value, which * half, half, value.ndim - 1)

    def halves_whole(parts):
        parts = parts.reshape(members, 2, -1, half)
        return parts.transpose(0, 2, 1, 3).reshape(width, column_count)

    def scattered(matrix, current):
        parts = contract(matrix, current, (0, 0)).reshape(members, width // members, half)
        return swap(parts, "row", row_groups)

    def gathered(parts):
        return swap(copies(parts.sum(0), members), "row", row_groups)

    def gathered_whole(parts):
        return swap(copies(parts.sum(0), row_size), "row")

    def summed(update):
        return swap(copies(update, col_size), "col").sum(0)

    def own_term(block_row):
        return jnp.where(col == 0, right_sides[block_row], 0.0)

    own_diag = diag_inverse.transpose(0, 2, 1)
    trail = [
        trail_panel[:, :, j, :].reshape(trail_count * local_rows, width) for j in range(step_count)
    ]

    def below_of(whole, block_row):
        return contract(whole, trail[block_row], (0, 1))

    out_width = column_count // row_size

    def out_of(whole):
        return lax.dynamic_slice_in_dim(whole, row * out_width, out_width, 1)

    local_term = contract(own_diag[0], right_sides[0], (0, 0))
    parts = swap(local_term.reshape(row_size, width // row_size, column_count), "row")
    part, own_later = lax.optimization_barrier((parts.sum(0), own_diag[1:]))
    parts = swap(copies(part, row_size), "row")
    parts, got_later = by_deadline(parts, from_partner(own_later))
    whole_0 = parts.reshape(width, column_count)

    term = own_term(1) - contract(lower_blocks[0], whole_0, (1, 0))
    parts = jnp.stack([term[:, :half], term[:, half:]])[:, None]
    parts = jnp.broadcast_to(parts, (2, col_size, local_rows, half))
    parts = swap(parts.reshape(2 * col_size, local_rows, half), ("row", "col"), pair_groups)
    diag = ordered(own_later, got_later, 1)
    term_2 = own_term(2) - contract(lower_blocks[1], whole_0, (1, 0))
    term_3 = own_term(3) - contract(lower_blocks[3], whole_0, (1, 0))
    shared = [lower_blocks[2], lower_blocks[4], lower_blocks[5]]
    sent = shared + [half_of(term_2, row % 2 ^ 1), half_of(term_3, row % 2 ^ 1)]
    kept = jnp.concatenate(shared + [half_of(term_2, row % 2), half_of(term_3, row % 2)], 1)
    got = from_partner(jnp.concatenate(sent, 1))
    parts, diag = by_deadline(parts, diag)
    current = parts.reshape(2, col_size, local_rows, half).sum(1).reshape(2 * local_rows, half)
    parts = scattered(diag[0], current)
    parts, got = by_deadline(parts, got)
    parts = gathered(parts)
    pair = ordered(kept, got, 0)
    lower_21, lower_31, lower_32 = [pair[:, i * width : (i + 1) * width] for i in range(3)]
    term_2 = pair[:, 3 * width : 3 * width + half]
    term_3 = pair[:, 3 * width + half :]
    below = below_of(whole_0, 0)
    parts, lower_21, lower_31, lower_32, term_2, term_3, below = by_deadline(
        parts, lower_21, lower_31, lower_32, term_2, term_3, below
    )
    solved_1 = parts.reshape(width, half)

    current = summed(term_2 - contract(lower_21, solved_1, (1, 0)))
    parts = scattered(diag[1], current)
    parts, got_1 = by_deadline(parts, from_partner(solved_1))
    parts = gathered(parts)
    whole_1 = ordered(solved_1, got_1, 1)
    term_3 = term_3 - contract(lower_31, solved_1, (1, 0))
    below = below + below_of(whole_1, 1)
    parts, term_3, below = by_deadline(parts, term_3, below)
    solved_2 = parts.reshape(width, half)

    current = summed(term_3 - contract(lower_32, solved_2, (1, 0)))
    parts = scattered(diag[2], current)
    outs = [out_of(whole_0), out_of(whole_1)]
    parts, got_2, outs = by_deadline(parts, from_partner(solved_2), outs)
    parts = gathered_whole(parts)
    whole_2 = ordered(solved_2, got_2, 1)
    below = below + below_of(whole_2, 2)
    parts, below = by_deadline(parts, below)
    whole_3 = halves_whole(parts)

    below = below + below_of(whole_3, 3)
    own_width = column_count // col_size
    shared = swap(below, "col").reshape(col_size, own_width, -1).sum(0)
    shared = shared.reshape(own_width, trail_count, local_rows).transpose(1, 2, 0)
    own_below = lax.dynamic_slice_in_dim(right_sides[step_count:], col * own_width, own_width, 2)
    trail_rest = own_below - shared
    return (jnp.stack(outs + [out_of(whole_2), out_of(whole_3)]), trail_rest)


def solution(mesh):
    placed = (
        P(None, "row", None),
        P(None, "col", "row"),
        P(None, "row", "col"),
        P(None, "row", None, "col"),
    )
    return jax.shard_map(
        shards,
        mesh=mesh,
        in_specs=placed,
        out_specs=(P(None, "col", "row"), P(None, "row", "col")),
        check_vma=False,
    )
```

time: 272 us -> 275 us (1.011)
  blocking collectives: 49.6 us -> 0 us
  waiting for transfers between devices: 99.2 us -> 125 us
  starting transfers between devices: 83.5 us -> 108 us
  local copies, waits for them, and re-layouts: 22.4 us -> 16.8 us
  other arithmetic: 1.08 us -> 6.43 us
    all_to_all x3 -> x0, blocking collectives: 49.6 us -> none  [swap(): lax.all_to_all(parts, axis, 0, 0, axis_index_groups=groups, tiled=True)]
    ppermute x1 -> x4, waiting for transfers between devices: 13.1 us -> 42 us  [from_partner(): return lax.ppermute(value, 'row', [(r, r ^ 1) for r in range(row_size)])]
    all_to_all x9 -> x12, starting transfers between devices: 80.3 us -> 96.9 us  [swap(): lax.all_to_all(parts, axis, 0, 0, axis_index_groups=groups, tiled=True)]
    ppermute x1 -> x4, starting transfers between devices: 3.28 us -> 11.4 us  [from_partner(): return lax.ppermute(value, 'row', [(r, r ^ 1) for r in range(row_size)])]
    slice x1, local copies, waits for them, and re-layouts: 6.69 us -> 2.6 us  [shards(): trail_panel[:, :, j, :].reshape(trail_count * local_rows, width)]
    all_to_all x9 -> x12, waiting for transfers between devices: 86.1 us -> 82.7 us  [swap(): lax.all_to_all(parts, axis, 0, 0, axis_index_groups=groups, tiled=True)]
    dynamic_slice x6 -> x4, local copies, waits for them, and re-layouts: 3.6 us -> 0.48 us  [out_of(): return lax.dynamic_slice_in_dim(whole, row * out_width, out_width, 1)]
    select_n x1 -> x4, other arithmetic: 0.07 us -> 3.13 us  [the longest x3 2.05 us: ordered(): jnp.where(even, own, got)]
  transfers between devices with their start and end apart: 10 -> 16, of which waited for: 8 -> 12; matrix products, arithmetic and copies ran while one was open for 8% -> 8% of each run, Pallas kernels for 0% -> 0%
where the time goes in v10:
time: 275 us; the launch traced here: 273 us
  waiting for transfers between devices  125 us (45%)
  starting transfers between devices  108 us (39%)
  local copies, waits for them, and re-layouts  16.8 us (6%)
  matrix products  16 us (6%)
  other arithmetic  6.43 us (2%)
    all_to_all x12, starting transfers between devices, swap(): lax.all_to_all(parts, axis, 0, 0, axis_index_groups=groups, tiled=True)  96.9 us
    all_to_all x12, waiting for transfers between devices, swap(): lax.all_to_all(parts, axis, 0, 0, axis_index_groups=groups, tiled=True)  82.7 us
    ppermute x4, waiting for transfers between devices, from_partner(): return lax.ppermute(value, 'row', [(r, r ^ 1) for r in range(row_size)])  42 us
    dot_general x14, matrix products, contract(): lax.dot_general(left, right, (((axes[0],), (axes[1],)), ((), ())), precis...  16 us
    ppermute x4, starting transfers between devices, from_partner(): return lax.ppermute(value, 'row', [(r, r ^ 1) for r in range(row_size)])  11.4 us
  transfers between devices with their start and end apart: 16, of which 12 were waited for; matrix products, arithmetic and copies ran while one was open for 8% of the time, Pallas kernels for 0%

profile of v10, /device:TPU:1, one launch (start us, length us, event | category | flops | bytes accessed | tf_op | source)
XLA Modules:
  0.0 273.3 jit_solution(14145985903606459385)
XLA Ops:
  1.7 2.2 fusion.8
  4.0 17.3 %all-to-all-start = ((f32[64,8,256]{2,1,0:T(8,128)}), f32[64,8,256]{2,1,0:T(8,128)S(1)}, u32[]{:S(2)}, u32[]{:S(2)}) async-start(f32[64,8,256]{2,1,0:T(8,128)} %fusion.8), calls=%async_computation | async-start | bytes 1048576 | tf_op jit(solution)/shard_map/all_to_all | solution.py:20
  21.3 16.3 %all-to-all-done = f32[64,8,256]{2,1,0:T(8,128)S(1)} async-done(((f32[64,8,256]{2,1,0:T(8,128)}), f32[64,8,256]{2,1,0:T(8,128)S(1)}, u32[]{:S(2)}, u32[]{:S(2)}) %all-to-all-start) | async-done | bytes 524320 | tf_op jit(solution)/shard_map/all_to_all | solution.py:20
  38.5 7.8 %all-to-all-start.1 = ((f32[64,8,256]{2,1,0:T(8,128)}), f32[64,8,256]{2,1,0:T(8,128)S(1)}, u32[]{:S(2)}, u32[]{:S(2)}) async-start(f32[64,8,256]{2,1,0:T(8,128)} %broadcast_in_dim.21), calls=%async_computation.1 | async-start | bytes 1048576 | tf_op jit(solution)/shard_map/all_to_all | solution.py:20
  46.4 2.9 %collective-permute-start = (f32[3,64,512]{2,1,0:T(8,128)S(1)}, f32[3,64,512]{2,1,0:T(8,128)S(1)}, u32[]{:S(2)}, u32[]{:S(2)}) collective-permute-start(f32[3,64,512]{2,1,0:T(8,128)S(1)} %slice.109), channel_id=1, source_target_pairs={{0,8},{8,0},{16,24},{24,16},{32,40},{40,32},{48,56},{56,48},{64,72... | collective-permute-start | bytes 1179656 | tf_op jit(solution)/shard_map/ppermute | solution.py:51
  50.1 19.0 %collective-permute-done = f32[3,64,512]{2,1,0:T(8,128)S(1)} collective-permute-done((f32[3,64,512]{2,1,0:T(8,128)S(1)}, f32[3,64,512]{2,1,0:T(8,128)S(1)}, u32[]{:S(2)}, u32[]{:S(2)}) %collective-permute-start) | collective-permute-done | bytes 393248 | tf_op jit(solution)/shard_map/ppermute | solution.py:51
  70.4 5.2 %all-to-all-start.2 = ((f32[16,64,128]{2,1,0:T(8,128)}), f32[16,64,128]{2,1,0:T(8,128)S(1)}, u32[]{:S(2)}, u32[]{:S(2)}) async-start(f32[16,64,128]{2,1,0:T(8,128)} %bitcast.12), calls=%async_computation.2 | async-start | bytes 1048576 | tf_op jit(solution)/shard_map/all_to_all | solution.py:20
  79.4 3.3 %collective-permute-start.1 = (f32[64,1792]{1,0:T(8,128)}, f32[64,1792]{1,0:T(8,128)}, u32[]{:S(2)}, u32[]{:S(2)}) collective-permute-start(f32[64,1792]{1,0:T(8,128)} %get-tuple-element.83), channel_id=1, source_target_pairs={{0,8},{8,0},{16,24},{24,16},{32,40},{40,32},{48,56},{56,48},{64,72... | collective-permute-start | bytes 1376264 | tf_op jit(solution)/shard_map/ppermute | solution.py:51
  82.9 2.6 all-to-all-done.2
  90.5 10.2 %all-to-all-start.3 = ((f32[32,16,128]{2,1,0:T(8,128)}), f32[32,16,128]{2,1,0:T(8,128)S(1)}, u32[]{:S(2)}, u32[]{:S(2)}) async-start(f32[32,16,128]{2,1,0:T(8,128)} %fusion.31), calls=%async_computation.3 | async-start | bytes 524288 | tf_op jit(solution)/shard_map/all_to_all | solution.py:20
  100.7 2.6 fusion.30
  104.4 8.1 %all-to-all-done.3 = f32[32,16,128]{2,1,0:T(8,128)S(1)} async-done(((f32[32,16,128]{2,1,0:T(8,128)}), f32[32,16,128]{2,1,0:T(8,128)S(1)}, u32[]{:S(2)}, u32[]{:S(2)}) %all-to-all-start.3) | async-done | bytes 262176 | tf_op jit(solution)/shard_map/all_to_all | solution.py:20
  113.2 6.4 %all-to-all-start.4 = ((f32[32,16,128]{2,1,0:T(8,128)}), f32[32,16,128]{2,1,0:T(8,128)S(1)}, u32[]{:S(2)}, u32[]{:S(2)}) async-start(f32[32,16,128]{2,1,0:T(8,128)} %broadcast_in_dim.23), calls=%async_computation.4 | async-start | bytes 524288 | tf_op jit(solution)/shard_map/all_to_all | solution.py:20
  121.5 9.6 %all-to-all-done.4 = f32[32,16,128]{2,1,0:T(8,128)S(1)} async-done(((f32[32,16,128]{2,1,0:T(8,128)}), f32[32,16,128]{2,1,0:T(8,128)S(1)}, u32[]{:S(2)}, u32[]{:S(2)}) %all-to-all-start.4) | async-done | bytes 262176 | tf_op jit(solution)/shard_map/all_to_all | solution.py:20
  132.4 6.8 %all-to-all-start.5 = ((f32[8,128,128]{2,1,0:T(8,128)}), f32[8,128,128]{2,1,0:T(8,128)S(1)}, u32[]{:S(2)}, u32[]{:S(2)}) async-start(f32[8,128,128]{2,1,0:T(8,128)} %broadcast_in_dim.24), calls=%async_computation.5 | async-start | bytes 1048576 | tf_op jit(solution)/shard_map/all_to_all | solution.py:20
  139.3 9.4 %all-to-all-done.5 = f32[8,128,128]{2,1,0:T(8,128)S(1)} async-done(((f32[8,128,128]{2,1,0:T(8,128)}), f32[8,128,128]{2,1,0:T(8,128)S(1)}, u32[]{:S(2)}, u32[]{:S(2)}) %all-to-all-start.5) | async-done | bytes 524320 | tf_op jit(solution)/shard_map/all_to_all | solution.py:20
  149.8 4.6 %all-to-all-start.6 = ((f32[32,16,128]{2,1,0:T(8,128)}), f32[32,16,128]{2,1,0:T(8,128)S(1)}, u32[]{:S(2)}, u32[]{:S(2)}) async-start(f32[32,16,128]{2,1,0:T(8,128)} %fusion.19), calls=%async_computation.6 | async-start | bytes 524288 | tf_op jit(solution)/shard_map/all_to_all | solution.py:20
  154.5 2.6 collective-permute-start.2
  157.1 11.7 %collective-permute-done.2 = f32[512,128]{1,0:T(8,128)S(1)} collective-permute-done((f32[512,128]{1,0:T(8,128)S(1)}, f32[512,128]{1,0:T(8,128)S(1)}, u32[]{:S(2)}, u32[]{:S(2)}) %collective-permute-start.2) | collective-permute-done | bytes 262176 | tf_op jit(solution)/shard_map/ppermute | solution.py:51
  169.5 10.4 %all-to-all-start.7 = ((f32[32,16,128]{2,1,0:T(8,128)}), f32[32,16,128]{2,1,0:T(8,128)S(1)}, u32[]{:S(2)}, u32[]{:S(2)}) async-start(f32[32,16,128]{2,1,0:T(8,128)} %broadcast_in_dim.25), calls=%async_computation.7 | async-start | bytes 524288 | tf_op jit(solution)/shard_map/all_to_all | solution.py:20
  182.3 1.7 convolution_add_fusion.2
  184.1 8.1 %all-to-all-done.7 = f32[32,16,128]{2,1,0:T(8,128)S(1)} async-done(((f32[32,16,128]{2,1,0:T(8,128)}), f32[32,16,128]{2,1,0:T(8,128)S(1)}, u32[]{:S(2)}, u32[]{:S(2)}) %all-to-all-start.7) | async-done | bytes 262176 | tf_op jit(solution)/shard_map/all_to_all | solution.py:20
  193.4 5.6 %all-to-all-start.8 = ((f32[8,128,128]{2,1,0:T(8,128)}), f32[8,128,128]{2,1,0:T(8,128)S(1)}, u32[]{:S(2)}, u32[]{:S(2)}) async-start(f32[8,128,128]{2,1,0:T(8,128)} %broadcast_in_dim.26), calls=%async_computation.8 | async-start | bytes 1048576 | tf_op jit(solution)/shard_map/all_to_all | solution.py:20
  199.1 9.4 %all-to-all-done.8 = f32[8,128,128]{2,1,0:T(8,128)S(1)} async-done(((f32[8,128,128]{2,1,0:T(8,128)}), f32[8,128,128]{2,1,0:T(8,128)S(1)}, u32[]{:S(2)}, u32[]{:S(2)}) %all-to-all-start.8) | async-done | bytes 524320 | tf_op jit(solution)/shard_map/all_to_all | solution.py:20
  209.6 4.9 %all-to-all-start.9 = ((f32[32,16,128]{2,1,0:T(8,128)}), f32[32,16,128]{2,1,0:T(8,128)S(1)}, u32[]{:S(2)}, u32[]{:S(2)}) async-start(f32[32,16,128]{2,1,0:T(8,128)} %fusion.17), calls=%async_computation.9 | async-start | bytes 524288 | tf_op jit(solution)/shard_map/all_to_all | solution.py:20
  214.5 2.6 collective-permute-start.3
  217.5 11.4 %collective-permute-done.3 = f32[512,128]{1,0:T(8,128)} collective-permute-done((f32[512,128]{1,0:T(8,128)S(1)}, f32[512,128]{1,0:T(8,128)}, u32[]{:S(2)}, u32[]{:S(2)}) %collective-permute-start.3) | collective-permute-done | bytes 262176 | tf_op jit(solution)/shard_map/ppermute | solution.py:51
  229.7 10.9 %all-to-all-start.10 = ((f32[64,16,128]{2,1,0:T(8,128)}), f32[64,16,128]{2,1,0:T(8,128)S(1)}, u32[]{:S(2)}, u32[]{:S(2)}) async-start(f32[64,16,128]{2,1,0:T(8,128)} %broadcast_in_dim.27), calls=%async_computation.10 | async-start | bytes 1048576 | tf_op jit(solution)/shard_map/all_to_all | solution.py:20
  243.6 13.6 %all-to-all-done.10 = f32[64,16,128]{2,1,0:T(8,128)S(1)} async-done(((f32[64,16,128]{2,1,0:T(8,128)}), f32[64,16,128]{2,1,0:T(8,128)S(1)}, u32[]{:S(2)}, u32[]{:S(2)}) %all-to-all-start.10) | async-done | bytes 524320 | tf_op jit(solution)/shard_map/all_to_all | solution.py:20
  257.5 1.7 convolution_add_fusion
  259.2 6.8 %all-to-all-start.11 = ((f32[8,32,256]{2,1,0:T(8,128)}), f32[8,32,256]{2,1,0:T(8,128)S(1)}, u32[]{:S(2)}, u32[]{:S(2)}) async-start(f32[8,32,256]{2,1,0:T(8,128)} %bitcast.48), calls=%async_computation.11 | async-start | bytes 524288 | tf_op jit(solution)/shard_map/all_to_all | solution.py:20
  266.9 5.6 %all-to-all-done.11 = f32[8,32,256]{2,1,0:T(8,128)S(1)} async-done(((f32[8,32,256]{2,1,0:T(8,128)}), f32[8,32,256]{2,1,0:T(8,128)S(1)}, u32[]{:S(2)}, u32[]{:S(2)}) %all-to-all-start.11) | async-done | bytes 262176 | tf_op jit(solution)/shard_map/all_to_all | solution.py:20
  (99 shorter events, 30.9 us)
Async XLA Ops:
  0.6 20.6 %copy-start.10 = (f32[4,512,64]{1,2,0:T(8,128)S(1)}, f32[4,512,64]{1,2,0:T(8,128)}, u32[]{:S(2)}) copy-start(f32[4,512,64]{1,2,0:T(8,128)} %param.5) | copy-start | bytes 1572868
  4.0 42.4 %copy-start.8 = (f32[6,64,512]{2,1,0:T(8,128)S(1)}, f32[6,64,512]{2,1,0:T(8,128)}, u32[]{:S(2)}) copy-start(f32[6,64,512]{2,1,0:T(8,128)} %param.6) | copy-start | bytes 2359300
  4.0 33.6 %all-to-all-start = ((f32[64,8,256]{2,1,0:T(8,128)}), f32[64,8,256]{2,1,0:T(8,128)S(1)}, u32[]{:S(2)}, u32[]{:S(2)}) async-start(f32[64,8,256]{2,1,0:T(8,128)} %fusion.8), calls=%async_computation | async-start | bytes 1048576 | tf_op jit(solution)/shard_map/all_to_all | solution.py:20
  21.3 47.8 %copy-start.9 = (f32[8,64,256]{2,1,0:T(8,128)S(1)}, f32[8,64,256]{2,1,0:T(8,128)}, u32[]{:S(2)}) copy-start(f32[8,64,256]{2,1,0:T(8,128)} %param.4) | copy-start | bytes 1572868
  38.5 30.6 %all-to-all-start.1 = ((f32[64,8,256]{2,1,0:T(8,128)}), f32[64,8,256]{2,1,0:T(8,128)S(1)}, u32[]{:S(2)}, u32[]{:S(2)}) async-start(f32[64,8,256]{2,1,0:T(8,128)} %broadcast_in_dim.21), calls=%async_computation.1 | async-start | bytes 1048576 | tf_op jit(solution)/shard_map/all_to_all | solution.py:20
  46.4 22.7 %collective-permute-start = (f32[3,64,512]{2,1,0:T(8,128)S(1)}, f32[3,64,512]{2,1,0:T(8,128)S(1)}, u32[]{:S(2)}, u32[]{:S(2)}) collective-permute-start(f32[3,64,512]{2,1,0:T(8,128)S(1)} %slice.109), channel_id=1, source_target_pairs={{0,8},{8,0},{16,24},{24,16},{32,40},{40,32},{48,56},{56,48},{64,72... | collective-permute-start | bytes 1179656 | tf_op jit(solution)/shard_map/ppermute | solution.py:51
  70.4 15.0 %all-to-all-start.2 = ((f32[16,64,128]{2,1,0:T(8,128)}), f32[16,64,128]{2,1,0:T(8,128)S(1)}, u32[]{:S(2)}, u32[]{:S(2)}) async-start(f32[16,64,128]{2,1,0:T(8,128)} %bitcast.12), calls=%async_computation.2 | async-start | bytes 1048576 | tf_op jit(solution)/shard_map/all_to_all | solution.py:20
  79.4 24.9 %collective-permute-start.1 = (f32[64,1792]{1,0:T(8,128)}, f32[64,1792]{1,0:T(8,128)}, u32[]{:S(2)}, u32[]{:S(2)}) collective-permute-start(f32[64,1792]{1,0:T(8,128)} %get-tuple-element.83), channel_id=1, source_target_pairs={{0,8},{8,0},{16,24},{24,16},{32,40},{40,32},{48,56},{56,48},{64,72... | collective-permute-start | bytes 1376264 | tf_op jit(solution)/shard_map/ppermute | solution.py:51
  85.4 0.8 copy-start.1
  87.2 13.6 %copy-start = (f32[4,64,4,512]{3,2,1,0:T(4,128)S(1)}, f32[4,64,4,512]{3,2,1,0:T(4,128)}, u32[]{:S(2)}) copy-start(f32[4,64,4,512]{3,2,1,0:T(4,128)} %param.7) | copy-start | bytes 6291460
  90.5 21.9 %all-to-all-start.3 = ((f32[32,16,128]{2,1,0:T(8,128)}), f32[32,16,128]{2,1,0:T(8,128)S(1)}, u32[]{:S(2)}, u32[]{:S(2)}) async-start(f32[32,16,128]{2,1,0:T(8,128)} %fusion.31), calls=%async_computation.3 | async-start | bytes 524288 | tf_op jit(solution)/shard_map/all_to_all | solution.py:20
  113.2 18.0 %all-to-all-start.4 = ((f32[32,16,128]{2,1,0:T(8,128)}), f32[32,16,128]{2,1,0:T(8,128)S(1)}, u32[]{:S(2)}, u32[]{:S(2)}) async-start(f32[32,16,128]{2,1,0:T(8,128)} %broadcast_in_dim.23), calls=%async_computation.4 | async-start | bytes 524288 | tf_op jit(solution)/shard_map/all_to_all | solution.py:20
  120.7 18.5 %copy-start.6 = (f32[512,128]{0,1:T(8,128)S(1)}, f32[512,128]{0,1:T(8,128)}, u32[]{:S(2)}) copy-start(f32[512,128]{0,1:T(8,128)} %get-tuple-element.74) | copy-start | bytes 786436
  131.5 25.5 %copy-start.4 = (f32[4,64,1,512]{3,2,1,0:T(1,128)S(1)}, f32[4,64,1,512]{3,2,1,0:T(1,128)}, u32[]{:S(2)}) copy-start(f32[4,64,1,512]{3,2,1,0:T(1,128)} %get-tuple-element.64) | copy-start | bytes 1572868
  132.4 16.3 %all-to-all-start.5 = ((f32[8,128,128]{2,1,0:T(8,128)}), f32[8,128,128]{2,1,0:T(8,128)S(1)}, u32[]{:S(2)}, u32[]{:S(2)}) async-start(f32[8,128,128]{2,1,0:T(8,128)} %broadcast_in_dim.24), calls=%async_computation.5 | async-start | bytes 1048576 | tf_op jit(solution)/shard_map/all_to_all | solution.py:20
  149.8 18.9 %all-to-all-start.6 = ((f32[32,16,128]{2,1,0:T(8,128)}), f32[32,16,128]{2,1,0:T(8,128)S(1)}, u32[]{:S(2)}, u32[]{:S(2)}) async-start(f32[32,16,128]{2,1,0:T(8,128)} %fusion.19), calls=%async_computation.6 | async-start | bytes 524288 | tf_op jit(solution)/shard_map/all_to_all | solution.py:20
  154.5 14.3 %collective-permute-start.2 = (f32[512,128]{1,0:T(8,128)S(1)}, f32[512,128]{1,0:T(8,128)S(1)}, u32[]{:S(2)}, u32[]{:S(2)}) collective-permute-start(f32[512,128]{1,0:T(8,128)S(1)} %bitcast.132), channel_id=1, source_target_pairs={{0,8},{8,0},{16,24},{24,16},{32,40},{40,32},{48,56},{56,48},{64,72... | collective-permute-start | bytes 786440 | tf_op jit(solution)/shard_map/ppermute | solution.py:51
  168.7 11.2 %copy-start.11 = (f32[512,128]{1,0:T(8,128)}, f32[512,128]{1,0:T(8,128)S(1)}, u32[]{:S(2)}) copy-start(f32[512,128]{1,0:T(8,128)S(1)} %collective-permute-done.2) | copy-start | bytes 786436
  169.5 22.7 %all-to-all-start.7 = ((f32[32,16,128]{2,1,0:T(8,128)}), f32[32,16,128]{2,1,0:T(8,128)S(1)}, u32[]{:S(2)}, u32[]{:S(2)}) async-start(f32[32,16,128]{2,1,0:T(8,128)} %broadcast_in_dim.25), calls=%async_computation.7 | async-start | bytes 524288 | tf_op jit(solution)/shard_map/all_to_all | solution.py:20
  182.3 16.7 %copy-start.5 = (f32[512,128]{0,1:T(8,128)S(1)}, f32[512,128]{0,1:T(8,128)}, u32[]{:S(2)}) copy-start(f32[512,128]{0,1:T(8,128)} %get-tuple-element.75) | copy-start | bytes 786436
  193.4 15.1 %all-to-all-start.8 = ((f32[8,128,128]{2,1,0:T(8,128)}), f32[8,128,128]{2,1,0:T(8,128)S(1)}, u32[]{:S(2)}, u32[]{:S(2)}) async-start(f32[8,128,128]{2,1,0:T(8,128)} %broadcast_in_dim.26), calls=%async_computation.8 | async-start | bytes 1048576 | tf_op jit(solution)/shard_map/all_to_all | solution.py:20
  209.6 31.1 %copy-start.3 = (f32[4,64,1,512]{3,2,1,0:T(1,128)S(1)}, f32[4,64,1,512]{3,2,1,0:T(1,128)}, u32[]{:S(2)}) copy-start(f32[4,64,1,512]{3,2,1,0:T(1,128)} %get-tuple-element.63) | copy-start | bytes 1572868
  209.6 19.3 %all-to-all-start.9 = ((f32[32,16,128]{2,1,0:T(8,128)}), f32[32,16,128]{2,1,0:T(8,128)S(1)}, u32[]{:S(2)}, u32[]{:S(2)}) async-start(f32[32,16,128]{2,1,0:T(8,128)} %fusion.17), calls=%async_computation.9 | async-start | bytes 524288 | tf_op jit(solution)/shard_map/all_to_all | solution.py:20
  214.5 14.4 %collective-permute-start.3 = (f32[512,128]{1,0:T(8,128)S(1)}, f32[512,128]{1,0:T(8,128)}, u32[]{:S(2)}, u32[]{:S(2)}) collective-permute-start(f32[512,128]{1,0:T(8,128)S(1)} %bitcast.135), channel_id=1, source_target_pairs={{0,8},{8,0},{16,24},{24,16},{32,40},{40,32},{48,56},{56,48},{64,72... | collective-permute-start | bytes 786440 | tf_op jit(solution)/shard_map/ppermute | solution.py:51
  217.5 23.3 %slice-start = ((f32[8,64,256]{2,1,0:T(8,128)}), f32[4,64,256]{2,1,0:T(8,128)S(1)}, s32[]{:S(2)}) async-start(f32[8,64,256]{2,1,0:T(8,128)} %param.4), calls=%async_computation.12 | async-start | bytes 524288 | tf_op jit(solution)/shard_map/slice | solution.py:149
  217.5 23.5 %copy-start.2 = (f32[4,64,1,512]{3,2,1,0:T(1,128)S(1)}, f32[4,64,1,512]{3,2,1,0:T(1,128)}, u32[]{:S(2)}) copy-start(f32[4,64,1,512]{3,2,1,0:T(1,128)} %get-tuple-element.62) | copy-start | bytes 1572868
  229.7 27.5 %all-to-all-start.10 = ((f32[64,16,128]{2,1,0:T(8,128)}), f32[64,16,128]{2,1,0:T(8,128)S(1)}, u32[]{:S(2)}, u32[]{:S(2)}) async-start(f32[64,16,128]{2,1,0:T(8,128)} %broadcast_in_dim.27), calls=%async_computation.10 | async-start | bytes 1048576 | tf_op jit(solution)/shard_map/all_to_all | solution.py:20
  240.7 1.8 copy-start.7
  259.2 13.3 %all-to-all-start.11 = ((f32[8,32,256]{2,1,0:T(8,128)}), f32[8,32,256]{2,1,0:T(8,128)S(1)}, u32[]{:S(2)}, u32[]{:S(2)}) async-start(f32[8,32,256]{2,1,0:T(8,128)} %bitcast.48), calls=%async_computation.11 | async-start | bytes 524288 | tf_op jit(solution)/shard_map/all_to_all | solution.py:20

commit v11 on v10

--- a/solution.py
+++ b/solution.py
@@ -71,7 +71,7 @@
         return swap(copies(parts.sum(0), row_size), "row")
 
     def summed(update):
-        return swap(copies(update, col_size), "col").sum(0)
+        return swap(copies(update, col_size), "col")
 
     def own_term(block_row):
         return jnp.where(col == 0, right_sides[block_row], 0.0)
@@ -84,6 +84,11 @@
     def below_of(whole, block_row):
         return contract(whole, trail[block_row], (0, 1))
 
+    own_width = column_count // col_size
+    own_below = lax.dynamic_slice_in_dim(
+        right_sides[step_count:].transpose(0, 2, 1), col * own_width, own_width, 1
+    )
+
     out_width = column_count // row_size
 
     def out_of(whole):
@@ -91,40 +96,35 @@
 
     local_term = contract(own_diag[0], right_sides[0], (0, 0))
     parts = swap(local_term.reshape(row_size, width // row_size, column_count), "row")
-    part, own_later = lax.optimization_barrier((parts.sum(0), own_diag[1:]))
-    parts = swap(copies(part, row_size), "row")
-    parts, got_later = by_deadline(parts, from_partner(own_later))
+    own_later = jnp.concatenate([own_diag[1:], lower_blocks[2:3], lower_blocks[4:]])
+    got_later = from_partner(own_later)
+    parts = swap(copies(parts.sum(0), row_size), "row")
+    parts, got_later = by_deadline(parts, got_later)
+    pair = ordered(own_later, got_later, 1)
+    diag_1, diag_2, diag_3, lower_21, lower_31, lower_32 = [pair[i] for i in range(6)]
     whole_0 = parts.reshape(width, column_count)
 
     term = own_term(1) - contract(lower_blocks[0], whole_0, (1, 0))
     parts = jnp.stack([term[:, :half], term[:, half:]])[:, None]
     parts = jnp.broadcast_to(parts, (2, col_size, local_rows, half))
     parts = swap(parts.reshape(2 * col_size, local_rows, half), ("row", "col"), pair_groups)
-    diag = ordered(own_later, got_later, 1)
     term_2 = own_term(2) - contract(lower_blocks[1], whole_0, (1, 0))
     term_3 = own_term(3) - contract(lower_blocks[3], whole_0, (1, 0))
-    shared = [lower_blocks[2], lower_blocks[4], lower_blocks[5]]
-    sent = shared + [half_of(term_2, row % 2 ^ 1), half_of(term_3, row % 2 ^ 1)]
-    kept = jnp.concatenate(shared + [half_of(term_2, row % 2), half_of(term_3, row % 2)], 1)
-    got = from_partner(jnp.concatenate(sent, 1))
-    parts, diag = by_deadline(parts, diag)
+    terms = jnp.stack([term_2, term_3])
+    got_terms = from_partner(half_of(terms, row % 2 ^ 1))
     current = parts.reshape(2, col_size, local_rows, half).sum(1).reshape(2 * local_rows, half)
-    parts = scattered(diag[0], current)
-    parts, got = by_deadline(parts, got)
+    parts = scattered(diag_1, current)
+    parts, got_terms = by_deadline(parts, got_terms)
     parts = gathered(parts)
-    pair = ordered(kept, got, 0)
-    lower_21, lower_31, lower_32 = [pair[:, i * width : (i + 1) * width] for i in range(3)]
-    term_2 = pair[:, 3 * width : 3 * width + half]
-    term_3 = pair[:, 3 * width + half :]
+    terms = ordered(half_of(terms, row % 2), got_terms, 1)
     below = below_of(whole_0, 0)
-    parts, lower_21, lower_31, lower_32, term_2, term_3, below = by_deadline(
-        parts, lower_21, lower_31, lower_32, term_2, term_3, below
-    )
+    parts, terms, below, trail = by_deadline(parts, terms, below, trail)
+    term_2, term_3 = terms[0], terms[1]
     solved_1 = parts.reshape(width, half)
 
-    current = summed(term_2 - contract(lower_21, solved_1, (1, 0)))
-    parts = scattered(diag[1], current)
+    parts = summed(term_2 - contract(lower_21, solved_1, (1, 0)))
     parts, got_1 = by_deadline(parts, from_partner(solved_1))
+    parts = scattered(diag_2, parts.sum(0))
     parts = gathered(parts)
     whole_1 = ordered(solved_1, got_1, 1)
     term_3 = term_3 - contract(lower_31, solved_1, (1, 0))
@@ -132,10 +132,11 @@
     parts, term_3, below = by_deadline(parts, term_3, below)
     solved_2 = parts.reshape(width, half)
 
-    current = summed(term_3 - contract(lower_32, solved_2, (1, 0)))
-    parts = scattered(diag[2], current)
+    parts = summed(term_3 - contract(lower_32, solved_2, (1, 0)))
+    parts, got_2 = by_deadline(parts, from_partner(solved_2))
+    parts = scattered(diag_3, parts.sum(0))
     outs = [out_of(whole_0), out_of(whole_1)]
-    parts, got_2, outs = by_deadline(parts, from_partner(solved_2), outs)
+    parts, outs = by_deadline(parts, outs)
     parts = gathered_whole(parts)
     whole_2 = ordered(solved_2, got_2, 1)
     below = below + below_of(whole_2, 2)
@@ -143,11 +144,9 @@
     whole_3 = halves_whole(parts)
 
     below = below + below_of(whole_3, 3)
-    own_width = column_count // col_size
     shared = swap(below, "col").reshape(col_size, own_width, -1).sum(0)
-    shared = shared.reshape(own_width, trail_count, local_rows).transpose(1, 2, 0)
-    own_below = lax.dynamic_slice_in_dim(right_sides[step_count:], col * own_width, own_width, 2)
-    trail_rest = own_below - shared
+    shared = shared.reshape(own_width, trail_count, local_rows).transpose(1, 0, 2)
+    trail_rest = (own_below - shared).transpose(0, 2, 1)
     return (jnp.stack(outs + [out_of(whole_2), out_of(whole_3)]), trail_rest)
 
 

time: 275 us -> 277 us (level)
  blocking collectives: 0 us -> 49.4 us
  waiting for transfers between devices: 125 us -> 94.2 us
  starting transfers between devices: 108 us -> 85.8 us
  local copies, waits for them, and re-layouts: 16.8 us -> 21.8 us
    all_to_all x0 -> x2, blocking collectives: none -> 49.4 us  [swap(): lax.all_to_all(parts, axis, 0, 0, axis_index_groups=groups, tiled=True)]
    all_to_all x12 -> x10, waiting for transfers between devices: 82.7 us -> 52.8 us  [swap(): lax.all_to_all(parts, axis, 0, 0, axis_index_groups=groups, tiled=True)]
    all_to_all x12 -> x10, starting transfers between devices: 96.9 us -> 74.8 us  [swap(): lax.all_to_all(parts, axis, 0, 0, axis_index_groups=groups, tiled=True)]
    slice x1, local copies, waits for them, and re-layouts: 2.6 us -> 6.83 us  [shards(): trail_panel[:, :, j, :].reshape(trail_count * local_rows, width)]
    unnamed x37 -> x33, local copies, waits for them, and re-layouts: 3.2 us -> 5.98 us
  transfers between devices with their start and end apart: 16 -> 14, of which waited for: 12 -> 9; matrix products, arithmetic and copies ran while one was open for 8% -> 10% of each run, Pallas kernels for 0% -> 0%
where the time goes in v11:
time: 277 us; the launch traced here: 276 us
  waiting for transfers between devices  94.2 us (34%)
  starting transfers between devices  85.8 us (31%)
  blocking collectives  49.4 us (18%)
  local copies, waits for them, and re-layouts  21.8 us (8%)
  matrix products  15.9 us (6%)
  other arithmetic  7.7 us (3%)
    all_to_all x10, starting transfers between devices, swap(): lax.all_to_all(parts, axis, 0, 0, axis_index_groups=groups, tiled=True)  74.8 us
    all_to_all x10, waiting for transfers between devices, swap(): lax.all_to_all(parts, axis, 0, 0, axis_index_groups=groups, tiled=True)  52.8 us
    all_to_all x2, blocking collectives, swap(): lax.all_to_all(parts, axis, 0, 0, axis_index_groups=groups, tiled=True)  49.4 us
    ppermute x4, waiting for transfers between devices, from_partner(): return lax.ppermute(value, 'row', [(r, r ^ 1) for r in range(row_size)])  41.4 us
    dot_general x14, matrix products, contract(): lax.dot_general(left, right, (((axes[0],), (axes[1],)), ((), ())), precis...  15.9 us
    ppermute x4, starting transfers between devices, from_partner(): return lax.ppermute(value, 'row', [(r, r ^ 1) for r in range(row_size)])  11 us
    slice x1, local copies, waits for them, and re-layouts, shards(): trail_panel[:, :, j, :].reshape(trail_count * local_rows, width)  6.83 us
    unnamed x33, local copies, waits for them, and re-layouts  5.98 us
  transfers between devices with their start and end apart: 14, of which 9 were waited for; matrix products, arithmetic and copies ran while one was open for 10% of the time, Pallas kernels for 0%

profile of v11, /device:TPU:1, one launch (start us, length us, event | category | flops | bytes accessed | tf_op | source)
XLA Modules:
  0.0 275.8 jit_solution(3123418351016446615)
XLA Ops:
  1.7 1.4 fusion.22
  3.1 33.4 %all_to_all.64 = f32[64,8,256]{2,1,0:T(8,128)S(1)} all-to-all(f32[64,8,256]{2,1,0:T(8,128)S(1)} %fusion.22), channel_id=1, replica_groups=mesh['row'=64,'col'=8] {'row'}, dimensions={0} | all-to-all | bytes 1048576 | tf_op jit(solution)/shard_map/all_to_all | solution.py:20
  37.4 7.8 %all-to-all-start.1 = ((f32[64,8,256]{2,1,0:T(8,128)}), f32[64,8,256]{2,1,0:T(8,128)S(1)}, u32[]{:S(2)}, u32[]{:S(2)}) async-start(f32[64,8,256]{2,1,0:T(8,128)} %broadcast_in_dim.20), calls=%async_computation.1 | async-start | bytes 1048576 | tf_op jit(solution)/shard_map/all_to_all | solution.py:20
  45.4 2.9 %collective-permute-start = (f32[6,64,512]{2,1,0:T(8,128)S(1)}, f32[6,64,512]{2,1,0:T(8,128)}, u32[]{:S(2)}, u32[]{:S(2)}) collective-permute-start(f32[6,64,512]{2,1,0:T(8,128)S(1)} %pad_maximum_fusion), channel_id=1, source_target_pairs={{0,8},{8,0},{16,24},{24,16},{32,40},{40,32},{48,56},{56,48},{64,72... | collective-permute-start | bytes 2359304 | tf_op jit(solution)/shard_map/ppermute | solution.py:51
  48.4 28.2 %collective-permute-done = f32[6,64,512]{2,1,0:T(8,128)} collective-permute-done((f32[6,64,512]{2,1,0:T(8,128)S(1)}, f32[6,64,512]{2,1,0:T(8,128)}, u32[]{:S(2)}, u32[]{:S(2)}) %collective-permute-start) | collective-permute-done | bytes 786464 | tf_op jit(solution)/shard_map/ppermute | solution.py:51
  77.9 5.2 %all-to-all-start.2 = ((f32[16,64,128]{2,1,0:T(8,128)}), f32[16,64,128]{2,1,0:T(8,128)S(1)}, u32[]{:S(2)}, u32[]{:S(2)}) async-start(f32[16,64,128]{2,1,0:T(8,128)} %bitcast.21), calls=%async_computation.2 | async-start | bytes 1048576 | tf_op jit(solution)/shard_map/all_to_all | solution.py:20
  83.1 1.4 broadcast_select_fusion
  88.0 4.9 %all-to-all-done.2 = f32[16,64,128]{2,1,0:T(8,128)S(1)} async-done(((f32[16,64,128]{2,1,0:T(8,128)}), f32[16,64,128]{2,1,0:T(8,128)S(1)}, u32[]{:S(2)}, u32[]{:S(2)}) %all-to-all-start.2) | async-done | bytes 524320 | tf_op jit(solution)/shard_map/all_to_all | solution.py:20
  94.0 10.3 %all-to-all-start.3 = ((f32[32,16,128]{2,1,0:T(8,128)}), f32[32,16,128]{2,1,0:T(8,128)}, u32[]{:S(2)}, u32[]{:S(2)}) async-start(f32[32,16,128]{2,1,0:T(8,128)} %fusion.49), calls=%async_computation.3 | async-start | bytes 524288 | tf_op jit(solution)/shard_map/all_to_all | solution.py:20
  104.9 2.6 collective-permute-start.1
  107.6 6.8 %fusion.48 = (f32[4,64,1,512]{3,2,1,0:T(1,128)S(1)}, f32[4,64,1,512]{3,2,1,0:T(1,128)}, f32[4,64,1,512]{3,2,1,0:T(1,128)}, f32[4,64,1,512]{3,2,1,0:T(1,128)}) fusion(f32[4,64,4,512]{3,2,1,0:T(4,128)} %param.7), kind=kLoop, calls=%fused_computation.96 | loop fusion | bytes 4194304 | tf_op jit(solution)/shard_map/slice | solution.py:81
  115.5 1.9 copy.67
  120.8 11.5 %all-to-all-start.4 = ((f32[32,16,128]{2,1,0:T(8,128)}), f32[32,16,128]{2,1,0:T(8,128)S(1)}, u32[]{:S(2)}, u32[]{:S(2)}) async-start(f32[32,16,128]{2,1,0:T(8,128)} %broadcast_in_dim.23), calls=%async_computation.4 | async-start | bytes 524288 | tf_op jit(solution)/shard_map/all_to_all | solution.py:20
  132.4 1.7 fusion.43
  134.9 9.2 %all-to-all-done.4 = f32[32,16,128]{2,1,0:T(8,128)S(1)} async-done(((f32[32,16,128]{2,1,0:T(8,128)}), f32[32,16,128]{2,1,0:T(8,128)S(1)}, u32[]{:S(2)}, u32[]{:S(2)}) %all-to-all-start.4) | async-done | bytes 262176 | tf_op jit(solution)/shard_map/all_to_all | solution.py:20
  145.4 6.7 %all-to-all-start.5 = ((f32[8,128,128]{2,1,0:T(8,128)}), f32[8,128,128]{2,1,0:T(8,128)S(1)}, u32[]{:S(2)}, u32[]{:S(2)}) async-start(f32[8,128,128]{2,1,0:T(8,128)} %broadcast_in_dim.24), calls=%async_computation.5 | async-start | bytes 1048576 | tf_op jit(solution)/shard_map/all_to_all | solution.py:20
  152.1 2.8 %collective-permute-start.2 = (f32[512,128]{1,0:T(8,128)S(1)}, f32[512,128]{1,0:T(8,128)}, u32[]{:S(2)}, u32[]{:S(2)}) collective-permute-start(f32[512,128]{1,0:T(8,128)S(1)} %bitcast.141), channel_id=1, source_target_pairs={{0,8},{8,0},{16,24},{24,16},{32,40},{40,32},{48,56},{56,48},{64,72... | collective-permute-start | bytes 786440 | tf_op jit(solution)/shard_map/ppermute | solution.py:51
  155.8 6.1 %collective-permute-done.2 = f32[512,128]{1,0:T(8,128)} collective-permute-done((f32[512,128]{1,0:T(8,128)S(1)}, f32[512,128]{1,0:T(8,128)}, u32[]{:S(2)}, u32[]{:S(2)}) %collective-permute-start.2) | collective-permute-done | bytes 262176 | tf_op jit(solution)/shard_map/ppermute | solution.py:51
  163.8 16.0 %all_to_all.65 = f32[32,16,128]{2,1,0:T(8,128)S(1)} all-to-all(f32[32,16,128]{2,1,0:T(8,128)S(1)} %fusion.34), channel_id=1, replica_groups={{0,16,32,48,64,80,96,112,128,144,160,176,192,208,224,240,256,272,288,30..., dimensions={0} | all-to-all | bytes 524288 | tf_op jit(solution)/shard_map/all_to_all | solution.py:20
  180.6 6.6 %all-to-all-start.7 = ((f32[32,16,128]{2,1,0:T(8,128)}), f32[32,16,128]{2,1,0:T(8,128)S(1)}, u32[]{:S(2)}, u32[]{:S(2)}) async-start(f32[32,16,128]{2,1,0:T(8,128)} %broadcast_in_dim.25), calls=%async_computation.7 | async-start | bytes 524288 | tf_op jit(solution)/shard_map/all_to_all | solution.py:20
  189.2 1.7 convolution_add_fusion.2
  190.9 7.7 %all-to-all-done.7 = f32[32,16,128]{2,1,0:T(8,128)S(1)} async-done(((f32[32,16,128]{2,1,0:T(8,128)}), f32[32,16,128]{2,1,0:T(8,128)S(1)}, u32[]{:S(2)}, u32[]{:S(2)}) %all-to-all-start.7) | async-done | bytes 262176 | tf_op jit(solution)/shard_map/all_to_all | solution.py:20
  199.9 7.3 %all-to-all-start.8 = ((f32[8,128,128]{2,1,0:T(8,128)}), f32[8,128,128]{2,1,0:T(8,128)S(1)}, u32[]{:S(2)}, u32[]{:S(2)}) async-start(f32[8,128,128]{2,1,0:T(8,128)} %broadcast_in_dim.26), calls=%async_computation.8 | async-start | bytes 1048576 | tf_op jit(solution)/shard_map/all_to_all | solution.py:20
  207.2 2.5 collective-permute-start.3
  209.9 7.1 %collective-permute-done.3 = f32[512,128]{1,0:T(8,128)S(1)} collective-permute-done((f32[512,128]{1,0:T(8,128)S(1)}, f32[512,128]{1,0:T(8,128)S(1)}, u32[]{:S(2)}, u32[]{:S(2)}) %collective-permute-start.3) | collective-permute-done | bytes 262176 | tf_op jit(solution)/shard_map/ppermute | solution.py:51
  218.1 4.4 %all-to-all-start.9 = ((f32[32,16,128]{2,1,0:T(8,128)}), f32[32,16,128]{2,1,0:T(8,128)S(1)}, u32[]{:S(2)}, u32[]{:S(2)}) async-start(f32[32,16,128]{2,1,0:T(8,128)} %fusion.32), calls=%async_computation.9 | async-start | bytes 524288 | tf_op jit(solution)/shard_map/all_to_all | solution.py:20
  222.9 11.8 %all-to-all-done.9 = f32[32,16,128]{2,1,0:T(8,128)S(1)} async-done(((f32[32,16,128]{2,1,0:T(8,128)}), f32[32,16,128]{2,1,0:T(8,128)S(1)}, u32[]{:S(2)}, u32[]{:S(2)}) %all-to-all-start.9) | async-done | bytes 262176 | tf_op jit(solution)/shard_map/all_to_all | solution.py:20
  235.5 7.0 %all-to-all-start.10 = ((f32[64,16,128]{2,1,0:T(8,128)}), f32[64,16,128]{2,1,0:T(8,128)S(1)}, u32[]{:S(2)}, u32[]{:S(2)}) async-start(f32[64,16,128]{2,1,0:T(8,128)} %broadcast_in_dim.27), calls=%async_computation.10 | async-start | bytes 1048576 | tf_op jit(solution)/shard_map/all_to_all | solution.py:20
  244.8 13.6 %all-to-all-done.10 = f32[64,16,128]{2,1,0:T(8,128)S(1)} async-done(((f32[64,16,128]{2,1,0:T(8,128)}), f32[64,16,128]{2,1,0:T(8,128)S(1)}, u32[]{:S(2)}, u32[]{:S(2)}) %all-to-all-start.10) | async-done | bytes 524320 | tf_op jit(solution)/shard_map/all_to_all | solution.py:20
  258.8 1.7 convolution_add_fusion
  260.5 8.1 %all-to-all-start.11 = ((f32[8,32,256]{2,1,0:T(8,128)}), f32[8,32,256]{2,1,0:T(8,128)S(1)}, u32[]{:S(2)}, u32[]{:S(2)}) async-start(f32[8,32,256]{2,1,0:T(8,128)} %bitcast.52), calls=%async_computation.11 | async-start | bytes 524288 | tf_op jit(solution)/shard_map/all_to_all | solution.py:20
  269.4 5.6 %all-to-all-done.11 = f32[8,32,256]{2,1,0:T(8,128)S(1)} async-done(((f32[8,32,256]{2,1,0:T(8,128)}), f32[8,32,256]{2,1,0:T(8,128)S(1)}, u32[]{:S(2)}, u32[]{:S(2)}) %all-to-all-start.11) | async-done | bytes 262176 | tf_op jit(solution)/shard_map/all_to_all | solution.py:20
  (94 shorter events, 28.8 us)
Async XLA Ops:
  3.1 42.2 %copy-start.7 = (f32[6,64,512]{2,1,0:T(8,128)S(1)}, f32[6,64,512]{2,1,0:T(8,128)}, u32[]{:S(2)}) copy-start(f32[6,64,512]{2,1,0:T(8,128)} %param.6) | copy-start | bytes 2359300
  36.5 8.8 %copy-start.9 = (f32[4,512,64]{1,2,0:T(8,128)S(1)}, f32[4,512,64]{1,2,0:T(8,128)}, u32[]{:S(2)}) copy-start(f32[4,512,64]{1,2,0:T(8,128)} %param.5) | copy-start | bytes 1572868
  37.4 39.1 %all-to-all-start.1 = ((f32[64,8,256]{2,1,0:T(8,128)}), f32[64,8,256]{2,1,0:T(8,128)S(1)}, u32[]{:S(2)}, u32[]{:S(2)}) async-start(f32[64,8,256]{2,1,0:T(8,128)} %broadcast_in_dim.20), calls=%async_computation.1 | async-start | bytes 1048576 | tf_op jit(solution)/shard_map/all_to_all | solution.py:20
  45.2 31.3 %copy-start.8 = (f32[8,64,256]{2,1,0:T(8,128)S(1)}, f32[8,64,256]{2,1,0:T(8,128)}, u32[]{:S(2)}) copy-start(f32[8,64,256]{2,1,0:T(8,128)} %param.4) | copy-start | bytes 1572868
  45.4 31.1 %collective-permute-start = (f32[6,64,512]{2,1,0:T(8,128)S(1)}, f32[6,64,512]{2,1,0:T(8,128)}, u32[]{:S(2)}, u32[]{:S(2)}) collective-permute-start(f32[6,64,512]{2,1,0:T(8,128)S(1)} %pad_maximum_fusion), channel_id=1, source_target_pairs={{0,8},{8,0},{16,24},{24,16},{32,40},{40,32},{48,56},{56,48},{64,72... | collective-permute-start | bytes 2359304 | tf_op jit(solution)/shard_map/ppermute | solution.py:51
  77.9 15.0 %all-to-all-start.2 = ((f32[16,64,128]{2,1,0:T(8,128)}), f32[16,64,128]{2,1,0:T(8,128)S(1)}, u32[]{:S(2)}, u32[]{:S(2)}) async-start(f32[16,64,128]{2,1,0:T(8,128)} %bitcast.21), calls=%async_computation.2 | async-start | bytes 1048576 | tf_op jit(solution)/shard_map/all_to_all | solution.py:20
  94.0 25.1 %all-to-all-start.3 = ((f32[32,16,128]{2,1,0:T(8,128)}), f32[32,16,128]{2,1,0:T(8,128)}, u32[]{:S(2)}, u32[]{:S(2)}) async-start(f32[32,16,128]{2,1,0:T(8,128)} %fusion.49), calls=%async_computation.3 | async-start | bytes 524288 | tf_op jit(solution)/shard_map/all_to_all | solution.py:20
  104.9 14.2 %collective-permute-start.1 = (f32[2,64,128]{2,1,0:T(8,128)}, f32[2,64,128]{2,1,0:T(8,128)}, u32[]{:S(2)}, u32[]{:S(2)}) collective-permute-start(f32[2,64,128]{2,1,0:T(8,128)} %fusion.31), channel_id=1, source_target_pairs={{0,8},{8,0},{16,24},{24,16},{32,40},{40,32},{48,56},{56,48},{64,72... | collective-permute-start | bytes 196616 | tf_op jit(solution)/shard_map/ppermute | solution.py:51
  114.4 3.0 %copy-start.3 = (f32[4,64,1,512]{3,2,1,0:T(1,128)S(1)}, f32[4,64,1,512]{3,2,1,0:T(1,128)}, u32[]{:S(2)}) copy-start(f32[4,64,1,512]{3,2,1,0:T(1,128)} %get-tuple-element.55) | copy-start | bytes 1572868
  120.8 23.4 %all-to-all-start.4 = ((f32[32,16,128]{2,1,0:T(8,128)}), f32[32,16,128]{2,1,0:T(8,128)S(1)}, u32[]{:S(2)}, u32[]{:S(2)}) async-start(f32[32,16,128]{2,1,0:T(8,128)} %broadcast_in_dim.23), calls=%async_computation.4 | async-start | bytes 524288 | tf_op jit(solution)/shard_map/all_to_all | solution.py:20
  144.2 10.8 %copy-start.4 = (f32[512,128]{0,1:T(8,128)S(1)}, f32[512,128]{0,1:T(8,128)}, u32[]{:S(2)}) copy-start(f32[512,128]{0,1:T(8,128)} %get-tuple-element.60) | copy-start | bytes 786436
  145.4 16.5 %all-to-all-start.5 = ((f32[8,128,128]{2,1,0:T(8,128)}), f32[8,128,128]{2,1,0:T(8,128)S(1)}, u32[]{:S(2)}, u32[]{:S(2)}) async-start(f32[8,128,128]{2,1,0:T(8,128)} %broadcast_in_dim.24), calls=%async_computation.5 | async-start | bytes 1048576 | tf_op jit(solution)/shard_map/all_to_all | solution.py:20
  152.1 9.8 %collective-permute-start.2 = (f32[512,128]{1,0:T(8,128)S(1)}, f32[512,128]{1,0:T(8,128)}, u32[]{:S(2)}, u32[]{:S(2)}) collective-permute-start(f32[512,128]{1,0:T(8,128)S(1)} %bitcast.141), channel_id=1, source_target_pairs={{0,8},{8,0},{16,24},{24,16},{32,40},{40,32},{48,56},{56,48},{64,72... | collective-permute-start | bytes 786440 | tf_op jit(solution)/shard_map/ppermute | solution.py:51
  180.6 18.1 %all-to-all-start.7 = ((f32[32,16,128]{2,1,0:T(8,128)}), f32[32,16,128]{2,1,0:T(8,128)S(1)}, u32[]{:S(2)}, u32[]{:S(2)}) async-start(f32[32,16,128]{2,1,0:T(8,128)} %broadcast_in_dim.25), calls=%async_computation.7 | async-start | bytes 524288 | tf_op jit(solution)/shard_map/all_to_all | solution.py:20
  187.1 2.1 copy-start.2
  187.1 2.1 copy-start.5
  188.2 10.5 %copy-start.10 = (f32[128,128]{1,0:T(8,128)S(1)}, f32[128,128]{1,0:T(8,128)}, u32[]{:S(2)}) copy-start(f32[128,128]{1,0:T(8,128)} %convolution_subtract_fusion.1) | copy-start | bytes 196612
  199.9 17.2 %all-to-all-start.8 = ((f32[8,128,128]{2,1,0:T(8,128)}), f32[8,128,128]{2,1,0:T(8,128)S(1)}, u32[]{:S(2)}, u32[]{:S(2)}) async-start(f32[8,128,128]{2,1,0:T(8,128)} %broadcast_in_dim.26), calls=%async_computation.8 | async-start | bytes 1048576 | tf_op jit(solution)/shard_map/all_to_all | solution.py:20
  207.2 9.8 %collective-permute-start.3 = (f32[512,128]{1,0:T(8,128)S(1)}, f32[512,128]{1,0:T(8,128)S(1)}, u32[]{:S(2)}, u32[]{:S(2)}) collective-permute-start(f32[512,128]{1,0:T(8,128)S(1)} %bitcast.144), channel_id=1, source_target_pairs={{0,8},{8,0},{16,24},{24,16},{32,40},{40,32},{48,56},{56,48},{64,72... | collective-permute-start | bytes 786440 | tf_op jit(solution)/shard_map/ppermute | solution.py:51
  217.0 17.7 %copy-start.11 = (f32[512,128]{1,0:T(8,128)}, f32[512,128]{1,0:T(8,128)S(1)}, u32[]{:S(2)}) copy-start(f32[512,128]{1,0:T(8,128)S(1)} %collective-permute-done.3) | copy-start | bytes 786436
  218.1 16.5 %all-to-all-start.9 = ((f32[32,16,128]{2,1,0:T(8,128)}), f32[32,16,128]{2,1,0:T(8,128)S(1)}, u32[]{:S(2)}, u32[]{:S(2)}) async-start(f32[32,16,128]{2,1,0:T(8,128)} %fusion.32), calls=%async_computation.9 | async-start | bytes 524288 | tf_op jit(solution)/shard_map/all_to_all | solution.py:20
  222.6 19.9 %slice-start = ((f32[8,64,256]{2,1,0:T(8,128)}), f32[4,64,256]{2,1,0:T(8,128)S(1)}, s32[]{:S(2)}) async-start(f32[8,64,256]{2,1,0:T(8,128)} %param.4), calls=%async_computation.12 | async-start | bytes 524288 | tf_op jit(solution)/shard_map/slice | solution.py:89
  235.5 7.2 %copy-start.12 = (f32[512,128]{1,0:T(8,128)S(1)}, f32[512,128]{1,0:T(8,128)}, u32[]{:S(2)}) copy-start(f32[512,128]{1,0:T(8,128)} %copy-done.11) | copy-start | bytes 786436
  235.5 22.9 %all-to-all-start.10 = ((f32[64,16,128]{2,1,0:T(8,128)}), f32[64,16,128]{2,1,0:T(8,128)S(1)}, u32[]{:S(2)}, u32[]{:S(2)}) async-start(f32[64,16,128]{2,1,0:T(8,128)} %broadcast_in_dim.27), calls=%async_computation.10 | async-start | bytes 1048576 | tf_op jit(solution)/shard_map/all_to_all | solution.py:20
  242.5 1.0 copy-start.1
  242.5 1.1 copy-start.6
  244.6 14.2 %copy-start = (f32[4,64,1,512]{3,1,0,2:T(8,128)S(1)}, f32[4,64,1,512]{3,1,0,2:T(8,128)}, u32[]{:S(2)}) copy-start(f32[4,64,1,512]{3,1,0,2:T(8,128)} %copy.69) | copy-start | bytes 1572868
  260.5 14.6 %all-to-all-start.11 = ((f32[8,32,256]{2,1,0:T(8,128)}), f32[8,32,256]{2,1,0:T(8,128)S(1)}, u32[]{:S(2)}, u32[]{:S(2)}) async-start(f32[8,32,256]{2,1,0:T(8,128)} %bitcast.52), calls=%async_computation.11 | async-start | bytes 524288 | tf_op jit(solution)/shard_map/all_to_all | solution.py:20

commit v12 on v11

--- a/solution.py
+++ b/solution.py
@@ -96,12 +96,14 @@
 
     local_term = contract(own_diag[0], right_sides[0], (0, 0))
     parts = swap(local_term.reshape(row_size, width // row_size, column_count), "row")
-    own_later = jnp.concatenate([own_diag[1:], lower_blocks[2:3], lower_blocks[4:]])
-    got_later = from_partner(own_later)
+    own_first = jnp.concatenate([own_diag[1:3], lower_blocks[2:3]])
+    own_rest = jnp.concatenate([own_diag[3:], lower_blocks[4:]])
+    own_rest = own_rest.reshape(-1, local_rows, width // half, half)
+    own_rest = own_rest.transpose(0, 2, 1, 3).reshape(-1, half)
+    parts, got_first, trail = by_deadline(parts, from_partner(own_first), trail)
+    pair = ordered(own_first, got_first, 1)
+    diag_1, diag_2, lower_21 = [pair[i] for i in range(3)]
     parts = swap(copies(parts.sum(0), row_size), "row")
-    parts, got_later = by_deadline(parts, got_later)
-    pair = ordered(own_later, got_later, 1)
-    diag_1, diag_2, diag_3, lower_21, lower_31, lower_32 = [pair[i] for i in range(6)]
     whole_0 = parts.reshape(width, column_count)
 
     term = own_term(1) - contract(lower_blocks[0], whole_0, (1, 0))
@@ -118,14 +120,24 @@
     parts = gathered(parts)
     terms = ordered(half_of(terms, row % 2), got_terms, 1)
     below = below_of(whole_0, 0)
-    parts, terms, below, trail = by_deadline(parts, terms, below, trail)
+    parts, terms, below = by_deadline(parts, terms, below)
     term_2, term_3 = terms[0], terms[1]
     solved_1 = parts.reshape(width, half)
 
     parts = summed(term_2 - contract(lower_21, solved_1, (1, 0)))
-    parts, got_1 = by_deadline(parts, from_partner(solved_1))
+    got = from_partner(jnp.concatenate([own_rest, solved_1]))
+    parts, got = by_deadline(parts, got)
+    got_rest, got_1 = got[: own_rest.shape[0]], got[own_rest.shape[0] :]
     parts = scattered(diag_2, parts.sum(0))
     parts = gathered(parts)
+    own_rest, got_rest = [
+        v.reshape(-1, width // half, local_rows, half)
+        .transpose(0, 2, 1, 3)
+        .reshape(-1, local_rows, width)
+        for v in (own_rest, got_rest)
+    ]
+    pair = ordered(own_rest, got_rest, 1)
+    diag_3, lower_31, lower_32 = [pair[i] for i in range(3)]
     whole_1 = ordered(solved_1, got_1, 1)
     term_3 = term_3 - contract(lower_31, solved_1, (1, 0))
     below = below + below_of(whole_1, 1)

time: 277 us -> 271 us (0.978)
  blocking collectives: 49.4 us -> 0 us
  starting transfers between devices: 85.8 us -> 107 us
  waiting for transfers between devices: 94.2 us -> 109 us
  matrix products: 15.9 us -> 19.6 us
  other arithmetic: 7.7 us -> 10.6 us
    all_to_all x2 -> x0, blocking collectives: 49.4 us -> none  [swap(): lax.all_to_all(parts, axis, 0, 0, axis_index_groups=groups, tiled=True)]
    all_to_all x10 -> x12, waiting for transfers between devices: 52.8 us -> 89.3 us  [swap(): lax.all_to_all(parts, axis, 0, 0, axis_index_groups=groups, tiled=True)]
    ppermute x4, waiting for transfers between devices: 41.4 us -> 20.2 us  [from_partner(): return lax.ppermute(value, 'row', [(r, r ^ 1) for r in range(row_size)])]
    all_to_all x10 -> x12, starting transfers between devices: 74.8 us -> 95.7 us  [swap(): lax.all_to_all(parts, axis, 0, 0, axis_index_groups=groups, tiled=True)]
    dot_general x14, matrix products: 15.9 us -> 19.6 us  [contract(): lax.dot_general(left, right, (((axes[0],), (axes[1],)), ((), ())), precis...]
    unnamed x33 -> x27, local copies, waits for them, and re-layouts: 5.98 us -> 2.54 us
  transfers between devices with their start and end apart: 14 -> 16, of which waited for: 9 -> 13; matrix products, arithmetic and copies ran while one was open for 10% -> 12% of each run, Pallas kernels for 0% -> 0%
where the time goes in v12:
time: 271 us; the launch traced here: 270 us
  waiting for transfers between devices  109 us (40%)
  starting transfers between devices  107 us (39%)
  local copies, waits for them, and re-layouts  22.1 us (8%)
  matrix products  19.6 us (7%)
  other arithmetic  10.6 us (4%)
    all_to_all x12, starting transfers between devices, swap(): lax.all_to_all(parts, axis, 0, 0, axis_index_groups=groups, tiled=True)  95.7 us
    all_to_all x12, waiting for transfers between devices, swap(): lax.all_to_all(parts, axis, 0, 0, axis_index_groups=groups, tiled=True)  89.3 us
    ppermute x4, waiting for transfers between devices, from_partner(): return lax.ppermute(value, 'row', [(r, r ^ 1) for r in range(row_size)])  20.2 us
    dot_general x14, matrix products, contract(): lax.dot_general(left, right, (((axes[0],), (axes[1],)), ((), ())), precis...  19.6 us
    ppermute x4, starting transfers between devices, from_partner(): return lax.ppermute(value, 'row', [(r, r ^ 1) for r in range(row_size)])  11.2 us
    slice x1, local copies, waits for them, and re-layouts, shards(): trail_panel[:, :, j, :].reshape(trail_count * local_rows, width)  5.81 us
  transfers between devices with their start and end apart: 16, of which 13 were waited for; matrix products, arithmetic and copies ran while one was open for 12% of the time, Pallas kernels for 0%

profile of v12, /device:TPU:1, one launch (start us, length us, event | category | flops | bytes accessed | tf_op | source)
XLA Modules:
  0.0 269.7 jit_solution(7582242513577972788)
XLA Ops:
  2.5 2.2 fusion.21
  4.7 17.1 %all-to-all-start = ((f32[64,8,256]{2,1,0:T(8,128)}), f32[64,8,256]{2,1,0:T(8,128)S(1)}, u32[]{:S(2)}, u32[]{:S(2)}) async-start(f32[64,8,256]{2,1,0:T(8,128)} %fusion.21), calls=%async_computation | async-start | bytes 1048576 | tf_op jit(solution)/shard_map/all_to_all | solution.py:20
  22.0 2.9 %collective-permute-start = (f32[3,64,512]{2,1,0:T(8,128)S(1)}, f32[3,64,512]{2,1,0:T(8,128)}, u32[]{:S(2)}, u32[]{:S(2)}) collective-permute-start(f32[3,64,512]{2,1,0:T(8,128)S(1)} %pad_maximum_fusion.6), channel_id=1, source_target_pairs={{0,8},{8,0},{16,24},{24,16},{32,40},{40,32},{48,56},{56,48},{64,72... | collective-permute-start | bytes 1179656 | tf_op jit(solution)/shard_map/ppermute | solution.py:51
  24.9 5.8 %fusion.47 = (f32[4,64,1,512]{3,2,1,0:T(1,128)S(1)}, f32[4,64,1,512]{3,2,1,0:T(1,128)S(1)}, f32[4,64,1,512]{3,2,1,0:T(1,128)S(1)}, f32[4,64,1,512]{3,2,1,0:T(1,128)S(1)}) fusion(f32[4,64,4,512]{3,2,1,0:T(4,128)} %param.7), kind=kLoop, calls=%fused_computation.98 | loop fusion | bytes 4194304 | tf_op jit(solution)/shard_map/slice | solution.py:81
  32.5 12.1 %collective-permute-done = f32[3,64,512]{2,1,0:T(8,128)} collective-permute-done((f32[3,64,512]{2,1,0:T(8,128)S(1)}, f32[3,64,512]{2,1,0:T(8,128)}, u32[]{:S(2)}, u32[]{:S(2)}) %collective-permute-start) | collective-permute-done | bytes 393248 | tf_op jit(solution)/shard_map/ppermute | solution.py:51
  45.5 10.4 %all-to-all-start.1 = ((f32[64,8,256]{2,1,0:T(8,128)}), f32[64,8,256]{2,1,0:T(8,128)S(1)}, u32[]{:S(2)}, u32[]{:S(2)}) async-start(f32[64,8,256]{2,1,0:T(8,128)} %broadcast_in_dim.21), calls=%async_computation.1 | async-start | bytes 1048576 | tf_op jit(solution)/shard_map/all_to_all | solution.py:20
  55.9 16.5 %all-to-all-done.1 = f32[64,8,256]{2,1,0:T(8,128)S(1)} async-done(((f32[64,8,256]{2,1,0:T(8,128)}), f32[64,8,256]{2,1,0:T(8,128)S(1)}, u32[]{:S(2)}, u32[]{:S(2)}) %all-to-all-start.1) | async-done | bytes 524320 | tf_op jit(solution)/shard_map/all_to_all | solution.py:20
  73.7 8.5 %all-to-all-start.2 = ((f32[16,64,128]{2,1,0:T(8,128)}), f32[16,64,128]{2,1,0:T(8,128)S(1)}, u32[]{:S(2)}, u32[]{:S(2)}) async-start(f32[16,64,128]{2,1,0:T(8,128)} %bitcast.19), calls=%async_computation.2 | async-start | bytes 1048576 | tf_op jit(solution)/shard_map/all_to_all | solution.py:20
  86.0 6.0 %all-to-all-done.2 = f32[16,64,128]{2,1,0:T(8,128)S(1)} async-done(((f32[16,64,128]{2,1,0:T(8,128)}), f32[16,64,128]{2,1,0:T(8,128)S(1)}, u32[]{:S(2)}, u32[]{:S(2)}) %all-to-all-start.2) | async-done | bytes 524320 | tf_op jit(solution)/shard_map/all_to_all | solution.py:20
  92.1 2.0 fusion.49
  94.1 5.0 %all-to-all-start.3 = ((f32[32,16,128]{2,1,0:T(8,128)}), f32[32,16,128]{2,1,0:T(8,128)}, u32[]{:S(2)}, u32[]{:S(2)}) async-start(f32[32,16,128]{2,1,0:T(8,128)} %fusion.49), calls=%async_computation.3 | async-start | bytes 524288 | tf_op jit(solution)/shard_map/all_to_all | solution.py:20
  102.4 2.6 collective-permute-start.1
  112.6 8.6 %all-to-all-start.4 = ((f32[32,16,128]{2,1,0:T(8,128)}), f32[32,16,128]{2,1,0:T(8,128)S(1)}, u32[]{:S(2)}, u32[]{:S(2)}) async-start(f32[32,16,128]{2,1,0:T(8,128)} %broadcast_in_dim.23), calls=%async_computation.4 | async-start | bytes 524288 | tf_op jit(solution)/shard_map/all_to_all | solution.py:20
  121.2 2.8 %fusion.42 = f32[256,256]{1,0:T(8,128)} fusion(f32[256,512]{1,0:T(8,128)} %bitcast.157, f32[64,8,256]{2,1,0:T(8,128)S(1)} %all-to-all-done.1), kind=kOutput, calls=%fused_computation.93 | convolution fusion | flops 402653184 | bytes 1310720 | tf_op jit(solution)/shard_map/dot_general | solution.py:10
  124.8 8.0 %all-to-all-done.4 = f32[32,16,128]{2,1,0:T(8,128)S(1)} async-done(((f32[32,16,128]{2,1,0:T(8,128)}), f32[32,16,128]{2,1,0:T(8,128)S(1)}, u32[]{:S(2)}, u32[]{:S(2)}) %all-to-all-start.4) | async-done | bytes 262176 | tf_op jit(solution)/shard_map/all_to_all | solution.py:20
  133.7 2.7 collective-permute-start.2
  137.7 7.5 %all-to-all-start.5 = ((f32[8,128,128]{2,1,0:T(8,128)}), f32[8,128,128]{2,1,0:T(8,128)S(1)}, u32[]{:S(2)}, u32[]{:S(2)}) async-start(f32[8,128,128]{2,1,0:T(8,128)} %broadcast_in_dim.24), calls=%async_computation.5 | async-start | bytes 1048576 | tf_op jit(solution)/shard_map/all_to_all | solution.py:20
  145.3 9.4 %all-to-all-done.5 = f32[8,128,128]{2,1,0:T(8,128)S(1)} async-done(((f32[8,128,128]{2,1,0:T(8,128)}), f32[8,128,128]{2,1,0:T(8,128)S(1)}, u32[]{:S(2)}, u32[]{:S(2)}) %all-to-all-start.5) | async-done | bytes 524320 | tf_op jit(solution)/shard_map/all_to_all | solution.py:20
  155.8 4.3 %all-to-all-start.6 = ((f32[32,16,128]{2,1,0:T(8,128)}), f32[32,16,128]{2,1,0:T(8,128)S(1)}, u32[]{:S(2)}, u32[]{:S(2)}) async-start(f32[32,16,128]{2,1,0:T(8,128)} %fusion.33), calls=%async_computation.6 | async-start | bytes 524288 | tf_op jit(solution)/shard_map/all_to_all | solution.py:20
  161.2 10.8 %all-to-all-done.6 = f32[32,16,128]{2,1,0:T(8,128)S(1)} async-done(((f32[32,16,128]{2,1,0:T(8,128)}), f32[32,16,128]{2,1,0:T(8,128)S(1)}, u32[]{:S(2)}, u32[]{:S(2)}) %all-to-all-start.6) | async-done | bytes 262176 | tf_op jit(solution)/shard_map/all_to_all | solution.py:20
  172.8 6.6 %all-to-all-start.7 = ((f32[32,16,128]{2,1,0:T(8,128)}), f32[32,16,128]{2,1,0:T(8,128)S(1)}, u32[]{:S(2)}, u32[]{:S(2)}) async-start(f32[32,16,128]{2,1,0:T(8,128)} %broadcast_in_dim.25), calls=%async_computation.7 | async-start | bytes 524288 | tf_op jit(solution)/shard_map/all_to_all | solution.py:20
  181.4 2.8 %convolution_add_fusion.2 = f32[256,256]{1,0:T(8,128)} fusion(f32[256,256]{1,0:T(8,128)} %fusion.42, f32[256,512]{1,0:T(8,128)} %bitcast.156, f32[512,128]{1,0:T(8,128)S(1)} %get-tuple-element.63, f32[512,128]{1,0:T(8,128)S(1)} %get-tuple-element.62), kind=kOutput, calls=%fused_computation.2 | convolution fusion | flops 402849792 | bytes 1572864 | tf_op jit(solution)/shard_map/dot_general | solution.py:10
  184.2 7.0 %all-to-all-done.7 = f32[32,16,128]{2,1,0:T(8,128)S(1)} async-done(((f32[32,16,128]{2,1,0:T(8,128)}), f32[32,16,128]{2,1,0:T(8,128)S(1)}, u32[]{:S(2)}, u32[]{:S(2)}) %all-to-all-start.7) | async-done | bytes 262176 | tf_op jit(solution)/shard_map/all_to_all | solution.py:20
  192.4 6.9 %all-to-all-start.8 = ((f32[8,128,128]{2,1,0:T(8,128)}), f32[8,128,128]{2,1,0:T(8,128)}, u32[]{:S(2)}, u32[]{:S(2)}) async-start(f32[8,128,128]{2,1,0:T(8,128)} %broadcast_in_dim.26), calls=%async_computation.8 | async-start | bytes 1048576 | tf_op jit(solution)/shard_map/all_to_all | solution.py:20
  199.4 2.9 %collective-permute-start.3 = (f32[512,128]{1,0:T(8,128)S(1)}, f32[512,128]{1,0:T(8,128)}, u32[]{:S(2)}, u32[]{:S(2)}) collective-permute-start(f32[512,128]{1,0:T(8,128)S(1)} %bitcast.153), channel_id=1, source_target_pairs={{0,8},{8,0},{16,24},{24,16},{32,40},{40,32},{48,56},{56,48},{64,72... | collective-permute-start | bytes 786440 | tf_op jit(solution)/shard_map/ppermute | solution.py:51
  202.5 6.6 %collective-permute-done.3 = f32[512,128]{1,0:T(8,128)} collective-permute-done((f32[512,128]{1,0:T(8,128)S(1)}, f32[512,128]{1,0:T(8,128)}, u32[]{:S(2)}, u32[]{:S(2)}) %collective-permute-start.3) | collective-permute-done | bytes 262176 | tf_op jit(solution)/shard_map/ppermute | solution.py:51
  211.3 4.7 %all-to-all-start.9 = ((f32[32,16,128]{2,1,0:T(8,128)}), f32[32,16,128]{2,1,0:T(8,128)S(1)}, u32[]{:S(2)}, u32[]{:S(2)}) async-start(f32[32,16,128]{2,1,0:T(8,128)} %fusion.31), calls=%async_computation.9 | async-start | bytes 524288 | tf_op jit(solution)/shard_map/all_to_all | solution.py:20
  216.4 11.5 %all-to-all-done.9 = f32[32,16,128]{2,1,0:T(8,128)S(1)} async-done(((f32[32,16,128]{2,1,0:T(8,128)}), f32[32,16,128]{2,1,0:T(8,128)S(1)}, u32[]{:S(2)}, u32[]{:S(2)}) %all-to-all-start.9) | async-done | bytes 262176 | tf_op jit(solution)/shard_map/all_to_all | solution.py:20
  228.7 7.2 %all-to-all-start.10 = ((f32[64,16,128]{2,1,0:T(8,128)}), f32[64,16,128]{2,1,0:T(8,128)S(1)}, u32[]{:S(2)}, u32[]{:S(2)}) async-start(f32[64,16,128]{2,1,0:T(8,128)} %broadcast_in_dim.27), calls=%async_computation.10 | async-start | bytes 1048576 | tf_op jit(solution)/shard_map/all_to_all | solution.py:20
  238.7 12.9 %all-to-all-done.10 = f32[64,16,128]{2,1,0:T(8,128)S(1)} async-done(((f32[64,16,128]{2,1,0:T(8,128)}), f32[64,16,128]{2,1,0:T(8,128)S(1)}, u32[]{:S(2)}, u32[]{:S(2)}) %all-to-all-start.10) | async-done | bytes 524320 | tf_op jit(solution)/shard_map/all_to_all | solution.py:20
  253.6 8.8 %all-to-all-start.11 = ((f32[8,32,256]{2,1,0:T(8,128)}), f32[8,32,256]{2,1,0:T(8,128)S(1)}, u32[]{:S(2)}, u32[]{:S(2)}) async-start(f32[8,32,256]{2,1,0:T(8,128)} %bitcast.56), calls=%async_computation.11 | async-start | bytes 524288 | tf_op jit(solution)/shard_map/all_to_all | solution.py:20
  263.3 5.6 %all-to-all-done.11 = f32[8,32,256]{2,1,0:T(8,128)S(1)} async-done(((f32[8,32,256]{2,1,0:T(8,128)}), f32[8,32,256]{2,1,0:T(8,128)S(1)}, u32[]{:S(2)}, u32[]{:S(2)}) %all-to-all-start.11) | async-done | bytes 262176 | tf_op jit(solution)/shard_map/all_to_all | solution.py:20
  (97 shorter events, 39.7 us)
Async XLA Ops:
  0.6 21.2 %copy-start.8 = (f32[4,512,64]{1,2,0:T(8,128)S(1)}, f32[4,512,64]{1,2,0:T(8,128)}, u32[]{:S(2)}) copy-start(f32[4,512,64]{1,2,0:T(8,128)} %param.5) | copy-start | bytes 1572868
  0.6 21.3 %copy-start.4 = (f32[6,64,512]{2,1,0:T(8,128)S(1)}, f32[6,64,512]{2,1,0:T(8,128)}, u32[]{:S(2)}) copy-start(f32[6,64,512]{2,1,0:T(8,128)} %param.6) | copy-start | bytes 2359300
  4.7 39.8 %all-to-all-start = ((f32[64,8,256]{2,1,0:T(8,128)}), f32[64,8,256]{2,1,0:T(8,128)S(1)}, u32[]{:S(2)}, u32[]{:S(2)}) async-start(f32[64,8,256]{2,1,0:T(8,128)} %fusion.21), calls=%async_computation | async-start | bytes 1048576 | tf_op jit(solution)/shard_map/all_to_all | solution.py:20
  22.0 22.6 %collective-permute-start = (f32[3,64,512]{2,1,0:T(8,128)S(1)}, f32[3,64,512]{2,1,0:T(8,128)}, u32[]{:S(2)}, u32[]{:S(2)}) collective-permute-start(f32[3,64,512]{2,1,0:T(8,128)S(1)} %pad_maximum_fusion.6), channel_id=1, source_target_pairs={{0,8},{8,0},{16,24},{24,16},{32,40},{40,32},{48,56},{56,48},{64,72... | collective-permute-start | bytes 1179656 | tf_op jit(solution)/shard_map/ppermute | solution.py:51
  30.8 41.6 %copy-start.5 = (f32[8,64,256]{2,1,0:T(8,128)S(1)}, f32[8,64,256]{2,1,0:T(8,128)}, u32[]{:S(2)}) copy-start(f32[8,64,256]{2,1,0:T(8,128)} %param.4) | copy-start | bytes 1572868
  45.5 27.0 %all-to-all-start.1 = ((f32[64,8,256]{2,1,0:T(8,128)}), f32[64,8,256]{2,1,0:T(8,128)S(1)}, u32[]{:S(2)}, u32[]{:S(2)}) async-start(f32[64,8,256]{2,1,0:T(8,128)} %broadcast_in_dim.21), calls=%async_computation.1 | async-start | bytes 1048576 | tf_op jit(solution)/shard_map/all_to_all | solution.py:20
  73.7 18.3 %all-to-all-start.2 = ((f32[16,64,128]{2,1,0:T(8,128)}), f32[16,64,128]{2,1,0:T(8,128)S(1)}, u32[]{:S(2)}, u32[]{:S(2)}) async-start(f32[16,64,128]{2,1,0:T(8,128)} %bitcast.19), calls=%async_computation.2 | async-start | bytes 1048576 | tf_op jit(solution)/shard_map/all_to_all | solution.py:20
  84.2 20.9 %copy-start.1 = (f32[1,64,512]{2,1,0:T(8,128)S(1)}, f32[1,64,512]{2,1,0:T(8,128)}, u32[]{:S(2)}) copy-start(f32[1,64,512]{2,1,0:T(8,128)} %get-tuple-element.72) | copy-start | bytes 393220
  94.1 16.8 %all-to-all-start.3 = ((f32[32,16,128]{2,1,0:T(8,128)}), f32[32,16,128]{2,1,0:T(8,128)}, u32[]{:S(2)}, u32[]{:S(2)}) async-start(f32[32,16,128]{2,1,0:T(8,128)} %fusion.49), calls=%async_computation.3 | async-start | bytes 524288 | tf_op jit(solution)/shard_map/all_to_all | solution.py:20
  102.4 6.8 %collective-permute-start.1 = (f32[2,64,128]{2,1,0:T(8,128)}, f32[2,64,128]{2,1,0:T(8,128)}, u32[]{:S(2)}, u32[]{:S(2)}) collective-permute-start(f32[2,64,128]{2,1,0:T(8,128)} %fusion.30), channel_id=1, source_target_pairs={{0,8},{8,0},{16,24},{24,16},{32,40},{40,32},{48,56},{56,48},{64,72... | collective-permute-start | bytes 196616 | tf_op jit(solution)/shard_map/ppermute | solution.py:51
  107.8 25.0 %copy-start = (f32[3,4,64,128]{3,2,1,0:T(8,128)S(1)}, f32[3,4,64,128]{3,2,1,0:T(8,128)}, u32[]{:S(2)}) copy-start(f32[3,4,64,128]{3,2,1,0:T(8,128)} %copy.77) | copy-start | bytes 1179652
  112.6 20.3 %all-to-all-start.4 = ((f32[32,16,128]{2,1,0:T(8,128)}), f32[32,16,128]{2,1,0:T(8,128)S(1)}, u32[]{:S(2)}, u32[]{:S(2)}) async-start(f32[32,16,128]{2,1,0:T(8,128)} %broadcast_in_dim.23), calls=%async_computation.4 | async-start | bytes 524288 | tf_op jit(solution)/shard_map/all_to_all | solution.py:20
  124.8 20.5 %copy-start.6 = (f32[2,128,128]{2,1,0:T(8,128)}, f32[2,128,128]{2,1,0:T(8,128)S(1)}, u32[]{:S(2)}) copy-start(f32[2,128,128]{2,1,0:T(8,128)S(1)} %pad_maximum_fusion.9) | copy-start | bytes 393220
  133.7 11.4 %copy-start.2 = (f32[512,128]{0,1:T(8,128)S(1)}, f32[512,128]{0,1:T(8,128)}, u32[]{:S(2)}) copy-start(f32[512,128]{0,1:T(8,128)} %get-tuple-element.64) | copy-start | bytes 786436
  133.7 20.9 %collective-permute-start.2 = (f32[1280,128]{1,0:T(8,128)}, f32[1280,128]{1,0:T(8,128)}, u32[]{:S(2)}, u32[]{:S(2)}) collective-permute-start(f32[1280,128]{1,0:T(8,128)} %pad_maximum_fusion), channel_id=1, source_target_pairs={{0,8},{8,0},{16,24},{24,16},{32,40},{40,32},{48,56},{56,48},{64,72... | collective-permute-start | bytes 1966088 | tf_op jit(solution)/shard_map/ppermute | solution.py:51
  137.7 17.0 %all-to-all-start.5 = ((f32[8,128,128]{2,1,0:T(8,128)}), f32[8,128,128]{2,1,0:T(8,128)S(1)}, u32[]{:S(2)}, u32[]{:S(2)}) async-start(f32[8,128,128]{2,1,0:T(8,128)} %broadcast_in_dim.24), calls=%async_computation.5 | async-start | bytes 1048576 | tf_op jit(solution)/shard_map/all_to_all | solution.py:20
  155.8 23.5 %copy-start.7 = (f32[2,128,128]{2,1,0:T(8,128)S(1)}, f32[2,128,128]{2,1,0:T(8,128)}, u32[]{:S(2)}) copy-start(f32[2,128,128]{2,1,0:T(8,128)} %copy-done.6) | copy-start | bytes 393220
  155.8 16.2 %all-to-all-start.6 = ((f32[32,16,128]{2,1,0:T(8,128)}), f32[32,16,128]{2,1,0:T(8,128)S(1)}, u32[]{:S(2)}, u32[]{:S(2)}) async-start(f32[32,16,128]{2,1,0:T(8,128)} %fusion.33), calls=%async_computation.6 | async-start | bytes 524288 | tf_op jit(solution)/shard_map/all_to_all | solution.py:20
  172.8 18.4 %all-to-all-start.7 = ((f32[32,16,128]{2,1,0:T(8,128)}), f32[32,16,128]{2,1,0:T(8,128)S(1)}, u32[]{:S(2)}, u32[]{:S(2)}) async-start(f32[32,16,128]{2,1,0:T(8,128)} %broadcast_in_dim.25), calls=%async_computation.7 | async-start | bytes 524288 | tf_op jit(solution)/shard_map/all_to_all | solution.py:20
  180.4 10.8 %copy-start.9 = (f32[128,128]{1,0:T(8,128)S(1)}, f32[128,128]{1,0:T(8,128)}, u32[]{:S(2)}) copy-start(f32[128,128]{1,0:T(8,128)} %convolution_subtract_fusion.1) | copy-start | bytes 196612
  192.4 16.7 %all-to-all-start.8 = ((f32[8,128,128]{2,1,0:T(8,128)}), f32[8,128,128]{2,1,0:T(8,128)}, u32[]{:S(2)}, u32[]{:S(2)}) async-start(f32[8,128,128]{2,1,0:T(8,128)} %broadcast_in_dim.26), calls=%async_computation.8 | async-start | bytes 1048576 | tf_op jit(solution)/shard_map/all_to_all | solution.py:20
  199.4 9.7 %collective-permute-start.3 = (f32[512,128]{1,0:T(8,128)S(1)}, f32[512,128]{1,0:T(8,128)}, u32[]{:S(2)}, u32[]{:S(2)}) collective-permute-start(f32[512,128]{1,0:T(8,128)S(1)} %bitcast.153), channel_id=1, source_target_pairs={{0,8},{8,0},{16,24},{24,16},{32,40},{40,32},{48,56},{56,48},{64,72... | collective-permute-start | bytes 786440 | tf_op jit(solution)/shard_map/ppermute | solution.py:51
  211.3 24.6 %slice-start = ((f32[8,64,256]{2,1,0:T(8,128)}), f32[4,64,256]{2,1,0:T(8,128)S(1)}, s32[]{:S(2)}) async-start(f32[8,64,256]{2,1,0:T(8,128)} %param.4), calls=%async_computation.12 | async-start | bytes 524288 | tf_op jit(solution)/shard_map/slice | solution.py:89
  211.3 16.6 %all-to-all-start.9 = ((f32[32,16,128]{2,1,0:T(8,128)}), f32[32,16,128]{2,1,0:T(8,128)S(1)}, u32[]{:S(2)}, u32[]{:S(2)}) async-start(f32[32,16,128]{2,1,0:T(8,128)} %fusion.31), calls=%async_computation.9 | async-start | bytes 524288 | tf_op jit(solution)/shard_map/all_to_all | solution.py:20
  228.7 8.7 %copy-start.3 = (f32[256,256]{1,0:T(8,128)S(1)}, f32[256,256]{1,0:T(8,128)}, u32[]{:S(2)}) copy-start(f32[256,256]{1,0:T(8,128)} %convolution_add_fusion.2) | copy-start | bytes 786436
  228.7 22.9 %all-to-all-start.10 = ((f32[64,16,128]{2,1,0:T(8,128)}), f32[64,16,128]{2,1,0:T(8,128)S(1)}, u32[]{:S(2)}, u32[]{:S(2)}) async-start(f32[64,16,128]{2,1,0:T(8,128)} %broadcast_in_dim.27), calls=%async_computation.10 | async-start | bytes 1048576 | tf_op jit(solution)/shard_map/all_to_all | solution.py:20
  253.6 15.3 %all-to-all-start.11 = ((f32[8,32,256]{2,1,0:T(8,128)}), f32[8,32,256]{2,1,0:T(8,128)S(1)}, u32[]{:S(2)}, u32[]{:S(2)}) async-start(f32[8,32,256]{2,1,0:T(8,128)} %bitcast.56), calls=%async_computation.11 | async-start | bytes 524288 | tf_op jit(solution)/shard_map/all_to_all | solution.py:20

commit v13 on v11

--- a/solution.py
+++ b/solution.py
@@ -42,10 +42,6 @@
     col = lax.axis_index("col")
     even = row % 2 == 0
     row_groups = [[r for r in range(row_size) if r % 2 == g] for g in range(2)]
-    pair_groups = [
-        [(r + g) * col_size + c for g in range(2) for c in range(col_size)]
-        for r in range(0, row_size, 2)
-    ]
 
     def from_partner(value):
         return lax.ppermute(value, "row", [(r, r ^ 1) for r in range(row_size)])
@@ -63,6 +59,10 @@
     def scattered(matrix, current):
         parts = contract(matrix, current, (0, 0)).reshape(members, width // members, half)
         return swap(parts, "row", row_groups)
+
+    def scattered_whole(matrix, current):
+        parts = contract(matrix, current, (0, 0))
+        return swap(parts.reshape(row_size, width // row_size, column_count), "row")
 
     def gathered(parts):
         return swap(copies(parts.sum(0), members), "row", row_groups)
@@ -94,42 +94,32 @@
     def out_of(whole):
         return lax.dynamic_slice_in_dim(whole, row * out_width, out_width, 1)
 
-    local_term = contract(own_diag[0], right_sides[0], (0, 0))
-    parts = swap(local_term.reshape(row_size, width // row_size, column_count), "row")
-    own_later = jnp.concatenate([own_diag[1:], lower_blocks[2:3], lower_blocks[4:]])
-    got_later = from_partner(own_later)
-    parts = swap(copies(parts.sum(0), row_size), "row")
-    parts, got_later = by_deadline(parts, got_later)
-    pair = ordered(own_later, got_later, 1)
-    diag_1, diag_2, diag_3, lower_21, lower_31, lower_32 = [pair[i] for i in range(6)]
-    whole_0 = parts.reshape(width, column_count)
+    parts = scattered_whole(own_diag[0], right_sides[0])
+    whole_0 = gathered_whole(parts).reshape(width, column_count)
 
-    term = own_term(1) - contract(lower_blocks[0], whole_0, (1, 0))
-    parts = jnp.stack([term[:, :half], term[:, half:]])[:, None]
-    parts = jnp.broadcast_to(parts, (2, col_size, local_rows, half))
-    parts = swap(parts.reshape(2 * col_size, local_rows, half), ("row", "col"), pair_groups)
+    parts = summed(contract(lower_blocks[0], whole_0, (1, 0)))
+    own_shared = jnp.concatenate([own_diag[2:], lower_blocks[2:3], lower_blocks[5:]])
+    parts, got_shared = by_deadline(parts, from_partner(own_shared))
+    parts = scattered_whole(own_diag[1], right_sides[1] - parts.sum(0))
     term_2 = own_term(2) - contract(lower_blocks[1], whole_0, (1, 0))
+    parts, got_2, trail = by_deadline(parts, from_partner(half_of(term_2, row % 2 ^ 1)), trail)
+    pair = ordered(own_shared, got_shared, 1)
+    diag_2, diag_3, lower_21, lower_32 = [pair[i] for i in range(4)]
+    term_2 = ordered(half_of(term_2, row % 2), got_2, 0)
     term_3 = own_term(3) - contract(lower_blocks[3], whole_0, (1, 0))
-    terms = jnp.stack([term_2, term_3])
-    got_terms = from_partner(half_of(terms, row % 2 ^ 1))
-    current = parts.reshape(2, col_size, local_rows, half).sum(1).reshape(2 * local_rows, half)
-    parts = scattered(diag_1, current)
-    parts, got_terms = by_deadline(parts, got_terms)
+    parts = gathered_whole(parts)
+    below = below_of(whole_0, 0)
+    parts, below, term_3 = by_deadline(parts, below, term_3)
+    whole_1 = parts.reshape(width, column_count)
+
+    parts = summed(term_2 - contract(lower_21, half_of(whole_1, row % 2), (1, 0)))
+    parts = scattered(diag_2, parts.sum(0))
+    term_3 = term_3 - contract(lower_blocks[4], whole_1, (1, 0))
+    parts, got_3 = by_deadline(parts, from_partner(half_of(term_3, row % 2 ^ 1)))
+    term_3 = ordered(half_of(term_3, row % 2), got_3, 0)
     parts = gathered(parts)
-    terms = ordered(half_of(terms, row % 2), got_terms, 1)
-    below = below_of(whole_0, 0)
-    parts, terms, below, trail = by_deadline(parts, terms, below, trail)
-    term_2, term_3 = terms[0], terms[1]
-    solved_1 = parts.reshape(width, half)
-
-    parts = summed(term_2 - contract(lower_21, solved_1, (1, 0)))
-    parts, got_1 = by_deadline(parts, from_partner(solved_1))
-    parts = scattered(diag_2, parts.sum(0))
-    parts = gathered(parts)
-    whole_1 = ordered(solved_1, got_1, 1)
-    term_3 = term_3 - contract(lower_31, solved_1, (1, 0))
     below = below + below_of(whole_1, 1)
-    parts, term_3, below = by_deadline(parts, term_3, below)
+    parts, below, term_3 = by_deadline(parts, below, term_3)
     solved_2 = parts.reshape(width, half)
 
     parts = summed(term_3 - contract(lower_32, solved_2, (1, 0)))

time: 277 us -> 267 us (0.964)
  blocking collectives: 49.4 us -> 33.3 us
  waiting for transfers between devices: 94.2 us -> 97.8 us
    all_to_all x10 -> x11, waiting for transfers between devices: 52.8 us -> 87.1 us  [swap(): lax.all_to_all(parts, axis, 0, 0, axis_index_groups=groups, tiled=True)]
    ppermute x4, waiting for transfers between devices: 41.4 us -> 10.7 us  [from_partner(): return lax.ppermute(value, 'row', [(r, r ^ 1) for r in range(row_size)])]
    all_to_all x2 -> x1, blocking collectives: 49.4 us -> 33.3 us  [swap(): lax.all_to_all(parts, axis, 0, 0, axis_index_groups=groups, tiled=True)]
    unnamed x33 -> x29, local copies, waits for them, and re-layouts: 5.98 us -> 3.21 us
    all_to_all x10 -> x11, starting transfers between devices: 74.8 us -> 76.5 us  [swap(): lax.all_to_all(parts, axis, 0, 0, axis_index_groups=groups, tiled=True)]
    broadcast_in_dim x6 -> x7, local copies, waits for them, and re-layouts: 4.78 us -> 5.75 us  [copies(): return jnp.broadcast_to(part[None], (count,) + part.shape)]
  transfers between devices with their start and end apart: 14 -> 15, of which waited for: 9 -> 12; matrix products, arithmetic and copies ran while one was open for 10% -> 10% of each run, Pallas kernels for 0% -> 0%
where the time goes in v13:
time: 267 us; the launch traced here: 266 us
  waiting for transfers between devices  97.8 us (37%)
  starting transfers between devices  88.1 us (33%)
  blocking collectives  33.3 us (12%)
  local copies, waits for them, and re-layouts  20.3 us (8%)
  matrix products  18.3 us (7%)
  other arithmetic  6.89 us (3%)
    all_to_all x11, waiting for transfers between devices, swap(): lax.all_to_all(parts, axis, 0, 0, axis_index_groups=groups, tiled=True)  87.1 us
    all_to_all x11, starting transfers between devices, swap(): lax.all_to_all(parts, axis, 0, 0, axis_index_groups=groups, tiled=True)  76.5 us
    all_to_all x1, blocking collectives, swap(): lax.all_to_all(parts, axis, 0, 0, axis_index_groups=groups, tiled=True)  33.3 us
    dot_general x14, matrix products, contract(): lax.dot_general(left, right, (((axes[0],), (axes[1],)), ((), ())), precis...  18.3 us
    ppermute x4, starting transfers between devices, from_partner(): return lax.ppermute(value, 'row', [(r, r ^ 1) for r in range(row_size)])  11.6 us
    ppermute x4, waiting for transfers between devices, from_partner(): return lax.ppermute(value, 'row', [(r, r ^ 1) for r in range(row_size)])  10.7 us
    slice x1, local copies, waits for them, and re-layouts, shards(): trail_panel[:, :, j, :].reshape(trail_count * local_rows, width)  5.81 us
    broadcast_in_dim x7, local copies, waits for them, and re-layouts, copies(): return jnp.broadcast_to(part[None], (count,) + part.shape)  5.75 us
  transfers between devices with their start and end apart: 15, of which 12 were waited for; matrix products, arithmetic and copies ran while one was open for 10% of the time, Pallas kernels for 0%

profile of v13, /device:TPU:1, one launch (start us, length us, event | category | flops | bytes accessed | tf_op | source)
XLA Modules:
  0.0 265.8 jit_solution(8315004545678977928)
XLA Ops:
  3.2 33.3 %all_to_all.64 = f32[64,8,256]{2,1,0:T(8,128)S(1)} all-to-all(f32[64,8,256]{2,1,0:T(8,128)S(1)} %fusion.14), channel_id=1, replica_groups=mesh['row'=64,'col'=8] {'row'}, dimensions={0} | all-to-all | bytes 1048576 | tf_op jit(solution)/shard_map/all_to_all | solution.py:20
  37.4 7.8 %all-to-all-start.1 = ((f32[64,8,256]{2,1,0:T(8,128)}), f32[64,8,256]{2,1,0:T(8,128)S(1)}, u32[]{:S(2)}, u32[]{:S(2)}) async-start(f32[64,8,256]{2,1,0:T(8,128)} %broadcast_in_dim.19), calls=%async_computation.1 | async-start | bytes 1048576 | tf_op jit(solution)/shard_map/all_to_all | solution.py:20
  46.2 2.9 %collective-permute-start = (f32[4,64,512]{2,1,0:T(8,128)}, f32[4,64,512]{2,1,0:T(8,128)S(1)}, u32[]{:S(2)}, u32[]{:S(2)}) collective-permute-start(f32[4,64,512]{2,1,0:T(8,128)} %pad_maximum_fusion.2), channel_id=1, source_target_pairs={{0,8},{8,0},{16,24},{24,16},{32,40},{40,32},{48,56},{56,48},{64,72... | collective-permute-start | bytes 1572872 | tf_op jit(solution)/shard_map/ppermute | solution.py:47
  49.1 12.3 %all-to-all-done.1 = f32[64,8,256]{2,1,0:T(8,128)S(1)} async-done(((f32[64,8,256]{2,1,0:T(8,128)}), f32[64,8,256]{2,1,0:T(8,128)S(1)}, u32[]{:S(2)}, u32[]{:S(2)}) %all-to-all-start.1) | async-done | bytes 524320 | tf_op jit(solution)/shard_map/all_to_all | solution.py:20
  62.6 8.4 %all-to-all-start.2 = ((f32[8,64,256]{2,1,0:T(8,128)}), f32[8,64,256]{2,1,0:T(8,128)S(1)}, u32[]{:S(2)}, u32[]{:S(2)}) async-start(f32[8,64,256]{2,1,0:T(8,128)} %broadcast_in_dim.20), calls=%async_computation.2 | async-start | bytes 1048576 | tf_op jit(solution)/shard_map/all_to_all | solution.py:20
  71.1 9.5 %all-to-all-done.2 = f32[8,64,256]{2,1,0:T(8,128)S(1)} async-done(((f32[8,64,256]{2,1,0:T(8,128)}), f32[8,64,256]{2,1,0:T(8,128)S(1)}, u32[]{:S(2)}, u32[]{:S(2)}) %all-to-all-start.2) | async-done | bytes 524320 | tf_op jit(solution)/shard_map/all_to_all | solution.py:20
  83.1 5.2 %all-to-all-start.3 = ((f32[64,8,256]{2,1,0:T(8,128)}), f32[64,8,256]{2,1,0:T(8,128)S(1)}, u32[]{:S(2)}, u32[]{:S(2)}) async-start(f32[64,8,256]{2,1,0:T(8,128)} %bitcast.22), calls=%async_computation.3 | async-start | bytes 1048576 | tf_op jit(solution)/shard_map/all_to_all | solution.py:20
  88.8 2.9 %collective-permute-start.1 = (f32[64,128]{1,0:T(8,128)S(1)}, f32[64,128]{1,0:T(8,128)S(1)}, u32[]{:S(2)}, u32[]{:S(2)}) collective-permute-start(f32[64,128]{1,0:T(8,128)S(1)} %constant_dynamic-slice_fusion.5), channel_id=1, source_target_pairs={{0,8},{8,0},{16,24},{24,16},{32,40},{40,32},{48,56},{56,48},{64,72... | collective-permute-start | bytes 98312 | tf_op jit(solution)/shard_map/ppermute | solution.py:47
  91.7 5.8 %fusion.44 = (f32[4,64,1,512]{3,2,1,0:T(1,128)S(1)}, f32[4,64,1,512]{3,2,1,0:T(1,128)S(1)}, f32[4,64,1,512]{3,2,1,0:T(1,128)S(1)}, f32[4,64,1,512]{3,2,1,0:T(1,128)S(1)}) fusion(f32[4,64,4,512]{3,2,1,0:T(4,128)} %param.7), kind=kLoop, calls=%fused_computation.84 | loop fusion | bytes 4194304 | tf_op jit(solution)/shard_map/slice | solution.py:81
  99.3 5.3 %all-to-all-done.3 = f32[64,8,256]{2,1,0:T(8,128)S(1)} async-done(((f32[64,8,256]{2,1,0:T(8,128)}), f32[64,8,256]{2,1,0:T(8,128)S(1)}, u32[]{:S(2)}, u32[]{:S(2)}) %all-to-all-start.3) | async-done | bytes 524320 | tf_op jit(solution)/shard_map/all_to_all | solution.py:20
  105.6 9.0 %all-to-all-start.4 = ((f32[64,8,256]{2,1,0:T(8,128)}), f32[64,8,256]{2,1,0:T(8,128)S(1)}, u32[]{:S(2)}, u32[]{:S(2)}) async-start(f32[64,8,256]{2,1,0:T(8,128)} %broadcast_in_dim.22), calls=%async_computation.4 | async-start | bytes 1048576 | tf_op jit(solution)/shard_map/all_to_all | solution.py:20
  114.5 1.9 fusion.1
  118.4 2.7 %fusion.40 = f32[256,256]{1,0:T(8,128)} fusion(f32[256,512]{1,0:T(8,128)} %bitcast.132, f32[64,8,256]{2,1,0:T(8,128)S(1)} %all-to-all-done.1), kind=kOutput, calls=%fused_computation.80 | convolution fusion | flops 402653184 | bytes 1310720 | tf_op jit(solution)/shard_map/dot_general | solution.py:10
  121.2 9.9 %all-to-all-done.4 = f32[64,8,256]{2,1,0:T(8,128)S(1)} async-done(((f32[64,8,256]{2,1,0:T(8,128)}), f32[64,8,256]{2,1,0:T(8,128)S(1)}, u32[]{:S(2)}, u32[]{:S(2)}) %all-to-all-start.4) | async-done | bytes 524320 | tf_op jit(solution)/shard_map/all_to_all | solution.py:20
  132.3 7.5 %all-to-all-start.5 = ((f32[8,128,128]{2,1,0:T(8,128)}), f32[8,128,128]{2,1,0:T(8,128)}, u32[]{:S(2)}, u32[]{:S(2)}) async-start(f32[8,128,128]{2,1,0:T(8,128)} %broadcast_in_dim.23), calls=%async_computation.5 | async-start | bytes 1048576 | tf_op jit(solution)/shard_map/all_to_all | solution.py:20
  141.7 7.7 %all-to-all-done.5 = f32[8,128,128]{2,1,0:T(8,128)} async-done(((f32[8,128,128]{2,1,0:T(8,128)}), f32[8,128,128]{2,1,0:T(8,128)}, u32[]{:S(2)}, u32[]{:S(2)}) %all-to-all-start.5) | async-done | bytes 524320 | tf_op jit(solution)/shard_map/all_to_all | solution.py:20
  151.5 4.6 %all-to-all-start.6 = ((f32[32,16,128]{2,1,0:T(8,128)}), f32[32,16,128]{2,1,0:T(8,128)S(1)}, u32[]{:S(2)}, u32[]{:S(2)}) async-start(f32[32,16,128]{2,1,0:T(8,128)} %fusion.27), calls=%async_computation.6 | async-start | bytes 524288 | tf_op jit(solution)/shard_map/all_to_all | solution.py:20
  157.5 3.2 %collective-permute-start.2 = (f32[64,128]{1,0:T(8,128)S(1)}, f32[64,128]{1,0:T(8,128)S(1)}, u32[]{:S(2)}, u32[]{:S(2)}) collective-permute-start(f32[64,128]{1,0:T(8,128)S(1)} %constant_dynamic-slice_fusion.4), channel_id=1, source_target_pairs={{0,8},{8,0},{16,24},{24,16},{32,40},{40,32},{48,56},{56,48},{64,72... | collective-permute-start | bytes 98312 | tf_op jit(solution)/shard_map/ppermute | solution.py:47
  160.7 4.7 %collective-permute-done.2 = f32[64,128]{1,0:T(8,128)S(1)} collective-permute-done((f32[64,128]{1,0:T(8,128)S(1)}, f32[64,128]{1,0:T(8,128)S(1)}, u32[]{:S(2)}, u32[]{:S(2)}) %collective-permute-start.2) | collective-permute-done | bytes 32800 | tf_op jit(solution)/shard_map/ppermute | solution.py:47
  165.4 2.7 all-to-all-done.6
  168.8 8.0 %all-to-all-start.7 = ((f32[32,16,128]{2,1,0:T(8,128)}), f32[32,16,128]{2,1,0:T(8,128)S(1)}, u32[]{:S(2)}, u32[]{:S(2)}) async-start(f32[32,16,128]{2,1,0:T(8,128)} %broadcast_in_dim.24), calls=%async_computation.7 | async-start | bytes 524288 | tf_op jit(solution)/shard_map/all_to_all | solution.py:20
  176.8 2.8 %convolution_add_fusion.2 = f32[256,256]{1,0:T(8,128)} fusion(f32[256,256]{1,0:T(8,128)} %fusion.40, f32[256,512]{1,0:T(8,128)} %bitcast.131, f32[64,8,256]{2,1,0:T(8,128)S(1)} %all-to-all-done.4), kind=kOutput, calls=%fused_computation.9 | convolution fusion | flops 402718720 | bytes 1572864 | tf_op jit(solution)/shard_map/dot_general | solution.py:10
  179.7 9.3 %all-to-all-done.7 = f32[32,16,128]{2,1,0:T(8,128)S(1)} async-done(((f32[32,16,128]{2,1,0:T(8,128)}), f32[32,16,128]{2,1,0:T(8,128)S(1)}, u32[]{:S(2)}, u32[]{:S(2)}) %all-to-all-start.7) | async-done | bytes 262176 | tf_op jit(solution)/shard_map/all_to_all | solution.py:20
  190.2 5.8 %all-to-all-start.8 = ((f32[8,128,128]{2,1,0:T(8,128)}), f32[8,128,128]{2,1,0:T(8,128)S(1)}, u32[]{:S(2)}, u32[]{:S(2)}) async-start(f32[8,128,128]{2,1,0:T(8,128)} %broadcast_in_dim.25), calls=%async_computation.8 | async-start | bytes 1048576 | tf_op jit(solution)/shard_map/all_to_all | solution.py:20
  196.0 2.6 collective-permute-start.3
  199.7 6.0 %collective-permute-done.3 = f32[512,128]{1,0:T(8,128)S(1)} collective-permute-done((f32[512,128]{1,0:T(8,128)S(1)}, f32[512,128]{1,0:T(8,128)S(1)}, u32[]{:S(2)}, u32[]{:S(2)}) %collective-permute-start.3) | collective-permute-done | bytes 262176 | tf_op jit(solution)/shard_map/ppermute | solution.py:47
  207.4 4.9 %all-to-all-start.9 = ((f32[32,16,128]{2,1,0:T(8,128)}), f32[32,16,128]{2,1,0:T(8,128)S(1)}, u32[]{:S(2)}, u32[]{:S(2)}) async-start(f32[32,16,128]{2,1,0:T(8,128)} %fusion.25), calls=%async_computation.9 | async-start | bytes 524288 | tf_op jit(solution)/shard_map/all_to_all | solution.py:20
  212.6 11.6 %all-to-all-done.9 = f32[32,16,128]{2,1,0:T(8,128)S(1)} async-done(((f32[32,16,128]{2,1,0:T(8,128)}), f32[32,16,128]{2,1,0:T(8,128)S(1)}, u32[]{:S(2)}, u32[]{:S(2)}) %all-to-all-start.9) | async-done | bytes 262176 | tf_op jit(solution)/shard_map/all_to_all | solution.py:20
  225.1 7.1 %all-to-all-start.10 = ((f32[64,16,128]{2,1,0:T(8,128)}), f32[64,16,128]{2,1,0:T(8,128)S(1)}, u32[]{:S(2)}, u32[]{:S(2)}) async-start(f32[64,16,128]{2,1,0:T(8,128)} %broadcast_in_dim.26), calls=%async_computation.10 | async-start | bytes 1048576 | tf_op jit(solution)/shard_map/all_to_all | solution.py:20
  235.0 13.3 %all-to-all-done.10 = f32[64,16,128]{2,1,0:T(8,128)S(1)} async-done(((f32[64,16,128]{2,1,0:T(8,128)}), f32[64,16,128]{2,1,0:T(8,128)S(1)}, u32[]{:S(2)}, u32[]{:S(2)}) %all-to-all-start.10) | async-done | bytes 524320 | tf_op jit(solution)/shard_map/all_to_all | solution.py:20
  250.4 8.1 %all-to-all-start.11 = ((f32[8,32,256]{2,1,0:T(8,128)}), f32[8,32,256]{2,1,0:T(8,128)S(1)}, u32[]{:S(2)}, u32[]{:S(2)}) async-start(f32[8,32,256]{2,1,0:T(8,128)} %bitcast.44), calls=%async_computation.11 | async-start | bytes 524288 | tf_op jit(solution)/shard_map/all_to_all | solution.py:20
  259.4 5.6 %all-to-all-done.11 = f32[8,32,256]{2,1,0:T(8,128)S(1)} async-done(((f32[8,32,256]{2,1,0:T(8,128)}), f32[8,32,256]{2,1,0:T(8,128)S(1)}, u32[]{:S(2)}, u32[]{:S(2)}) %all-to-all-start.11) | async-done | bytes 262176 | tf_op jit(solution)/shard_map/all_to_all | solution.py:20
  (89 shorter events, 32.2 us)
Async XLA Ops:
  1.7 43.5 %copy-start.5 = (f32[4,512,64]{1,2,0:T(8,128)S(1)}, f32[4,512,64]{1,2,0:T(8,128)}, u32[]{:S(2)}) copy-start(f32[4,512,64]{1,2,0:T(8,128)} %param.5) | copy-start | bytes 1572868
  1.7 43.6 %copy-start.2 = (f32[6,64,512]{2,1,0:T(8,128)S(1)}, f32[6,64,512]{2,1,0:T(8,128)}, u32[]{:S(2)}) copy-start(f32[6,64,512]{2,1,0:T(8,128)} %param.6) | copy-start | bytes 2359300
  37.4 23.9 %all-to-all-start.1 = ((f32[64,8,256]{2,1,0:T(8,128)}), f32[64,8,256]{2,1,0:T(8,128)S(1)}, u32[]{:S(2)}, u32[]{:S(2)}) async-start(f32[64,8,256]{2,1,0:T(8,128)} %broadcast_in_dim.19), calls=%async_computation.1 | async-start | bytes 1048576 | tf_op jit(solution)/shard_map/all_to_all | solution.py:20
  45.3 17.3 %copy-start = (f32[1,64,512]{2,1,0:T(8,128)}, f32[1,64,512]{2,1,0:T(8,128)S(1)}, u32[]{:S(2)}) copy-start(f32[1,64,512]{2,1,0:T(8,128)S(1)} %get-tuple-element.65) | copy-start | bytes 393220
  45.3 35.3 %copy-start.3 = (f32[8,64,256]{2,1,0:T(8,128)S(1)}, f32[8,64,256]{2,1,0:T(8,128)}, u32[]{:S(2)}) copy-start(f32[8,64,256]{2,1,0:T(8,128)} %param.4) | copy-start | bytes 1572868
  46.2 24.9 %collective-permute-start = (f32[4,64,512]{2,1,0:T(8,128)}, f32[4,64,512]{2,1,0:T(8,128)S(1)}, u32[]{:S(2)}, u32[]{:S(2)}) collective-permute-start(f32[4,64,512]{2,1,0:T(8,128)} %pad_maximum_fusion.2), channel_id=1, source_target_pairs={{0,8},{8,0},{16,24},{24,16},{32,40},{40,32},{48,56},{56,48},{64,72... | collective-permute-start | bytes 1572872 | tf_op jit(solution)/shard_map/ppermute | solution.py:47
  62.6 17.9 %all-to-all-start.2 = ((f32[8,64,256]{2,1,0:T(8,128)}), f32[8,64,256]{2,1,0:T(8,128)S(1)}, u32[]{:S(2)}, u32[]{:S(2)}) async-start(f32[8,64,256]{2,1,0:T(8,128)} %broadcast_in_dim.20), calls=%async_computation.2 | async-start | bytes 1048576 | tf_op jit(solution)/shard_map/all_to_all | solution.py:20
  71.1 12.1 %copy-start.4 = (f32[4,64,512]{2,1,0:T(8,128)}, f32[4,64,512]{2,1,0:T(8,128)S(1)}, u32[]{:S(2)}) copy-start(f32[4,64,512]{2,1,0:T(8,128)S(1)} %collective-permute-done) | copy-start | bytes 1572868
  83.1 21.5 %all-to-all-start.3 = ((f32[64,8,256]{2,1,0:T(8,128)}), f32[64,8,256]{2,1,0:T(8,128)S(1)}, u32[]{:S(2)}, u32[]{:S(2)}) async-start(f32[64,8,256]{2,1,0:T(8,128)} %bitcast.22), calls=%async_computation.3 | async-start | bytes 1048576 | tf_op jit(solution)/shard_map/all_to_all | solution.py:20
  88.8 8.8 %copy-start.8 = (f32[64,256]{1,0:T(8,128)}, f32[64,256]{1,0:T(8,128)S(1)}, u32[]{:S(2)}) copy-start(f32[64,256]{1,0:T(8,128)S(1)} %fusion.2) | copy-start | bytes 196612
  88.8 10.5 %collective-permute-start.1 = (f32[64,128]{1,0:T(8,128)S(1)}, f32[64,128]{1,0:T(8,128)S(1)}, u32[]{:S(2)}, u32[]{:S(2)}) collective-permute-start(f32[64,128]{1,0:T(8,128)S(1)} %constant_dynamic-slice_fusion.5), channel_id=1, source_target_pairs={{0,8},{8,0},{16,24},{24,16},{32,40},{40,32},{48,56},{56,48},{64,72... | collective-permute-start | bytes 98312 | tf_op jit(solution)/shard_map/ppermute | solution.py:47
  99.3 15.2 %copy-start.9 = (f32[64,128]{1,0:T(8,128)}, f32[64,128]{1,0:T(8,128)S(1)}, u32[]{:S(2)}) copy-start(f32[64,128]{1,0:T(8,128)S(1)} %collective-permute-done.1) | copy-start | bytes 98308
  105.6 25.5 %all-to-all-start.4 = ((f32[64,8,256]{2,1,0:T(8,128)}), f32[64,8,256]{2,1,0:T(8,128)S(1)}, u32[]{:S(2)}, u32[]{:S(2)}) async-start(f32[64,8,256]{2,1,0:T(8,128)} %broadcast_in_dim.22), calls=%async_computation.4 | async-start | bytes 1048576 | tf_op jit(solution)/shard_map/all_to_all | solution.py:20
  116.4 1.2 copy-start.10
  132.3 17.1 %all-to-all-start.5 = ((f32[8,128,128]{2,1,0:T(8,128)}), f32[8,128,128]{2,1,0:T(8,128)}, u32[]{:S(2)}, u32[]{:S(2)}) async-start(f32[8,128,128]{2,1,0:T(8,128)} %broadcast_in_dim.23), calls=%async_computation.5 | async-start | bytes 1048576 | tf_op jit(solution)/shard_map/all_to_all | solution.py:20
  139.8 16.4 %copy-start.7 = (f32[64,256]{1,0:T(8,128)S(1)}, f32[64,256]{1,0:T(8,128)}, u32[]{:S(2)}) copy-start(f32[64,256]{1,0:T(8,128)} %fusion.1) | copy-start | bytes 196612
  151.5 16.5 %all-to-all-start.6 = ((f32[32,16,128]{2,1,0:T(8,128)}), f32[32,16,128]{2,1,0:T(8,128)S(1)}, u32[]{:S(2)}, u32[]{:S(2)}) async-start(f32[32,16,128]{2,1,0:T(8,128)} %fusion.27), calls=%async_computation.6 | async-start | bytes 524288 | tf_op jit(solution)/shard_map/all_to_all | solution.py:20
  157.5 7.9 %collective-permute-start.2 = (f32[64,128]{1,0:T(8,128)S(1)}, f32[64,128]{1,0:T(8,128)S(1)}, u32[]{:S(2)}, u32[]{:S(2)}) collective-permute-start(f32[64,128]{1,0:T(8,128)S(1)} %constant_dynamic-slice_fusion.4), channel_id=1, source_target_pairs={{0,8},{8,0},{16,24},{24,16},{32,40},{40,32},{48,56},{56,48},{64,72... | collective-permute-start | bytes 98312 | tf_op jit(solution)/shard_map/ppermute | solution.py:47
  168.8 20.1 %all-to-all-start.7 = ((f32[32,16,128]{2,1,0:T(8,128)}), f32[32,16,128]{2,1,0:T(8,128)S(1)}, u32[]{:S(2)}, u32[]{:S(2)}) async-start(f32[32,16,128]{2,1,0:T(8,128)} %broadcast_in_dim.24), calls=%async_computation.7 | async-start | bytes 524288 | tf_op jit(solution)/shard_map/all_to_all | solution.py:20
  190.2 15.5 %all-to-all-start.8 = ((f32[8,128,128]{2,1,0:T(8,128)}), f32[8,128,128]{2,1,0:T(8,128)S(1)}, u32[]{:S(2)}, u32[]{:S(2)}) async-start(f32[8,128,128]{2,1,0:T(8,128)} %broadcast_in_dim.25), calls=%async_computation.8 | async-start | bytes 1048576 | tf_op jit(solution)/shard_map/all_to_all | solution.py:20
  196.0 9.7 %collective-permute-start.3 = (f32[512,128]{1,0:T(8,128)S(1)}, f32[512,128]{1,0:T(8,128)S(1)}, u32[]{:S(2)}, u32[]{:S(2)}) collective-permute-start(f32[512,128]{1,0:T(8,128)S(1)} %bitcast.128), channel_id=1, source_target_pairs={{0,8},{8,0},{16,24},{24,16},{32,40},{40,32},{48,56},{56,48},{64,72... | collective-permute-start | bytes 786440 | tf_op jit(solution)/shard_map/ppermute | solution.py:47
  205.7 0.7 copy-start.6
  207.4 24.8 %slice-start = ((f32[8,64,256]{2,1,0:T(8,128)}), f32[4,64,256]{2,1,0:T(8,128)S(1)}, s32[]{:S(2)}) async-start(f32[8,64,256]{2,1,0:T(8,128)} %param.4), calls=%async_computation.12 | async-start | bytes 524288 | tf_op jit(solution)/shard_map/slice | solution.py:89
  207.4 16.8 %all-to-all-start.9 = ((f32[32,16,128]{2,1,0:T(8,128)}), f32[32,16,128]{2,1,0:T(8,128)S(1)}, u32[]{:S(2)}, u32[]{:S(2)}) async-start(f32[32,16,128]{2,1,0:T(8,128)} %fusion.25), calls=%async_computation.9 | async-start | bytes 524288 | tf_op jit(solution)/shard_map/all_to_all | solution.py:20
  225.1 8.7 %copy-start.1 = (f32[256,256]{1,0:T(8,128)S(1)}, f32[256,256]{1,0:T(8,128)}, u32[]{:S(2)}) copy-start(f32[256,256]{1,0:T(8,128)} %convolution_add_fusion.2) | copy-start | bytes 786436
  225.1 23.3 %all-to-all-start.10 = ((f32[64,16,128]{2,1,0:T(8,128)}), f32[64,16,128]{2,1,0:T(8,128)S(1)}, u32[]{:S(2)}, u32[]{:S(2)}) async-start(f32[64,16,128]{2,1,0:T(8,128)} %broadcast_in_dim.26), calls=%async_computation.10 | async-start | bytes 1048576 | tf_op jit(solution)/shard_map/all_to_all | solution.py:20
  250.4 14.6 %all-to-all-start.11 = ((f32[8,32,256]{2,1,0:T(8,128)}), f32[8,32,256]{2,1,0:T(8,128)S(1)}, u32[]{:S(2)}, u32[]{:S(2)}) async-start(f32[8,32,256]{2,1,0:T(8,128)} %bitcast.44), calls=%async_computation.11 | async-start | bytes 524288 | tf_op jit(solution)/shard_map/all_to_all | solution.py:20

commit v14 on v13

--- a/solution.py
+++ b/solution.py
@@ -42,6 +42,10 @@
     col = lax.axis_index("col")
     even = row % 2 == 0
     row_groups = [[r for r in range(row_size) if r % 2 == g] for g in range(2)]
+    pair_groups = [
+        [(r + g) * col_size + c for g in range(2) for c in range(col_size)]
+        for r in range(0, row_size, 2)
+    ]
 
     def from_partner(value):
         return lax.ppermute(value, "row", [(r, r ^ 1) for r in range(row_size)])
@@ -97,22 +101,30 @@
     parts = scattered_whole(own_diag[0], right_sides[0])
     whole_0 = gathered_whole(parts).reshape(width, column_count)
 
-    parts = summed(contract(lower_blocks[0], whole_0, (1, 0)))
-    own_shared = jnp.concatenate([own_diag[2:], lower_blocks[2:3], lower_blocks[5:]])
-    parts, got_shared = by_deadline(parts, from_partner(own_shared))
-    parts = scattered_whole(own_diag[1], right_sides[1] - parts.sum(0))
+    own_shared = jnp.concatenate([own_diag[1:], lower_blocks[2:3], lower_blocks[5:]])
+    got_shared = from_partner(own_shared)
+
+    term = own_term(1) - contract(lower_blocks[0], whole_0, (1, 0))
+    parts = jnp.stack([term[:, :half], term[:, half:]])[:, None]
+    parts = jnp.broadcast_to(parts, (2, col_size, local_rows, half))
+    parts = swap(parts.reshape(2 * col_size, local_rows, half), ("row", "col"), pair_groups)
+    parts, got_shared = by_deadline(parts, got_shared)
+    pair = ordered(own_shared, got_shared, 1)
+    diag_1, diag_2, diag_3, lower_21, lower_32 = [pair[i] for i in range(5)]
+    current = parts.reshape(2, col_size, local_rows, half).sum(1).reshape(2 * local_rows, half)
+    parts = scattered(diag_1, current)
     term_2 = own_term(2) - contract(lower_blocks[1], whole_0, (1, 0))
     parts, got_2, trail = by_deadline(parts, from_partner(half_of(term_2, row % 2 ^ 1)), trail)
-    pair = ordered(own_shared, got_shared, 1)
-    diag_2, diag_3, lower_21, lower_32 = [pair[i] for i in range(4)]
     term_2 = ordered(half_of(term_2, row % 2), got_2, 0)
     term_3 = own_term(3) - contract(lower_blocks[3], whole_0, (1, 0))
-    parts = gathered_whole(parts)
+    parts = gathered(parts)
     below = below_of(whole_0, 0)
-    parts, below, term_3 = by_deadline(parts, below, term_3)
-    whole_1 = parts.reshape(width, column_count)
+    parts, below, term_2, term_3 = by_deadline(parts, below, term_2, term_3)
+    solved_1 = parts.reshape(width, half)
 
-    parts = summed(term_2 - contract(lower_21, half_of(whole_1, row % 2), (1, 0)))
+    parts = summed(term_2 - contract(lower_21, solved_1, (1, 0)))
+    parts, got_1 = by_deadline(parts, from_partner(solved_1))
+    whole_1 = ordered(solved_1, got_1, 1)
     parts = scattered(diag_2, parts.sum(0))
     term_3 = term_3 - contract(lower_blocks[4], whole_1, (1, 0))
     parts, got_3 = by_deadline(parts, from_partner(half_of(term_3, row % 2 ^ 1)))

time: 267 us -> 271 us (1.015)
    ppermute x4 -> x5, waiting for transfers between devices: 10.7 us -> 30.9 us  [from_partner(): return lax.ppermute(value, 'row', [(r, r ^ 1) for r in range(row_size)])]
    all_to_all x11, waiting for transfers between devices: 87.1 us -> 69 us  [swap(): lax.all_to_all(parts, axis, 0, 0, axis_index_groups=groups, tiled=True)]
    ppermute x4 -> x5, starting transfers between devices: 11.6 us -> 14.5 us  [from_partner(): return lax.ppermute(value, 'row', [(r, r ^ 1) for r in range(row_size)])]
    broadcast_in_dim x7 -> x6, local copies, waits for them, and re-layouts: 5.75 us -> 4.8 us  [copies(): return jnp.broadcast_to(part[None], (count,) + part.shape)]
  transfers between devices with their start and end apart: 15 -> 16, of which waited for: 12 -> 13; matrix products, arithmetic and copies ran while one was open for 10% -> 9% of each run, Pallas kernels for 0% -> 0%
where the time goes in v14:
time: 271 us; the launch traced here: 270 us
  waiting for transfers between devices  99.9 us (37%)
  starting transfers between devices  90.2 us (33%)
  blocking collectives  33.3 us (12%)
  local copies, waits for them, and re-layouts  19.1 us (7%)
  matrix products  18.1 us (7%)
  other arithmetic  7.98 us (3%)
    all_to_all x11, starting transfers between devices, swap(): lax.all_to_all(parts, axis, 0, 0, axis_index_groups=groups, tiled=True)  75.7 us
    all_to_all x11, waiting for transfers between devices, swap(): lax.all_to_all(parts, axis, 0, 0, axis_index_groups=groups, tiled=True)  69 us
    all_to_all x1, blocking collectives, swap(): lax.all_to_all(parts, axis, 0, 0, axis_index_groups=groups, tiled=True)  33.3 us
    ppermute x5, waiting for transfers between devices, from_partner(): return lax.ppermute(value, 'row', [(r, r ^ 1) for r in range(row_size)])  30.9 us
    dot_general x14, matrix products, contract(): lax.dot_general(left, right, (((axes[0],), (axes[1],)), ((), ())), precis...  18.1 us
    ppermute x5, starting transfers between devices, from_partner(): return lax.ppermute(value, 'row', [(r, r ^ 1) for r in range(row_size)])  14.5 us
    slice x1, local copies, waits for them, and re-layouts, shards(): trail_panel[:, :, j, :].reshape(trail_count * local_rows, width)  5.82 us
  transfers between devices with their start and end apart: 16, of which 13 were waited for; matrix products, arithmetic and copies ran while one was open for 9% of the time, Pallas kernels for 0%

profile of v14, /device:TPU:1, one launch (start us, length us, event | category | flops | bytes accessed | tf_op | source)
XLA Modules:
  0.0 269.7 jit_solution(9033679701156784951)
XLA Ops:
  3.1 33.3 %all_to_all.64 = f32[64,8,256]{2,1,0:T(8,128)S(1)} all-to-all(f32[64,8,256]{2,1,0:T(8,128)S(1)} %fusion.18), channel_id=1, replica_groups=mesh['row'=64,'col'=8] {'row'}, dimensions={0} | all-to-all | bytes 1048576 | tf_op jit(solution)/shard_map/all_to_all | solution.py:20
  37.3 7.8 %all-to-all-start.1 = ((f32[64,8,256]{2,1,0:T(8,128)}), f32[64,8,256]{2,1,0:T(8,128)S(1)}, u32[]{:S(2)}, u32[]{:S(2)}) async-start(f32[64,8,256]{2,1,0:T(8,128)} %broadcast_in_dim.21), calls=%async_computation.1 | async-start | bytes 1048576 | tf_op jit(solution)/shard_map/all_to_all | solution.py:20
  45.2 16.1 %all-to-all-done.1 = f32[64,8,256]{2,1,0:T(8,128)S(1)} async-done(((f32[64,8,256]{2,1,0:T(8,128)}), f32[64,8,256]{2,1,0:T(8,128)S(1)}, u32[]{:S(2)}, u32[]{:S(2)}) %all-to-all-start.1) | async-done | bytes 524320 | tf_op jit(solution)/shard_map/all_to_all | solution.py:20
  62.5 8.9 %all-to-all-start.2 = ((f32[16,64,128]{2,1,0:T(8,128)}), f32[16,64,128]{2,1,0:T(8,128)S(1)}, u32[]{:S(2)}, u32[]{:S(2)}) async-start(f32[16,64,128]{2,1,0:T(8,128)} %bitcast.12), calls=%async_computation.2 | async-start | bytes 1048576 | tf_op jit(solution)/shard_map/all_to_all | solution.py:20
  72.4 3.3 %collective-permute-start = (f32[5,64,512]{2,1,0:T(8,128)}, f32[5,64,512]{2,1,0:T(8,128)}, u32[]{:S(2)}, u32[]{:S(2)}) collective-permute-start(f32[5,64,512]{2,1,0:T(8,128)} %pad_maximum_fusion), channel_id=1, source_target_pairs={{0,8},{8,0},{16,24},{24,16},{32,40},{40,32},{48,56},{56,48},{64,72... | collective-permute-start | bytes 1966088 | tf_op jit(solution)/shard_map/ppermute | solution.py:51
  75.7 5.8 %fusion.44 = (f32[4,64,1,512]{3,2,1,0:T(1,128)S(1)}, f32[4,64,1,512]{3,2,1,0:T(1,128)S(1)}, f32[4,64,1,512]{3,2,1,0:T(1,128)S(1)}, f32[4,64,1,512]{3,2,1,0:T(1,128)S(1)}) fusion(f32[4,64,4,512]{3,2,1,0:T(4,128)} %param.7), kind=kLoop, calls=%fused_computation.92 | loop fusion | bytes 4194304 | tf_op jit(solution)/shard_map/slice | solution.py:85
  84.1 9.5 %collective-permute-done = f32[5,64,512]{2,1,0:T(8,128)} collective-permute-done((f32[5,64,512]{2,1,0:T(8,128)}, f32[5,64,512]{2,1,0:T(8,128)}, u32[]{:S(2)}, u32[]{:S(2)}) %collective-permute-start) | collective-permute-done | bytes 655392 | tf_op jit(solution)/shard_map/ppermute | solution.py:51
  97.0 4.9 %all-to-all-start.3 = ((f32[32,16,128]{2,1,0:T(8,128)}), f32[32,16,128]{2,1,0:T(8,128)S(1)}, u32[]{:S(2)}, u32[]{:S(2)}) async-start(f32[32,16,128]{2,1,0:T(8,128)} %fusion.46), calls=%async_computation.3 | async-start | bytes 524288 | tf_op jit(solution)/shard_map/all_to_all | solution.py:20
  103.3 2.4 collective-permute-start.1
  107.0 4.4 %collective-permute-done.1 = f32[64,128]{1,0:T(8,128)S(1)} collective-permute-done((f32[64,128]{1,0:T(8,128)S(1)}, f32[64,128]{1,0:T(8,128)S(1)}, u32[]{:S(2)}, u32[]{:S(2)}) %collective-permute-start.1) | collective-permute-done | bytes 32800 | tf_op jit(solution)/shard_map/ppermute | solution.py:51
  111.4 2.4 all-to-all-done.3
  114.5 7.1 %all-to-all-start.4 = ((f32[32,16,128]{2,1,0:T(8,128)}), f32[32,16,128]{2,1,0:T(8,128)S(1)}, u32[]{:S(2)}, u32[]{:S(2)}) async-start(f32[32,16,128]{2,1,0:T(8,128)} %broadcast_in_dim.23), calls=%async_computation.4 | async-start | bytes 524288 | tf_op jit(solution)/shard_map/all_to_all | solution.py:20
  123.3 9.9 %all-to-all-done.4 = f32[32,16,128]{2,1,0:T(8,128)S(1)} async-done(((f32[32,16,128]{2,1,0:T(8,128)}), f32[32,16,128]{2,1,0:T(8,128)S(1)}, u32[]{:S(2)}, u32[]{:S(2)}) %all-to-all-start.4) | async-done | bytes 262176 | tf_op jit(solution)/shard_map/all_to_all | solution.py:20
  135.3 7.6 %all-to-all-start.5 = ((f32[8,128,128]{2,1,0:T(8,128)}), f32[8,128,128]{2,1,0:T(8,128)S(1)}, u32[]{:S(2)}, u32[]{:S(2)}) async-start(f32[8,128,128]{2,1,0:T(8,128)} %broadcast_in_dim.24), calls=%async_computation.5 | async-start | bytes 1048576 | tf_op jit(solution)/shard_map/all_to_all | solution.py:20
  142.9 2.9 %collective-permute-start.2 = (f32[512,128]{1,0:T(8,128)S(1)}, f32[512,128]{1,0:T(8,128)}, u32[]{:S(2)}, u32[]{:S(2)}) collective-permute-start(f32[512,128]{1,0:T(8,128)S(1)} %bitcast.134), channel_id=1, source_target_pairs={{0,8},{8,0},{16,24},{24,16},{32,40},{40,32},{48,56},{56,48},{64,72... | collective-permute-start | bytes 786440 | tf_op jit(solution)/shard_map/ppermute | solution.py:51
  147.6 5.2 %collective-permute-done.2 = f32[512,128]{1,0:T(8,128)} collective-permute-done((f32[512,128]{1,0:T(8,128)S(1)}, f32[512,128]{1,0:T(8,128)}, u32[]{:S(2)}, u32[]{:S(2)}) %collective-permute-start.2) | collective-permute-done | bytes 262176 | tf_op jit(solution)/shard_map/ppermute | solution.py:51
  152.8 2.0 fusion.30
  154.9 4.6 %all-to-all-start.6 = ((f32[32,16,128]{2,1,0:T(8,128)}), f32[32,16,128]{2,1,0:T(8,128)}, u32[]{:S(2)}, u32[]{:S(2)}) async-start(f32[32,16,128]{2,1,0:T(8,128)} %fusion.30), calls=%async_computation.6 | async-start | bytes 524288 | tf_op jit(solution)/shard_map/all_to_all | solution.py:20
  161.8 3.1 %collective-permute-start.3 = (f32[64,128]{1,0:T(8,128)S(1)}, f32[64,128]{1,0:T(8,128)S(1)}, u32[]{:S(2)}, u32[]{:S(2)}) collective-permute-start(f32[64,128]{1,0:T(8,128)S(1)} %constant_dynamic-slice_fusion.3), channel_id=1, source_target_pairs={{0,8},{8,0},{16,24},{24,16},{32,40},{40,32},{48,56},{56,48},{64,72... | collective-permute-start | bytes 98312 | tf_op jit(solution)/shard_map/ppermute | solution.py:51
  164.9 4.9 %collective-permute-done.3 = f32[64,128]{1,0:T(8,128)S(1)} collective-permute-done((f32[64,128]{1,0:T(8,128)S(1)}, f32[64,128]{1,0:T(8,128)S(1)}, u32[]{:S(2)}, u32[]{:S(2)}) %collective-permute-start.3) | collective-permute-done | bytes 32800 | tf_op jit(solution)/shard_map/ppermute | solution.py:51
  173.2 7.4 %all-to-all-start.7 = ((f32[32,16,128]{2,1,0:T(8,128)}), f32[32,16,128]{2,1,0:T(8,128)S(1)}, u32[]{:S(2)}, u32[]{:S(2)}) async-start(f32[32,16,128]{2,1,0:T(8,128)} %broadcast_in_dim.25), calls=%async_computation.7 | async-start | bytes 524288 | tf_op jit(solution)/shard_map/all_to_all | solution.py:20
  180.6 2.7 %convolution_add_fusion.2 = f32[256,256]{1,0:T(8,128)} fusion(f32[256,256]{1,0:T(8,128)S(1)} %fusion.40, f32[256,512]{1,0:T(8,128)} %bitcast.137, f32[512,128]{1,0:T(8,128)S(1)} %get-tuple-element.76, f32[512,128]{1,0:T(8,128)S(1)} %get-tuple-element.75), kind=kOutput, calls=%fused_computation.10 | convolution fusion | flops 402849792 | bytes 1572864 | tf_op jit(solution)/shard_map/dot_general | solution.py:10
  183.4 9.0 %all-to-all-done.7 = f32[32,16,128]{2,1,0:T(8,128)S(1)} async-done(((f32[32,16,128]{2,1,0:T(8,128)}), f32[32,16,128]{2,1,0:T(8,128)S(1)}, u32[]{:S(2)}, u32[]{:S(2)}) %all-to-all-start.7) | async-done | bytes 262176 | tf_op jit(solution)/shard_map/all_to_all | solution.py:20
  193.6 7.5 %all-to-all-start.8 = ((f32[8,128,128]{2,1,0:T(8,128)}), f32[8,128,128]{2,1,0:T(8,128)S(1)}, u32[]{:S(2)}, u32[]{:S(2)}) async-start(f32[8,128,128]{2,1,0:T(8,128)} %broadcast_in_dim.26), calls=%async_computation.8 | async-start | bytes 1048576 | tf_op jit(solution)/shard_map/all_to_all | solution.py:20
  201.2 2.8 %collective-permute-start.4 = (f32[512,128]{1,0:T(8,128)S(1)}, f32[512,128]{1,0:T(8,128)S(1)}, u32[]{:S(2)}, u32[]{:S(2)}) collective-permute-start(f32[512,128]{1,0:T(8,128)S(1)} %bitcast.132), channel_id=1, source_target_pairs={{0,8},{8,0},{16,24},{24,16},{32,40},{40,32},{48,56},{56,48},{64,72... | collective-permute-start | bytes 786440 | tf_op jit(solution)/shard_map/ppermute | solution.py:51
  204.1 6.9 %collective-permute-done.4 = f32[512,128]{1,0:T(8,128)S(1)} collective-permute-done((f32[512,128]{1,0:T(8,128)S(1)}, f32[512,128]{1,0:T(8,128)S(1)}, u32[]{:S(2)}, u32[]{:S(2)}) %collective-permute-start.4) | collective-permute-done | bytes 262176 | tf_op jit(solution)/shard_map/ppermute | solution.py:51
  212.1 4.0 %all-to-all-start.9 = ((f32[32,16,128]{2,1,0:T(8,128)}), f32[32,16,128]{2,1,0:T(8,128)S(1)}, u32[]{:S(2)}, u32[]{:S(2)}) async-start(f32[32,16,128]{2,1,0:T(8,128)} %fusion.28), calls=%async_computation.9 | async-start | bytes 524288 | tf_op jit(solution)/shard_map/all_to_all | solution.py:20
  216.4 11.7 %all-to-all-done.9 = f32[32,16,128]{2,1,0:T(8,128)S(1)} async-done(((f32[32,16,128]{2,1,0:T(8,128)}), f32[32,16,128]{2,1,0:T(8,128)S(1)}, u32[]{:S(2)}, u32[]{:S(2)}) %all-to-all-start.9) | async-done | bytes 262176 | tf_op jit(solution)/shard_map/all_to_all | solution.py:20
  229.0 7.0 %all-to-all-start.10 = ((f32[64,16,128]{2,1,0:T(8,128)}), f32[64,16,128]{2,1,0:T(8,128)S(1)}, u32[]{:S(2)}, u32[]{:S(2)}) async-start(f32[64,16,128]{2,1,0:T(8,128)} %broadcast_in_dim.27), calls=%async_computation.10 | async-start | bytes 1048576 | tf_op jit(solution)/shard_map/all_to_all | solution.py:20
  238.8 12.7 %all-to-all-done.10 = f32[64,16,128]{2,1,0:T(8,128)S(1)} async-done(((f32[64,16,128]{2,1,0:T(8,128)}), f32[64,16,128]{2,1,0:T(8,128)S(1)}, u32[]{:S(2)}, u32[]{:S(2)}) %all-to-all-start.10) | async-done | bytes 524320 | tf_op jit(solution)/shard_map/all_to_all | solution.py:20
  253.5 8.9 %all-to-all-start.11 = ((f32[8,32,256]{2,1,0:T(8,128)}), f32[8,32,256]{2,1,0:T(8,128)S(1)}, u32[]{:S(2)}, u32[]{:S(2)}) async-start(f32[8,32,256]{2,1,0:T(8,128)} %bitcast.49), calls=%async_computation.11 | async-start | bytes 524288 | tf_op jit(solution)/shard_map/all_to_all | solution.py:20
  263.3 5.6 %all-to-all-done.11 = f32[8,32,256]{2,1,0:T(8,128)S(1)} async-done(((f32[8,32,256]{2,1,0:T(8,128)}), f32[8,32,256]{2,1,0:T(8,128)S(1)}, u32[]{:S(2)}, u32[]{:S(2)}) %all-to-all-start.11) | async-done | bytes 262176 | tf_op jit(solution)/shard_map/all_to_all | solution.py:20
  (89 shorter events, 36.3 us)
Async XLA Ops:
  36.4 8.8 %copy-start.6 = (f32[4,512,64]{1,2,0:T(8,128)S(1)}, f32[4,512,64]{1,2,0:T(8,128)}, u32[]{:S(2)}) copy-start(f32[4,512,64]{1,2,0:T(8,128)} %param.5) | copy-start | bytes 1572868
  36.4 24.8 %copy-start.4 = (f32[6,64,512]{2,1,0:T(8,128)S(1)}, f32[6,64,512]{2,1,0:T(8,128)}, u32[]{:S(2)}) copy-start(f32[6,64,512]{2,1,0:T(8,128)} %param.6) | copy-start | bytes 2359300
  36.5 24.8 %copy-start.5 = (f32[8,64,256]{2,1,0:T(8,128)S(1)}, f32[8,64,256]{2,1,0:T(8,128)}, u32[]{:S(2)}) copy-start(f32[8,64,256]{2,1,0:T(8,128)} %param.4) | copy-start | bytes 1572868
  37.3 23.9 %all-to-all-start.1 = ((f32[64,8,256]{2,1,0:T(8,128)}), f32[64,8,256]{2,1,0:T(8,128)S(1)}, u32[]{:S(2)}, u32[]{:S(2)}) async-start(f32[64,8,256]{2,1,0:T(8,128)} %broadcast_in_dim.21), calls=%async_computation.1 | async-start | bytes 1048576 | tf_op jit(solution)/shard_map/all_to_all | solution.py:20
  62.5 31.1 %all-to-all-start.2 = ((f32[16,64,128]{2,1,0:T(8,128)}), f32[16,64,128]{2,1,0:T(8,128)S(1)}, u32[]{:S(2)}, u32[]{:S(2)}) async-start(f32[16,64,128]{2,1,0:T(8,128)} %bitcast.12), calls=%async_computation.2 | async-start | bytes 1048576 | tf_op jit(solution)/shard_map/all_to_all | solution.py:20
  72.4 21.2 %collective-permute-start = (f32[5,64,512]{2,1,0:T(8,128)}, f32[5,64,512]{2,1,0:T(8,128)}, u32[]{:S(2)}, u32[]{:S(2)}) collective-permute-start(f32[5,64,512]{2,1,0:T(8,128)} %pad_maximum_fusion), channel_id=1, source_target_pairs={{0,8},{8,0},{16,24},{24,16},{32,40},{40,32},{48,56},{56,48},{64,72... | collective-permute-start | bytes 1966088 | tf_op jit(solution)/shard_map/ppermute | solution.py:51
  97.0 16.8 %all-to-all-start.3 = ((f32[32,16,128]{2,1,0:T(8,128)}), f32[32,16,128]{2,1,0:T(8,128)S(1)}, u32[]{:S(2)}, u32[]{:S(2)}) async-start(f32[32,16,128]{2,1,0:T(8,128)} %fusion.46), calls=%async_computation.3 | async-start | bytes 524288 | tf_op jit(solution)/shard_map/all_to_all | solution.py:20
  101.8 20.4 %copy-start.1 = (f32[4,64,1,512]{3,1,0,2:T(8,128)S(1)}, f32[4,64,1,512]{3,1,0,2:T(8,128)}, u32[]{:S(2)}) copy-start(f32[4,64,1,512]{3,1,0,2:T(8,128)} %copy.66) | copy-start | bytes 1572868
  103.3 8.1 %collective-permute-start.1 = (f32[64,128]{1,0:T(8,128)S(1)}, f32[64,128]{1,0:T(8,128)S(1)}, u32[]{:S(2)}, u32[]{:S(2)}) collective-permute-start(f32[64,128]{1,0:T(8,128)S(1)} %constant_dynamic-slice_fusion.4), channel_id=1, source_target_pairs={{0,8},{8,0},{16,24},{24,16},{32,40},{40,32},{48,56},{56,48},{64,72... | collective-permute-start | bytes 98312 | tf_op jit(solution)/shard_map/ppermute | solution.py:51
  114.5 18.7 %all-to-all-start.4 = ((f32[32,16,128]{2,1,0:T(8,128)}), f32[32,16,128]{2,1,0:T(8,128)S(1)}, u32[]{:S(2)}, u32[]{:S(2)}) async-start(f32[32,16,128]{2,1,0:T(8,128)} %broadcast_in_dim.23), calls=%async_computation.4 | async-start | bytes 524288 | tf_op jit(solution)/shard_map/all_to_all | solution.py:20
  135.3 17.5 %all-to-all-start.5 = ((f32[8,128,128]{2,1,0:T(8,128)}), f32[8,128,128]{2,1,0:T(8,128)S(1)}, u32[]{:S(2)}, u32[]{:S(2)}) async-start(f32[8,128,128]{2,1,0:T(8,128)} %broadcast_in_dim.24), calls=%async_computation.5 | async-start | bytes 1048576 | tf_op jit(solution)/shard_map/all_to_all | solution.py:20
  142.9 9.9 %collective-permute-start.2 = (f32[512,128]{1,0:T(8,128)S(1)}, f32[512,128]{1,0:T(8,128)}, u32[]{:S(2)}, u32[]{:S(2)}) collective-permute-start(f32[512,128]{1,0:T(8,128)S(1)} %bitcast.134), channel_id=1, source_target_pairs={{0,8},{8,0},{16,24},{24,16},{32,40},{40,32},{48,56},{56,48},{64,72... | collective-permute-start | bytes 786440 | tf_op jit(solution)/shard_map/ppermute | solution.py:51
  154.9 16.6 %all-to-all-start.6 = ((f32[32,16,128]{2,1,0:T(8,128)}), f32[32,16,128]{2,1,0:T(8,128)}, u32[]{:S(2)}, u32[]{:S(2)}) async-start(f32[32,16,128]{2,1,0:T(8,128)} %fusion.30), calls=%async_computation.6 | async-start | bytes 524288 | tf_op jit(solution)/shard_map/all_to_all | solution.py:20
  161.8 8.0 %collective-permute-start.3 = (f32[64,128]{1,0:T(8,128)S(1)}, f32[64,128]{1,0:T(8,128)S(1)}, u32[]{:S(2)}, u32[]{:S(2)}) collective-permute-start(f32[64,128]{1,0:T(8,128)S(1)} %constant_dynamic-slice_fusion.3), channel_id=1, source_target_pairs={{0,8},{8,0},{16,24},{24,16},{32,40},{40,32},{48,56},{56,48},{64,72... | collective-permute-start | bytes 98312 | tf_op jit(solution)/shard_map/ppermute | solution.py:51
  173.2 19.2 %all-to-all-start.7 = ((f32[32,16,128]{2,1,0:T(8,128)}), f32[32,16,128]{2,1,0:T(8,128)S(1)}, u32[]{:S(2)}, u32[]{:S(2)}) async-start(f32[32,16,128]{2,1,0:T(8,128)} %broadcast_in_dim.25), calls=%async_computation.7 | async-start | bytes 524288 | tf_op jit(solution)/shard_map/all_to_all | solution.py:20
  192.4 11.6 %copy-start.3 = (f32[512,128]{0,1:T(8,128)S(1)}, f32[512,128]{0,1:T(8,128)}, u32[]{:S(2)}) copy-start(f32[512,128]{0,1:T(8,128)} %get-tuple-element.67) | copy-start | bytes 786436
  193.6 17.4 %all-to-all-start.8 = ((f32[8,128,128]{2,1,0:T(8,128)}), f32[8,128,128]{2,1,0:T(8,128)S(1)}, u32[]{:S(2)}, u32[]{:S(2)}) async-start(f32[8,128,128]{2,1,0:T(8,128)} %broadcast_in_dim.26), calls=%async_computation.8 | async-start | bytes 1048576 | tf_op jit(solution)/shard_map/all_to_all | solution.py:20
  201.2 9.8 %collective-permute-start.4 = (f32[512,128]{1,0:T(8,128)S(1)}, f32[512,128]{1,0:T(8,128)S(1)}, u32[]{:S(2)}, u32[]{:S(2)}) collective-permute-start(f32[512,128]{1,0:T(8,128)S(1)} %bitcast.132), channel_id=1, source_target_pairs={{0,8},{8,0},{16,24},{24,16},{32,40},{40,32},{48,56},{56,48},{64,72... | collective-permute-start | bytes 786440 | tf_op jit(solution)/shard_map/ppermute | solution.py:51
  211.0 5.4 %copy-start.7 = (f32[512,128]{1,0:T(8,128)}, f32[512,128]{1,0:T(8,128)S(1)}, u32[]{:S(2)}) copy-start(f32[512,128]{1,0:T(8,128)S(1)} %collective-permute-done.4) | copy-start | bytes 786436
  212.1 16.0 %all-to-all-start.9 = ((f32[32,16,128]{2,1,0:T(8,128)}), f32[32,16,128]{2,1,0:T(8,128)S(1)}, u32[]{:S(2)}, u32[]{:S(2)}) async-start(f32[32,16,128]{2,1,0:T(8,128)} %fusion.28), calls=%async_computation.9 | async-start | bytes 524288 | tf_op jit(solution)/shard_map/all_to_all | solution.py:20
  216.4 19.6 %slice-start = ((f32[8,64,256]{2,1,0:T(8,128)}), f32[4,64,256]{2,1,0:T(8,128)S(1)}, s32[]{:S(2)}) async-start(f32[8,64,256]{2,1,0:T(8,128)} %param.4), calls=%async_computation.12 | async-start | bytes 524288 | tf_op jit(solution)/shard_map/slice | solution.py:93
  229.0 22.5 %all-to-all-start.10 = ((f32[64,16,128]{2,1,0:T(8,128)}), f32[64,16,128]{2,1,0:T(8,128)S(1)}, u32[]{:S(2)}, u32[]{:S(2)}) async-start(f32[64,16,128]{2,1,0:T(8,128)} %broadcast_in_dim.27), calls=%async_computation.10 | async-start | bytes 1048576 | tf_op jit(solution)/shard_map/all_to_all | solution.py:20
  236.0 1.6 copy-start
  236.0 1.6 copy-start.2
  253.5 15.4 %all-to-all-start.11 = ((f32[8,32,256]{2,1,0:T(8,128)}), f32[8,32,256]{2,1,0:T(8,128)S(1)}, u32[]{:S(2)}, u32[]{:S(2)}) async-start(f32[8,32,256]{2,1,0:T(8,128)} %bitcast.49), calls=%async_computation.11 | async-start | bytes 524288 | tf_op jit(solution)/shard_map/all_to_all | solution.py:20

commit v15 on v14

--- a/solution.py
+++ b/solution.py
@@ -81,10 +81,6 @@
         return jnp.where(col == 0, right_sides[block_row], 0.0)
 
     own_diag = diag_inverse.transpose(0, 2, 1)
-    trail = [
-        trail_panel[:, :, j, :].reshape(trail_count * local_rows, width) for j in range(step_count)
-    ]
-
     def below_of(whole, block_row):
         return contract(whole, trail[block_row], (0, 1))
 
@@ -108,18 +104,26 @@
     parts = jnp.stack([term[:, :half], term[:, half:]])[:, None]
     parts = jnp.broadcast_to(parts, (2, col_size, local_rows, half))
     parts = swap(parts.reshape(2 * col_size, local_rows, half), ("row", "col"), pair_groups)
-    parts, got_shared = by_deadline(parts, got_shared)
-    pair = ordered(own_shared, got_shared, 1)
-    diag_1, diag_2, diag_3, lower_21, lower_32 = [pair[i] for i in range(5)]
+    diag_1 = ordered(own_shared[0], got_shared[0], 0)
+    parts, diag_1, trail_panel, own_shared, got_shared = by_deadline(
+        parts, diag_1, trail_panel, own_shared, got_shared
+    )
+    pair = ordered(own_shared[1:], got_shared[1:], 1)
+    diag_2, diag_3, lower_21, lower_32 = [pair[i] for i in range(4)]
+    trail = [
+        trail_panel[:, :, j, :].reshape(trail_count * local_rows, width) for j in range(step_count)
+    ]
     current = parts.reshape(2, col_size, local_rows, half).sum(1).reshape(2 * local_rows, half)
     parts = scattered(diag_1, current)
     term_2 = own_term(2) - contract(lower_blocks[1], whole_0, (1, 0))
-    parts, got_2, trail = by_deadline(parts, from_partner(half_of(term_2, row % 2 ^ 1)), trail)
+    parts, got_2 = by_deadline(parts, from_partner(half_of(term_2, row % 2 ^ 1)))
     term_2 = ordered(half_of(term_2, row % 2), got_2, 0)
     term_3 = own_term(3) - contract(lower_blocks[3], whole_0, (1, 0))
     parts = gathered(parts)
     below = below_of(whole_0, 0)
-    parts, below, term_2, term_3 = by_deadline(parts, below, term_2, term_3)
+    parts, below, term_2, term_3, lower_21, trail = by_deadline(
+        parts, below, term_2, term_3, lower_21, trail
+    )
     solved_1 = parts.reshape(width, half)
 
     parts = summed(term_2 - contract(lower_21, solved_1, (1, 0)))

time: 271 us -> 266 us (0.982)
  waiting for transfers between devices: 99.9 us -> 83.1 us
  starting transfers between devices: 90.2 us -> 94.3 us
  local copies, waits for them, and re-layouts: 19.1 us -> 22.8 us
  other arithmetic: 7.98 us -> 11.1 us
    ppermute x5, waiting for transfers between devices: 30.9 us -> 21.7 us  [from_partner(): return lax.ppermute(value, 'row', [(r, r ^ 1) for r in range(row_size)])]
    all_to_all x11, waiting for transfers between devices: 69 us -> 61.4 us  [swap(): lax.all_to_all(parts, axis, 0, 0, axis_index_groups=groups, tiled=True)]
    all_to_all x11, starting transfers between devices: 75.7 us -> 82.3 us  [swap(): lax.all_to_all(parts, axis, 0, 0, axis_index_groups=groups, tiled=True)]
    optimization_barrier x0 -> x2, local copies, waits for them, and re-layouts: none -> 6.18 us  [by_deadline(): return lax.optimization_barrier(values)]
    slice x1, local copies, waits for them, and re-layouts: 5.82 us -> 1.2 us  [shards(): trail_panel[:, :, j, :].reshape(trail_count * local_rows, width)]
    dot_general x5 -> x0, local copies, waits for them, and re-layouts: 3.06 us -> none  [contract(): lax.dot_general(left, right, (((axes[0],), (axes[1],)), ((), ())), precis...]
  transfers between devices with their start and end apart: 16 -> 16, of which waited for: 13 -> 12; matrix products, arithmetic and copies ran while one was open for 9% -> 14% of each run, Pallas kernels for 0% -> 0%
where the time goes in v15:
time: 266 us; the launch traced here: 264 us
  starting transfers between devices  94.3 us (35%)
  waiting for transfers between devices  83.1 us (31%)
  blocking collectives  33.3 us (13%)
  local copies, waits for them, and re-layouts  22.8 us (9%)
  matrix products  18.6 us (7%)
  other arithmetic  11.1 us (4%)
    all_to_all x11, starting transfers between devices, swap(): lax.all_to_all(parts, axis, 0, 0, axis_index_groups=groups, tiled=True)  82.3 us
    all_to_all x11, waiting for transfers between devices, swap(): lax.all_to_all(parts, axis, 0, 0, axis_index_groups=groups, tiled=True)  61.4 us
    all_to_all x1, blocking collectives, swap(): lax.all_to_all(parts, axis, 0, 0, axis_index_groups=groups, tiled=True)  33.3 us
    ppermute x5, waiting for transfers between devices, from_partner(): return lax.ppermute(value, 'row', [(r, r ^ 1) for r in range(row_size)])  21.7 us
    dot_general x14, matrix products, contract(): lax.dot_general(left, right, (((axes[0],), (axes[1],)), ((), ())), precis...  18.6 us
    ppermute x5, starting transfers between devices, from_partner(): return lax.ppermute(value, 'row', [(r, r ^ 1) for r in range(row_size)])  12.1 us
    optimization_barrier x2, local copies, waits for them, and re-layouts, by_deadline(): return lax.optimization_barrier(values)  6.18 us
  transfers between devices with their start and end apart: 16, of which 12 were waited for; matrix products, arithmetic and copies ran while one was open for 14% of the time, Pallas kernels for 0%

profile of v15, /device:TPU:1, one launch (start us, length us, event | category | flops | bytes accessed | tf_op | source)
XLA Modules:
  0.0 264.2 jit_solution(6128538219065764043)
XLA Ops:
  2.6 33.3 %all_to_all.64 = f32[64,8,256]{2,1,0:T(8,128)S(1)} all-to-all(f32[64,8,256]{2,1,0:T(8,128)S(1)} %fusion.13), channel_id=1, replica_groups=mesh['row'=64,'col'=8] {'row'}, dimensions={0} | all-to-all | bytes 1048576 | tf_op jit(solution)/shard_map/all_to_all | solution.py:20
  36.9 7.8 %all-to-all-start.1 = ((f32[64,8,256]{2,1,0:T(8,128)}), f32[64,8,256]{2,1,0:T(8,128)S(1)}, u32[]{:S(2)}, u32[]{:S(2)}) async-start(f32[64,8,256]{2,1,0:T(8,128)} %broadcast_in_dim.21), calls=%async_computation.1 | async-start | bytes 1048576 | tf_op jit(solution)/shard_map/all_to_all | solution.py:20
  49.4 2.9 %collective-permute-start = (f32[5,64,512]{2,1,0:T(8,128)}, f32[5,64,512]{2,1,0:T(8,128)}, u32[]{:S(2)}, u32[]{:S(2)}) collective-permute-start(f32[5,64,512]{2,1,0:T(8,128)} %copy.57), channel_id=1, source_target_pairs={{0,8},{8,0},{16,24},{24,16},{32,40},{40,32},{48,56},{56,48},{64,72... | collective-permute-start | bytes 1966088 | tf_op jit(solution)/shard_map/ppermute | solution.py:51
  52.3 8.5 %all-to-all-done.1 = f32[64,8,256]{2,1,0:T(8,128)S(1)} async-done(((f32[64,8,256]{2,1,0:T(8,128)}), f32[64,8,256]{2,1,0:T(8,128)S(1)}, u32[]{:S(2)}, u32[]{:S(2)}) %all-to-all-start.1) | async-done | bytes 524320 | tf_op jit(solution)/shard_map/all_to_all | solution.py:20
  63.0 8.9 %all-to-all-start.2 = ((f32[16,64,128]{2,1,0:T(8,128)}), f32[16,64,128]{2,1,0:T(8,128)S(1)}, u32[]{:S(2)}, u32[]{:S(2)}) async-start(f32[16,64,128]{2,1,0:T(8,128)} %bitcast.140), calls=%async_computation.2 | async-start | bytes 1048576 | tf_op jit(solution)/shard_map/all_to_all | solution.py:20
  78.5 2.8 %collective-permute-start.1 = (f32[64,128]{1,0:T(8,128)}, f32[64,128]{1,0:T(8,128)}, u32[]{:S(2)}, u32[]{:S(2)}) collective-permute-start(f32[64,128]{1,0:T(8,128)} %constant_dynamic-slice_fusion.4), channel_id=1, source_target_pairs={{0,8},{8,0},{16,24},{24,16},{32,40},{40,32},{48,56},{56,48},{64,72... | collective-permute-start | bytes 98312 | tf_op jit(solution)/shard_map/ppermute | solution.py:51
  83.7 9.9 %all-to-all-start.3 = ((f32[32,16,128]{2,1,0:T(8,128)}), f32[32,16,128]{2,1,0:T(8,128)}, u32[]{:S(2)}, u32[]{:S(2)}) async-start(f32[32,16,128]{2,1,0:T(8,128)} %fusion.39), calls=%async_computation.3 | async-start | bytes 524288 | tf_op jit(solution)/shard_map/all_to_all | solution.py:20
  93.7 3.6 %copy.60 = f32[4,64,4,512]{3,1,0,2:T(8,128)} copy(f32[4,64,4,512]{3,2,1,0:T(4,128)} %param.7) | data formatting | bytes 4194304 | tf_op jit(solution)/shard_map/optimization_barrier | solution.py:28
  97.2 2.6 copy.59
  99.8 2.5 slice_select_fusion
  107.3 9.7 %all-to-all-start.4 = ((f32[32,16,128]{2,1,0:T(8,128)}), f32[32,16,128]{2,1,0:T(8,128)S(1)}, u32[]{:S(2)}, u32[]{:S(2)}) async-start(f32[32,16,128]{2,1,0:T(8,128)} %broadcast_in_dim.23), calls=%async_computation.4 | async-start | bytes 524288 | tf_op jit(solution)/shard_map/all_to_all | solution.py:20
  120.5 8.0 %all-to-all-done.4 = f32[32,16,128]{2,1,0:T(8,128)S(1)} async-done(((f32[32,16,128]{2,1,0:T(8,128)}), f32[32,16,128]{2,1,0:T(8,128)S(1)}, u32[]{:S(2)}, u32[]{:S(2)}) %all-to-all-start.4) | async-done | bytes 262176 | tf_op jit(solution)/shard_map/all_to_all | solution.py:20
  130.0 7.6 %all-to-all-start.5 = ((f32[8,128,128]{2,1,0:T(8,128)}), f32[8,128,128]{2,1,0:T(8,128)S(1)}, u32[]{:S(2)}, u32[]{:S(2)}) async-start(f32[8,128,128]{2,1,0:T(8,128)} %broadcast_in_dim.24), calls=%async_computation.5 | async-start | bytes 1048576 | tf_op jit(solution)/shard_map/all_to_all | solution.py:20
  137.6 2.0 collective-permute-start.2
  139.7 7.9 %collective-permute-done.2 = f32[512,128]{1,0:T(8,128)} collective-permute-done((f32[512,128]{1,0:T(8,128)S(1)}, f32[512,128]{1,0:T(8,128)}, u32[]{:S(2)}, u32[]{:S(2)}) %collective-permute-start.2) | collective-permute-done | bytes 262176 | tf_op jit(solution)/shard_map/ppermute | solution.py:51
  147.6 2.0 fusion.24
  149.6 4.6 %all-to-all-start.6 = ((f32[32,16,128]{2,1,0:T(8,128)}), f32[32,16,128]{2,1,0:T(8,128)}, u32[]{:S(2)}, u32[]{:S(2)}) async-start(f32[32,16,128]{2,1,0:T(8,128)} %fusion.24), calls=%async_computation.6 | async-start | bytes 524288 | tf_op jit(solution)/shard_map/all_to_all | solution.py:20
  156.6 2.1 collective-permute-start.3
  158.6 4.7 %collective-permute-done.3 = f32[64,128]{1,0:T(8,128)S(1)} collective-permute-done((f32[64,128]{1,0:T(8,128)S(1)}, f32[64,128]{1,0:T(8,128)S(1)}, u32[]{:S(2)}, u32[]{:S(2)}) %collective-permute-start.3) | collective-permute-done | bytes 32800 | tf_op jit(solution)/shard_map/ppermute | solution.py:51
  163.3 2.9 %all-to-all-done.6 = f32[32,16,128]{2,1,0:T(8,128)} async-done(((f32[32,16,128]{2,1,0:T(8,128)}), f32[32,16,128]{2,1,0:T(8,128)}, u32[]{:S(2)}, u32[]{:S(2)}) %all-to-all-start.6) | async-done | bytes 262176 | tf_op jit(solution)/shard_map/all_to_all | solution.py:20
  168.0 7.0 %all-to-all-start.7 = ((f32[32,16,128]{2,1,0:T(8,128)}), f32[32,16,128]{2,1,0:T(8,128)S(1)}, u32[]{:S(2)}, u32[]{:S(2)}) async-start(f32[32,16,128]{2,1,0:T(8,128)} %broadcast_in_dim.25), calls=%async_computation.7 | async-start | bytes 524288 | tf_op jit(solution)/shard_map/all_to_all | solution.py:20
  175.0 2.8 %convolution_add_fusion.2 = f32[256,256]{1,0:T(8,128)} fusion(f32[256,256]{1,0:T(8,128)} %fusion.33, f32[256,512]{1,0:T(8,128)} %bitcast.144, f32[512,128]{1,0:T(8,128)S(1)} %get-tuple-element.84, f32[512,128]{1,0:T(8,128)S(1)} %get-tuple-element.83), kind=kOutput, calls=%fused_computation.3 | convolution fusion | flops 402849792 | bytes 1572864 | tf_op jit(solution)/shard_map/dot_general | solution.py:10
  177.8 8.6 %all-to-all-done.7 = f32[32,16,128]{2,1,0:T(8,128)S(1)} async-done(((f32[32,16,128]{2,1,0:T(8,128)}), f32[32,16,128]{2,1,0:T(8,128)S(1)}, u32[]{:S(2)}, u32[]{:S(2)}) %all-to-all-start.7) | async-done | bytes 262176 | tf_op jit(solution)/shard_map/all_to_all | solution.py:20
  188.0 7.9 %all-to-all-start.8 = ((f32[8,128,128]{2,1,0:T(8,128)}), f32[8,128,128]{2,1,0:T(8,128)S(1)}, u32[]{:S(2)}, u32[]{:S(2)}) async-start(f32[8,128,128]{2,1,0:T(8,128)} %broadcast_in_dim.26), calls=%async_computation.8 | async-start | bytes 1048576 | tf_op jit(solution)/shard_map/all_to_all | solution.py:20
  195.9 2.3 collective-permute-start.4
  198.1 7.5 %collective-permute-done.4 = f32[512,128]{1,0:T(8,128)S(1)} collective-permute-done((f32[512,128]{1,0:T(8,128)S(1)}, f32[512,128]{1,0:T(8,128)S(1)}, u32[]{:S(2)}, u32[]{:S(2)}) %collective-permute-start.4) | collective-permute-done | bytes 262176 | tf_op jit(solution)/shard_map/ppermute | solution.py:51
  206.8 4.3 %all-to-all-start.9 = ((f32[32,16,128]{2,1,0:T(8,128)}), f32[32,16,128]{2,1,0:T(8,128)S(1)}, u32[]{:S(2)}, u32[]{:S(2)}) async-start(f32[32,16,128]{2,1,0:T(8,128)} %fusion.22), calls=%async_computation.9 | async-start | bytes 524288 | tf_op jit(solution)/shard_map/all_to_all | solution.py:20
  211.5 11.8 %all-to-all-done.9 = f32[32,16,128]{2,1,0:T(8,128)S(1)} async-done(((f32[32,16,128]{2,1,0:T(8,128)}), f32[32,16,128]{2,1,0:T(8,128)S(1)}, u32[]{:S(2)}, u32[]{:S(2)}) %all-to-all-start.9) | async-done | bytes 262176 | tf_op jit(solution)/shard_map/all_to_all | solution.py:20
  224.1 6.8 %all-to-all-start.10 = ((f32[64,16,128]{2,1,0:T(8,128)}), f32[64,16,128]{2,1,0:T(8,128)S(1)}, u32[]{:S(2)}, u32[]{:S(2)}) async-start(f32[64,16,128]{2,1,0:T(8,128)} %broadcast_in_dim.27), calls=%async_computation.10 | async-start | bytes 1048576 | tf_op jit(solution)/shard_map/all_to_all | solution.py:20
  233.3 13.9 %all-to-all-done.10 = f32[64,16,128]{2,1,0:T(8,128)S(1)} async-done(((f32[64,16,128]{2,1,0:T(8,128)}), f32[64,16,128]{2,1,0:T(8,128)S(1)}, u32[]{:S(2)}, u32[]{:S(2)}) %all-to-all-start.10) | async-done | bytes 524320 | tf_op jit(solution)/shard_map/all_to_all | solution.py:20
  249.2 7.7 %all-to-all-start.11 = ((f32[8,32,256]{2,1,0:T(8,128)}), f32[8,32,256]{2,1,0:T(8,128)S(1)}, u32[]{:S(2)}, u32[]{:S(2)}) async-start(f32[8,32,256]{2,1,0:T(8,128)} %bitcast.50), calls=%async_computation.11 | async-start | bytes 524288 | tf_op jit(solution)/shard_map/all_to_all | solution.py:20
  257.8 5.6 %all-to-all-done.11 = f32[8,32,256]{2,1,0:T(8,128)S(1)} async-done(((f32[8,32,256]{2,1,0:T(8,128)}), f32[8,32,256]{2,1,0:T(8,128)S(1)}, u32[]{:S(2)}, u32[]{:S(2)}) %all-to-all-start.11) | async-done | bytes 262176 | tf_op jit(solution)/shard_map/all_to_all | solution.py:20
  (96 shorter events, 42.5 us)
Async XLA Ops:
  0.6 1.4 copy-start.6
  36.9 23.9 %all-to-all-start.1 = ((f32[64,8,256]{2,1,0:T(8,128)}), f32[64,8,256]{2,1,0:T(8,128)S(1)}, u32[]{:S(2)}, u32[]{:S(2)}) async-start(f32[64,8,256]{2,1,0:T(8,128)} %broadcast_in_dim.21), calls=%async_computation.1 | async-start | bytes 1048576 | tf_op jit(solution)/shard_map/all_to_all | solution.py:20
  48.1 12.7 %copy-start.7 = (f32[8,64,256]{2,1,0:T(8,128)S(1)}, f32[8,64,256]{2,1,0:T(8,128)}, u32[]{:S(2)}) copy-start(f32[8,64,256]{2,1,0:T(8,128)} %param.4) | copy-start | bytes 1572868
  49.4 24.2 %collective-permute-start = (f32[5,64,512]{2,1,0:T(8,128)}, f32[5,64,512]{2,1,0:T(8,128)}, u32[]{:S(2)}, u32[]{:S(2)}) collective-permute-start(f32[5,64,512]{2,1,0:T(8,128)} %copy.57), channel_id=1, source_target_pairs={{0,8},{8,0},{16,24},{24,16},{32,40},{40,32},{48,56},{56,48},{64,72... | collective-permute-start | bytes 1966088 | tf_op jit(solution)/shard_map/ppermute | solution.py:51
  63.0 19.6 %all-to-all-start.2 = ((f32[16,64,128]{2,1,0:T(8,128)}), f32[16,64,128]{2,1,0:T(8,128)S(1)}, u32[]{:S(2)}, u32[]{:S(2)}) async-start(f32[16,64,128]{2,1,0:T(8,128)} %bitcast.140), calls=%async_computation.2 | async-start | bytes 1048576 | tf_op jit(solution)/shard_map/all_to_all | solution.py:20
  75.3 1.2 copy-start.8
  78.5 25.1 %collective-permute-start.1 = (f32[64,128]{1,0:T(8,128)}, f32[64,128]{1,0:T(8,128)}, u32[]{:S(2)}, u32[]{:S(2)}) collective-permute-start(f32[64,128]{1,0:T(8,128)} %constant_dynamic-slice_fusion.4), channel_id=1, source_target_pairs={{0,8},{8,0},{16,24},{24,16},{32,40},{40,32},{48,56},{56,48},{64,72... | collective-permute-start | bytes 98312 | tf_op jit(solution)/shard_map/ppermute | solution.py:51
  83.7 21.8 %all-to-all-start.3 = ((f32[32,16,128]{2,1,0:T(8,128)}), f32[32,16,128]{2,1,0:T(8,128)}, u32[]{:S(2)}, u32[]{:S(2)}) async-start(f32[32,16,128]{2,1,0:T(8,128)} %fusion.39), calls=%async_computation.3 | async-start | bytes 524288 | tf_op jit(solution)/shard_map/all_to_all | solution.py:20
  99.8 2.5 copy-start.1
  103.6 15.1 %copy-start = (f32[4,64,512]{1,2,0:T(8,128)S(1)}, f32[4,64,512]{1,2,0:T(8,128)}, u32[]{:S(2)}) copy-start(f32[4,64,512]{1,2,0:T(8,128)} %get-tuple-element.69) | copy-start | bytes 1572868
  107.3 21.3 %all-to-all-start.4 = ((f32[32,16,128]{2,1,0:T(8,128)}), f32[32,16,128]{2,1,0:T(8,128)S(1)}, u32[]{:S(2)}, u32[]{:S(2)}) async-start(f32[32,16,128]{2,1,0:T(8,128)} %broadcast_in_dim.23), calls=%async_computation.4 | async-start | bytes 524288 | tf_op jit(solution)/shard_map/all_to_all | solution.py:20
  130.0 17.6 %all-to-all-start.5 = ((f32[8,128,128]{2,1,0:T(8,128)}), f32[8,128,128]{2,1,0:T(8,128)S(1)}, u32[]{:S(2)}, u32[]{:S(2)}) async-start(f32[8,128,128]{2,1,0:T(8,128)} %broadcast_in_dim.24), calls=%async_computation.5 | async-start | bytes 1048576 | tf_op jit(solution)/shard_map/all_to_all | solution.py:20
  137.6 9.9 %collective-permute-start.2 = (f32[512,128]{1,0:T(8,128)S(1)}, f32[512,128]{1,0:T(8,128)}, u32[]{:S(2)}, u32[]{:S(2)}) collective-permute-start(f32[512,128]{1,0:T(8,128)S(1)} %bitcast.139), channel_id=1, source_target_pairs={{0,8},{8,0},{16,24},{24,16},{32,40},{40,32},{48,56},{56,48},{64,72... | collective-permute-start | bytes 786440 | tf_op jit(solution)/shard_map/ppermute | solution.py:51
  149.6 16.6 %all-to-all-start.6 = ((f32[32,16,128]{2,1,0:T(8,128)}), f32[32,16,128]{2,1,0:T(8,128)}, u32[]{:S(2)}, u32[]{:S(2)}) async-start(f32[32,16,128]{2,1,0:T(8,128)} %fusion.24), calls=%async_computation.6 | async-start | bytes 524288 | tf_op jit(solution)/shard_map/all_to_all | solution.py:20
  156.6 6.7 %collective-permute-start.3 = (f32[64,128]{1,0:T(8,128)S(1)}, f32[64,128]{1,0:T(8,128)S(1)}, u32[]{:S(2)}, u32[]{:S(2)}) collective-permute-start(f32[64,128]{1,0:T(8,128)S(1)} %constant_dynamic-slice_fusion.3), channel_id=1, source_target_pairs={{0,8},{8,0},{16,24},{24,16},{32,40},{40,32},{48,56},{56,48},{64,72... | collective-permute-start | bytes 98312 | tf_op jit(solution)/shard_map/ppermute | solution.py:51
  168.0 18.5 %all-to-all-start.7 = ((f32[32,16,128]{2,1,0:T(8,128)}), f32[32,16,128]{2,1,0:T(8,128)S(1)}, u32[]{:S(2)}, u32[]{:S(2)}) async-start(f32[32,16,128]{2,1,0:T(8,128)} %broadcast_in_dim.25), calls=%async_computation.7 | async-start | bytes 524288 | tf_op jit(solution)/shard_map/all_to_all | solution.py:20
  187.1 18.6 %copy-start.5 = (f32[1,128,512]{1,2,0:T(8,128)S(1)}, f32[1,128,512]{1,2,0:T(8,128)}, u32[]{:S(2)}) copy-start(f32[1,128,512]{1,2,0:T(8,128)} %get-tuple-element.75) | copy-start | bytes 786436
  188.0 17.7 %all-to-all-start.8 = ((f32[8,128,128]{2,1,0:T(8,128)}), f32[8,128,128]{2,1,0:T(8,128)S(1)}, u32[]{:S(2)}, u32[]{:S(2)}) async-start(f32[8,128,128]{2,1,0:T(8,128)} %broadcast_in_dim.26), calls=%async_computation.8 | async-start | bytes 1048576 | tf_op jit(solution)/shard_map/all_to_all | solution.py:20
  195.9 9.8 %collective-permute-start.4 = (f32[512,128]{1,0:T(8,128)S(1)}, f32[512,128]{1,0:T(8,128)S(1)}, u32[]{:S(2)}, u32[]{:S(2)}) collective-permute-start(f32[512,128]{1,0:T(8,128)S(1)} %bitcast.137), channel_id=1, source_target_pairs={{0,8},{8,0},{16,24},{24,16},{32,40},{40,32},{48,56},{56,48},{64,72... | collective-permute-start | bytes 786440 | tf_op jit(solution)/shard_map/ppermute | solution.py:51
  205.7 5.8 %copy-start.9 = (f32[512,128]{1,0:T(8,128)}, f32[512,128]{1,0:T(8,128)S(1)}, u32[]{:S(2)}) copy-start(f32[512,128]{1,0:T(8,128)S(1)} %collective-permute-done.4) | copy-start | bytes 786436
  206.8 16.4 %all-to-all-start.9 = ((f32[32,16,128]{2,1,0:T(8,128)}), f32[32,16,128]{2,1,0:T(8,128)S(1)}, u32[]{:S(2)}, u32[]{:S(2)}) async-start(f32[32,16,128]{2,1,0:T(8,128)} %fusion.22), calls=%async_computation.9 | async-start | bytes 524288 | tf_op jit(solution)/shard_map/all_to_all | solution.py:20
  211.5 19.5 %slice-start = ((f32[8,64,256]{2,1,0:T(8,128)}), f32[4,64,256]{2,1,0:T(8,128)S(1)}, s32[]{:S(2)}) async-start(f32[8,64,256]{2,1,0:T(8,128)} %param.4), calls=%async_computation.12 | async-start | bytes 524288 | tf_op jit(solution)/shard_map/slice | solution.py:89
  223.3 7.9 %copy-start.10 = (f32[512,128]{1,0:T(8,128)S(1)}, f32[512,128]{1,0:T(8,128)}, u32[]{:S(2)}) copy-start(f32[512,128]{1,0:T(8,128)} %copy-done.9) | copy-start | bytes 786436
  224.1 23.1 %all-to-all-start.10 = ((f32[64,16,128]{2,1,0:T(8,128)}), f32[64,16,128]{2,1,0:T(8,128)S(1)}, u32[]{:S(2)}, u32[]{:S(2)}) async-start(f32[64,16,128]{2,1,0:T(8,128)} %broadcast_in_dim.27), calls=%async_computation.10 | async-start | bytes 1048576 | tf_op jit(solution)/shard_map/all_to_all | solution.py:20
  231.0 1.0 copy-start.3
  231.0 1.1 copy-start.4
  233.1 14.4 %copy-start.2 = (f32[4,64,1,512]{3,1,0,2:T(8,128)S(1)}, f32[4,64,1,512]{3,1,0,2:T(8,128)}, u32[]{:S(2)}) copy-start(f32[4,64,1,512]{3,1,0,2:T(8,128)} %get-tuple-element.70) | copy-start | bytes 1572868
  249.2 14.2 %all-to-all-start.11 = ((f32[8,32,256]{2,1,0:T(8,128)}), f32[8,32,256]{2,1,0:T(8,128)S(1)}, u32[]{:S(2)}, u32[]{:S(2)}) async-start(f32[8,32,256]{2,1,0:T(8,128)} %bitcast.50), calls=%async_computation.11 | async-start | bytes 524288 | tf_op jit(solution)/shard_map/all_to_all | solution.py:20

commit v16 on v14

--- a/solution.py
+++ b/solution.py
@@ -108,18 +108,18 @@
     parts = jnp.stack([term[:, :half], term[:, half:]])[:, None]
     parts = jnp.broadcast_to(parts, (2, col_size, local_rows, half))
     parts = swap(parts.reshape(2 * col_size, local_rows, half), ("row", "col"), pair_groups)
-    parts, got_shared = by_deadline(parts, got_shared)
-    pair = ordered(own_shared, got_shared, 1)
-    diag_1, diag_2, diag_3, lower_21, lower_32 = [pair[i] for i in range(5)]
+    diag_1 = ordered(own_shared[0], got_shared[0], 0)
+    parts, diag_1, whole_0 = by_deadline(parts, diag_1, whole_0)
+    pair = ordered(own_shared[1:], got_shared[1:], 1)
+    diag_2, diag_3, lower_21, lower_32 = [pair[i] for i in range(4)]
     current = parts.reshape(2, col_size, local_rows, half).sum(1).reshape(2 * local_rows, half)
     parts = scattered(diag_1, current)
     term_2 = own_term(2) - contract(lower_blocks[1], whole_0, (1, 0))
-    parts, got_2, trail = by_deadline(parts, from_partner(half_of(term_2, row % 2 ^ 1)), trail)
+    parts, got_2 = by_deadline(parts, from_partner(half_of(term_2, row % 2 ^ 1)))
     term_2 = ordered(half_of(term_2, row % 2), got_2, 0)
     term_3 = own_term(3) - contract(lower_blocks[3], whole_0, (1, 0))
     parts = gathered(parts)
-    below = below_of(whole_0, 0)
-    parts, below, term_2, term_3 = by_deadline(parts, below, term_2, term_3)
+    parts, term_2, term_3 = by_deadline(parts, term_2, term_3)
     solved_1 = parts.reshape(width, half)
 
     parts = summed(term_2 - contract(lower_21, solved_1, (1, 0)))
@@ -130,7 +130,7 @@
     parts, got_3 = by_deadline(parts, from_partner(half_of(term_3, row % 2 ^ 1)))
     term_3 = ordered(half_of(term_3, row % 2), got_3, 0)
     parts = gathered(parts)
-    below = below + below_of(whole_1, 1)
+    below = below_of(whole_0, 0)
     parts, below, term_3 = by_deadline(parts, below, term_3)
     solved_2 = parts.reshape(width, half)
 
@@ -138,7 +138,8 @@
     parts, got_2 = by_deadline(parts, from_partner(solved_2))
     parts = scattered(diag_3, parts.sum(0))
     outs = [out_of(whole_0), out_of(whole_1)]
-    parts, outs = by_deadline(parts, outs)
+    below = below + below_of(whole_1, 1)
+    parts, outs, below = by_deadline(parts, outs, below)
     parts = gathered_whole(parts)
     whole_2 = ordered(solved_2, got_2, 1)
     below = below + below_of(whole_2, 2)

time: 271 us -> 267 us (0.985)
  waiting for transfers between devices: 99.9 us -> 82.9 us
  starting transfers between devices: 90.2 us -> 97.4 us
  local copies, waits for them, and re-layouts: 19.1 us -> 23.5 us
    ppermute x5, waiting for transfers between devices: 30.9 us -> 18.3 us  [from_partner(): return lax.ppermute(value, 'row', [(r, r ^ 1) for r in range(row_size)])]
    all_to_all x11, starting transfers between devices: 75.7 us -> 83.3 us  [swap(): lax.all_to_all(parts, axis, 0, 0, axis_index_groups=groups, tiled=True)]
    all_to_all x11, waiting for transfers between devices: 69 us -> 64.5 us  [swap(): lax.all_to_all(parts, axis, 0, 0, axis_index_groups=groups, tiled=True)]
    dot_general x5 -> x0, local copies, waits for them, and re-layouts: 3.06 us -> none  [contract(): lax.dot_general(left, right, (((axes[0],), (axes[1],)), ((), ())), precis...]
    unnamed x23 -> x38, local copies, waits for them, and re-layouts: 3.35 us -> 5.94 us
  transfers between devices with their start and end apart: 16 -> 16, of which waited for: 13 -> 13; matrix products, arithmetic and copies ran while one was open for 9% -> 12% of each run, Pallas kernels for 0% -> 0%
where the time goes in v16:
time: 267 us; the launch traced here: 265 us
  starting transfers between devices  97.4 us (36%)
  waiting for transfers between devices  82.9 us (31%)
  blocking collectives  33.3 us (12%)
  local copies, waits for them, and re-layouts  23.5 us (9%)
  matrix products  18.6 us (7%)
  other arithmetic  8.32 us (3%)
    all_to_all x11, starting transfers between devices, swap(): lax.all_to_all(parts, axis, 0, 0, axis_index_groups=groups, tiled=True)  83.3 us
    all_to_all x11, waiting for transfers between devices, swap(): lax.all_to_all(parts, axis, 0, 0, axis_index_groups=groups, tiled=True)  64.5 us
    all_to_all x1, blocking collectives, swap(): lax.all_to_all(parts, axis, 0, 0, axis_index_groups=groups, tiled=True)  33.3 us
    dot_general x14, matrix products, contract(): lax.dot_general(left, right, (((axes[0],), (axes[1],)), ((), ())), precis...  18.6 us
    ppermute x5, waiting for transfers between devices, from_partner(): return lax.ppermute(value, 'row', [(r, r ^ 1) for r in range(row_size)])  18.3 us
    ppermute x5, starting transfers between devices, from_partner(): return lax.ppermute(value, 'row', [(r, r ^ 1) for r in range(row_size)])  14.1 us
    slice x1, local copies, waits for them, and re-layouts, shards(): trail_panel[:, :, j, :].reshape(trail_count * local_rows, width)  6.66 us
    unnamed x38, local copies, waits for them, and re-layouts  5.94 us
  transfers between devices with their start and end apart: 16, of which 13 were waited for; matrix products, arithmetic and copies ran while one was open for 12% of the time, Pallas kernels for 0%

profile of v16, /device:TPU:1, one launch (start us, length us, event | category | flops | bytes accessed | tf_op | source)
XLA Modules:
  0.0 265.2 jit_solution(8397923589029350169)
XLA Ops:
  2.6 33.3 %all_to_all.64 = f32[64,8,256]{2,1,0:T(8,128)S(1)} all-to-all(f32[64,8,256]{2,1,0:T(8,128)S(1)} %fusion.14), channel_id=1, replica_groups=mesh['row'=64,'col'=8] {'row'}, dimensions={0} | all-to-all | bytes 1048576 | tf_op jit(solution)/shard_map/all_to_all | solution.py:20
  36.8 7.8 %all-to-all-start.1 = ((f32[64,8,256]{2,1,0:T(8,128)}), f32[64,8,256]{2,1,0:T(8,128)S(1)}, u32[]{:S(2)}, u32[]{:S(2)}) async-start(f32[64,8,256]{2,1,0:T(8,128)} %broadcast_in_dim.21), calls=%async_computation.1 | async-start | bytes 1048576 | tf_op jit(solution)/shard_map/all_to_all | solution.py:20
  49.4 2.9 %collective-permute-start = (f32[5,64,512]{2,1,0:T(8,128)}, f32[5,64,512]{2,1,0:T(8,128)S(1)}, u32[]{:S(2)}, u32[]{:S(2)}) collective-permute-start(f32[5,64,512]{2,1,0:T(8,128)} %copy.57), channel_id=1, source_target_pairs={{0,8},{8,0},{16,24},{24,16},{32,40},{40,32},{48,56},{56,48},{64,72... | collective-permute-start | bytes 1966088 | tf_op jit(solution)/shard_map/ppermute | solution.py:51
  52.3 8.5 %all-to-all-done.1 = f32[64,8,256]{2,1,0:T(8,128)S(1)} async-done(((f32[64,8,256]{2,1,0:T(8,128)}), f32[64,8,256]{2,1,0:T(8,128)S(1)}, u32[]{:S(2)}, u32[]{:S(2)}) %all-to-all-start.1) | async-done | bytes 524320 | tf_op jit(solution)/shard_map/all_to_all | solution.py:20
  63.0 8.9 %all-to-all-start.2 = ((f32[16,64,128]{2,1,0:T(8,128)}), f32[16,64,128]{2,1,0:T(8,128)S(1)}, u32[]{:S(2)}, u32[]{:S(2)}) async-start(f32[16,64,128]{2,1,0:T(8,128)} %bitcast.18), calls=%async_computation.2 | async-start | bytes 1048576 | tf_op jit(solution)/shard_map/all_to_all | solution.py:20
  75.1 6.6 %all-to-all-done.2 = f32[16,64,128]{2,1,0:T(8,128)S(1)} async-done(((f32[16,64,128]{2,1,0:T(8,128)}), f32[16,64,128]{2,1,0:T(8,128)S(1)}, u32[]{:S(2)}, u32[]{:S(2)}) %all-to-all-start.2) | async-done | bytes 524320 | tf_op jit(solution)/shard_map/all_to_all | solution.py:20
  82.8 8.2 %all-to-all-start.3 = ((f32[32,16,128]{2,1,0:T(8,128)}), f32[32,16,128]{2,1,0:T(8,128)S(1)}, u32[]{:S(2)}, u32[]{:S(2)}) async-start(f32[32,16,128]{2,1,0:T(8,128)} %fusion.37), calls=%async_computation.3 | async-start | bytes 524288 | tf_op jit(solution)/shard_map/all_to_all | solution.py:20
  92.4 3.9 %collective-permute-start.1 = (f32[64,128]{1,0:T(8,128)S(1)}, f32[64,128]{1,0:T(8,128)S(1)}, u32[]{:S(2)}, u32[]{:S(2)}) collective-permute-start(f32[64,128]{1,0:T(8,128)S(1)} %constant_dynamic-slice_fusion.4), channel_id=1, source_target_pairs={{0,8},{8,0},{16,24},{24,16},{32,40},{40,32},{48,56},{56,48},{64,72... | collective-permute-start | bytes 98312 | tf_op jit(solution)/shard_map/ppermute | solution.py:51
  96.3 1.7 slice_select_fusion
  98.0 3.5 %collective-permute-done.1 = f32[64,128]{1,0:T(8,128)S(1)} collective-permute-done((f32[64,128]{1,0:T(8,128)S(1)}, f32[64,128]{1,0:T(8,128)S(1)}, u32[]{:S(2)}, u32[]{:S(2)}) %collective-permute-start.1) | collective-permute-done | bytes 32800 | tf_op jit(solution)/shard_map/ppermute | solution.py:51
  103.4 9.1 %all-to-all-start.4 = ((f32[32,16,128]{2,1,0:T(8,128)}), f32[32,16,128]{2,1,0:T(8,128)S(1)}, u32[]{:S(2)}, u32[]{:S(2)}) async-start(f32[32,16,128]{2,1,0:T(8,128)} %broadcast_in_dim.23), calls=%async_computation.4 | async-start | bytes 524288 | tf_op jit(solution)/shard_map/all_to_all | solution.py:20
  113.9 11.3 %all-to-all-done.4 = f32[32,16,128]{2,1,0:T(8,128)S(1)} async-done(((f32[32,16,128]{2,1,0:T(8,128)}), f32[32,16,128]{2,1,0:T(8,128)S(1)}, u32[]{:S(2)}, u32[]{:S(2)}) %all-to-all-start.4) | async-done | bytes 262176 | tf_op jit(solution)/shard_map/all_to_all | solution.py:20
  126.7 6.0 %all-to-all-start.5 = ((f32[8,128,128]{2,1,0:T(8,128)}), f32[8,128,128]{2,1,0:T(8,128)}, u32[]{:S(2)}, u32[]{:S(2)}) async-start(f32[8,128,128]{2,1,0:T(8,128)} %broadcast_in_dim.24), calls=%async_computation.5 | async-start | bytes 1048576 | tf_op jit(solution)/shard_map/all_to_all | solution.py:20
  132.8 2.0 collective-permute-start.2
  135.8 6.7 %collective-permute-done.2 = f32[512,128]{1,0:T(8,128)S(1)} collective-permute-done((f32[512,128]{1,0:T(8,128)S(1)}, f32[512,128]{1,0:T(8,128)S(1)}, u32[]{:S(2)}, u32[]{:S(2)}) %collective-permute-start.2) | collective-permute-done | bytes 262176 | tf_op jit(solution)/shard_map/ppermute | solution.py:51
  145.3 2.0 fusion.25
  147.3 4.6 %all-to-all-start.6 = ((f32[32,16,128]{2,1,0:T(8,128)}), f32[32,16,128]{2,1,0:T(8,128)S(1)}, u32[]{:S(2)}, u32[]{:S(2)}) async-start(f32[32,16,128]{2,1,0:T(8,128)} %fusion.25), calls=%async_computation.6 | async-start | bytes 524288 | tf_op jit(solution)/shard_map/all_to_all | solution.py:20
  153.3 2.1 collective-permute-start.3
  155.4 6.7 %fusion.35 = (f32[4,64,1,512]{3,2,1,0:T(1,128)}, f32[4,64,1,512]{3,2,1,0:T(1,128)}, f32[4,64,1,512]{3,2,1,0:T(1,128)}, f32[4,64,1,512]{3,2,1,0:T(1,128)S(1)}) fusion(f32[4,64,4,512]{3,2,1,0:T(4,128)} %param.7), kind=kLoop, calls=%fused_computation.84 | loop fusion | bytes 4194304 | tf_op jit(solution)/shard_map/slice | solution.py:85
  164.6 10.6 %all-to-all-start.7 = ((f32[32,16,128]{2,1,0:T(8,128)}), f32[32,16,128]{2,1,0:T(8,128)S(1)}, u32[]{:S(2)}, u32[]{:S(2)}) async-start(f32[32,16,128]{2,1,0:T(8,128)} %broadcast_in_dim.25), calls=%async_computation.7 | async-start | bytes 524288 | tf_op jit(solution)/shard_map/all_to_all | solution.py:20
  175.3 2.8 %fusion.38 = f32[256,256]{1,0:T(8,128)} fusion(f32[512,256]{1,0:T(8,128)S(1)} %bitcast.129, f32[256,512]{1,0:T(8,128)} %bitcast.144), kind=kOutput, calls=%fused_computation.87 | convolution fusion | flops 402653184 | bytes 1310720 | tf_op jit(solution)/shard_map/dot_general | solution.py:10
  178.1 8.9 %all-to-all-done.7 = f32[32,16,128]{2,1,0:T(8,128)S(1)} async-done(((f32[32,16,128]{2,1,0:T(8,128)}), f32[32,16,128]{2,1,0:T(8,128)S(1)}, u32[]{:S(2)}, u32[]{:S(2)}) %all-to-all-start.7) | async-done | bytes 262176 | tf_op jit(solution)/shard_map/all_to_all | solution.py:20
  188.6 7.8 %all-to-all-start.8 = ((f32[8,128,128]{2,1,0:T(8,128)}), f32[8,128,128]{2,1,0:T(8,128)S(1)}, u32[]{:S(2)}, u32[]{:S(2)}) async-start(f32[8,128,128]{2,1,0:T(8,128)} %broadcast_in_dim.26), calls=%async_computation.8 | async-start | bytes 1048576 | tf_op jit(solution)/shard_map/all_to_all | solution.py:20
  196.4 3.3 %collective-permute-start.4 = (f32[512,128]{1,0:T(8,128)S(1)}, f32[512,128]{1,0:T(8,128)S(1)}, u32[]{:S(2)}, u32[]{:S(2)}) collective-permute-start(f32[512,128]{1,0:T(8,128)S(1)} %bitcast.137), channel_id=1, source_target_pairs={{0,8},{8,0},{16,24},{24,16},{32,40},{40,32},{48,56},{56,48},{64,72... | collective-permute-start | bytes 786440 | tf_op jit(solution)/shard_map/ppermute | solution.py:51
  199.6 6.5 %collective-permute-done.4 = f32[512,128]{1,0:T(8,128)S(1)} collective-permute-done((f32[512,128]{1,0:T(8,128)S(1)}, f32[512,128]{1,0:T(8,128)S(1)}, u32[]{:S(2)}, u32[]{:S(2)}) %collective-permute-start.4) | collective-permute-done | bytes 262176 | tf_op jit(solution)/shard_map/ppermute | solution.py:51
  207.3 4.2 %all-to-all-start.9 = ((f32[32,16,128]{2,1,0:T(8,128)}), f32[32,16,128]{2,1,0:T(8,128)S(1)}, u32[]{:S(2)}, u32[]{:S(2)}) async-start(f32[32,16,128]{2,1,0:T(8,128)} %fusion.23), calls=%async_computation.9 | async-start | bytes 524288 | tf_op jit(solution)/shard_map/all_to_all | solution.py:20
  214.4 9.2 %all-to-all-done.9 = f32[32,16,128]{2,1,0:T(8,128)S(1)} async-done(((f32[32,16,128]{2,1,0:T(8,128)}), f32[32,16,128]{2,1,0:T(8,128)S(1)}, u32[]{:S(2)}, u32[]{:S(2)}) %all-to-all-start.9) | async-done | bytes 262176 | tf_op jit(solution)/shard_map/all_to_all | solution.py:20
  224.5 7.0 %all-to-all-start.10 = ((f32[64,16,128]{2,1,0:T(8,128)}), f32[64,16,128]{2,1,0:T(8,128)S(1)}, u32[]{:S(2)}, u32[]{:S(2)}) async-start(f32[64,16,128]{2,1,0:T(8,128)} %broadcast_in_dim.27), calls=%async_computation.10 | async-start | bytes 1048576 | tf_op jit(solution)/shard_map/all_to_all | solution.py:20
  234.7 12.3 %all-to-all-done.10 = f32[64,16,128]{2,1,0:T(8,128)S(1)} async-done(((f32[64,16,128]{2,1,0:T(8,128)}), f32[64,16,128]{2,1,0:T(8,128)S(1)}, u32[]{:S(2)}, u32[]{:S(2)}) %all-to-all-start.10) | async-done | bytes 524320 | tf_op jit(solution)/shard_map/all_to_all | solution.py:20
  247.3 1.7 convolution_add_fusion
  249.0 8.9 %all-to-all-start.11 = ((f32[8,32,256]{2,1,0:T(8,128)}), f32[8,32,256]{2,1,0:T(8,128)S(1)}, u32[]{:S(2)}, u32[]{:S(2)}) async-start(f32[8,32,256]{2,1,0:T(8,128)} %bitcast.50), calls=%async_computation.11 | async-start | bytes 524288 | tf_op jit(solution)/shard_map/all_to_all | solution.py:20
  258.8 5.6 %all-to-all-done.11 = f32[8,32,256]{2,1,0:T(8,128)S(1)} async-done(((f32[8,32,256]{2,1,0:T(8,128)}), f32[8,32,256]{2,1,0:T(8,128)S(1)}, u32[]{:S(2)}, u32[]{:S(2)}) %all-to-all-start.11) | async-done | bytes 262176 | tf_op jit(solution)/shard_map/all_to_all | solution.py:20
  (104 shorter events, 39.2 us)
Async XLA Ops:
  0.6 1.4 copy-start.8
  36.8 23.9 %all-to-all-start.1 = ((f32[64,8,256]{2,1,0:T(8,128)}), f32[64,8,256]{2,1,0:T(8,128)S(1)}, u32[]{:S(2)}, u32[]{:S(2)}) async-start(f32[64,8,256]{2,1,0:T(8,128)} %broadcast_in_dim.21), calls=%async_computation.1 | async-start | bytes 1048576 | tf_op jit(solution)/shard_map/all_to_all | solution.py:20
  48.1 14.0 %copy-start = (f32[5,64,512]{1,2,0:T(8,128)}, f32[5,64,512]{1,2,0:T(8,128)S(1)}, u32[]{:S(2)}) copy-start(f32[5,64,512]{1,2,0:T(8,128)S(1)} %pad_maximum_fusion) | copy-start | bytes 1966084
  49.4 24.0 %collective-permute-start = (f32[5,64,512]{2,1,0:T(8,128)}, f32[5,64,512]{2,1,0:T(8,128)S(1)}, u32[]{:S(2)}, u32[]{:S(2)}) collective-permute-start(f32[5,64,512]{2,1,0:T(8,128)} %copy.57), channel_id=1, source_target_pairs={{0,8},{8,0},{16,24},{24,16},{32,40},{40,32},{48,56},{56,48},{64,72... | collective-permute-start | bytes 1966088 | tf_op jit(solution)/shard_map/ppermute | solution.py:51
  63.0 18.7 %all-to-all-start.2 = ((f32[16,64,128]{2,1,0:T(8,128)}), f32[16,64,128]{2,1,0:T(8,128)S(1)}, u32[]{:S(2)}, u32[]{:S(2)}) async-start(f32[16,64,128]{2,1,0:T(8,128)} %bitcast.18), calls=%async_computation.2 | async-start | bytes 1048576 | tf_op jit(solution)/shard_map/all_to_all | solution.py:20
  75.0 16.1 %copy-start.9 = (f32[8,64,256]{2,1,0:T(8,128)S(1)}, f32[8,64,256]{2,1,0:T(8,128)}, u32[]{:S(2)}) copy-start(f32[8,64,256]{2,1,0:T(8,128)} %param.4) | copy-start | bytes 1572868
  82.8 19.8 %all-to-all-start.3 = ((f32[32,16,128]{2,1,0:T(8,128)}), f32[32,16,128]{2,1,0:T(8,128)S(1)}, u32[]{:S(2)}, u32[]{:S(2)}) async-start(f32[32,16,128]{2,1,0:T(8,128)} %fusion.37), calls=%async_computation.3 | async-start | bytes 524288 | tf_op jit(solution)/shard_map/all_to_all | solution.py:20
  92.4 9.1 %collective-permute-start.1 = (f32[64,128]{1,0:T(8,128)S(1)}, f32[64,128]{1,0:T(8,128)S(1)}, u32[]{:S(2)}, u32[]{:S(2)}) collective-permute-start(f32[64,128]{1,0:T(8,128)S(1)} %constant_dynamic-slice_fusion.4), channel_id=1, source_target_pairs={{0,8},{8,0},{16,24},{24,16},{32,40},{40,32},{48,56},{56,48},{64,72... | collective-permute-start | bytes 98312 | tf_op jit(solution)/shard_map/ppermute | solution.py:51
  103.4 21.8 %all-to-all-start.4 = ((f32[32,16,128]{2,1,0:T(8,128)}), f32[32,16,128]{2,1,0:T(8,128)S(1)}, u32[]{:S(2)}, u32[]{:S(2)}) async-start(f32[32,16,128]{2,1,0:T(8,128)} %broadcast_in_dim.23), calls=%async_computation.4 | async-start | bytes 524288 | tf_op jit(solution)/shard_map/all_to_all | solution.py:20
  126.7 16.5 %all-to-all-start.5 = ((f32[8,128,128]{2,1,0:T(8,128)}), f32[8,128,128]{2,1,0:T(8,128)}, u32[]{:S(2)}, u32[]{:S(2)}) async-start(f32[8,128,128]{2,1,0:T(8,128)} %broadcast_in_dim.24), calls=%async_computation.5 | async-start | bytes 1048576 | tf_op jit(solution)/shard_map/all_to_all | solution.py:20
  132.8 9.7 %collective-permute-start.2 = (f32[512,128]{1,0:T(8,128)S(1)}, f32[512,128]{1,0:T(8,128)S(1)}, u32[]{:S(2)}, u32[]{:S(2)}) collective-permute-start(f32[512,128]{1,0:T(8,128)S(1)} %bitcast.139), channel_id=1, source_target_pairs={{0,8},{8,0},{16,24},{24,16},{32,40},{40,32},{48,56},{56,48},{64,72... | collective-permute-start | bytes 786440 | tf_op jit(solution)/shard_map/ppermute | solution.py:51
  142.5 0.7 copy-start.12
  147.3 16.5 %all-to-all-start.6 = ((f32[32,16,128]{2,1,0:T(8,128)}), f32[32,16,128]{2,1,0:T(8,128)S(1)}, u32[]{:S(2)}, u32[]{:S(2)}) async-start(f32[32,16,128]{2,1,0:T(8,128)} %fusion.25), calls=%async_computation.6 | async-start | bytes 524288 | tf_op jit(solution)/shard_map/all_to_all | solution.py:20
  153.3 9.6 %collective-permute-start.3 = (f32[64,128]{1,0:T(8,128)S(1)}, f32[64,128]{1,0:T(8,128)S(1)}, u32[]{:S(2)}, u32[]{:S(2)}) collective-permute-start(f32[64,128]{1,0:T(8,128)S(1)} %constant_dynamic-slice_fusion.3), channel_id=1, source_target_pairs={{0,8},{8,0},{16,24},{24,16},{32,40},{40,32},{48,56},{56,48},{64,72... | collective-permute-start | bytes 98312 | tf_op jit(solution)/shard_map/ppermute | solution.py:51
  164.6 22.4 %all-to-all-start.7 = ((f32[32,16,128]{2,1,0:T(8,128)}), f32[32,16,128]{2,1,0:T(8,128)S(1)}, u32[]{:S(2)}, u32[]{:S(2)}) async-start(f32[32,16,128]{2,1,0:T(8,128)} %broadcast_in_dim.25), calls=%async_computation.7 | async-start | bytes 524288 | tf_op jit(solution)/shard_map/all_to_all | solution.py:20
  187.7 18.5 %copy-start.4 = (f32[1,128,512]{1,2,0:T(8,128)S(1)}, f32[1,128,512]{1,2,0:T(8,128)}, u32[]{:S(2)}) copy-start(f32[1,128,512]{1,2,0:T(8,128)} %get-tuple-element.63) | copy-start | bytes 786436
  188.5 23.0 %copy-start.3 = (f32[4,64,1,512]{3,2,1,0:T(1,128)S(1)}, f32[4,64,1,512]{3,2,1,0:T(1,128)}, u32[]{:S(2)}) copy-start(f32[4,64,1,512]{3,2,1,0:T(1,128)} %get-tuple-element.60) | copy-start | bytes 1572868
  188.6 17.6 %all-to-all-start.8 = ((f32[8,128,128]{2,1,0:T(8,128)}), f32[8,128,128]{2,1,0:T(8,128)S(1)}, u32[]{:S(2)}, u32[]{:S(2)}) async-start(f32[8,128,128]{2,1,0:T(8,128)} %broadcast_in_dim.26), calls=%async_computation.8 | async-start | bytes 1048576 | tf_op jit(solution)/shard_map/all_to_all | solution.py:20
  196.4 9.8 %collective-permute-start.4 = (f32[512,128]{1,0:T(8,128)S(1)}, f32[512,128]{1,0:T(8,128)S(1)}, u32[]{:S(2)}, u32[]{:S(2)}) collective-permute-start(f32[512,128]{1,0:T(8,128)S(1)} %bitcast.137), channel_id=1, source_target_pairs={{0,8},{8,0},{16,24},{24,16},{32,40},{40,32},{48,56},{56,48},{64,72... | collective-permute-start | bytes 786440 | tf_op jit(solution)/shard_map/ppermute | solution.py:51
  206.2 5.4 %copy-start.10 = (f32[512,128]{1,0:T(8,128)}, f32[512,128]{1,0:T(8,128)S(1)}, u32[]{:S(2)}) copy-start(f32[512,128]{1,0:T(8,128)S(1)} %collective-permute-done.4) | copy-start | bytes 786436
  207.3 16.3 %all-to-all-start.9 = ((f32[32,16,128]{2,1,0:T(8,128)}), f32[32,16,128]{2,1,0:T(8,128)S(1)}, u32[]{:S(2)}, u32[]{:S(2)}) async-start(f32[32,16,128]{2,1,0:T(8,128)} %fusion.23), calls=%async_computation.9 | async-start | bytes 524288 | tf_op jit(solution)/shard_map/all_to_all | solution.py:20
  211.5 1.2 copy-start.5
  214.4 17.1 %copy-start.2 = (f32[4,64,1,512]{3,2,1,0:T(1,128)S(1)}, f32[4,64,1,512]{3,2,1,0:T(1,128)}, u32[]{:S(2)}) copy-start(f32[4,64,1,512]{3,2,1,0:T(1,128)} %get-tuple-element.59) | copy-start | bytes 1572868
  224.5 7.1 %copy-start.1 = (f32[4,64,1,512]{3,2,1,0:T(1,128)S(1)}, f32[4,64,1,512]{3,2,1,0:T(1,128)}, u32[]{:S(2)}) copy-start(f32[4,64,1,512]{3,2,1,0:T(1,128)} %get-tuple-element.58) | copy-start | bytes 1572868
  224.5 22.5 %all-to-all-start.10 = ((f32[64,16,128]{2,1,0:T(8,128)}), f32[64,16,128]{2,1,0:T(8,128)S(1)}, u32[]{:S(2)}, u32[]{:S(2)}) async-start(f32[64,16,128]{2,1,0:T(8,128)} %broadcast_in_dim.27), calls=%async_computation.10 | async-start | bytes 1048576 | tf_op jit(solution)/shard_map/all_to_all | solution.py:20
  231.5 1.0 slice-start
  231.5 1.2 copy-start.11
  232.6 1.0 copy-start.6
  232.7 1.0 copy-start.7
  249.0 15.4 %all-to-all-start.11 = ((f32[8,32,256]{2,1,0:T(8,128)}), f32[8,32,256]{2,1,0:T(8,128)S(1)}, u32[]{:S(2)}, u32[]{:S(2)}) async-start(f32[8,32,256]{2,1,0:T(8,128)} %bitcast.50), calls=%async_computation.11 | async-start | bytes 524288 | tf_op jit(solution)/shard_map/all_to_all | solution.py:20

commit v17 on v14

--- a/solution.py
+++ b/solution.py
@@ -60,9 +60,8 @@
         parts = parts.reshape(members, 2, -1, half)
         return parts.transpose(0, 2, 1, 3).reshape(width, column_count)
 
-    def scattered(matrix, current):
-        parts = contract(matrix, current, (0, 0)).reshape(members, width // members, half)
-        return swap(parts, "row", row_groups)
+    def scattered(value):
+        return swap(value.reshape(members, width // members, half), "row", row_groups)
 
     def scattered_whole(matrix, current):
         parts = contract(matrix, current, (0, 0))
@@ -99,44 +98,53 @@
         return lax.dynamic_slice_in_dim(whole, row * out_width, out_width, 1)
 
     parts = scattered_whole(own_diag[0], right_sides[0])
-    whole_0 = gathered_whole(parts).reshape(width, column_count)
+    parts, trail = by_deadline(gathered_whole(parts), trail)
+    whole_0 = parts.reshape(width, column_count)
 
-    own_shared = jnp.concatenate([own_diag[1:], lower_blocks[2:3], lower_blocks[5:]])
+    own_shared = jnp.concatenate([own_diag[1:], lower_blocks[2:3], lower_blocks[4:]])
     got_shared = from_partner(own_shared)
 
     term = own_term(1) - contract(lower_blocks[0], whole_0, (1, 0))
     parts = jnp.stack([term[:, :half], term[:, half:]])[:, None]
     parts = jnp.broadcast_to(parts, (2, col_size, local_rows, half))
     parts = swap(parts.reshape(2 * col_size, local_rows, half), ("row", "col"), pair_groups)
-    parts, got_shared = by_deadline(parts, got_shared)
-    pair = ordered(own_shared, got_shared, 1)
-    diag_1, diag_2, diag_3, lower_21, lower_32 = [pair[i] for i in range(5)]
+    diag_1 = ordered(own_shared[0], got_shared[0], 0)
+    parts, diag_1, whole_0 = by_deadline(parts, diag_1, whole_0)
+    pair = ordered(own_shared[1:], got_shared[1:], 1)
+    diag_2, diag_3, lower_21, lower_31, lower_32 = [pair[i] for i in range(5)]
     current = parts.reshape(2, col_size, local_rows, half).sum(1).reshape(2 * local_rows, half)
-    parts = scattered(diag_1, current)
-    term_2 = own_term(2) - contract(lower_blocks[1], whole_0, (1, 0))
-    parts, got_2, trail = by_deadline(parts, from_partner(half_of(term_2, row % 2 ^ 1)), trail)
-    term_2 = ordered(half_of(term_2, row % 2), got_2, 0)
-    term_3 = own_term(3) - contract(lower_blocks[3], whole_0, (1, 0))
+    parts = scattered(contract(diag_1, current, (0, 0)))
+    terms = jnp.stack(
+        [
+            own_term(2) - contract(lower_blocks[1], whole_0, (1, 0)),
+            own_term(3) - contract(lower_blocks[3], whole_0, (1, 0)),
+        ]
+    )
+    parts, got_terms = by_deadline(parts, from_partner(half_of(terms, row % 2 ^ 1)))
+    terms = ordered(half_of(terms, row % 2), got_terms, 1)
     parts = gathered(parts)
     below = below_of(whole_0, 0)
-    parts, below, term_2, term_3 = by_deadline(parts, below, term_2, term_3)
+    parts, terms, below = by_deadline(parts, terms, below)
     solved_1 = parts.reshape(width, half)
 
-    parts = summed(term_2 - contract(lower_21, solved_1, (1, 0)))
+    parts = summed(terms[0] - contract(lower_21, solved_1, (1, 0)))
     parts, got_1 = by_deadline(parts, from_partner(solved_1))
+    local_term = contract(diag_2, parts.sum(0), (0, 0))
+    local_term, got_1, solved_1 = by_deadline(local_term, got_1, solved_1)
+    parts = scattered(local_term)
+    term_3 = terms[1] - contract(lower_31, solved_1, (1, 0))
     whole_1 = ordered(solved_1, got_1, 1)
-    parts = scattered(diag_2, parts.sum(0))
-    term_3 = term_3 - contract(lower_blocks[4], whole_1, (1, 0))
-    parts, got_3 = by_deadline(parts, from_partner(half_of(term_3, row % 2 ^ 1)))
-    term_3 = ordered(half_of(term_3, row % 2), got_3, 0)
+    parts, term_3, whole_1 = by_deadline(parts, term_3, whole_1)
     parts = gathered(parts)
     below = below + below_of(whole_1, 1)
-    parts, below, term_3 = by_deadline(parts, below, term_3)
+    parts, below = by_deadline(parts, below)
     solved_2 = parts.reshape(width, half)
 
     parts = summed(term_3 - contract(lower_32, solved_2, (1, 0)))
     parts, got_2 = by_deadline(parts, from_partner(solved_2))
-    parts = scattered(diag_3, parts.sum(0))
+    local_term = contract(diag_3, parts.sum(0), (0, 0))
+    local_term, got_2, solved_2 = by_deadline(local_term, got_2, solved_2)
+    parts = scattered(local_term)
     outs = [out_of(whole_0), out_of(whole_1)]
     parts, outs = by_deadline(parts, outs)
     parts = gathered_whole(parts)

time: 271 us -> 269 us (level)
  waiting for transfers between devices: 99.9 us -> 83.5 us
  local copies, waits for them, and re-layouts: 19.1 us -> 28 us
  other arithmetic: 7.98 us -> 13.1 us
    all_to_all x11, waiting for transfers between devices: 69 us -> 58.8 us  [swap(): lax.all_to_all(parts, axis, 0, 0, axis_index_groups=groups, tiled=True)]
    unnamed x23 -> x42, local copies, waits for them, and re-layouts: 3.35 us -> 9.72 us
    ppermute x5 -> x4, waiting for transfers between devices: 30.9 us -> 24.7 us  [from_partner(): return lax.ppermute(value, 'row', [(r, r ^ 1) for r in range(row_size)])]
    ppermute x5 -> x4, starting transfers between devices: 14.5 us -> 11.3 us  [from_partner(): return lax.ppermute(value, 'row', [(r, r ^ 1) for r in range(row_size)])]
    all_to_all x11, starting transfers between devices: 75.7 us -> 78.8 us  [swap(): lax.all_to_all(parts, axis, 0, 0, axis_index_groups=groups, tiled=True)]
    dot_general x5 -> x0, local copies, waits for them, and re-layouts: 3.06 us -> none  [contract(): lax.dot_general(left, right, (((axes[0],), (axes[1],)), ((), ())), precis...]
    reduce_sum x2, other arithmetic: 0.06 us -> 2.78 us  [the longest x1 1.7 us: shards(): local_term = contract(diag_2, parts.sum(0), (0, 0))]
  transfers between devices with their start and end apart: 16 -> 15, of which waited for: 13 -> 12; matrix products, arithmetic and copies ran while one was open for 9% -> 14% of each run, Pallas kernels for 0% -> 0%
where the time goes in v17:
time: 269 us; the launch traced here: 267 us
  starting transfers between devices  90.1 us (33%)
  waiting for transfers between devices  83.5 us (31%)
  blocking collectives  33.3 us (12%)
  local copies, waits for them, and re-layouts  28 us (10%)
  matrix products  18.1 us (7%)
  other arithmetic  13.1 us (5%)
    all_to_all x11, starting transfers between devices, swap(): lax.all_to_all(parts, axis, 0, 0, axis_index_groups=groups, tiled=True)  78.8 us
    all_to_all x11, waiting for transfers between devices, swap(): lax.all_to_all(parts, axis, 0, 0, axis_index_groups=groups, tiled=True)  58.8 us
    all_to_all x1, blocking collectives, swap(): lax.all_to_all(parts, axis, 0, 0, axis_index_groups=groups, tiled=True)  33.3 us
    ppermute x4, waiting for transfers between devices, from_partner(): return lax.ppermute(value, 'row', [(r, r ^ 1) for r in range(row_size)])  24.7 us
    dot_general x14, matrix products, contract(): lax.dot_general(left, right, (((axes[0],), (axes[1],)), ((), ())), precis...  18.1 us
    ppermute x4, starting transfers between devices, from_partner(): return lax.ppermute(value, 'row', [(r, r ^ 1) for r in range(row_size)])  11.3 us
    unnamed x42, local copies, waits for them, and re-layouts  9.72 us
    slice x1, local copies, waits for them, and re-layouts, shards(): trail_panel[:, :, j, :].reshape(trail_count * local_rows, width)  5.85 us
  transfers between devices with their start and end apart: 15, of which 12 were waited for; matrix products, arithmetic and copies ran while one was open for 14% of the time, Pallas kernels for 0%

profile of v17, /device:TPU:1, one launch (start us, length us, event | category | flops | bytes accessed | tf_op | source)
XLA Modules:
  0.0 267.3 jit_solution(3061758425179748426)
XLA Ops:
  2.6 33.3 %all_to_all.64 = f32[64,8,256]{2,1,0:T(8,128)S(1)} all-to-all(f32[64,8,256]{2,1,0:T(8,128)S(1)} %fusion.23), channel_id=1, replica_groups=mesh['row'=64,'col'=8] {'row'}, dimensions={0} | all-to-all | bytes 1048576 | tf_op jit(solution)/shard_map/all_to_all | solution.py:20
  36.8 7.8 %all-to-all-start.1 = ((f32[64,8,256]{2,1,0:T(8,128)}), f32[64,8,256]{2,1,0:T(8,128)S(1)}, u32[]{:S(2)}, u32[]{:S(2)}) async-start(f32[64,8,256]{2,1,0:T(8,128)} %broadcast_in_dim.21), calls=%async_computation.1 | async-start | bytes 1048576 | tf_op jit(solution)/shard_map/all_to_all | solution.py:20
  49.7 2.9 %collective-permute-start = (f32[6,64,512]{2,1,0:T(8,128)}, f32[6,64,512]{2,1,0:T(8,128)}, u32[]{:S(2)}, u32[]{:S(2)}) collective-permute-start(f32[6,64,512]{2,1,0:T(8,128)} %copy.55), channel_id=1, source_target_pairs={{0,8},{8,0},{16,24},{24,16},{32,40},{40,32},{48,56},{56,48},{64,72... | collective-permute-start | bytes 2359304 | tf_op jit(solution)/shard_map/ppermute | solution.py:51
  52.6 5.8 %fusion.41 = (f32[4,64,1,512]{3,2,1,0:T(1,128)S(1)}, f32[4,64,1,512]{3,2,1,0:T(1,128)S(1)}, f32[4,64,1,512]{3,2,1,0:T(1,128)S(1)}, f32[4,64,1,512]{3,2,1,0:T(1,128)S(1)}) fusion(f32[4,64,4,512]{3,2,1,0:T(4,128)} %param.7), kind=kLoop, calls=%fused_computation.87 | loop fusion | bytes 4194304 | tf_op jit(solution)/shard_map/slice | solution.py:84
  63.2 7.8 %all-to-all-start.2 = ((f32[16,64,128]{2,1,0:T(8,128)}), f32[16,64,128]{2,1,0:T(8,128)S(1)}, u32[]{:S(2)}, u32[]{:S(2)}) async-start(f32[16,64,128]{2,1,0:T(8,128)} %bitcast.18), calls=%async_computation.2 | async-start | bytes 1048576 | tf_op jit(solution)/shard_map/all_to_all | solution.py:20
  71.0 5.3 %collective-permute-done = f32[6,64,512]{2,1,0:T(8,128)} collective-permute-done((f32[6,64,512]{2,1,0:T(8,128)}, f32[6,64,512]{2,1,0:T(8,128)}, u32[]{:S(2)}, u32[]{:S(2)}) %collective-permute-start) | collective-permute-done | bytes 786464 | tf_op jit(solution)/shard_map/ppermute | solution.py:51
  81.8 2.2 all-to-all-done.2
  86.4 8.9 %all-to-all-start.3 = ((f32[32,16,128]{2,1,0:T(8,128)}), f32[32,16,128]{2,1,0:T(8,128)}, u32[]{:S(2)}, u32[]{:S(2)}) async-start(f32[32,16,128]{2,1,0:T(8,128)} %fusion.42), calls=%async_computation.3 | async-start | bytes 524288 | tf_op jit(solution)/shard_map/all_to_all | solution.py:20
  96.4 3.9 %collective-permute-start.1 = (f32[2,64,128]{2,1,0:T(8,128)S(1)}, f32[2,64,128]{2,1,0:T(8,128)S(1)}, u32[]{:S(2)}, u32[]{:S(2)}) collective-permute-start(f32[2,64,128]{2,1,0:T(8,128)S(1)} %fusion.31), channel_id=1, source_target_pairs={{0,8},{8,0},{16,24},{24,16},{32,40},{40,32},{48,56},{56,48},{64,72... | collective-permute-start | bytes 196616 | tf_op jit(solution)/shard_map/ppermute | solution.py:51
  100.2 1.9 slice_select_fusion
  102.2 4.3 %collective-permute-done.1 = f32[2,64,128]{2,1,0:T(8,128)S(1)} collective-permute-done((f32[2,64,128]{2,1,0:T(8,128)S(1)}, f32[2,64,128]{2,1,0:T(8,128)S(1)}, u32[]{:S(2)}, u32[]{:S(2)}) %collective-permute-start.1) | collective-permute-done | bytes 65568 | tf_op jit(solution)/shard_map/ppermute | solution.py:51
  108.6 9.7 %all-to-all-start.4 = ((f32[32,16,128]{2,1,0:T(8,128)}), f32[32,16,128]{2,1,0:T(8,128)S(1)}, u32[]{:S(2)}, u32[]{:S(2)}) async-start(f32[32,16,128]{2,1,0:T(8,128)} %broadcast_in_dim.23), calls=%async_computation.4 | async-start | bytes 524288 | tf_op jit(solution)/shard_map/all_to_all | solution.py:20
  118.3 2.8 %fusion.43 = f32[256,256]{1,0:T(8,128)} fusion(f32[512,256]{1,0:T(8,128)S(1)} %bitcast.127, f32[256,512]{1,0:T(8,128)} %bitcast.144), kind=kOutput, calls=%fused_computation.89 | convolution fusion | flops 402653184 | bytes 1310720 | tf_op jit(solution)/shard_map/dot_general | solution.py:10
  121.2 9.8 %all-to-all-done.4 = f32[32,16,128]{2,1,0:T(8,128)S(1)} async-done(((f32[32,16,128]{2,1,0:T(8,128)}), f32[32,16,128]{2,1,0:T(8,128)S(1)}, u32[]{:S(2)}, u32[]{:S(2)}) %all-to-all-start.4) | async-done | bytes 262176 | tf_op jit(solution)/shard_map/all_to_all | solution.py:20
  132.5 6.0 %all-to-all-start.5 = ((f32[8,128,128]{2,1,0:T(8,128)}), f32[8,128,128]{2,1,0:T(8,128)}, u32[]{:S(2)}, u32[]{:S(2)}) async-start(f32[8,128,128]{2,1,0:T(8,128)} %broadcast_in_dim.24), calls=%async_computation.5 | async-start | bytes 1048576 | tf_op jit(solution)/shard_map/all_to_all | solution.py:20
  138.6 2.1 collective-permute-start.2
  140.6 7.6 %collective-permute-done.2 = f32[512,128]{1,0:T(8,128)} collective-permute-done((f32[512,128]{1,0:T(8,128)S(1)}, f32[512,128]{1,0:T(8,128)}, u32[]{:S(2)}, u32[]{:S(2)}) %collective-permute-start.2) | collective-permute-done | bytes 262176 | tf_op jit(solution)/shard_map/ppermute | solution.py:51
  150.0 2.0 fusion.15
  152.0 4.7 %all-to-all-start.6 = ((f32[32,16,128]{2,1,0:T(8,128)}), f32[32,16,128]{2,1,0:T(8,128)}, u32[]{:S(2)}, u32[]{:S(2)}) async-start(f32[32,16,128]{2,1,0:T(8,128)} %bitcast.148), calls=%async_computation.6 | async-start | bytes 524288 | tf_op jit(solution)/shard_map/all_to_all | solution.py:20
  159.9 8.6 %all-to-all-done.6 = f32[32,16,128]{2,1,0:T(8,128)} async-done(((f32[32,16,128]{2,1,0:T(8,128)}), f32[32,16,128]{2,1,0:T(8,128)}, u32[]{:S(2)}, u32[]{:S(2)}) %all-to-all-start.6) | async-done | bytes 262176 | tf_op jit(solution)/shard_map/all_to_all | solution.py:20
  170.3 6.4 %all-to-all-start.7 = ((f32[32,16,128]{2,1,0:T(8,128)}), f32[32,16,128]{2,1,0:T(8,128)S(1)}, u32[]{:S(2)}, u32[]{:S(2)}) async-start(f32[32,16,128]{2,1,0:T(8,128)} %broadcast_in_dim.25), calls=%async_computation.7 | async-start | bytes 524288 | tf_op jit(solution)/shard_map/all_to_all | solution.py:20
  176.7 3.0 %convolution_add_fusion.2 = f32[256,256]{1,0:T(8,128)} fusion(f32[256,256]{1,0:T(8,128)} %fusion.43, f32[512,256]{1,0:T(8,128)} %pad_maximum_fusion.3, f32[256,512]{1,0:T(8,128)} %bitcast.143), kind=kOutput, calls=%fused_computation.5 | convolution fusion | flops 402718720 | bytes 1572864 | tf_op jit(solution)/shard_map/dot_general | solution.py:10
  179.7 8.7 %all-to-all-done.7 = f32[32,16,128]{2,1,0:T(8,128)S(1)} async-done(((f32[32,16,128]{2,1,0:T(8,128)}), f32[32,16,128]{2,1,0:T(8,128)S(1)}, u32[]{:S(2)}, u32[]{:S(2)}) %all-to-all-start.7) | async-done | bytes 262176 | tf_op jit(solution)/shard_map/all_to_all | solution.py:20
  189.9 7.4 %all-to-all-start.8 = ((f32[8,128,128]{2,1,0:T(8,128)}), f32[8,128,128]{2,1,0:T(8,128)}, u32[]{:S(2)}, u32[]{:S(2)}) async-start(f32[8,128,128]{2,1,0:T(8,128)} %broadcast_in_dim.26), calls=%async_computation.8 | async-start | bytes 1048576 | tf_op jit(solution)/shard_map/all_to_all | solution.py:20
  197.3 2.4 collective-permute-start.3
  199.7 7.4 %collective-permute-done.3 = f32[512,128]{1,0:T(8,128)} collective-permute-done((f32[512,128]{1,0:T(8,128)S(1)}, f32[512,128]{1,0:T(8,128)}, u32[]{:S(2)}, u32[]{:S(2)}) %collective-permute-start.3) | collective-permute-done | bytes 262176 | tf_op jit(solution)/shard_map/ppermute | solution.py:51
  209.4 4.4 %all-to-all-start.9 = ((f32[32,16,128]{2,1,0:T(8,128)}), f32[32,16,128]{2,1,0:T(8,128)S(1)}, u32[]{:S(2)}, u32[]{:S(2)}) async-start(f32[32,16,128]{2,1,0:T(8,128)} %bitcast.147), calls=%async_computation.9 | async-start | bytes 524288 | tf_op jit(solution)/shard_map/all_to_all | solution.py:20
  215.0 10.7 %all-to-all-done.9 = f32[32,16,128]{2,1,0:T(8,128)S(1)} async-done(((f32[32,16,128]{2,1,0:T(8,128)}), f32[32,16,128]{2,1,0:T(8,128)S(1)}, u32[]{:S(2)}, u32[]{:S(2)}) %all-to-all-start.9) | async-done | bytes 262176 | tf_op jit(solution)/shard_map/all_to_all | solution.py:20
  226.6 7.0 %all-to-all-start.10 = ((f32[64,16,128]{2,1,0:T(8,128)}), f32[64,16,128]{2,1,0:T(8,128)S(1)}, u32[]{:S(2)}, u32[]{:S(2)}) async-start(f32[64,16,128]{2,1,0:T(8,128)} %broadcast_in_dim.27), calls=%async_computation.10 | async-start | bytes 1048576 | tf_op jit(solution)/shard_map/all_to_all | solution.py:20
  236.4 12.9 %all-to-all-done.10 = f32[64,16,128]{2,1,0:T(8,128)S(1)} async-done(((f32[64,16,128]{2,1,0:T(8,128)}), f32[64,16,128]{2,1,0:T(8,128)S(1)}, u32[]{:S(2)}, u32[]{:S(2)}) %all-to-all-start.10) | async-done | bytes 524320 | tf_op jit(solution)/shard_map/all_to_all | solution.py:20
  251.3 8.6 %all-to-all-start.11 = ((f32[8,32,256]{2,1,0:T(8,128)}), f32[8,32,256]{2,1,0:T(8,128)S(1)}, u32[]{:S(2)}, u32[]{:S(2)}) async-start(f32[8,32,256]{2,1,0:T(8,128)} %bitcast.49), calls=%async_computation.11 | async-start | bytes 524288 | tf_op jit(solution)/shard_map/all_to_all | solution.py:20
  260.9 5.6 %all-to-all-done.11 = f32[8,32,256]{2,1,0:T(8,128)S(1)} async-done(((f32[8,32,256]{2,1,0:T(8,128)}), f32[8,32,256]{2,1,0:T(8,128)S(1)}, u32[]{:S(2)}, u32[]{:S(2)}) %all-to-all-start.11) | async-done | bytes 262176 | tf_op jit(solution)/shard_map/all_to_all | solution.py:20
  (106 shorter events, 44.0 us)
Async XLA Ops:
  0.6 1.4 copy-start.5
  36.8 25.0 %all-to-all-start.1 = ((f32[64,8,256]{2,1,0:T(8,128)}), f32[64,8,256]{2,1,0:T(8,128)S(1)}, u32[]{:S(2)}, u32[]{:S(2)}) async-start(f32[64,8,256]{2,1,0:T(8,128)} %broadcast_in_dim.21), calls=%async_computation.1 | async-start | bytes 1048576 | tf_op jit(solution)/shard_map/all_to_all | solution.py:20
  44.7 1.0 slice-start
  44.7 1.2 slice-start.1
  48.3 10.2 %copy-start = (f32[6,64,512]{1,2,0:T(8,128)}, f32[6,64,512]{1,2,0:T(8,128)S(1)}, u32[]{:S(2)}) copy-start(f32[6,64,512]{1,2,0:T(8,128)S(1)} %pad_maximum_fusion) | copy-start | bytes 2359300
  49.7 26.6 %collective-permute-start = (f32[6,64,512]{2,1,0:T(8,128)}, f32[6,64,512]{2,1,0:T(8,128)}, u32[]{:S(2)}, u32[]{:S(2)}) collective-permute-start(f32[6,64,512]{2,1,0:T(8,128)} %copy.55), channel_id=1, source_target_pairs={{0,8},{8,0},{16,24},{24,16},{32,40},{40,32},{48,56},{56,48},{64,72... | collective-permute-start | bytes 2359304 | tf_op jit(solution)/shard_map/ppermute | solution.py:51
  60.2 1.7 copy-start.3
  60.2 1.7 copy-start.6
  63.2 20.8 %all-to-all-start.2 = ((f32[16,64,128]{2,1,0:T(8,128)}), f32[16,64,128]{2,1,0:T(8,128)S(1)}, u32[]{:S(2)}, u32[]{:S(2)}) async-start(f32[16,64,128]{2,1,0:T(8,128)} %bitcast.18), calls=%async_computation.2 | async-start | bytes 1048576 | tf_op jit(solution)/shard_map/all_to_all | solution.py:20
  81.8 13.5 %copy-start.7 = (f32[8,64,256]{2,1,0:T(8,128)S(1)}, f32[8,64,256]{2,1,0:T(8,128)}, u32[]{:S(2)}) copy-start(f32[8,64,256]{2,1,0:T(8,128)} %param.4) | copy-start | bytes 1572868
  85.3 10.5 %copy-start.8 = (f32[1,64,256]{2,1,0:T(8,128)}, f32[1,64,256]{2,1,0:T(8,128)S(1)}, u32[]{:S(2)}) copy-start(f32[1,64,256]{2,1,0:T(8,128)S(1)} %fusion.1) | copy-start | bytes 196612
  86.4 20.4 %all-to-all-start.3 = ((f32[32,16,128]{2,1,0:T(8,128)}), f32[32,16,128]{2,1,0:T(8,128)}, u32[]{:S(2)}, u32[]{:S(2)}) async-start(f32[32,16,128]{2,1,0:T(8,128)} %fusion.42), calls=%async_computation.3 | async-start | bytes 524288 | tf_op jit(solution)/shard_map/all_to_all | solution.py:20
  96.4 10.2 %collective-permute-start.1 = (f32[2,64,128]{2,1,0:T(8,128)S(1)}, f32[2,64,128]{2,1,0:T(8,128)S(1)}, u32[]{:S(2)}, u32[]{:S(2)}) collective-permute-start(f32[2,64,128]{2,1,0:T(8,128)S(1)} %fusion.31), channel_id=1, source_target_pairs={{0,8},{8,0},{16,24},{24,16},{32,40},{40,32},{48,56},{56,48},{64,72... | collective-permute-start | bytes 196616 | tf_op jit(solution)/shard_map/ppermute | solution.py:51
  102.2 18.9 %copy-start.9 = (f32[1,64,256]{2,1,0:T(8,128)S(1)}, f32[1,64,256]{2,1,0:T(8,128)}, u32[]{:S(2)}) copy-start(f32[1,64,256]{2,1,0:T(8,128)} %copy-done.8) | copy-start | bytes 196612
  102.2 18.9 %copy-start.11 = (f32[1,64,256]{2,1,0:T(8,128)S(1)}, f32[1,64,256]{2,1,0:T(8,128)}, u32[]{:S(2)}) copy-start(f32[1,64,256]{2,1,0:T(8,128)} %copy-done.10) | copy-start | bytes 196612
  106.5 2.0 copy-start.13
  108.6 22.4 %all-to-all-start.4 = ((f32[32,16,128]{2,1,0:T(8,128)}), f32[32,16,128]{2,1,0:T(8,128)S(1)}, u32[]{:S(2)}, u32[]{:S(2)}) async-start(f32[32,16,128]{2,1,0:T(8,128)} %broadcast_in_dim.23), calls=%async_computation.4 | async-start | bytes 524288 | tf_op jit(solution)/shard_map/all_to_all | solution.py:20
  118.3 2.8 %copy-start.14 = (f32[2,64,128]{2,1,0:T(8,128)S(1)}, f32[2,64,128]{2,1,0:T(8,128)}, u32[]{:S(2)}) copy-start(f32[2,64,128]{2,1,0:T(8,128)} %copy-done.13) | copy-start | bytes 196612
  132.5 15.8 %all-to-all-start.5 = ((f32[8,128,128]{2,1,0:T(8,128)}), f32[8,128,128]{2,1,0:T(8,128)}, u32[]{:S(2)}, u32[]{:S(2)}) async-start(f32[8,128,128]{2,1,0:T(8,128)} %broadcast_in_dim.24), calls=%async_computation.5 | async-start | bytes 1048576 | tf_op jit(solution)/shard_map/all_to_all | solution.py:20
  138.6 9.7 %collective-permute-start.2 = (f32[512,128]{1,0:T(8,128)S(1)}, f32[512,128]{1,0:T(8,128)}, u32[]{:S(2)}, u32[]{:S(2)}) collective-permute-start(f32[512,128]{1,0:T(8,128)S(1)} %bitcast.135), channel_id=1, source_target_pairs={{0,8},{8,0},{16,24},{24,16},{32,40},{40,32},{48,56},{56,48},{64,72... | collective-permute-start | bytes 786440 | tf_op jit(solution)/shard_map/ppermute | solution.py:51
  152.0 16.6 %all-to-all-start.6 = ((f32[32,16,128]{2,1,0:T(8,128)}), f32[32,16,128]{2,1,0:T(8,128)}, u32[]{:S(2)}, u32[]{:S(2)}) async-start(f32[32,16,128]{2,1,0:T(8,128)} %bitcast.148), calls=%async_computation.6 | async-start | bytes 524288 | tf_op jit(solution)/shard_map/all_to_all | solution.py:20
  159.9 28.4 %copy-start.12 = (f32[128,128]{1,0:T(8,128)S(1)}, f32[128,128]{1,0:T(8,128)}, u32[]{:S(2)}) copy-start(f32[128,128]{1,0:T(8,128)} %convolution_subtract_fusion.1) | copy-start | bytes 196612
  170.3 18.1 %all-to-all-start.7 = ((f32[32,16,128]{2,1,0:T(8,128)}), f32[32,16,128]{2,1,0:T(8,128)S(1)}, u32[]{:S(2)}, u32[]{:S(2)}) async-start(f32[32,16,128]{2,1,0:T(8,128)} %broadcast_in_dim.25), calls=%async_computation.7 | async-start | bytes 524288 | tf_op jit(solution)/shard_map/all_to_all | solution.py:20
  189.9 17.2 %all-to-all-start.8 = ((f32[8,128,128]{2,1,0:T(8,128)}), f32[8,128,128]{2,1,0:T(8,128)}, u32[]{:S(2)}, u32[]{:S(2)}) async-start(f32[8,128,128]{2,1,0:T(8,128)} %broadcast_in_dim.26), calls=%async_computation.8 | async-start | bytes 1048576 | tf_op jit(solution)/shard_map/all_to_all | solution.py:20
  197.3 9.9 %collective-permute-start.3 = (f32[512,128]{1,0:T(8,128)S(1)}, f32[512,128]{1,0:T(8,128)}, u32[]{:S(2)}, u32[]{:S(2)}) collective-permute-start(f32[512,128]{1,0:T(8,128)S(1)} %bitcast.139), channel_id=1, source_target_pairs={{0,8},{8,0},{16,24},{24,16},{32,40},{40,32},{48,56},{56,48},{64,72... | collective-permute-start | bytes 786440 | tf_op jit(solution)/shard_map/ppermute | solution.py:51
  209.4 16.3 %all-to-all-start.9 = ((f32[32,16,128]{2,1,0:T(8,128)}), f32[32,16,128]{2,1,0:T(8,128)S(1)}, u32[]{:S(2)}, u32[]{:S(2)}) async-start(f32[32,16,128]{2,1,0:T(8,128)} %bitcast.147), calls=%async_computation.9 | async-start | bytes 524288 | tf_op jit(solution)/shard_map/all_to_all | solution.py:20
  215.0 18.6 %slice-start.2 = ((f32[8,64,256]{2,1,0:T(8,128)}), f32[4,64,256]{2,1,0:T(8,128)S(1)}, s32[]{:S(2)}) async-start(f32[8,64,256]{2,1,0:T(8,128)} %param.4), calls=%async_computation.14 | async-start | bytes 524288 | tf_op jit(solution)/shard_map/slice | solution.py:92
  226.6 22.7 %all-to-all-start.10 = ((f32[64,16,128]{2,1,0:T(8,128)}), f32[64,16,128]{2,1,0:T(8,128)S(1)}, u32[]{:S(2)}, u32[]{:S(2)}) async-start(f32[64,16,128]{2,1,0:T(8,128)} %broadcast_in_dim.27), calls=%async_computation.10 | async-start | bytes 1048576 | tf_op jit(solution)/shard_map/all_to_all | solution.py:20
  233.6 1.6 copy-start.2
  233.6 1.5 copy-start.4
  236.2 13.4 %copy-start.1 = (f32[4,64,1,512]{3,1,0,2:T(8,128)S(1)}, f32[4,64,1,512]{3,1,0,2:T(8,128)}, u32[]{:S(2)}) copy-start(f32[4,64,1,512]{3,1,0,2:T(8,128)} %copy.75) | copy-start | bytes 1572868
  251.3 15.1 %all-to-all-start.11 = ((f32[8,32,256]{2,1,0:T(8,128)}), f32[8,32,256]{2,1,0:T(8,128)S(1)}, u32[]{:S(2)}, u32[]{:S(2)}) async-start(f32[8,32,256]{2,1,0:T(8,128)} %bitcast.49), calls=%async_computation.11 | async-start | bytes 524288 | tf_op jit(solution)/shard_map/all_to_all | solution.py:20
  (1 other events, 0.6 us)

commit v18 on v16

--- a/solution.py
+++ b/solution.py
@@ -99,7 +99,8 @@
         return lax.dynamic_slice_in_dim(whole, row * out_width, out_width, 1)
 
     parts = scattered_whole(own_diag[0], right_sides[0])
-    whole_0 = gathered_whole(parts).reshape(width, column_count)
+    parts, trail = by_deadline(gathered_whole(parts), trail)
+    whole_0 = parts.reshape(width, column_count)
 
     own_shared = jnp.concatenate([own_diag[1:], lower_blocks[2:3], lower_blocks[5:]])
     got_shared = from_partner(own_shared)
@@ -119,7 +120,8 @@
     term_2 = ordered(half_of(term_2, row % 2), got_2, 0)
     term_3 = own_term(3) - contract(lower_blocks[3], whole_0, (1, 0))
     parts = gathered(parts)
-    parts, term_2, term_3 = by_deadline(parts, term_2, term_3)
+    below = below_of(whole_0, 0)
+    parts, term_2, term_3, below = by_deadline(parts, term_2, term_3, below)
     solved_1 = parts.reshape(width, half)
 
     parts = summed(term_2 - contract(lower_21, solved_1, (1, 0)))
@@ -130,7 +132,7 @@
     parts, got_3 = by_deadline(parts, from_partner(half_of(term_3, row % 2 ^ 1)))
     term_3 = ordered(half_of(term_3, row % 2), got_3, 0)
     parts = gathered(parts)
-    below = below_of(whole_0, 0)
+    below = below + below_of(whole_1, 1)
     parts, below, term_3 = by_deadline(parts, below, term_3)
     solved_2 = parts.reshape(width, half)
 
@@ -138,8 +140,7 @@
     parts, got_2 = by_deadline(parts, from_partner(solved_2))
     parts = scattered(diag_3, parts.sum(0))
     outs = [out_of(whole_0), out_of(whole_1)]
-    below = below + below_of(whole_1, 1)
-    parts, outs, below = by_deadline(parts, outs, below)
+    parts, outs = by_deadline(parts, outs)
     parts = gathered_whole(parts)
     whole_2 = ordered(solved_2, got_2, 1)
     below = below + below_of(whole_2, 2)

time: 267 us -> 262 us (0.981)
  starting transfers between devices: 97.4 us -> 91.2 us
    all_to_all x11, starting transfers between devices: 83.3 us -> 78 us  [swap(): lax.all_to_all(parts, axis, 0, 0, axis_index_groups=groups, tiled=True)]
    all_to_all x11, waiting for transfers between devices: 64.5 us -> 59.3 us  [swap(): lax.all_to_all(parts, axis, 0, 0, axis_index_groups=groups, tiled=True)]
    ppermute x5, waiting for transfers between devices: 18.3 us -> 23.4 us  [from_partner(): return lax.ppermute(value, 'row', [(r, r ^ 1) for r in range(row_size)])]
    unnamed x38 -> x34, local copies, waits for them, and re-layouts: 5.94 us -> 7.12 us
  transfers between devices with their start and end apart: 16 -> 16, of which waited for: 13 -> 14; matrix products, arithmetic and copies ran while one was open for 12% -> 13% of each run, Pallas kernels for 0% -> 0%
where the time goes in v18:
time: 262 us; the launch traced here: 260 us
  starting transfers between devices  91.2 us (35%)
  waiting for transfers between devices  82.7 us (32%)
  blocking collectives  33.3 us (13%)
  local copies, waits for them, and re-layouts  24.1 us (9%)
  matrix products  18.6 us (7%)
  other arithmetic  8.98 us (3%)
    all_to_all x11, starting transfers between devices, swap(): lax.all_to_all(parts, axis, 0, 0, axis_index_groups=groups, tiled=True)  78 us
    all_to_all x11, waiting for transfers between devices, swap(): lax.all_to_all(parts, axis, 0, 0, axis_index_groups=groups, tiled=True)  59.3 us
    all_to_all x1, blocking collectives, swap(): lax.all_to_all(parts, axis, 0, 0, axis_index_groups=groups, tiled=True)  33.3 us
    ppermute x5, waiting for transfers between devices, from_partner(): return lax.ppermute(value, 'row', [(r, r ^ 1) for r in range(row_size)])  23.4 us
    dot_general x14, matrix products, contract(): lax.dot_general(left, right, (((axes[0],), (axes[1],)), ((), ())), precis...  18.6 us
    ppermute x5, starting transfers between devices, from_partner(): return lax.ppermute(value, 'row', [(r, r ^ 1) for r in range(row_size)])  13.2 us
    unnamed x34, local copies, waits for them, and re-layouts  7.12 us
    slice x1, local copies, waits for them, and re-layouts, shards(): trail_panel[:, :, j, :].reshape(trail_count * local_rows, width)  5.81 us
  transfers between devices with their start and end apart: 16, of which 14 were waited for; matrix products, arithmetic and copies ran while one was open for 13% of the time, Pallas kernels for 0%

profile of v18, /device:TPU:1, one launch (start us, length us, event | category | flops | bytes accessed | tf_op | source)
XLA Modules:
  0.0 260.0 jit_solution(15715116188446766906)
XLA Ops:
  2.7 33.3 %all_to_all.64 = f32[64,8,256]{2,1,0:T(8,128)S(1)} all-to-all(f32[64,8,256]{2,1,0:T(8,128)S(1)} %fusion.14), channel_id=1, replica_groups=mesh['row'=64,'col'=8] {'row'}, dimensions={0} | all-to-all | bytes 1048576 | tf_op jit(solution)/shard_map/all_to_all | solution.py:20
  36.9 7.8 %all-to-all-start.1 = ((f32[64,8,256]{2,1,0:T(8,128)}), f32[64,8,256]{2,1,0:T(8,128)S(1)}, u32[]{:S(2)}, u32[]{:S(2)}) async-start(f32[64,8,256]{2,1,0:T(8,128)} %broadcast_in_dim.21), calls=%async_computation.1 | async-start | bytes 1048576 | tf_op jit(solution)/shard_map/all_to_all | solution.py:20
  47.4 2.9 %collective-permute-start = (f32[5,64,512]{2,1,0:T(8,128)}, f32[5,64,512]{2,1,0:T(8,128)}, u32[]{:S(2)}, u32[]{:S(2)}) collective-permute-start(f32[5,64,512]{2,1,0:T(8,128)} %copy.57), channel_id=1, source_target_pairs={{0,8},{8,0},{16,24},{24,16},{32,40},{40,32},{48,56},{56,48},{64,72... | collective-permute-start | bytes 1966088 | tf_op jit(solution)/shard_map/ppermute | solution.py:51
  50.3 5.8 %fusion.35 = (f32[4,64,1,512]{3,2,1,0:T(1,128)S(1)}, f32[4,64,1,512]{3,2,1,0:T(1,128)S(1)}, f32[4,64,1,512]{3,2,1,0:T(1,128)S(1)}, f32[4,64,1,512]{3,2,1,0:T(1,128)S(1)}) fusion(f32[4,64,4,512]{3,2,1,0:T(4,128)} %param.7), kind=kLoop, calls=%fused_computation.84 | loop fusion | bytes 4194304 | tf_op jit(solution)/shard_map/slice | solution.py:85
  58.6 2.2 all-to-all-done.1
  63.0 8.9 %all-to-all-start.2 = ((f32[16,64,128]{2,1,0:T(8,128)}), f32[16,64,128]{2,1,0:T(8,128)}, u32[]{:S(2)}, u32[]{:S(2)}) async-start(f32[16,64,128]{2,1,0:T(8,128)} %bitcast.22), calls=%async_computation.2 | async-start | bytes 1048576 | tf_op jit(solution)/shard_map/all_to_all | solution.py:20
  79.6 2.2 all-to-all-done.2
  84.0 8.2 %all-to-all-start.3 = ((f32[32,16,128]{2,1,0:T(8,128)}), f32[32,16,128]{2,1,0:T(8,128)S(1)}, u32[]{:S(2)}, u32[]{:S(2)}) async-start(f32[32,16,128]{2,1,0:T(8,128)} %fusion.37), calls=%async_computation.3 | async-start | bytes 524288 | tf_op jit(solution)/shard_map/all_to_all | solution.py:20
  93.6 3.7 %collective-permute-start.1 = (f32[64,128]{1,0:T(8,128)S(1)}, f32[64,128]{1,0:T(8,128)}, u32[]{:S(2)}, u32[]{:S(2)}) collective-permute-start(f32[64,128]{1,0:T(8,128)S(1)} %constant_dynamic-slice_fusion.4), channel_id=1, source_target_pairs={{0,8},{8,0},{16,24},{24,16},{32,40},{40,32},{48,56},{56,48},{64,72... | collective-permute-start | bytes 98312 | tf_op jit(solution)/shard_map/ppermute | solution.py:51
  98.9 3.1 %collective-permute-done.1 = f32[64,128]{1,0:T(8,128)} collective-permute-done((f32[64,128]{1,0:T(8,128)S(1)}, f32[64,128]{1,0:T(8,128)}, u32[]{:S(2)}, u32[]{:S(2)}) %collective-permute-start.1) | collective-permute-done | bytes 32800 | tf_op jit(solution)/shard_map/ppermute | solution.py:51
  104.6 9.0 %all-to-all-start.4 = ((f32[32,16,128]{2,1,0:T(8,128)}), f32[32,16,128]{2,1,0:T(8,128)S(1)}, u32[]{:S(2)}, u32[]{:S(2)}) async-start(f32[32,16,128]{2,1,0:T(8,128)} %broadcast_in_dim.23), calls=%async_computation.4 | async-start | bytes 524288 | tf_op jit(solution)/shard_map/all_to_all | solution.py:20
  115.7 10.5 %all-to-all-done.4 = f32[32,16,128]{2,1,0:T(8,128)S(1)} async-done(((f32[32,16,128]{2,1,0:T(8,128)}), f32[32,16,128]{2,1,0:T(8,128)S(1)}, u32[]{:S(2)}, u32[]{:S(2)}) %all-to-all-start.4) | async-done | bytes 262176 | tf_op jit(solution)/shard_map/all_to_all | solution.py:20
  127.7 5.4 %all-to-all-start.5 = ((f32[8,128,128]{2,1,0:T(8,128)}), f32[8,128,128]{2,1,0:T(8,128)S(1)}, u32[]{:S(2)}, u32[]{:S(2)}) async-start(f32[8,128,128]{2,1,0:T(8,128)} %broadcast_in_dim.24), calls=%async_computation.5 | async-start | bytes 1048576 | tf_op jit(solution)/shard_map/all_to_all | solution.py:20
  133.2 2.2 collective-permute-start.2
  136.5 6.5 %collective-permute-done.2 = f32[512,128]{1,0:T(8,128)} collective-permute-done((f32[512,128]{1,0:T(8,128)S(1)}, f32[512,128]{1,0:T(8,128)}, u32[]{:S(2)}, u32[]{:S(2)}) %collective-permute-start.2) | collective-permute-done | bytes 262176 | tf_op jit(solution)/shard_map/ppermute | solution.py:51
  143.0 2.0 fusion.25
  145.0 4.7 %all-to-all-start.6 = ((f32[32,16,128]{2,1,0:T(8,128)}), f32[32,16,128]{2,1,0:T(8,128)}, u32[]{:S(2)}, u32[]{:S(2)}) async-start(f32[32,16,128]{2,1,0:T(8,128)} %fusion.25), calls=%async_computation.6 | async-start | bytes 524288 | tf_op jit(solution)/shard_map/all_to_all | solution.py:20
  152.1 2.1 collective-permute-start.3
  154.2 4.8 %collective-permute-done.3 = f32[64,128]{1,0:T(8,128)S(1)} collective-permute-done((f32[64,128]{1,0:T(8,128)S(1)}, f32[64,128]{1,0:T(8,128)S(1)}, u32[]{:S(2)}, u32[]{:S(2)}) %collective-permute-start.3) | collective-permute-done | bytes 32800 | tf_op jit(solution)/shard_map/ppermute | solution.py:51
  159.1 2.5 all-to-all-done.6
  163.3 7.0 %all-to-all-start.7 = ((f32[32,16,128]{2,1,0:T(8,128)}), f32[32,16,128]{2,1,0:T(8,128)S(1)}, u32[]{:S(2)}, u32[]{:S(2)}) async-start(f32[32,16,128]{2,1,0:T(8,128)} %broadcast_in_dim.25), calls=%async_computation.7 | async-start | bytes 524288 | tf_op jit(solution)/shard_map/all_to_all | solution.py:20
  170.3 2.8 %convolution_add_fusion.2 = f32[256,256]{1,0:T(8,128)} fusion(f32[256,256]{1,0:T(8,128)} %fusion.38, f32[256,512]{1,0:T(8,128)} %bitcast.142, f32[512,128]{1,0:T(8,128)S(1)} %get-tuple-element.81, f32[512,128]{1,0:T(8,128)S(1)} %get-tuple-element.80), kind=kOutput, calls=%fused_computation.3 | convolution fusion | flops 402849792 | bytes 1572864 | tf_op jit(solution)/shard_map/dot_general | solution.py:10
  173.1 8.7 %all-to-all-done.7 = f32[32,16,128]{2,1,0:T(8,128)S(1)} async-done(((f32[32,16,128]{2,1,0:T(8,128)}), f32[32,16,128]{2,1,0:T(8,128)S(1)}, u32[]{:S(2)}, u32[]{:S(2)}) %all-to-all-start.7) | async-done | bytes 262176 | tf_op jit(solution)/shard_map/all_to_all | solution.py:20
  183.4 8.3 %all-to-all-start.8 = ((f32[8,128,128]{2,1,0:T(8,128)}), f32[8,128,128]{2,1,0:T(8,128)S(1)}, u32[]{:S(2)}, u32[]{:S(2)}) async-start(f32[8,128,128]{2,1,0:T(8,128)} %broadcast_in_dim.26), calls=%async_computation.8 | async-start | bytes 1048576 | tf_op jit(solution)/shard_map/all_to_all | solution.py:20
  191.7 2.2 collective-permute-start.4
  193.9 7.6 %collective-permute-done.4 = f32[512,128]{1,0:T(8,128)S(1)} collective-permute-done((f32[512,128]{1,0:T(8,128)S(1)}, f32[512,128]{1,0:T(8,128)S(1)}, u32[]{:S(2)}, u32[]{:S(2)}) %collective-permute-start.4) | collective-permute-done | bytes 262176 | tf_op jit(solution)/shard_map/ppermute | solution.py:51
  202.6 4.2 %all-to-all-start.9 = ((f32[32,16,128]{2,1,0:T(8,128)}), f32[32,16,128]{2,1,0:T(8,128)S(1)}, u32[]{:S(2)}, u32[]{:S(2)}) async-start(f32[32,16,128]{2,1,0:T(8,128)} %fusion.23), calls=%async_computation.9 | async-start | bytes 524288 | tf_op jit(solution)/shard_map/all_to_all | solution.py:20
  207.3 11.8 %all-to-all-done.9 = f32[32,16,128]{2,1,0:T(8,128)S(1)} async-done(((f32[32,16,128]{2,1,0:T(8,128)}), f32[32,16,128]{2,1,0:T(8,128)S(1)}, u32[]{:S(2)}, u32[]{:S(2)}) %all-to-all-start.9) | async-done | bytes 262176 | tf_op jit(solution)/shard_map/all_to_all | solution.py:20
  219.9 6.8 %all-to-all-start.10 = ((f32[64,16,128]{2,1,0:T(8,128)}), f32[64,16,128]{2,1,0:T(8,128)S(1)}, u32[]{:S(2)}, u32[]{:S(2)}) async-start(f32[64,16,128]{2,1,0:T(8,128)} %broadcast_in_dim.27), calls=%async_computation.10 | async-start | bytes 1048576 | tf_op jit(solution)/shard_map/all_to_all | solution.py:20
  229.1 13.9 %all-to-all-done.10 = f32[64,16,128]{2,1,0:T(8,128)S(1)} async-done(((f32[64,16,128]{2,1,0:T(8,128)}), f32[64,16,128]{2,1,0:T(8,128)S(1)}, u32[]{:S(2)}, u32[]{:S(2)}) %all-to-all-start.10) | async-done | bytes 524320 | tf_op jit(solution)/shard_map/all_to_all | solution.py:20
  245.1 7.7 %all-to-all-start.11 = ((f32[8,32,256]{2,1,0:T(8,128)}), f32[8,32,256]{2,1,0:T(8,128)S(1)}, u32[]{:S(2)}, u32[]{:S(2)}) async-start(f32[8,32,256]{2,1,0:T(8,128)} %bitcast.50), calls=%async_computation.11 | async-start | bytes 524288 | tf_op jit(solution)/shard_map/all_to_all | solution.py:20
  253.6 5.6 %all-to-all-done.11 = f32[8,32,256]{2,1,0:T(8,128)S(1)} async-done(((f32[8,32,256]{2,1,0:T(8,128)}), f32[8,32,256]{2,1,0:T(8,128)S(1)}, u32[]{:S(2)}, u32[]{:S(2)}) %all-to-all-start.11) | async-done | bytes 262176 | tf_op jit(solution)/shard_map/all_to_all | solution.py:20
  (100 shorter events, 44.2 us)
Async XLA Ops:
  0.6 1.5 copy-start.7
  2.1 42.6 %copy-start.2 = (f32[4,512,64]{2,1,0:T(8,128)}, f32[4,512,64]{2,1,0:T(8,128)S(1)}, u32[]{:S(2)}) copy-start(f32[4,512,64]{2,1,0:T(8,128)S(1)} %copy.54) | copy-start | bytes 1572868
  36.9 23.9 %all-to-all-start.1 = ((f32[64,8,256]{2,1,0:T(8,128)}), f32[64,8,256]{2,1,0:T(8,128)S(1)}, u32[]{:S(2)}, u32[]{:S(2)}) async-start(f32[64,8,256]{2,1,0:T(8,128)} %broadcast_in_dim.21), calls=%async_computation.1 | async-start | bytes 1048576 | tf_op jit(solution)/shard_map/all_to_all | solution.py:20
  46.1 10.0 %copy-start = (f32[5,64,512]{1,2,0:T(8,128)}, f32[5,64,512]{1,2,0:T(8,128)S(1)}, u32[]{:S(2)}) copy-start(f32[5,64,512]{1,2,0:T(8,128)S(1)} %pad_maximum_fusion) | copy-start | bytes 1966084
  47.4 25.9 %collective-permute-start = (f32[5,64,512]{2,1,0:T(8,128)}, f32[5,64,512]{2,1,0:T(8,128)}, u32[]{:S(2)}, u32[]{:S(2)}) collective-permute-start(f32[5,64,512]{2,1,0:T(8,128)} %copy.57), channel_id=1, source_target_pairs={{0,8},{8,0},{16,24},{24,16},{32,40},{40,32},{48,56},{56,48},{64,72... | collective-permute-start | bytes 1966088 | tf_op jit(solution)/shard_map/ppermute | solution.py:51
  57.0 3.8 %copy-start.8 = (f32[8,64,256]{2,1,0:T(8,128)S(1)}, f32[8,64,256]{2,1,0:T(8,128)}, u32[]{:S(2)}) copy-start(f32[8,64,256]{2,1,0:T(8,128)} %param.4) | copy-start | bytes 1572868
  63.0 18.8 %all-to-all-start.2 = ((f32[16,64,128]{2,1,0:T(8,128)}), f32[16,64,128]{2,1,0:T(8,128)}, u32[]{:S(2)}, u32[]{:S(2)}) async-start(f32[16,64,128]{2,1,0:T(8,128)} %bitcast.22), calls=%async_computation.2 | async-start | bytes 1048576 | tf_op jit(solution)/shard_map/all_to_all | solution.py:20
  76.8 1.4 copy-start.1
  84.0 19.9 %all-to-all-start.3 = ((f32[32,16,128]{2,1,0:T(8,128)}), f32[32,16,128]{2,1,0:T(8,128)S(1)}, u32[]{:S(2)}, u32[]{:S(2)}) async-start(f32[32,16,128]{2,1,0:T(8,128)} %fusion.37), calls=%async_computation.3 | async-start | bytes 524288 | tf_op jit(solution)/shard_map/all_to_all | solution.py:20
  93.6 8.4 %collective-permute-start.1 = (f32[64,128]{1,0:T(8,128)S(1)}, f32[64,128]{1,0:T(8,128)}, u32[]{:S(2)}, u32[]{:S(2)}) collective-permute-start(f32[64,128]{1,0:T(8,128)S(1)} %constant_dynamic-slice_fusion.4), channel_id=1, source_target_pairs={{0,8},{8,0},{16,24},{24,16},{32,40},{40,32},{48,56},{56,48},{64,72... | collective-permute-start | bytes 98312 | tf_op jit(solution)/shard_map/ppermute | solution.py:51
  104.6 21.6 %all-to-all-start.4 = ((f32[32,16,128]{2,1,0:T(8,128)}), f32[32,16,128]{2,1,0:T(8,128)S(1)}, u32[]{:S(2)}, u32[]{:S(2)}) async-start(f32[32,16,128]{2,1,0:T(8,128)} %broadcast_in_dim.23), calls=%async_computation.4 | async-start | bytes 524288 | tf_op jit(solution)/shard_map/all_to_all | solution.py:20
  127.7 15.2 %all-to-all-start.5 = ((f32[8,128,128]{2,1,0:T(8,128)}), f32[8,128,128]{2,1,0:T(8,128)S(1)}, u32[]{:S(2)}, u32[]{:S(2)}) async-start(f32[8,128,128]{2,1,0:T(8,128)} %broadcast_in_dim.24), calls=%async_computation.5 | async-start | bytes 1048576 | tf_op jit(solution)/shard_map/all_to_all | solution.py:20
  133.2 9.8 %collective-permute-start.2 = (f32[512,128]{1,0:T(8,128)S(1)}, f32[512,128]{1,0:T(8,128)}, u32[]{:S(2)}, u32[]{:S(2)}) collective-permute-start(f32[512,128]{1,0:T(8,128)S(1)} %bitcast.139), channel_id=1, source_target_pairs={{0,8},{8,0},{16,24},{24,16},{32,40},{40,32},{48,56},{56,48},{64,72... | collective-permute-start | bytes 786440 | tf_op jit(solution)/shard_map/ppermute | solution.py:51
  145.0 16.6 %all-to-all-start.6 = ((f32[32,16,128]{2,1,0:T(8,128)}), f32[32,16,128]{2,1,0:T(8,128)}, u32[]{:S(2)}, u32[]{:S(2)}) async-start(f32[32,16,128]{2,1,0:T(8,128)} %fusion.25), calls=%async_computation.6 | async-start | bytes 524288 | tf_op jit(solution)/shard_map/all_to_all | solution.py:20
  152.1 7.0 %collective-permute-start.3 = (f32[64,128]{1,0:T(8,128)S(1)}, f32[64,128]{1,0:T(8,128)S(1)}, u32[]{:S(2)}, u32[]{:S(2)}) collective-permute-start(f32[64,128]{1,0:T(8,128)S(1)} %constant_dynamic-slice_fusion.3), channel_id=1, source_target_pairs={{0,8},{8,0},{16,24},{24,16},{32,40},{40,32},{48,56},{56,48},{64,72... | collective-permute-start | bytes 98312 | tf_op jit(solution)/shard_map/ppermute | solution.py:51
  163.3 18.6 %all-to-all-start.7 = ((f32[32,16,128]{2,1,0:T(8,128)}), f32[32,16,128]{2,1,0:T(8,128)S(1)}, u32[]{:S(2)}, u32[]{:S(2)}) async-start(f32[32,16,128]{2,1,0:T(8,128)} %broadcast_in_dim.25), calls=%async_computation.7 | async-start | bytes 524288 | tf_op jit(solution)/shard_map/all_to_all | solution.py:20
  182.6 19.0 %copy-start.5 = (f32[1,128,512]{1,2,0:T(8,128)S(1)}, f32[1,128,512]{1,2,0:T(8,128)}, u32[]{:S(2)}) copy-start(f32[1,128,512]{1,2,0:T(8,128)} %get-tuple-element.73) | copy-start | bytes 786436
  183.4 18.1 %all-to-all-start.8 = ((f32[8,128,128]{2,1,0:T(8,128)}), f32[8,128,128]{2,1,0:T(8,128)S(1)}, u32[]{:S(2)}, u32[]{:S(2)}) async-start(f32[8,128,128]{2,1,0:T(8,128)} %broadcast_in_dim.26), calls=%async_computation.8 | async-start | bytes 1048576 | tf_op jit(solution)/shard_map/all_to_all | solution.py:20
  191.7 9.8 %collective-permute-start.4 = (f32[512,128]{1,0:T(8,128)S(1)}, f32[512,128]{1,0:T(8,128)S(1)}, u32[]{:S(2)}, u32[]{:S(2)}) collective-permute-start(f32[512,128]{1,0:T(8,128)S(1)} %bitcast.137), channel_id=1, source_target_pairs={{0,8},{8,0},{16,24},{24,16},{32,40},{40,32},{48,56},{56,48},{64,72... | collective-permute-start | bytes 786440 | tf_op jit(solution)/shard_map/ppermute | solution.py:51
  201.5 5.7 %copy-start.9 = (f32[512,128]{1,0:T(8,128)}, f32[512,128]{1,0:T(8,128)S(1)}, u32[]{:S(2)}) copy-start(f32[512,128]{1,0:T(8,128)S(1)} %collective-permute-done.4) | copy-start | bytes 786436
  202.6 16.4 %all-to-all-start.9 = ((f32[32,16,128]{2,1,0:T(8,128)}), f32[32,16,128]{2,1,0:T(8,128)S(1)}, u32[]{:S(2)}, u32[]{:S(2)}) async-start(f32[32,16,128]{2,1,0:T(8,128)} %fusion.23), calls=%async_computation.9 | async-start | bytes 524288 | tf_op jit(solution)/shard_map/all_to_all | solution.py:20
  207.2 19.5 %slice-start = ((f32[8,64,256]{2,1,0:T(8,128)}), f32[4,64,256]{2,1,0:T(8,128)S(1)}, s32[]{:S(2)}) async-start(f32[8,64,256]{2,1,0:T(8,128)} %param.4), calls=%async_computation.12 | async-start | bytes 524288 | tf_op jit(solution)/shard_map/slice | solution.py:93
  219.1 7.9 %copy-start.10 = (f32[512,128]{1,0:T(8,128)S(1)}, f32[512,128]{1,0:T(8,128)}, u32[]{:S(2)}) copy-start(f32[512,128]{1,0:T(8,128)} %copy-done.9) | copy-start | bytes 786436
  219.9 23.1 %all-to-all-start.10 = ((f32[64,16,128]{2,1,0:T(8,128)}), f32[64,16,128]{2,1,0:T(8,128)S(1)}, u32[]{:S(2)}, u32[]{:S(2)}) async-start(f32[64,16,128]{2,1,0:T(8,128)} %broadcast_in_dim.27), calls=%async_computation.10 | async-start | bytes 1048576 | tf_op jit(solution)/shard_map/all_to_all | solution.py:20
  226.7 1.0 copy-start.4
  226.7 1.1 copy-start.6
  228.8 14.5 %copy-start.3 = (f32[4,64,1,512]{3,1,0,2:T(8,128)S(1)}, f32[4,64,1,512]{3,1,0,2:T(8,128)}, u32[]{:S(2)}) copy-start(f32[4,64,1,512]{3,1,0,2:T(8,128)} %copy.77) | copy-start | bytes 1572868
  245.1 14.2 %all-to-all-start.11 = ((f32[8,32,256]{2,1,0:T(8,128)}), f32[8,32,256]{2,1,0:T(8,128)S(1)}, u32[]{:S(2)}, u32[]{:S(2)}) async-start(f32[8,32,256]{2,1,0:T(8,128)} %bitcast.50), calls=%async_computation.11 | async-start | bytes 524288 | tf_op jit(solution)/shard_map/all_to_all | solution.py:20

commit v19 on v18

--- a/solution.py
+++ b/solution.py
@@ -42,10 +42,6 @@
     col = lax.axis_index("col")
     even = row % 2 == 0
     row_groups = [[r for r in range(row_size) if r % 2 == g] for g in range(2)]
-    pair_groups = [
-        [(r + g) * col_size + c for g in range(2) for c in range(col_size)]
-        for r in range(0, row_size, 2)
-    ]
 
     def from_partner(value):
         return lax.ppermute(value, "row", [(r, r ^ 1) for r in range(row_size)])
@@ -99,21 +95,27 @@
         return lax.dynamic_slice_in_dim(whole, row * out_width, out_width, 1)
 
     parts = scattered_whole(own_diag[0], right_sides[0])
-    parts, trail = by_deadline(gathered_whole(parts), trail)
-    whole_0 = parts.reshape(width, column_count)
-
+    part = parts.sum(0)
+    part = jnp.stack([part[:, :half], part[:, half:]])
+    parts = swap(copies(part, members).reshape(row_size, -1, half), "row")
+    own_first = lower_blocks[0]
+    got_first = from_partner(
+        jnp.concatenate([own_first, half_of(right_sides[1], row % 2 ^ 1)], 1)
+    )
+    lower_10 = ordered(own_first, got_first[:, :width], 0)
+    side_1 = ordered(half_of(right_sides[1], row % 2), got_first[:, width:], 0)
+    parts, trail, lower_10, side_1 = by_deadline(parts, trail, lower_10, side_1)
+    solved_0 = parts.reshape(width, half)
     own_shared = jnp.concatenate([own_diag[1:], lower_blocks[2:3], lower_blocks[5:]])
     got_shared = from_partner(own_shared)
 
-    term = own_term(1) - contract(lower_blocks[0], whole_0, (1, 0))
-    parts = jnp.stack([term[:, :half], term[:, half:]])[:, None]
-    parts = jnp.broadcast_to(parts, (2, col_size, local_rows, half))
-    parts = swap(parts.reshape(2 * col_size, local_rows, half), ("row", "col"), pair_groups)
+    parts = summed(contract(lower_10, solved_0, (1, 0)))
     diag_1 = ordered(own_shared[0], got_shared[0], 0)
-    parts, diag_1, whole_0 = by_deadline(parts, diag_1, whole_0)
+    parts, diag_1, got_0 = by_deadline(parts, diag_1, from_partner(solved_0))
+    whole_0 = ordered(solved_0, got_0, 1)
     pair = ordered(own_shared[1:], got_shared[1:], 1)
     diag_2, diag_3, lower_21, lower_32 = [pair[i] for i in range(4)]
-    current = parts.reshape(2, col_size, local_rows, half).sum(1).reshape(2 * local_rows, half)
+    current = side_1 - parts.sum(0)
     parts = scattered(diag_1, current)
     term_2 = own_term(2) - contract(lower_blocks[1], whole_0, (1, 0))
     parts, got_2 = by_deadline(parts, from_partner(half_of(term_2, row % 2 ^ 1)))

time: 262 us -> 274 us (1.046)
  blocking collectives: 33.3 us -> 0 us
  starting transfers between devices: 91.2 us -> 114 us
  waiting for transfers between devices: 82.7 us -> 105 us
  local copies, waits for them, and re-layouts: 24.1 us -> 19.3 us
  other arithmetic: 8.98 us -> 13.2 us
    all_to_all x1 -> x0, blocking collectives: 33.3 us -> none  [swap(): lax.all_to_all(parts, axis, 0, 0, axis_index_groups=groups, tiled=True)]
    all_to_all x11 -> x12, starting transfers between devices: 78 us -> 92.3 us  [swap(): lax.all_to_all(parts, axis, 0, 0, axis_index_groups=groups, tiled=True)]
    ppermute x5 -> x7, waiting for transfers between devices: 23.4 us -> 35.5 us  [from_partner(): return lax.ppermute(value, 'row', [(r, r ^ 1) for r in range(row_size)])]
    all_to_all x11 -> x12, waiting for transfers between devices: 59.3 us -> 69.3 us  [swap(): lax.all_to_all(parts, axis, 0, 0, axis_index_groups=groups, tiled=True)]
    ppermute x5 -> x7, starting transfers between devices: 13.2 us -> 21.5 us  [from_partner(): return lax.ppermute(value, 'row', [(r, r ^ 1) for r in range(row_size)])]
    unnamed x34 -> x25, local copies, waits for them, and re-layouts: 7.12 us -> 1.76 us
    dot_general x0 -> x3, local copies, waits for them, and re-layouts: none -> 2.98 us  [contract(): lax.dot_general(left, right, (((axes[0],), (axes[1],)), ((), ())), precis...]
    slice x3 -> x1, local copies, waits for them, and re-layouts: 2.99 us -> 0.01 us  [shards(): right_sides[1]]
  transfers between devices with their start and end apart: 16 -> 19, of which waited for: 14 -> 15; matrix products, arithmetic and copies ran while one was open for 13% -> 11% of each run, Pallas kernels for 0% -> 0%
where the time goes in v19:
time: 274 us; the launch traced here: 272 us
  starting transfers between devices  114 us (42%)
  waiting for transfers between devices  105 us (38%)
  matrix products  19.7 us (7%)
  local copies, waits for them, and re-layouts  19.3 us (7%)
  other arithmetic  13.2 us (5%)
    all_to_all x12, starting transfers between devices, swap(): lax.all_to_all(parts, axis, 0, 0, axis_index_groups=groups, tiled=True)  92.3 us
    all_to_all x12, waiting for transfers between devices, swap(): lax.all_to_all(parts, axis, 0, 0, axis_index_groups=groups, tiled=True)  69.3 us
    ppermute x7, waiting for transfers between devices, from_partner(): return lax.ppermute(value, 'row', [(r, r ^ 1) for r in range(row_size)])  35.5 us
    ppermute x7, starting transfers between devices, from_partner(): return lax.ppermute(value, 'row', [(r, r ^ 1) for r in range(row_size)])  21.5 us
    dot_general x14, matrix products, contract(): lax.dot_general(left, right, (((axes[0],), (axes[1],)), ((), ())), precis...  19.7 us
    slice x1, local copies, waits for them, and re-layouts, shards(): trail_panel[:, :, j, :].reshape(trail_count * local_rows, width)  5.82 us
    select_n x8, other arithmetic, ordered(): jnp.where(even, own, got)  5.56 us
    broadcast_in_dim x7, local copies, waits for them, and re-layouts, copies(): return jnp.broadcast_to(part[None], (count,) + part.shape)  5.52 us
  transfers between devices with their start and end apart: 19, of which 15 were waited for; matrix products, arithmetic and copies ran while one was open for 11% of the time, Pallas kernels for 0%

profile of v19, /device:TPU:1, one launch (start us, length us, event | category | flops | bytes accessed | tf_op | source)
XLA Modules:
  0.0 271.9 jit_solution(13234443280632509637)
XLA Ops:
  2.9 4.8 %collective-permute-start = (f32[5,64,512]{2,1,0:T(8,128)S(1)}, f32[5,64,512]{2,1,0:T(8,128)S(1)}, u32[]{:S(2)}, u32[]{:S(2)}) collective-permute-start(f32[5,64,512]{2,1,0:T(8,128)S(1)} %pad_maximum_fusion), channel_id=1, source_target_pairs={{0,8},{8,0},{16,24},{24,16},{32,40},{40,32},{48,56},{56,48},{64,72... | collective-permute-start | bytes 1966088 | tf_op jit(solution)/shard_map/ppermute | solution.py:47
  7.7 10.3 %collective-permute-done = f32[5,64,512]{2,1,0:T(8,128)S(1)} collective-permute-done((f32[5,64,512]{2,1,0:T(8,128)S(1)}, f32[5,64,512]{2,1,0:T(8,128)S(1)}, u32[]{:S(2)}, u32[]{:S(2)}) %collective-permute-start) | collective-permute-done | bytes 655392 | tf_op jit(solution)/shard_map/ppermute | solution.py:47
  20.3 19.5 %all-to-all-start = ((f32[64,8,256]{2,1,0:T(8,128)}), f32[64,8,256]{2,1,0:T(8,128)S(1)}, u32[]{:S(2)}, u32[]{:S(2)}) async-start(f32[64,8,256]{2,1,0:T(8,128)} %fusion.17), calls=%async_computation | async-start | bytes 1048576 | tf_op jit(solution)/shard_map/all_to_all | solution.py:20
  40.5 2.9 %collective-permute-start.1 = (f32[64,640]{1,0:T(8,128)}, f32[64,640]{1,0:T(8,128)}, u32[]{:S(2)}, u32[]{:S(2)}) collective-permute-start(f32[64,640]{1,0:T(8,128)} %pad_maximum_fusion.13), channel_id=1, source_target_pairs={{0,8},{8,0},{16,24},{24,16},{32,40},{40,32},{48,56},{56,48},{64,72... | collective-permute-start | bytes 491528 | tf_op jit(solution)/shard_map/ppermute | solution.py:47
  43.5 5.8 %fusion.43 = (f32[4,64,1,512]{3,2,1,0:T(1,128)S(1)}, f32[4,64,1,512]{3,2,1,0:T(1,128)S(1)}, f32[4,64,1,512]{3,2,1,0:T(1,128)S(1)}, f32[4,64,1,512]{3,2,1,0:T(1,128)S(1)}) fusion(f32[4,64,4,512]{3,2,1,0:T(4,128)} %param.7), kind=kLoop, calls=%fused_computation.103 | loop fusion | bytes 4194304 | tf_op jit(solution)/shard_map/slice | solution.py:81
  50.3 5.3 %all-to-all-done = f32[64,8,256]{2,1,0:T(8,128)S(1)} async-done(((f32[64,8,256]{2,1,0:T(8,128)}), f32[64,8,256]{2,1,0:T(8,128)S(1)}, u32[]{:S(2)}, u32[]{:S(2)}) %all-to-all-start) | async-done | bytes 524320 | tf_op jit(solution)/shard_map/all_to_all | solution.py:20
  56.4 7.8 %all-to-all-start.1 = ((f32[64,8,128]{2,1,0:T(8,128)}), f32[64,8,128]{2,1,0:T(8,128)S(1)}, u32[]{:S(2)}, u32[]{:S(2)}) async-start(f32[64,8,128]{2,1,0:T(8,128)} %bitcast.14), calls=%async_computation.1 | async-start | bytes 524288 | tf_op jit(solution)/shard_map/all_to_all | solution.py:20
  66.6 10.0 %all-to-all-done.1 = f32[64,8,128]{2,1,0:T(8,128)S(1)} async-done(((f32[64,8,128]{2,1,0:T(8,128)}), f32[64,8,128]{2,1,0:T(8,128)S(1)}, u32[]{:S(2)}, u32[]{:S(2)}) %all-to-all-start.1) | async-done | bytes 262176 | tf_op jit(solution)/shard_map/all_to_all | solution.py:20
  77.9 7.9 %all-to-all-start.2 = ((f32[8,128,128]{2,1,0:T(8,128)}), f32[8,128,128]{2,1,0:T(8,128)}, u32[]{:S(2)}, u32[]{:S(2)}) async-start(f32[8,128,128]{2,1,0:T(8,128)} %broadcast_in_dim.20), calls=%async_computation.2 | async-start | bytes 1048576 | tf_op jit(solution)/shard_map/all_to_all | solution.py:20
  90.0 6.4 %collective-permute-done.2 = f32[512,128]{1,0:T(8,128)} collective-permute-done((f32[512,128]{1,0:T(8,128)S(1)}, f32[512,128]{1,0:T(8,128)}, u32[]{:S(2)}, u32[]{:S(2)}) %collective-permute-start.2) | collective-permute-done | bytes 262176 | tf_op jit(solution)/shard_map/ppermute | solution.py:47
  100.8 3.9 %all-to-all-start.3 = ((f32[32,16,128]{2,1,0:T(8,128)}), f32[32,16,128]{2,1,0:T(8,128)S(1)}, u32[]{:S(2)}, u32[]{:S(2)}) async-start(f32[32,16,128]{2,1,0:T(8,128)} %bitcast.134), calls=%async_computation.3 | async-start | bytes 524288 | tf_op jit(solution)/shard_map/all_to_all | solution.py:20
  110.0 3.9 %collective-permute-done.3 = f32[64,128]{1,0:T(8,128)S(1)} collective-permute-done((f32[64,128]{1,0:T(8,128)S(1)}, f32[64,128]{1,0:T(8,128)S(1)}, u32[]{:S(2)}, u32[]{:S(2)}) %collective-permute-start.3) | collective-permute-done | bytes 32800 | tf_op jit(solution)/shard_map/ppermute | solution.py:47
  113.9 3.0 %all-to-all-done.3 = f32[32,16,128]{2,1,0:T(8,128)S(1)} async-done(((f32[32,16,128]{2,1,0:T(8,128)}), f32[32,16,128]{2,1,0:T(8,128)S(1)}, u32[]{:S(2)}, u32[]{:S(2)}) %all-to-all-start.3) | async-done | bytes 262176 | tf_op jit(solution)/shard_map/all_to_all | solution.py:20
  117.7 7.2 %all-to-all-start.4 = ((f32[32,16,128]{2,1,0:T(8,128)}), f32[32,16,128]{2,1,0:T(8,128)S(1)}, u32[]{:S(2)}, u32[]{:S(2)}) async-start(f32[32,16,128]{2,1,0:T(8,128)} %broadcast_in_dim.22), calls=%async_computation.4 | async-start | bytes 524288 | tf_op jit(solution)/shard_map/all_to_all | solution.py:20
  126.8 10.4 %all-to-all-done.4 = f32[32,16,128]{2,1,0:T(8,128)S(1)} async-done(((f32[32,16,128]{2,1,0:T(8,128)}), f32[32,16,128]{2,1,0:T(8,128)S(1)}, u32[]{:S(2)}, u32[]{:S(2)}) %all-to-all-start.4) | async-done | bytes 262176 | tf_op jit(solution)/shard_map/all_to_all | solution.py:20
  138.5 6.2 %all-to-all-start.5 = ((f32[8,128,128]{2,1,0:T(8,128)}), f32[8,128,128]{2,1,0:T(8,128)S(1)}, u32[]{:S(2)}, u32[]{:S(2)}) async-start(f32[8,128,128]{2,1,0:T(8,128)} %broadcast_in_dim.23), calls=%async_computation.5 | async-start | bytes 1048576 | tf_op jit(solution)/shard_map/all_to_all | solution.py:20
  144.7 3.1 %collective-permute-start.4 = (f32[512,128]{1,0:T(8,128)S(1)}, f32[512,128]{1,0:T(8,128)}, u32[]{:S(2)}, u32[]{:S(2)}) collective-permute-start(f32[512,128]{1,0:T(8,128)S(1)} %bitcast.127), channel_id=1, source_target_pairs={{0,8},{8,0},{16,24},{24,16},{32,40},{40,32},{48,56},{56,48},{64,72... | collective-permute-start | bytes 786440 | tf_op jit(solution)/shard_map/ppermute | solution.py:47
  150.5 4.3 %collective-permute-done.4 = f32[512,128]{1,0:T(8,128)} collective-permute-done((f32[512,128]{1,0:T(8,128)S(1)}, f32[512,128]{1,0:T(8,128)}, u32[]{:S(2)}, u32[]{:S(2)}) %collective-permute-start.4) | collective-permute-done | bytes 262176 | tf_op jit(solution)/shard_map/ppermute | solution.py:47
  156.8 4.8 %all-to-all-start.6 = ((f32[32,16,128]{2,1,0:T(8,128)}), f32[32,16,128]{2,1,0:T(8,128)}, u32[]{:S(2)}, u32[]{:S(2)}) async-start(f32[32,16,128]{2,1,0:T(8,128)} %fusion.27), calls=%async_computation.6 | async-start | bytes 524288 | tf_op jit(solution)/shard_map/all_to_all | solution.py:20
  164.0 3.1 %collective-permute-start.5 = (f32[64,128]{1,0:T(8,128)S(1)}, f32[64,128]{1,0:T(8,128)S(1)}, u32[]{:S(2)}, u32[]{:S(2)}) collective-permute-start(f32[64,128]{1,0:T(8,128)S(1)} %constant_dynamic-slice_fusion.2), channel_id=1, source_target_pairs={{0,8},{8,0},{16,24},{24,16},{32,40},{40,32},{48,56},{56,48},{64,72... | collective-permute-start | bytes 98312 | tf_op jit(solution)/shard_map/ppermute | solution.py:47
  167.1 4.7 %collective-permute-done.5 = f32[64,128]{1,0:T(8,128)S(1)} collective-permute-done((f32[64,128]{1,0:T(8,128)S(1)}, f32[64,128]{1,0:T(8,128)S(1)}, u32[]{:S(2)}, u32[]{:S(2)}) %collective-permute-start.5) | collective-permute-done | bytes 32800 | tf_op jit(solution)/shard_map/ppermute | solution.py:47
  175.1 7.5 %all-to-all-start.7 = ((f32[32,16,128]{2,1,0:T(8,128)}), f32[32,16,128]{2,1,0:T(8,128)S(1)}, u32[]{:S(2)}, u32[]{:S(2)}) async-start(f32[32,16,128]{2,1,0:T(8,128)} %broadcast_in_dim.24), calls=%async_computation.7 | async-start | bytes 524288 | tf_op jit(solution)/shard_map/all_to_all | solution.py:20
  185.4 9.0 %all-to-all-done.7 = f32[32,16,128]{2,1,0:T(8,128)S(1)} async-done(((f32[32,16,128]{2,1,0:T(8,128)}), f32[32,16,128]{2,1,0:T(8,128)S(1)}, u32[]{:S(2)}, u32[]{:S(2)}) %all-to-all-start.7) | async-done | bytes 262176 | tf_op jit(solution)/shard_map/all_to_all | solution.py:20
  195.6 7.5 %all-to-all-start.8 = ((f32[8,128,128]{2,1,0:T(8,128)}), f32[8,128,128]{2,1,0:T(8,128)S(1)}, u32[]{:S(2)}, u32[]{:S(2)}) async-start(f32[8,128,128]{2,1,0:T(8,128)} %broadcast_in_dim.25), calls=%async_computation.8 | async-start | bytes 1048576 | tf_op jit(solution)/shard_map/all_to_all | solution.py:20
  203.1 2.9 %collective-permute-start.6 = (f32[512,128]{1,0:T(8,128)S(1)}, f32[512,128]{1,0:T(8,128)S(1)}, u32[]{:S(2)}, u32[]{:S(2)}) collective-permute-start(f32[512,128]{1,0:T(8,128)S(1)} %bitcast.125), channel_id=1, source_target_pairs={{0,8},{8,0},{16,24},{24,16},{32,40},{40,32},{48,56},{56,48},{64,72... | collective-permute-start | bytes 786440 | tf_op jit(solution)/shard_map/ppermute | solution.py:47
  207.1 5.8 %collective-permute-done.6 = f32[512,128]{1,0:T(8,128)S(1)} collective-permute-done((f32[512,128]{1,0:T(8,128)S(1)}, f32[512,128]{1,0:T(8,128)S(1)}, u32[]{:S(2)}, u32[]{:S(2)}) %collective-permute-start.6) | collective-permute-done | bytes 262176 | tf_op jit(solution)/shard_map/ppermute | solution.py:47
  214.1 4.0 %all-to-all-start.9 = ((f32[32,16,128]{2,1,0:T(8,128)}), f32[32,16,128]{2,1,0:T(8,128)S(1)}, u32[]{:S(2)}, u32[]{:S(2)}) async-start(f32[32,16,128]{2,1,0:T(8,128)} %fusion.25), calls=%async_computation.9 | async-start | bytes 524288 | tf_op jit(solution)/shard_map/all_to_all | solution.py:20
  218.5 11.6 %all-to-all-done.9 = f32[32,16,128]{2,1,0:T(8,128)S(1)} async-done(((f32[32,16,128]{2,1,0:T(8,128)}), f32[32,16,128]{2,1,0:T(8,128)S(1)}, u32[]{:S(2)}, u32[]{:S(2)}) %all-to-all-start.9) | async-done | bytes 262176 | tf_op jit(solution)/shard_map/all_to_all | solution.py:20
  231.0 7.1 %all-to-all-start.10 = ((f32[64,16,128]{2,1,0:T(8,128)}), f32[64,16,128]{2,1,0:T(8,128)S(1)}, u32[]{:S(2)}, u32[]{:S(2)}) async-start(f32[64,16,128]{2,1,0:T(8,128)} %broadcast_in_dim.26), calls=%async_computation.10 | async-start | bytes 1048576 | tf_op jit(solution)/shard_map/all_to_all | solution.py:20
  241.0 12.7 %all-to-all-done.10 = f32[64,16,128]{2,1,0:T(8,128)S(1)} async-done(((f32[64,16,128]{2,1,0:T(8,128)}), f32[64,16,128]{2,1,0:T(8,128)S(1)}, u32[]{:S(2)}, u32[]{:S(2)}) %all-to-all-start.10) | async-done | bytes 524320 | tf_op jit(solution)/shard_map/all_to_all | solution.py:20
  255.7 8.9 %all-to-all-start.11 = ((f32[8,32,256]{2,1,0:T(8,128)}), f32[8,32,256]{2,1,0:T(8,128)S(1)}, u32[]{:S(2)}, u32[]{:S(2)}) async-start(f32[8,32,256]{2,1,0:T(8,128)} %bitcast.46), calls=%async_computation.11 | async-start | bytes 524288 | tf_op jit(solution)/shard_map/all_to_all | solution.py:20
  265.5 5.6 %all-to-all-done.11 = f32[8,32,256]{2,1,0:T(8,128)S(1)} async-done(((f32[8,32,256]{2,1,0:T(8,128)}), f32[8,32,256]{2,1,0:T(8,128)S(1)}, u32[]{:S(2)}, u32[]{:S(2)}) %all-to-all-start.11) | async-done | bytes 262176 | tf_op jit(solution)/shard_map/all_to_all | solution.py:20
  (104 shorter events, 52.7 us)
Async XLA Ops:
  0.6 17.4 %copy-start.1 = (f32[4,512,64]{1,2,0:T(8,128)S(1)}, f32[4,512,64]{1,2,0:T(8,128)}, u32[]{:S(2)}) copy-start(f32[4,512,64]{1,2,0:T(8,128)} %param.5) | copy-start | bytes 1572868
  0.6 18.3 %copy-start.3 = (f32[8,64,256]{2,1,0:T(8,128)S(1)}, f32[8,64,256]{2,1,0:T(8,128)}, u32[]{:S(2)}) copy-start(f32[8,64,256]{2,1,0:T(8,128)} %param.4) | copy-start | bytes 1572868
  2.9 15.1 %collective-permute-start = (f32[5,64,512]{2,1,0:T(8,128)S(1)}, f32[5,64,512]{2,1,0:T(8,128)S(1)}, u32[]{:S(2)}, u32[]{:S(2)}) collective-permute-start(f32[5,64,512]{2,1,0:T(8,128)S(1)} %pad_maximum_fusion), channel_id=1, source_target_pairs={{0,8},{8,0},{16,24},{24,16},{32,40},{40,32},{48,56},{56,48},{64,72... | collective-permute-start | bytes 1966088 | tf_op jit(solution)/shard_map/ppermute | solution.py:47
  18.0 2.3 copy-start.2
  20.3 35.2 %all-to-all-start = ((f32[64,8,256]{2,1,0:T(8,128)}), f32[64,8,256]{2,1,0:T(8,128)S(1)}, u32[]{:S(2)}, u32[]{:S(2)}) async-start(f32[64,8,256]{2,1,0:T(8,128)} %fusion.17), calls=%async_computation | async-start | bytes 1048576 | tf_op jit(solution)/shard_map/all_to_all | solution.py:20
  39.8 3.6 %copy-start.6 = (f32[1,64,256]{2,1,0:T(8,128)}, f32[1,64,256]{2,1,0:T(8,128)S(1)}, u32[]{:S(2)}) copy-start(f32[1,64,256]{2,1,0:T(8,128)S(1)} %slice.105) | copy-start | bytes 196612
  40.5 23.6 %collective-permute-start.1 = (f32[64,640]{1,0:T(8,128)}, f32[64,640]{1,0:T(8,128)}, u32[]{:S(2)}, u32[]{:S(2)}) collective-permute-start(f32[64,640]{1,0:T(8,128)} %pad_maximum_fusion.13), channel_id=1, source_target_pairs={{0,8},{8,0},{16,24},{24,16},{32,40},{40,32},{48,56},{56,48},{64,72... | collective-permute-start | bytes 491528 | tf_op jit(solution)/shard_map/ppermute | solution.py:47
  56.4 29.4 %copy-start.4 = (f32[64,512]{1,0:T(8,128)S(1)}, f32[64,512]{1,0:T(8,128)}, u32[]{:S(2)}) copy-start(f32[64,512]{1,0:T(8,128)} %get-tuple-element.74) | copy-start | bytes 393220
  56.4 29.4 %copy-start.5 = (f32[64,512]{1,0:T(8,128)S(1)}, f32[64,512]{1,0:T(8,128)}, u32[]{:S(2)}) copy-start(f32[64,512]{1,0:T(8,128)} %get-tuple-element.75) | copy-start | bytes 393220
  56.4 20.3 %all-to-all-start.1 = ((f32[64,8,128]{2,1,0:T(8,128)}), f32[64,8,128]{2,1,0:T(8,128)S(1)}, u32[]{:S(2)}, u32[]{:S(2)}) async-start(f32[64,8,128]{2,1,0:T(8,128)} %bitcast.14), calls=%async_computation.1 | async-start | bytes 524288 | tf_op jit(solution)/shard_map/all_to_all | solution.py:20
  77.9 18.6 %all-to-all-start.2 = ((f32[8,128,128]{2,1,0:T(8,128)}), f32[8,128,128]{2,1,0:T(8,128)}, u32[]{:S(2)}, u32[]{:S(2)}) async-start(f32[8,128,128]{2,1,0:T(8,128)} %broadcast_in_dim.20), calls=%async_computation.2 | async-start | bytes 1048576 | tf_op jit(solution)/shard_map/all_to_all | solution.py:20
  86.5 9.9 %collective-permute-start.2 = (f32[512,128]{1,0:T(8,128)S(1)}, f32[512,128]{1,0:T(8,128)}, u32[]{:S(2)}, u32[]{:S(2)}) collective-permute-start(f32[512,128]{1,0:T(8,128)S(1)} %bitcast.123), channel_id=1, source_target_pairs={{0,8},{8,0},{16,24},{24,16},{32,40},{40,32},{48,56},{56,48},{64,72... | collective-permute-start | bytes 786440 | tf_op jit(solution)/shard_map/ppermute | solution.py:47
  100.8 16.1 %all-to-all-start.3 = ((f32[32,16,128]{2,1,0:T(8,128)}), f32[32,16,128]{2,1,0:T(8,128)S(1)}, u32[]{:S(2)}, u32[]{:S(2)}) async-start(f32[32,16,128]{2,1,0:T(8,128)} %bitcast.134), calls=%async_computation.3 | async-start | bytes 524288 | tf_op jit(solution)/shard_map/all_to_all | solution.py:20
  106.0 7.9 %collective-permute-start.3 = (f32[64,128]{1,0:T(8,128)S(1)}, f32[64,128]{1,0:T(8,128)S(1)}, u32[]{:S(2)}, u32[]{:S(2)}) collective-permute-start(f32[64,128]{1,0:T(8,128)S(1)} %constant_dynamic-slice_fusion.3), channel_id=1, source_target_pairs={{0,8},{8,0},{16,24},{24,16},{32,40},{40,32},{48,56},{56,48},{64,72... | collective-permute-start | bytes 98312 | tf_op jit(solution)/shard_map/ppermute | solution.py:47
  117.7 19.6 %all-to-all-start.4 = ((f32[32,16,128]{2,1,0:T(8,128)}), f32[32,16,128]{2,1,0:T(8,128)S(1)}, u32[]{:S(2)}, u32[]{:S(2)}) async-start(f32[32,16,128]{2,1,0:T(8,128)} %broadcast_in_dim.22), calls=%async_computation.4 | async-start | bytes 524288 | tf_op jit(solution)/shard_map/all_to_all | solution.py:20
  138.5 16.3 %all-to-all-start.5 = ((f32[8,128,128]{2,1,0:T(8,128)}), f32[8,128,128]{2,1,0:T(8,128)S(1)}, u32[]{:S(2)}, u32[]{:S(2)}) async-start(f32[8,128,128]{2,1,0:T(8,128)} %broadcast_in_dim.23), calls=%async_computation.5 | async-start | bytes 1048576 | tf_op jit(solution)/shard_map/all_to_all | solution.py:20
  144.7 17.9 %copy-start.8 = (f32[64,256]{1,0:T(8,128)S(1)}, f32[64,256]{1,0:T(8,128)}, u32[]{:S(2)}) copy-start(f32[64,256]{1,0:T(8,128)} %fusion.1) | copy-start | bytes 196612
  144.7 10.0 %collective-permute-start.4 = (f32[512,128]{1,0:T(8,128)S(1)}, f32[512,128]{1,0:T(8,128)}, u32[]{:S(2)}, u32[]{:S(2)}) collective-permute-start(f32[512,128]{1,0:T(8,128)S(1)} %bitcast.127), channel_id=1, source_target_pairs={{0,8},{8,0},{16,24},{24,16},{32,40},{40,32},{48,56},{56,48},{64,72... | collective-permute-start | bytes 786440 | tf_op jit(solution)/shard_map/ppermute | solution.py:47
  156.8 16.5 %all-to-all-start.6 = ((f32[32,16,128]{2,1,0:T(8,128)}), f32[32,16,128]{2,1,0:T(8,128)}, u32[]{:S(2)}, u32[]{:S(2)}) async-start(f32[32,16,128]{2,1,0:T(8,128)} %fusion.27), calls=%async_computation.6 | async-start | bytes 524288 | tf_op jit(solution)/shard_map/all_to_all | solution.py:20
  164.0 7.8 %collective-permute-start.5 = (f32[64,128]{1,0:T(8,128)S(1)}, f32[64,128]{1,0:T(8,128)S(1)}, u32[]{:S(2)}, u32[]{:S(2)}) collective-permute-start(f32[64,128]{1,0:T(8,128)S(1)} %constant_dynamic-slice_fusion.2), channel_id=1, source_target_pairs={{0,8},{8,0},{16,24},{24,16},{32,40},{40,32},{48,56},{56,48},{64,72... | collective-permute-start | bytes 98312 | tf_op jit(solution)/shard_map/ppermute | solution.py:47
  175.1 19.3 %all-to-all-start.7 = ((f32[32,16,128]{2,1,0:T(8,128)}), f32[32,16,128]{2,1,0:T(8,128)S(1)}, u32[]{:S(2)}, u32[]{:S(2)}) async-start(f32[32,16,128]{2,1,0:T(8,128)} %broadcast_in_dim.24), calls=%async_computation.7 | async-start | bytes 524288 | tf_op jit(solution)/shard_map/all_to_all | solution.py:20
  195.6 17.3 %all-to-all-start.8 = ((f32[8,128,128]{2,1,0:T(8,128)}), f32[8,128,128]{2,1,0:T(8,128)S(1)}, u32[]{:S(2)}, u32[]{:S(2)}) async-start(f32[8,128,128]{2,1,0:T(8,128)} %broadcast_in_dim.25), calls=%async_computation.8 | async-start | bytes 1048576 | tf_op jit(solution)/shard_map/all_to_all | solution.py:20
  203.1 9.8 %collective-permute-start.6 = (f32[512,128]{1,0:T(8,128)S(1)}, f32[512,128]{1,0:T(8,128)S(1)}, u32[]{:S(2)}, u32[]{:S(2)}) collective-permute-start(f32[512,128]{1,0:T(8,128)S(1)} %bitcast.125), channel_id=1, source_target_pairs={{0,8},{8,0},{16,24},{24,16},{32,40},{40,32},{48,56},{56,48},{64,72... | collective-permute-start | bytes 786440 | tf_op jit(solution)/shard_map/ppermute | solution.py:47
  212.9 5.2 %copy-start.7 = (f32[512,128]{1,0:T(8,128)}, f32[512,128]{1,0:T(8,128)S(1)}, u32[]{:S(2)}) copy-start(f32[512,128]{1,0:T(8,128)S(1)} %collective-permute-done.6) | copy-start | bytes 786436
  214.1 16.1 %all-to-all-start.9 = ((f32[32,16,128]{2,1,0:T(8,128)}), f32[32,16,128]{2,1,0:T(8,128)S(1)}, u32[]{:S(2)}, u32[]{:S(2)}) async-start(f32[32,16,128]{2,1,0:T(8,128)} %fusion.25), calls=%async_computation.9 | async-start | bytes 524288 | tf_op jit(solution)/shard_map/all_to_all | solution.py:20
  218.1 20.1 %slice-start = ((f32[8,64,256]{2,1,0:T(8,128)}), f32[4,64,256]{2,1,0:T(8,128)S(1)}, s32[]{:S(2)}) async-start(f32[8,64,256]{2,1,0:T(8,128)} %param.4), calls=%async_computation.12 | async-start | bytes 524288 | tf_op jit(solution)/shard_map/slice | solution.py:89
  231.0 8.7 %copy-start = (f32[256,256]{1,0:T(8,128)S(1)}, f32[256,256]{1,0:T(8,128)}, u32[]{:S(2)}) copy-start(f32[256,256]{1,0:T(8,128)} %convolution_add_fusion.2) | copy-start | bytes 786436
  231.0 22.6 %all-to-all-start.10 = ((f32[64,16,128]{2,1,0:T(8,128)}), f32[64,16,128]{2,1,0:T(8,128)S(1)}, u32[]{:S(2)}, u32[]{:S(2)}) async-start(f32[64,16,128]{2,1,0:T(8,128)} %broadcast_in_dim.26), calls=%async_computation.10 | async-start | bytes 1048576 | tf_op jit(solution)/shard_map/all_to_all | solution.py:20
  255.7 15.4 %all-to-all-start.11 = ((f32[8,32,256]{2,1,0:T(8,128)}), f32[8,32,256]{2,1,0:T(8,128)S(1)}, u32[]{:S(2)}, u32[]{:S(2)}) async-start(f32[8,32,256]{2,1,0:T(8,128)} %bitcast.46), calls=%async_computation.11 | async-start | bytes 524288 | tf_op jit(solution)/shard_map/all_to_all | solution.py:20

commit v20 on v19

--- a/solution.py
+++ b/solution.py
@@ -95,19 +95,18 @@
         return lax.dynamic_slice_in_dim(whole, row * out_width, out_width, 1)
 
     parts = scattered_whole(own_diag[0], right_sides[0])
-    part = parts.sum(0)
+    sent_first = jnp.concatenate([lower_blocks[0], half_of(right_sides[1], row % 2 ^ 1)], 1)
+    part, sent_first = by_deadline(parts.sum(0), sent_first)
     part = jnp.stack([part[:, :half], part[:, half:]])
     parts = swap(copies(part, members).reshape(row_size, -1, half), "row")
-    own_first = lower_blocks[0]
-    got_first = from_partner(
-        jnp.concatenate([own_first, half_of(right_sides[1], row % 2 ^ 1)], 1)
-    )
-    lower_10 = ordered(own_first, got_first[:, :width], 0)
+    got_first = from_partner(sent_first)
+    own_shared = jnp.concatenate([own_diag[1:], lower_blocks[2:3], lower_blocks[5:]])
+    got_first, own_shared = by_deadline(got_first, own_shared)
+    got_shared = from_partner(own_shared)
+    lower_10 = ordered(lower_blocks[0], got_first[:, :width], 0)
     side_1 = ordered(half_of(right_sides[1], row % 2), got_first[:, width:], 0)
     parts, trail, lower_10, side_1 = by_deadline(parts, trail, lower_10, side_1)
     solved_0 = parts.reshape(width, half)
-    own_shared = jnp.concatenate([own_diag[1:], lower_blocks[2:3], lower_blocks[5:]])
-    got_shared = from_partner(own_shared)
 
     parts = summed(contract(lower_10, solved_0, (1, 0)))
     diag_1 = ordered(own_shared[0], got_shared[0], 0)

time: 274 us -> 262 us (0.956)
  waiting for transfers between devices: 105 us -> 97.6 us
  starting transfers between devices: 114 us -> 111 us
    ppermute x7, waiting for transfers between devices: 35.5 us -> 24.9 us  [from_partner(): return lax.ppermute(value, 'row', [(r, r ^ 1) for r in range(row_size)])]
    slice x1, local copies, waits for them, and re-layouts: 5.82 us -> 1.53 us  [shards(): trail_panel[:, :, j, :].reshape(trail_count * local_rows, width)]
    all_to_all x12, waiting for transfers between devices: 69.3 us -> 72.7 us  [swap(): lax.all_to_all(parts, axis, 0, 0, axis_index_groups=groups, tiled=True)]
    ppermute x7, starting transfers between devices: 21.5 us -> 18.5 us  [from_partner(): return lax.ppermute(value, 'row', [(r, r ^ 1) for r in range(row_size)])]
  transfers between devices with their start and end apart: 19 -> 19, of which waited for: 15 -> 14; matrix products, arithmetic and copies ran while one was open for 11% -> 11% of each run, Pallas kernels for 0% -> 0%
where the time goes in v20:
time: 262 us; the launch traced here: 260 us
  starting transfers between devices  111 us (42%)
  waiting for transfers between devices  97.6 us (37%)
  matrix products  19.9 us (8%)
  local copies, waits for them, and re-layouts  17.3 us (7%)
  other arithmetic  13.2 us (5%)
    all_to_all x12, starting transfers between devices, swap(): lax.all_to_all(parts, axis, 0, 0, axis_index_groups=groups, tiled=True)  92.4 us
    all_to_all x12, waiting for transfers between devices, swap(): lax.all_to_all(parts, axis, 0, 0, axis_index_groups=groups, tiled=True)  72.7 us
    ppermute x7, waiting for transfers between devices, from_partner(): return lax.ppermute(value, 'row', [(r, r ^ 1) for r in range(row_size)])  24.9 us
    dot_general x14, matrix products, contract(): lax.dot_general(left, right, (((axes[0],), (axes[1],)), ((), ())), precis...  19.9 us
    ppermute x7, starting transfers between devices, from_partner(): return lax.ppermute(value, 'row', [(r, r ^ 1) for r in range(row_size)])  18.5 us
    broadcast_in_dim x7, local copies, waits for them, and re-layouts, copies(): return jnp.broadcast_to(part[None], (count,) + part.shape)  5.43 us
  transfers between devices with their start and end apart: 19, of which 14 were waited for; matrix products, arithmetic and copies ran while one was open for 11% of the time, Pallas kernels for 0%

profile of v20, /device:TPU:1, one launch (start us, length us, event | category | flops | bytes accessed | tf_op | source)
XLA Modules:
  0.0 260.0 jit_solution(15755263155440023029)
XLA Ops:
  4.1 17.4 %all-to-all-start = ((f32[64,8,256]{2,1,0:T(8,128)}), f32[64,8,256]{2,1,0:T(8,128)}, u32[]{:S(2)}, u32[]{:S(2)}) async-start(f32[64,8,256]{2,1,0:T(8,128)} %fusion.17), calls=%async_computation | async-start | bytes 1048576 | tf_op jit(solution)/shard_map/all_to_all | solution.py:20
  27.5 10.2 %all-to-all-done = f32[64,8,256]{2,1,0:T(8,128)} async-done(((f32[64,8,256]{2,1,0:T(8,128)}), f32[64,8,256]{2,1,0:T(8,128)}, u32[]{:S(2)}, u32[]{:S(2)}) %all-to-all-start) | async-done | bytes 524320 | tf_op jit(solution)/shard_map/all_to_all | solution.py:20
  38.8 3.0 %collective-permute-start = (f32[64,640]{1,0:T(8,128)}, f32[64,640]{1,0:T(8,128)}, u32[]{:S(2)}, u32[]{:S(2)}) collective-permute-start(f32[64,640]{1,0:T(8,128)} %pad_maximum_fusion.13), channel_id=1, source_target_pairs={{0,8},{8,0},{16,24},{24,16},{32,40},{40,32},{48,56},{56,48},{64,72... | collective-permute-start | bytes 491528 | tf_op jit(solution)/shard_map/ppermute | solution.py:47
  42.5 7.6 %all-to-all-start.1 = ((f32[64,8,128]{2,1,0:T(8,128)}), f32[64,8,128]{2,1,0:T(8,128)S(1)}, u32[]{:S(2)}, u32[]{:S(2)}) async-start(f32[64,8,128]{2,1,0:T(8,128)} %bitcast.16), calls=%async_computation.1 | async-start | bytes 524288 | tf_op jit(solution)/shard_map/all_to_all | solution.py:20
  50.1 2.9 %collective-permute-start.1 = (f32[5,64,512]{2,1,0:T(8,128)S(1)}, f32[5,64,512]{2,1,0:T(8,128)S(1)}, u32[]{:S(2)}, u32[]{:S(2)}) collective-permute-start(f32[5,64,512]{2,1,0:T(8,128)S(1)} %pad_maximum_fusion), channel_id=1, source_target_pairs={{0,8},{8,0},{16,24},{24,16},{32,40},{40,32},{48,56},{56,48},{64,72... | collective-permute-start | bytes 1966088 | tf_op jit(solution)/shard_map/ppermute | solution.py:47
  55.4 7.2 %all-to-all-done.1 = f32[64,8,128]{2,1,0:T(8,128)S(1)} async-done(((f32[64,8,128]{2,1,0:T(8,128)}), f32[64,8,128]{2,1,0:T(8,128)S(1)}, u32[]{:S(2)}, u32[]{:S(2)}) %all-to-all-start.1) | async-done | bytes 262176 | tf_op jit(solution)/shard_map/all_to_all | solution.py:20
  63.9 7.9 %all-to-all-start.2 = ((f32[8,128,128]{2,1,0:T(8,128)}), f32[8,128,128]{2,1,0:T(8,128)}, u32[]{:S(2)}, u32[]{:S(2)}) async-start(f32[8,128,128]{2,1,0:T(8,128)} %broadcast_in_dim.20), calls=%async_computation.2 | async-start | bytes 1048576 | tf_op jit(solution)/shard_map/all_to_all | solution.py:20
  71.8 2.3 collective-permute-start.2
  76.8 4.9 %collective-permute-done.2 = f32[512,128]{1,0:T(8,128)} collective-permute-done((f32[512,128]{1,0:T(8,128)S(1)}, f32[512,128]{1,0:T(8,128)}, u32[]{:S(2)}, u32[]{:S(2)}) %collective-permute-start.2) | collective-permute-done | bytes 262176 | tf_op jit(solution)/shard_map/ppermute | solution.py:47
  86.0 6.2 %all-to-all-start.3 = ((f32[32,16,128]{2,1,0:T(8,128)}), f32[32,16,128]{2,1,0:T(8,128)S(1)}, u32[]{:S(2)}, u32[]{:S(2)}) async-start(f32[32,16,128]{2,1,0:T(8,128)} %bitcast.134), calls=%async_computation.3 | async-start | bytes 524288 | tf_op jit(solution)/shard_map/all_to_all | solution.py:20
  93.5 3.4 %collective-permute-start.3 = (f32[64,128]{1,0:T(8,128)S(1)}, f32[64,128]{1,0:T(8,128)}, u32[]{:S(2)}, u32[]{:S(2)}) collective-permute-start(f32[64,128]{1,0:T(8,128)S(1)} %constant_dynamic-slice_fusion.3), channel_id=1, source_target_pairs={{0,8},{8,0},{16,24},{24,16},{32,40},{40,32},{48,56},{56,48},{64,72... | collective-permute-start | bytes 98312 | tf_op jit(solution)/shard_map/ppermute | solution.py:47
  98.7 3.9 %collective-permute-done.3 = f32[64,128]{1,0:T(8,128)} collective-permute-done((f32[64,128]{1,0:T(8,128)S(1)}, f32[64,128]{1,0:T(8,128)}, u32[]{:S(2)}, u32[]{:S(2)}) %collective-permute-start.3) | collective-permute-done | bytes 32800 | tf_op jit(solution)/shard_map/ppermute | solution.py:47
  104.8 8.4 %all-to-all-start.4 = ((f32[32,16,128]{2,1,0:T(8,128)}), f32[32,16,128]{2,1,0:T(8,128)S(1)}, u32[]{:S(2)}, u32[]{:S(2)}) async-start(f32[32,16,128]{2,1,0:T(8,128)} %broadcast_in_dim.22), calls=%async_computation.4 | async-start | bytes 524288 | tf_op jit(solution)/shard_map/all_to_all | solution.py:20
  115.4 10.2 %all-to-all-done.4 = f32[32,16,128]{2,1,0:T(8,128)S(1)} async-done(((f32[32,16,128]{2,1,0:T(8,128)}), f32[32,16,128]{2,1,0:T(8,128)S(1)}, u32[]{:S(2)}, u32[]{:S(2)}) %all-to-all-start.4) | async-done | bytes 262176 | tf_op jit(solution)/shard_map/all_to_all | solution.py:20
  126.8 6.5 %all-to-all-start.5 = ((f32[8,128,128]{2,1,0:T(8,128)}), f32[8,128,128]{2,1,0:T(8,128)S(1)}, u32[]{:S(2)}, u32[]{:S(2)}) async-start(f32[8,128,128]{2,1,0:T(8,128)} %broadcast_in_dim.23), calls=%async_computation.5 | async-start | bytes 1048576 | tf_op jit(solution)/shard_map/all_to_all | solution.py:20
  133.3 2.4 collective-permute-start.4
  138.3 5.0 %collective-permute-done.4 = f32[512,128]{1,0:T(8,128)} collective-permute-done((f32[512,128]{1,0:T(8,128)S(1)}, f32[512,128]{1,0:T(8,128)}, u32[]{:S(2)}, u32[]{:S(2)}) %collective-permute-start.4) | collective-permute-done | bytes 262176 | tf_op jit(solution)/shard_map/ppermute | solution.py:47
  145.3 4.9 %all-to-all-start.6 = ((f32[32,16,128]{2,1,0:T(8,128)}), f32[32,16,128]{2,1,0:T(8,128)}, u32[]{:S(2)}, u32[]{:S(2)}) async-start(f32[32,16,128]{2,1,0:T(8,128)} %fusion.27), calls=%async_computation.6 | async-start | bytes 524288 | tf_op jit(solution)/shard_map/all_to_all | solution.py:20
  154.6 4.7 %collective-permute-done.5 = f32[64,128]{1,0:T(8,128)S(1)} collective-permute-done((f32[64,128]{1,0:T(8,128)S(1)}, f32[64,128]{1,0:T(8,128)S(1)}, u32[]{:S(2)}, u32[]{:S(2)}) %collective-permute-start.5) | collective-permute-done | bytes 32800 | tf_op jit(solution)/shard_map/ppermute | solution.py:47
  159.3 3.0 %all-to-all-done.6 = f32[32,16,128]{2,1,0:T(8,128)} async-done(((f32[32,16,128]{2,1,0:T(8,128)}), f32[32,16,128]{2,1,0:T(8,128)}, u32[]{:S(2)}, u32[]{:S(2)}) %all-to-all-start.6) | async-done | bytes 262176 | tf_op jit(solution)/shard_map/all_to_all | solution.py:20
  164.0 6.7 %all-to-all-start.7 = ((f32[32,16,128]{2,1,0:T(8,128)}), f32[32,16,128]{2,1,0:T(8,128)S(1)}, u32[]{:S(2)}, u32[]{:S(2)}) async-start(f32[32,16,128]{2,1,0:T(8,128)} %broadcast_in_dim.24), calls=%async_computation.7 | async-start | bytes 524288 | tf_op jit(solution)/shard_map/all_to_all | solution.py:20
  170.7 2.8 %convolution_add_fusion.2 = f32[256,256]{1,0:T(8,128)} fusion(f32[256,256]{1,0:T(8,128)} %fusion.3, f32[256,512]{1,0:T(8,128)} %bitcast.130, f32[512,128]{1,0:T(8,128)S(1)} %get-tuple-element.94, f32[512,128]{1,0:T(8,128)S(1)} %get-tuple-element.93), kind=kOutput, calls=%fused_computation.8 | convolution fusion | flops 402849792 | bytes 1572864 | tf_op jit(solution)/shard_map/dot_general | solution.py:10
  173.5 8.9 %all-to-all-done.7 = f32[32,16,128]{2,1,0:T(8,128)S(1)} async-done(((f32[32,16,128]{2,1,0:T(8,128)}), f32[32,16,128]{2,1,0:T(8,128)S(1)}, u32[]{:S(2)}, u32[]{:S(2)}) %all-to-all-start.7) | async-done | bytes 262176 | tf_op jit(solution)/shard_map/all_to_all | solution.py:20
  183.6 8.0 %all-to-all-start.8 = ((f32[8,128,128]{2,1,0:T(8,128)}), f32[8,128,128]{2,1,0:T(8,128)S(1)}, u32[]{:S(2)}, u32[]{:S(2)}) async-start(f32[8,128,128]{2,1,0:T(8,128)} %broadcast_in_dim.25), calls=%async_computation.8 | async-start | bytes 1048576 | tf_op jit(solution)/shard_map/all_to_all | solution.py:20
  191.6 2.4 collective-permute-start.6
  195.0 6.4 %collective-permute-done.6 = f32[512,128]{1,0:T(8,128)S(1)} collective-permute-done((f32[512,128]{1,0:T(8,128)S(1)}, f32[512,128]{1,0:T(8,128)S(1)}, u32[]{:S(2)}, u32[]{:S(2)}) %collective-permute-start.6) | collective-permute-done | bytes 262176 | tf_op jit(solution)/shard_map/ppermute | solution.py:47
  202.5 4.2 %all-to-all-start.9 = ((f32[32,16,128]{2,1,0:T(8,128)}), f32[32,16,128]{2,1,0:T(8,128)S(1)}, u32[]{:S(2)}, u32[]{:S(2)}) async-start(f32[32,16,128]{2,1,0:T(8,128)} %fusion.25), calls=%async_computation.9 | async-start | bytes 524288 | tf_op jit(solution)/shard_map/all_to_all | solution.py:20
  207.2 11.7 %all-to-all-done.9 = f32[32,16,128]{2,1,0:T(8,128)S(1)} async-done(((f32[32,16,128]{2,1,0:T(8,128)}), f32[32,16,128]{2,1,0:T(8,128)S(1)}, u32[]{:S(2)}, u32[]{:S(2)}) %all-to-all-start.9) | async-done | bytes 262176 | tf_op jit(solution)/shard_map/all_to_all | solution.py:20
  219.8 6.9 %all-to-all-start.10 = ((f32[64,16,128]{2,1,0:T(8,128)}), f32[64,16,128]{2,1,0:T(8,128)S(1)}, u32[]{:S(2)}, u32[]{:S(2)}) async-start(f32[64,16,128]{2,1,0:T(8,128)} %broadcast_in_dim.26), calls=%async_computation.10 | async-start | bytes 1048576 | tf_op jit(solution)/shard_map/all_to_all | solution.py:20
  228.6 14.4 %all-to-all-done.10 = f32[64,16,128]{2,1,0:T(8,128)S(1)} async-done(((f32[64,16,128]{2,1,0:T(8,128)}), f32[64,16,128]{2,1,0:T(8,128)S(1)}, u32[]{:S(2)}, u32[]{:S(2)}) %all-to-all-start.10) | async-done | bytes 524320 | tf_op jit(solution)/shard_map/all_to_all | solution.py:20
  245.0 7.7 %all-to-all-start.11 = ((f32[8,32,256]{2,1,0:T(8,128)}), f32[8,32,256]{2,1,0:T(8,128)S(1)}, u32[]{:S(2)}, u32[]{:S(2)}) async-start(f32[8,32,256]{2,1,0:T(8,128)} %bitcast.46), calls=%async_computation.11 | async-start | bytes 524288 | tf_op jit(solution)/shard_map/all_to_all | solution.py:20
  253.6 5.6 %all-to-all-done.11 = f32[8,32,256]{2,1,0:T(8,128)S(1)} async-done(((f32[8,32,256]{2,1,0:T(8,128)}), f32[8,32,256]{2,1,0:T(8,128)S(1)}, u32[]{:S(2)}, u32[]{:S(2)}) %all-to-all-start.11) | async-done | bytes 262176 | tf_op jit(solution)/shard_map/all_to_all | solution.py:20
  (109 shorter events, 51.2 us)
Async XLA Ops:
  0.6 20.9 %copy-start.6 = (f32[8,64,256]{2,1,0:T(8,128)S(1)}, f32[8,64,256]{2,1,0:T(8,128)}, u32[]{:S(2)}) copy-start(f32[8,64,256]{2,1,0:T(8,128)} %param.4) | copy-start | bytes 1572868
  0.6 22.7 %copy-start = (f32[4,64,4,512]{3,2,1,0:T(4,128)S(1)}, f32[4,64,4,512]{3,2,1,0:T(4,128)}, u32[]{:S(2)}) copy-start(f32[4,64,4,512]{3,2,1,0:T(4,128)} %param.7) | copy-start | bytes 6291460
  4.1 33.6 %all-to-all-start = ((f32[64,8,256]{2,1,0:T(8,128)}), f32[64,8,256]{2,1,0:T(8,128)}, u32[]{:S(2)}, u32[]{:S(2)}) async-start(f32[64,8,256]{2,1,0:T(8,128)} %fusion.17), calls=%async_computation | async-start | bytes 1048576 | tf_op jit(solution)/shard_map/all_to_all | solution.py:20
  21.5 5.2 %copy-start.7 = (f32[1,64,256]{2,1,0:T(8,128)}, f32[1,64,256]{2,1,0:T(8,128)S(1)}, u32[]{:S(2)}) copy-start(f32[1,64,256]{2,1,0:T(8,128)S(1)} %slice.92) | copy-start | bytes 196612
  24.9 1.8 copy-start.3
  25.7 1.7 copy-start.2
  26.7 26.3 %copy-start.8 = (f32[1,64,256]{2,1,0:T(8,128)S(1)}, f32[1,64,256]{2,1,0:T(8,128)}, u32[]{:S(2)}) copy-start(f32[1,64,256]{2,1,0:T(8,128)} %copy-done.7) | copy-start | bytes 196612
  38.8 11.3 %collective-permute-start = (f32[64,640]{1,0:T(8,128)}, f32[64,640]{1,0:T(8,128)}, u32[]{:S(2)}, u32[]{:S(2)}) collective-permute-start(f32[64,640]{1,0:T(8,128)} %pad_maximum_fusion.13), channel_id=1, source_target_pairs={{0,8},{8,0},{16,24},{24,16},{32,40},{40,32},{48,56},{56,48},{64,72... | collective-permute-start | bytes 491528 | tf_op jit(solution)/shard_map/ppermute | solution.py:47
  42.5 20.1 %all-to-all-start.1 = ((f32[64,8,128]{2,1,0:T(8,128)}), f32[64,8,128]{2,1,0:T(8,128)S(1)}, u32[]{:S(2)}, u32[]{:S(2)}) async-start(f32[64,8,128]{2,1,0:T(8,128)} %bitcast.16), calls=%async_computation.1 | async-start | bytes 524288 | tf_op jit(solution)/shard_map/all_to_all | solution.py:20
  50.1 24.0 %collective-permute-start.1 = (f32[5,64,512]{2,1,0:T(8,128)S(1)}, f32[5,64,512]{2,1,0:T(8,128)S(1)}, u32[]{:S(2)}, u32[]{:S(2)}) collective-permute-start(f32[5,64,512]{2,1,0:T(8,128)S(1)} %pad_maximum_fusion), channel_id=1, source_target_pairs={{0,8},{8,0},{16,24},{24,16},{32,40},{40,32},{48,56},{56,48},{64,72... | collective-permute-start | bytes 1966088 | tf_op jit(solution)/shard_map/ppermute | solution.py:47
  63.9 17.9 %all-to-all-start.2 = ((f32[8,128,128]{2,1,0:T(8,128)}), f32[8,128,128]{2,1,0:T(8,128)}, u32[]{:S(2)}, u32[]{:S(2)}) async-start(f32[8,128,128]{2,1,0:T(8,128)} %broadcast_in_dim.20), calls=%async_computation.2 | async-start | bytes 1048576 | tf_op jit(solution)/shard_map/all_to_all | solution.py:20
  71.8 9.9 %collective-permute-start.2 = (f32[512,128]{1,0:T(8,128)S(1)}, f32[512,128]{1,0:T(8,128)}, u32[]{:S(2)}, u32[]{:S(2)}) collective-permute-start(f32[512,128]{1,0:T(8,128)S(1)} %bitcast.123), channel_id=1, source_target_pairs={{0,8},{8,0},{16,24},{24,16},{32,40},{40,32},{48,56},{56,48},{64,72... | collective-permute-start | bytes 786440 | tf_op jit(solution)/shard_map/ppermute | solution.py:47
  74.1 0.8 copy-start.5
  76.8 20.2 %copy-start.1 = (f32[4,64,1,512]{3,1,0,2:T(8,128)S(1)}, f32[4,64,1,512]{3,1,0,2:T(8,128)}, u32[]{:S(2)}) copy-start(f32[4,64,1,512]{3,1,0,2:T(8,128)} %copy.48) | copy-start | bytes 1572868
  86.0 18.1 %all-to-all-start.3 = ((f32[32,16,128]{2,1,0:T(8,128)}), f32[32,16,128]{2,1,0:T(8,128)S(1)}, u32[]{:S(2)}, u32[]{:S(2)}) async-start(f32[32,16,128]{2,1,0:T(8,128)} %bitcast.134), calls=%async_computation.3 | async-start | bytes 524288 | tf_op jit(solution)/shard_map/all_to_all | solution.py:20
  93.5 9.0 %collective-permute-start.3 = (f32[64,128]{1,0:T(8,128)S(1)}, f32[64,128]{1,0:T(8,128)}, u32[]{:S(2)}, u32[]{:S(2)}) collective-permute-start(f32[64,128]{1,0:T(8,128)S(1)} %constant_dynamic-slice_fusion.3), channel_id=1, source_target_pairs={{0,8},{8,0},{16,24},{24,16},{32,40},{40,32},{48,56},{56,48},{64,72... | collective-permute-start | bytes 98312 | tf_op jit(solution)/shard_map/ppermute | solution.py:47
  104.8 20.7 %all-to-all-start.4 = ((f32[32,16,128]{2,1,0:T(8,128)}), f32[32,16,128]{2,1,0:T(8,128)S(1)}, u32[]{:S(2)}, u32[]{:S(2)}) async-start(f32[32,16,128]{2,1,0:T(8,128)} %broadcast_in_dim.22), calls=%async_computation.4 | async-start | bytes 524288 | tf_op jit(solution)/shard_map/all_to_all | solution.py:20
  126.8 16.4 %all-to-all-start.5 = ((f32[8,128,128]{2,1,0:T(8,128)}), f32[8,128,128]{2,1,0:T(8,128)S(1)}, u32[]{:S(2)}, u32[]{:S(2)}) async-start(f32[8,128,128]{2,1,0:T(8,128)} %broadcast_in_dim.23), calls=%async_computation.5 | async-start | bytes 1048576 | tf_op jit(solution)/shard_map/all_to_all | solution.py:20
  133.3 9.9 %collective-permute-start.4 = (f32[512,128]{1,0:T(8,128)S(1)}, f32[512,128]{1,0:T(8,128)}, u32[]{:S(2)}, u32[]{:S(2)}) collective-permute-start(f32[512,128]{1,0:T(8,128)S(1)} %bitcast.127), channel_id=1, source_target_pairs={{0,8},{8,0},{16,24},{24,16},{32,40},{40,32},{48,56},{56,48},{64,72... | collective-permute-start | bytes 786440 | tf_op jit(solution)/shard_map/ppermute | solution.py:47
  145.3 17.0 %all-to-all-start.6 = ((f32[32,16,128]{2,1,0:T(8,128)}), f32[32,16,128]{2,1,0:T(8,128)}, u32[]{:S(2)}, u32[]{:S(2)}) async-start(f32[32,16,128]{2,1,0:T(8,128)} %fusion.27), calls=%async_computation.6 | async-start | bytes 524288 | tf_op jit(solution)/shard_map/all_to_all | solution.py:20
  152.5 6.8 %collective-permute-start.5 = (f32[64,128]{1,0:T(8,128)S(1)}, f32[64,128]{1,0:T(8,128)S(1)}, u32[]{:S(2)}, u32[]{:S(2)}) collective-permute-start(f32[64,128]{1,0:T(8,128)S(1)} %constant_dynamic-slice_fusion.2), channel_id=1, source_target_pairs={{0,8},{8,0},{16,24},{24,16},{32,40},{40,32},{48,56},{56,48},{64,72... | collective-permute-start | bytes 98312 | tf_op jit(solution)/shard_map/ppermute | solution.py:47
  164.0 18.4 %all-to-all-start.7 = ((f32[32,16,128]{2,1,0:T(8,128)}), f32[32,16,128]{2,1,0:T(8,128)S(1)}, u32[]{:S(2)}, u32[]{:S(2)}) async-start(f32[32,16,128]{2,1,0:T(8,128)} %broadcast_in_dim.24), calls=%async_computation.7 | async-start | bytes 524288 | tf_op jit(solution)/shard_map/all_to_all | solution.py:20
  183.6 17.8 %all-to-all-start.8 = ((f32[8,128,128]{2,1,0:T(8,128)}), f32[8,128,128]{2,1,0:T(8,128)S(1)}, u32[]{:S(2)}, u32[]{:S(2)}) async-start(f32[8,128,128]{2,1,0:T(8,128)} %broadcast_in_dim.25), calls=%async_computation.8 | async-start | bytes 1048576 | tf_op jit(solution)/shard_map/all_to_all | solution.py:20
  191.6 9.8 %collective-permute-start.6 = (f32[512,128]{1,0:T(8,128)S(1)}, f32[512,128]{1,0:T(8,128)S(1)}, u32[]{:S(2)}, u32[]{:S(2)}) collective-permute-start(f32[512,128]{1,0:T(8,128)S(1)} %bitcast.125), channel_id=1, source_target_pairs={{0,8},{8,0},{16,24},{24,16},{32,40},{40,32},{48,56},{56,48},{64,72... | collective-permute-start | bytes 786440 | tf_op jit(solution)/shard_map/ppermute | solution.py:47
  201.4 5.4 %copy-start.9 = (f32[512,128]{1,0:T(8,128)}, f32[512,128]{1,0:T(8,128)S(1)}, u32[]{:S(2)}) copy-start(f32[512,128]{1,0:T(8,128)S(1)} %collective-permute-done.6) | copy-start | bytes 786436
  202.5 16.4 %all-to-all-start.9 = ((f32[32,16,128]{2,1,0:T(8,128)}), f32[32,16,128]{2,1,0:T(8,128)S(1)}, u32[]{:S(2)}, u32[]{:S(2)}) async-start(f32[32,16,128]{2,1,0:T(8,128)} %fusion.25), calls=%async_computation.9 | async-start | bytes 524288 | tf_op jit(solution)/shard_map/all_to_all | solution.py:20
  206.8 20.0 %slice-start = ((f32[8,64,256]{2,1,0:T(8,128)}), f32[4,64,256]{2,1,0:T(8,128)S(1)}, s32[]{:S(2)}) async-start(f32[8,64,256]{2,1,0:T(8,128)} %param.4), calls=%async_computation.12 | async-start | bytes 524288 | tf_op jit(solution)/shard_map/slice | solution.py:89
  207.2 19.7 %copy-start.10 = (f32[512,128]{1,0:T(8,128)S(1)}, f32[512,128]{1,0:T(8,128)}, u32[]{:S(2)}) copy-start(f32[512,128]{1,0:T(8,128)} %copy-done.9) | copy-start | bytes 786436
  219.8 7.5 %copy-start.4 = (f32[256,256]{1,0:T(8,128)S(1)}, f32[256,256]{1,0:T(8,128)}, u32[]{:S(2)}) copy-start(f32[256,256]{1,0:T(8,128)} %convolution_add_fusion.2) | copy-start | bytes 786436
  219.8 23.2 %all-to-all-start.10 = ((f32[64,16,128]{2,1,0:T(8,128)}), f32[64,16,128]{2,1,0:T(8,128)S(1)}, u32[]{:S(2)}, u32[]{:S(2)}) async-start(f32[64,16,128]{2,1,0:T(8,128)} %broadcast_in_dim.26), calls=%async_computation.10 | async-start | bytes 1048576 | tf_op jit(solution)/shard_map/all_to_all | solution.py:20
  245.0 14.2 %all-to-all-start.11 = ((f32[8,32,256]{2,1,0:T(8,128)}), f32[8,32,256]{2,1,0:T(8,128)S(1)}, u32[]{:S(2)}, u32[]{:S(2)}) async-start(f32[8,32,256]{2,1,0:T(8,128)} %bitcast.46), calls=%async_computation.11 | async-start | bytes 524288 | tf_op jit(solution)/shard_map/all_to_all | solution.py:20

commit v21 on v20

--- a/solution.py
+++ b/solution.py
@@ -96,9 +96,11 @@
 
     parts = scattered_whole(own_diag[0], right_sides[0])
     sent_first = jnp.concatenate([lower_blocks[0], half_of(right_sides[1], row % 2 ^ 1)], 1)
-    part, sent_first = by_deadline(parts.sum(0), sent_first)
+    part = parts.sum(0)
     part = jnp.stack([part[:, :half], part[:, half:]])
-    parts = swap(copies(part, members).reshape(row_size, -1, half), "row")
+    sent = copies(part, members).reshape(row_size, -1, half)
+    sent, sent_first = by_deadline(sent, sent_first)
+    parts = swap(sent, "row")
     got_first = from_partner(sent_first)
     own_shared = jnp.concatenate([own_diag[1:], lower_blocks[2:3], lower_blocks[5:]])
     got_first, own_shared = by_deadline(got_first, own_shared)

time: 262 us -> 267 us (1.019)
  waiting for transfers between devices: 97.6 us -> 101 us
    all_to_all x12, waiting for transfers between devices: 72.7 us -> 76.4 us  [swap(): lax.all_to_all(parts, axis, 0, 0, axis_index_groups=groups, tiled=True)]
where the time goes in v21:
time: 267 us; the launch traced here: 265 us
  starting transfers between devices  111 us (42%)
  waiting for transfers between devices  101 us (38%)
  matrix products  20 us (7%)
  local copies, waits for them, and re-layouts  19.2 us (7%)
  other arithmetic  12.2 us (5%)
    all_to_all x12, starting transfers between devices, swap(): lax.all_to_all(parts, axis, 0, 0, axis_index_groups=groups, tiled=True)  92.1 us
    all_to_all x12, waiting for transfers between devices, swap(): lax.all_to_all(parts, axis, 0, 0, axis_index_groups=groups, tiled=True)  76.4 us
    ppermute x7, waiting for transfers between devices, from_partner(): return lax.ppermute(value, 'row', [(r, r ^ 1) for r in range(row_size)])  24.9 us
    dot_general x14, matrix products, contract(): lax.dot_general(left, right, (((axes[0],), (axes[1],)), ((), ())), precis...  20 us
    ppermute x7, starting transfers between devices, from_partner(): return lax.ppermute(value, 'row', [(r, r ^ 1) for r in range(row_size)])  18.6 us
    broadcast_in_dim x7, local copies, waits for them, and re-layouts, copies(): return jnp.broadcast_to(part[None], (count,) + part.shape)  5.44 us
  transfers between devices with their start and end apart: 19, of which 14 were waited for; matrix products, arithmetic and copies ran while one was open for 11% of the time, Pallas kernels for 0%

profile of v21, /device:TPU:1, one launch (start us, length us, event | category | flops | bytes accessed | tf_op | source)
XLA Modules:
  0.0 264.6 jit_solution(10106208538287453255)
XLA Ops:
  4.1 17.1 %all-to-all-start = ((f32[64,8,256]{2,1,0:T(8,128)}), f32[64,8,256]{2,1,0:T(8,128)S(1)}, u32[]{:S(2)}, u32[]{:S(2)}) async-start(f32[64,8,256]{2,1,0:T(8,128)} %fusion.17), calls=%async_computation | async-start | bytes 1048576 | tf_op jit(solution)/shard_map/all_to_all | solution.py:20
  23.6 13.9 %all-to-all-done = f32[64,8,256]{2,1,0:T(8,128)S(1)} async-done(((f32[64,8,256]{2,1,0:T(8,128)}), f32[64,8,256]{2,1,0:T(8,128)S(1)}, u32[]{:S(2)}, u32[]{:S(2)}) %all-to-all-start) | async-done | bytes 524320 | tf_op jit(solution)/shard_map/all_to_all | solution.py:20
  38.4 3.1 %collective-permute-start = (f32[64,640]{1,0:T(8,128)}, f32[64,640]{1,0:T(8,128)}, u32[]{:S(2)}, u32[]{:S(2)}) collective-permute-start(f32[64,640]{1,0:T(8,128)} %pad_maximum_fusion.13), channel_id=1, source_target_pairs={{0,8},{8,0},{16,24},{24,16},{32,40},{40,32},{48,56},{56,48},{64,72... | collective-permute-start | bytes 491528 | tf_op jit(solution)/shard_map/ppermute | solution.py:47
  41.6 2.6 fusion.43
  47.1 7.6 %all-to-all-start.1 = ((f32[64,8,128]{2,1,0:T(8,128)}), f32[64,8,128]{2,1,0:T(8,128)S(1)}, u32[]{:S(2)}, u32[]{:S(2)}) async-start(f32[64,8,128]{2,1,0:T(8,128)} %bitcast.8), calls=%async_computation.1 | async-start | bytes 524288 | tf_op jit(solution)/shard_map/all_to_all | solution.py:20
  54.7 2.9 %collective-permute-start.1 = (f32[5,64,512]{2,1,0:T(8,128)S(1)}, f32[5,64,512]{2,1,0:T(8,128)S(1)}, u32[]{:S(2)}, u32[]{:S(2)}) collective-permute-start(f32[5,64,512]{2,1,0:T(8,128)S(1)} %pad_maximum_fusion), channel_id=1, source_target_pairs={{0,8},{8,0},{16,24},{24,16},{32,40},{40,32},{48,56},{56,48},{64,72... | collective-permute-start | bytes 1966088 | tf_op jit(solution)/shard_map/ppermute | solution.py:47
  60.1 7.1 %all-to-all-done.1 = f32[64,8,128]{2,1,0:T(8,128)S(1)} async-done(((f32[64,8,128]{2,1,0:T(8,128)}), f32[64,8,128]{2,1,0:T(8,128)S(1)}, u32[]{:S(2)}, u32[]{:S(2)}) %all-to-all-start.1) | async-done | bytes 262176 | tf_op jit(solution)/shard_map/all_to_all | solution.py:20
  68.5 7.9 %all-to-all-start.2 = ((f32[8,128,128]{2,1,0:T(8,128)}), f32[8,128,128]{2,1,0:T(8,128)}, u32[]{:S(2)}, u32[]{:S(2)}) async-start(f32[8,128,128]{2,1,0:T(8,128)} %broadcast_in_dim.20), calls=%async_computation.2 | async-start | bytes 1048576 | tf_op jit(solution)/shard_map/all_to_all | solution.py:20
  81.4 4.9 %collective-permute-done.2 = f32[512,128]{1,0:T(8,128)} collective-permute-done((f32[512,128]{1,0:T(8,128)S(1)}, f32[512,128]{1,0:T(8,128)}, u32[]{:S(2)}, u32[]{:S(2)}) %collective-permute-start.2) | collective-permute-done | bytes 262176 | tf_op jit(solution)/shard_map/ppermute | solution.py:47
  90.6 6.2 %all-to-all-start.3 = ((f32[32,16,128]{2,1,0:T(8,128)}), f32[32,16,128]{2,1,0:T(8,128)S(1)}, u32[]{:S(2)}, u32[]{:S(2)}) async-start(f32[32,16,128]{2,1,0:T(8,128)} %bitcast.134), calls=%async_computation.3 | async-start | bytes 524288 | tf_op jit(solution)/shard_map/all_to_all | solution.py:20
  98.1 3.4 %collective-permute-start.3 = (f32[64,128]{1,0:T(8,128)S(1)}, f32[64,128]{1,0:T(8,128)}, u32[]{:S(2)}, u32[]{:S(2)}) collective-permute-start(f32[64,128]{1,0:T(8,128)S(1)} %constant_dynamic-slice_fusion.3), channel_id=1, source_target_pairs={{0,8},{8,0},{16,24},{24,16},{32,40},{40,32},{48,56},{56,48},{64,72... | collective-permute-start | bytes 98312 | tf_op jit(solution)/shard_map/ppermute | solution.py:47
  103.3 3.9 %collective-permute-done.3 = f32[64,128]{1,0:T(8,128)} collective-permute-done((f32[64,128]{1,0:T(8,128)S(1)}, f32[64,128]{1,0:T(8,128)}, u32[]{:S(2)}, u32[]{:S(2)}) %collective-permute-start.3) | collective-permute-done | bytes 32800 | tf_op jit(solution)/shard_map/ppermute | solution.py:47
  109.5 8.4 %all-to-all-start.4 = ((f32[32,16,128]{2,1,0:T(8,128)}), f32[32,16,128]{2,1,0:T(8,128)S(1)}, u32[]{:S(2)}, u32[]{:S(2)}) async-start(f32[32,16,128]{2,1,0:T(8,128)} %broadcast_in_dim.22), calls=%async_computation.4 | async-start | bytes 524288 | tf_op jit(solution)/shard_map/all_to_all | solution.py:20
  120.0 10.2 %all-to-all-done.4 = f32[32,16,128]{2,1,0:T(8,128)S(1)} async-done(((f32[32,16,128]{2,1,0:T(8,128)}), f32[32,16,128]{2,1,0:T(8,128)S(1)}, u32[]{:S(2)}, u32[]{:S(2)}) %all-to-all-start.4) | async-done | bytes 262176 | tf_op jit(solution)/shard_map/all_to_all | solution.py:20
  131.4 6.5 %all-to-all-start.5 = ((f32[8,128,128]{2,1,0:T(8,128)}), f32[8,128,128]{2,1,0:T(8,128)S(1)}, u32[]{:S(2)}, u32[]{:S(2)}) async-start(f32[8,128,128]{2,1,0:T(8,128)} %broadcast_in_dim.23), calls=%async_computation.5 | async-start | bytes 1048576 | tf_op jit(solution)/shard_map/all_to_all | solution.py:20
  137.9 2.4 collective-permute-start.4
  142.9 5.0 %collective-permute-done.4 = f32[512,128]{1,0:T(8,128)} collective-permute-done((f32[512,128]{1,0:T(8,128)S(1)}, f32[512,128]{1,0:T(8,128)}, u32[]{:S(2)}, u32[]{:S(2)}) %collective-permute-start.4) | collective-permute-done | bytes 262176 | tf_op jit(solution)/shard_map/ppermute | solution.py:47
  149.9 4.9 %all-to-all-start.6 = ((f32[32,16,128]{2,1,0:T(8,128)}), f32[32,16,128]{2,1,0:T(8,128)}, u32[]{:S(2)}, u32[]{:S(2)}) async-start(f32[32,16,128]{2,1,0:T(8,128)} %fusion.27), calls=%async_computation.6 | async-start | bytes 524288 | tf_op jit(solution)/shard_map/all_to_all | solution.py:20
  159.2 4.7 %collective-permute-done.5 = f32[64,128]{1,0:T(8,128)S(1)} collective-permute-done((f32[64,128]{1,0:T(8,128)S(1)}, f32[64,128]{1,0:T(8,128)S(1)}, u32[]{:S(2)}, u32[]{:S(2)}) %collective-permute-start.5) | collective-permute-done | bytes 32800 | tf_op jit(solution)/shard_map/ppermute | solution.py:47
  163.9 3.0 %all-to-all-done.6 = f32[32,16,128]{2,1,0:T(8,128)} async-done(((f32[32,16,128]{2,1,0:T(8,128)}), f32[32,16,128]{2,1,0:T(8,128)}, u32[]{:S(2)}, u32[]{:S(2)}) %all-to-all-start.6) | async-done | bytes 262176 | tf_op jit(solution)/shard_map/all_to_all | solution.py:20
  168.6 6.7 %all-to-all-start.7 = ((f32[32,16,128]{2,1,0:T(8,128)}), f32[32,16,128]{2,1,0:T(8,128)S(1)}, u32[]{:S(2)}, u32[]{:S(2)}) async-start(f32[32,16,128]{2,1,0:T(8,128)} %broadcast_in_dim.24), calls=%async_computation.7 | async-start | bytes 524288 | tf_op jit(solution)/shard_map/all_to_all | solution.py:20
  175.3 2.8 %convolution_add_fusion.2 = f32[256,256]{1,0:T(8,128)} fusion(f32[256,256]{1,0:T(8,128)} %fusion.3, f32[256,512]{1,0:T(8,128)} %bitcast.130, f32[512,128]{1,0:T(8,128)S(1)} %get-tuple-element.94, f32[512,128]{1,0:T(8,128)S(1)} %get-tuple-element.93), kind=kOutput, calls=%fused_computation.8 | convolution fusion | flops 402849792 | bytes 1572864 | tf_op jit(solution)/shard_map/dot_general | solution.py:10
  178.1 8.9 %all-to-all-done.7 = f32[32,16,128]{2,1,0:T(8,128)S(1)} async-done(((f32[32,16,128]{2,1,0:T(8,128)}), f32[32,16,128]{2,1,0:T(8,128)S(1)}, u32[]{:S(2)}, u32[]{:S(2)}) %all-to-all-start.7) | async-done | bytes 262176 | tf_op jit(solution)/shard_map/all_to_all | solution.py:20
  188.2 8.0 %all-to-all-start.8 = ((f32[8,128,128]{2,1,0:T(8,128)}), f32[8,128,128]{2,1,0:T(8,128)S(1)}, u32[]{:S(2)}, u32[]{:S(2)}) async-start(f32[8,128,128]{2,1,0:T(8,128)} %broadcast_in_dim.25), calls=%async_computation.8 | async-start | bytes 1048576 | tf_op jit(solution)/shard_map/all_to_all | solution.py:20
  196.2 2.4 collective-permute-start.6
  199.6 6.4 %collective-permute-done.6 = f32[512,128]{1,0:T(8,128)S(1)} collective-permute-done((f32[512,128]{1,0:T(8,128)S(1)}, f32[512,128]{1,0:T(8,128)S(1)}, u32[]{:S(2)}, u32[]{:S(2)}) %collective-permute-start.6) | collective-permute-done | bytes 262176 | tf_op jit(solution)/shard_map/ppermute | solution.py:47
  207.1 4.2 %all-to-all-start.9 = ((f32[32,16,128]{2,1,0:T(8,128)}), f32[32,16,128]{2,1,0:T(8,128)S(1)}, u32[]{:S(2)}, u32[]{:S(2)}) async-start(f32[32,16,128]{2,1,0:T(8,128)} %fusion.25), calls=%async_computation.9 | async-start | bytes 524288 | tf_op jit(solution)/shard_map/all_to_all | solution.py:20
  211.8 11.7 %all-to-all-done.9 = f32[32,16,128]{2,1,0:T(8,128)S(1)} async-done(((f32[32,16,128]{2,1,0:T(8,128)}), f32[32,16,128]{2,1,0:T(8,128)S(1)}, u32[]{:S(2)}, u32[]{:S(2)}) %all-to-all-start.9) | async-done | bytes 262176 | tf_op jit(solution)/shard_map/all_to_all | solution.py:20
  224.4 6.9 %all-to-all-start.10 = ((f32[64,16,128]{2,1,0:T(8,128)}), f32[64,16,128]{2,1,0:T(8,128)S(1)}, u32[]{:S(2)}, u32[]{:S(2)}) async-start(f32[64,16,128]{2,1,0:T(8,128)} %broadcast_in_dim.26), calls=%async_computation.10 | async-start | bytes 1048576 | tf_op jit(solution)/shard_map/all_to_all | solution.py:20
  233.2 14.4 %all-to-all-done.10 = f32[64,16,128]{2,1,0:T(8,128)S(1)} async-done(((f32[64,16,128]{2,1,0:T(8,128)}), f32[64,16,128]{2,1,0:T(8,128)S(1)}, u32[]{:S(2)}, u32[]{:S(2)}) %all-to-all-start.10) | async-done | bytes 524320 | tf_op jit(solution)/shard_map/all_to_all | solution.py:20
  249.7 7.7 %all-to-all-start.11 = ((f32[8,32,256]{2,1,0:T(8,128)}), f32[8,32,256]{2,1,0:T(8,128)S(1)}, u32[]{:S(2)}, u32[]{:S(2)}) async-start(f32[8,32,256]{2,1,0:T(8,128)} %bitcast.46), calls=%async_computation.11 | async-start | bytes 524288 | tf_op jit(solution)/shard_map/all_to_all | solution.py:20
  258.2 5.6 %all-to-all-done.11 = f32[8,32,256]{2,1,0:T(8,128)S(1)} async-done(((f32[8,32,256]{2,1,0:T(8,128)}), f32[8,32,256]{2,1,0:T(8,128)S(1)}, u32[]{:S(2)}, u32[]{:S(2)}) %all-to-all-start.11) | async-done | bytes 262176 | tf_op jit(solution)/shard_map/all_to_all | solution.py:20
  (109 shorter events, 51.9 us)
Async XLA Ops:
  0.6 20.6 %copy-start.5 = (f32[8,64,256]{2,1,0:T(8,128)S(1)}, f32[8,64,256]{2,1,0:T(8,128)}, u32[]{:S(2)}) copy-start(f32[8,64,256]{2,1,0:T(8,128)} %param.4) | copy-start | bytes 1572868
  1.7 39.8 %copy-start = (f32[4,64,4,512]{3,2,1,0:T(4,128)S(1)}, f32[4,64,4,512]{3,2,1,0:T(4,128)}, u32[]{:S(2)}) copy-start(f32[4,64,4,512]{3,2,1,0:T(4,128)} %param.7) | copy-start | bytes 6291460
  4.1 33.5 %all-to-all-start = ((f32[64,8,256]{2,1,0:T(8,128)}), f32[64,8,256]{2,1,0:T(8,128)S(1)}, u32[]{:S(2)}, u32[]{:S(2)}) async-start(f32[64,8,256]{2,1,0:T(8,128)} %fusion.17), calls=%async_computation | async-start | bytes 1048576 | tf_op jit(solution)/shard_map/all_to_all | solution.py:20
  21.3 0.6 copy-start.7
  38.4 5.7 %copy-start.6 = (f32[4,512,64]{1,2,0:T(8,128)S(1)}, f32[4,512,64]{1,2,0:T(8,128)}, u32[]{:S(2)}) copy-start(f32[4,512,64]{1,2,0:T(8,128)} %param.5) | copy-start | bytes 1572868
  38.4 16.3 %collective-permute-start = (f32[64,640]{1,0:T(8,128)}, f32[64,640]{1,0:T(8,128)}, u32[]{:S(2)}, u32[]{:S(2)}) collective-permute-start(f32[64,640]{1,0:T(8,128)} %pad_maximum_fusion.13), channel_id=1, source_target_pairs={{0,8},{8,0},{16,24},{24,16},{32,40},{40,32},{48,56},{56,48},{64,72... | collective-permute-start | bytes 491528 | tf_op jit(solution)/shard_map/ppermute | solution.py:47
  44.1 2.9 %copy-start.2 = (f32[4,64,1,512]{3,2,1,0:T(1,128)S(1)}, f32[4,64,1,512]{3,2,1,0:T(1,128)}, u32[]{:S(2)}) copy-start(f32[4,64,1,512]{3,2,1,0:T(1,128)} %get-tuple-element.76) | copy-start | bytes 1572868
  46.9 10.7 %copy-start.8 = (f32[1,64,256]{2,1,0:T(8,128)S(1)}, f32[1,64,256]{2,1,0:T(8,128)}, u32[]{:S(2)}) copy-start(f32[1,64,256]{2,1,0:T(8,128)} %copy-done.7) | copy-start | bytes 196612
  47.1 20.1 %all-to-all-start.1 = ((f32[64,8,128]{2,1,0:T(8,128)}), f32[64,8,128]{2,1,0:T(8,128)S(1)}, u32[]{:S(2)}, u32[]{:S(2)}) async-start(f32[64,8,128]{2,1,0:T(8,128)} %bitcast.8), calls=%async_computation.1 | async-start | bytes 524288 | tf_op jit(solution)/shard_map/all_to_all | solution.py:20
  54.7 24.0 %collective-permute-start.1 = (f32[5,64,512]{2,1,0:T(8,128)S(1)}, f32[5,64,512]{2,1,0:T(8,128)S(1)}, u32[]{:S(2)}, u32[]{:S(2)}) collective-permute-start(f32[5,64,512]{2,1,0:T(8,128)S(1)} %pad_maximum_fusion), channel_id=1, source_target_pairs={{0,8},{8,0},{16,24},{24,16},{32,40},{40,32},{48,56},{56,48},{64,72... | collective-permute-start | bytes 1966088 | tf_op jit(solution)/shard_map/ppermute | solution.py:47
  68.5 17.9 %all-to-all-start.2 = ((f32[8,128,128]{2,1,0:T(8,128)}), f32[8,128,128]{2,1,0:T(8,128)}, u32[]{:S(2)}, u32[]{:S(2)}) async-start(f32[8,128,128]{2,1,0:T(8,128)} %broadcast_in_dim.20), calls=%async_computation.2 | async-start | bytes 1048576 | tf_op jit(solution)/shard_map/all_to_all | solution.py:20
  76.4 9.9 %collective-permute-start.2 = (f32[512,128]{1,0:T(8,128)S(1)}, f32[512,128]{1,0:T(8,128)}, u32[]{:S(2)}, u32[]{:S(2)}) collective-permute-start(f32[512,128]{1,0:T(8,128)S(1)} %bitcast.123), channel_id=1, source_target_pairs={{0,8},{8,0},{16,24},{24,16},{32,40},{40,32},{48,56},{56,48},{64,72... | collective-permute-start | bytes 786440 | tf_op jit(solution)/shard_map/ppermute | solution.py:47
  78.7 0.8 copy-start.4
  81.4 20.2 %copy-start.1 = (f32[4,64,1,512]{3,1,0,2:T(8,128)S(1)}, f32[4,64,1,512]{3,1,0,2:T(8,128)}, u32[]{:S(2)}) copy-start(f32[4,64,1,512]{3,1,0,2:T(8,128)} %copy.48) | copy-start | bytes 1572868
  90.6 18.1 %all-to-all-start.3 = ((f32[32,16,128]{2,1,0:T(8,128)}), f32[32,16,128]{2,1,0:T(8,128)S(1)}, u32[]{:S(2)}, u32[]{:S(2)}) async-start(f32[32,16,128]{2,1,0:T(8,128)} %bitcast.134), calls=%async_computation.3 | async-start | bytes 524288 | tf_op jit(solution)/shard_map/all_to_all | solution.py:20
  98.1 9.0 %collective-permute-start.3 = (f32[64,128]{1,0:T(8,128)S(1)}, f32[64,128]{1,0:T(8,128)}, u32[]{:S(2)}, u32[]{:S(2)}) collective-permute-start(f32[64,128]{1,0:T(8,128)S(1)} %constant_dynamic-slice_fusion.3), channel_id=1, source_target_pairs={{0,8},{8,0},{16,24},{24,16},{32,40},{40,32},{48,56},{56,48},{64,72... | collective-permute-start | bytes 98312 | tf_op jit(solution)/shard_map/ppermute | solution.py:47
  109.5 20.7 %all-to-all-start.4 = ((f32[32,16,128]{2,1,0:T(8,128)}), f32[32,16,128]{2,1,0:T(8,128)S(1)}, u32[]{:S(2)}, u32[]{:S(2)}) async-start(f32[32,16,128]{2,1,0:T(8,128)} %broadcast_in_dim.22), calls=%async_computation.4 | async-start | bytes 524288 | tf_op jit(solution)/shard_map/all_to_all | solution.py:20
  131.4 16.4 %all-to-all-start.5 = ((f32[8,128,128]{2,1,0:T(8,128)}), f32[8,128,128]{2,1,0:T(8,128)S(1)}, u32[]{:S(2)}, u32[]{:S(2)}) async-start(f32[8,128,128]{2,1,0:T(8,128)} %broadcast_in_dim.23), calls=%async_computation.5 | async-start | bytes 1048576 | tf_op jit(solution)/shard_map/all_to_all | solution.py:20
  137.9 9.9 %collective-permute-start.4 = (f32[512,128]{1,0:T(8,128)S(1)}, f32[512,128]{1,0:T(8,128)}, u32[]{:S(2)}, u32[]{:S(2)}) collective-permute-start(f32[512,128]{1,0:T(8,128)S(1)} %bitcast.127), channel_id=1, source_target_pairs={{0,8},{8,0},{16,24},{24,16},{32,40},{40,32},{48,56},{56,48},{64,72... | collective-permute-start | bytes 786440 | tf_op jit(solution)/shard_map/ppermute | solution.py:47
  149.9 17.0 %all-to-all-start.6 = ((f32[32,16,128]{2,1,0:T(8,128)}), f32[32,16,128]{2,1,0:T(8,128)}, u32[]{:S(2)}, u32[]{:S(2)}) async-start(f32[32,16,128]{2,1,0:T(8,128)} %fusion.27), calls=%async_computation.6 | async-start | bytes 524288 | tf_op jit(solution)/shard_map/all_to_all | solution.py:20
  157.1 6.8 %collective-permute-start.5 = (f32[64,128]{1,0:T(8,128)S(1)}, f32[64,128]{1,0:T(8,128)S(1)}, u32[]{:S(2)}, u32[]{:S(2)}) collective-permute-start(f32[64,128]{1,0:T(8,128)S(1)} %constant_dynamic-slice_fusion.2), channel_id=1, source_target_pairs={{0,8},{8,0},{16,24},{24,16},{32,40},{40,32},{48,56},{56,48},{64,72... | collective-permute-start | bytes 98312 | tf_op jit(solution)/shard_map/ppermute | solution.py:47
  168.6 18.4 %all-to-all-start.7 = ((f32[32,16,128]{2,1,0:T(8,128)}), f32[32,16,128]{2,1,0:T(8,128)S(1)}, u32[]{:S(2)}, u32[]{:S(2)}) async-start(f32[32,16,128]{2,1,0:T(8,128)} %broadcast_in_dim.24), calls=%async_computation.7 | async-start | bytes 524288 | tf_op jit(solution)/shard_map/all_to_all | solution.py:20
  188.2 17.8 %all-to-all-start.8 = ((f32[8,128,128]{2,1,0:T(8,128)}), f32[8,128,128]{2,1,0:T(8,128)S(1)}, u32[]{:S(2)}, u32[]{:S(2)}) async-start(f32[8,128,128]{2,1,0:T(8,128)} %broadcast_in_dim.25), calls=%async_computation.8 | async-start | bytes 1048576 | tf_op jit(solution)/shard_map/all_to_all | solution.py:20
  196.2 9.8 %collective-permute-start.6 = (f32[512,128]{1,0:T(8,128)S(1)}, f32[512,128]{1,0:T(8,128)S(1)}, u32[]{:S(2)}, u32[]{:S(2)}) collective-permute-start(f32[512,128]{1,0:T(8,128)S(1)} %bitcast.125), channel_id=1, source_target_pairs={{0,8},{8,0},{16,24},{24,16},{32,40},{40,32},{48,56},{56,48},{64,72... | collective-permute-start | bytes 786440 | tf_op jit(solution)/shard_map/ppermute | solution.py:47
  206.0 5.4 %copy-start.9 = (f32[512,128]{1,0:T(8,128)}, f32[512,128]{1,0:T(8,128)S(1)}, u32[]{:S(2)}) copy-start(f32[512,128]{1,0:T(8,128)S(1)} %collective-permute-done.6) | copy-start | bytes 786436
  207.1 16.4 %all-to-all-start.9 = ((f32[32,16,128]{2,1,0:T(8,128)}), f32[32,16,128]{2,1,0:T(8,128)S(1)}, u32[]{:S(2)}, u32[]{:S(2)}) async-start(f32[32,16,128]{2,1,0:T(8,128)} %fusion.25), calls=%async_computation.9 | async-start | bytes 524288 | tf_op jit(solution)/shard_map/all_to_all | solution.py:20
  211.4 20.0 %slice-start = ((f32[8,64,256]{2,1,0:T(8,128)}), f32[4,64,256]{2,1,0:T(8,128)S(1)}, s32[]{:S(2)}) async-start(f32[8,64,256]{2,1,0:T(8,128)} %param.4), calls=%async_computation.12 | async-start | bytes 524288 | tf_op jit(solution)/shard_map/slice | solution.py:89
  211.8 19.7 %copy-start.10 = (f32[512,128]{1,0:T(8,128)S(1)}, f32[512,128]{1,0:T(8,128)}, u32[]{:S(2)}) copy-start(f32[512,128]{1,0:T(8,128)} %copy-done.9) | copy-start | bytes 786436
  224.4 7.5 %copy-start.3 = (f32[256,256]{1,0:T(8,128)S(1)}, f32[256,256]{1,0:T(8,128)}, u32[]{:S(2)}) copy-start(f32[256,256]{1,0:T(8,128)} %convolution_add_fusion.2) | copy-start | bytes 786436
  224.4 23.2 %all-to-all-start.10 = ((f32[64,16,128]{2,1,0:T(8,128)}), f32[64,16,128]{2,1,0:T(8,128)S(1)}, u32[]{:S(2)}, u32[]{:S(2)}) async-start(f32[64,16,128]{2,1,0:T(8,128)} %broadcast_in_dim.26), calls=%async_computation.10 | async-start | bytes 1048576 | tf_op jit(solution)/shard_map/all_to_all | solution.py:20
  249.7 14.2 %all-to-all-start.11 = ((f32[8,32,256]{2,1,0:T(8,128)}), f32[8,32,256]{2,1,0:T(8,128)S(1)}, u32[]{:S(2)}, u32[]{:S(2)}) async-start(f32[8,32,256]{2,1,0:T(8,128)} %bitcast.46), calls=%async_computation.11 | async-start | bytes 524288 | tf_op jit(solution)/shard_map/all_to_all | solution.py:20

commit v22 on v21

--- a/solution.py
+++ b/solution.py
@@ -96,18 +96,18 @@
 
     parts = scattered_whole(own_diag[0], right_sides[0])
     sent_first = jnp.concatenate([lower_blocks[0], half_of(right_sides[1], row % 2 ^ 1)], 1)
+    got_first = from_partner(sent_first)
+    parts, got_first, trail = by_deadline(parts, got_first, trail)
     part = parts.sum(0)
     part = jnp.stack([part[:, :half], part[:, half:]])
     sent = copies(part, members).reshape(row_size, -1, half)
-    sent, sent_first = by_deadline(sent, sent_first)
     parts = swap(sent, "row")
-    got_first = from_partner(sent_first)
     own_shared = jnp.concatenate([own_diag[1:], lower_blocks[2:3], lower_blocks[5:]])
     got_first, own_shared = by_deadline(got_first, own_shared)
     got_shared = from_partner(own_shared)
     lower_10 = ordered(lower_blocks[0], got_first[:, :width], 0)
     side_1 = ordered(half_of(right_sides[1], row % 2), got_first[:, width:], 0)
-    parts, trail, lower_10, side_1 = by_deadline(parts, trail, lower_10, side_1)
+    parts, lower_10, side_1 = by_deadline(parts, lower_10, side_1)
     solved_0 = parts.reshape(width, half)
 
     parts = summed(contract(lower_10, solved_0, (1, 0)))

time: 267 us -> 263 us (0.985)
  waiting for transfers between devices: 101 us -> 94.5 us
    all_to_all x12, waiting for transfers between devices: 76.4 us -> 65.2 us  [swap(): lax.all_to_all(parts, axis, 0, 0, axis_index_groups=groups, tiled=True)]
    ppermute x7, waiting for transfers between devices: 24.9 us -> 29.3 us  [from_partner(): return lax.ppermute(value, 'row', [(r, r ^ 1) for r in range(row_size)])]
  transfers between devices with their start and end apart: 19 -> 19, of which waited for: 14 -> 14; matrix products, arithmetic and copies ran while one was open for 11% -> 12% of each run, Pallas kernels for 0% -> 0%
where the time goes in v22:
time: 263 us; the launch traced here: 261 us
  starting transfers between devices  112 us (43%)
  waiting for transfers between devices  94.5 us (36%)
  matrix products  19.9 us (8%)
  local copies, waits for them, and re-layouts  19.4 us (7%)
  other arithmetic  14.3 us (5%)
    all_to_all x12, starting transfers between devices, swap(): lax.all_to_all(parts, axis, 0, 0, axis_index_groups=groups, tiled=True)  92.4 us
    all_to_all x12, waiting for transfers between devices, swap(): lax.all_to_all(parts, axis, 0, 0, axis_index_groups=groups, tiled=True)  65.2 us
    ppermute x7, waiting for transfers between devices, from_partner(): return lax.ppermute(value, 'row', [(r, r ^ 1) for r in range(row_size)])  29.3 us
    dot_general x14, matrix products, contract(): lax.dot_general(left, right, (((axes[0],), (axes[1],)), ((), ())), precis...  19.9 us
    ppermute x7, starting transfers between devices, from_partner(): return lax.ppermute(value, 'row', [(r, r ^ 1) for r in range(row_size)])  19.6 us
    broadcast_in_dim x7, local copies, waits for them, and re-layouts, copies(): return jnp.broadcast_to(part[None], (count,) + part.shape)  5.56 us
  transfers between devices with their start and end apart: 19, of which 14 were waited for; matrix products, arithmetic and copies ran while one was open for 12% of the time, Pallas kernels for 0%

profile of v22, /device:TPU:1, one launch (start us, length us, event | category | flops | bytes accessed | tf_op | source)
XLA Modules:
  0.0 261.4 jit_solution(2320442858155409658)
XLA Ops:
  4.0 17.4 %all-to-all-start = ((f32[64,8,256]{2,1,0:T(8,128)}), f32[64,8,256]{2,1,0:T(8,128)}, u32[]{:S(2)}, u32[]{:S(2)}) async-start(f32[64,8,256]{2,1,0:T(8,128)} %fusion.17), calls=%async_computation | async-start | bytes 1048576 | tf_op jit(solution)/shard_map/all_to_all | solution.py:20
  23.6 3.0 %collective-permute-start = (f32[64,640]{1,0:T(8,128)}, f32[64,640]{1,0:T(8,128)}, u32[]{:S(2)}, u32[]{:S(2)}) collective-permute-start(f32[64,640]{1,0:T(8,128)} %pad_maximum_fusion.13), channel_id=1, source_target_pairs={{0,8},{8,0},{16,24},{24,16},{32,40},{40,32},{48,56},{56,48},{64,72... | collective-permute-start | bytes 491528 | tf_op jit(solution)/shard_map/ppermute | solution.py:47
  26.6 2.7 %fusion.43 = (f32[4,64,1,512]{3,2,1,0:T(1,128)}, f32[4,64,1,512]{3,2,1,0:T(1,128)S(1)}, f32[4,64,1,512]{3,2,1,0:T(1,128)}, f32[4,64,1,512]{3,2,1,0:T(1,128)}) fusion(f32[4,64,4,512]{3,2,1,0:T(4,128)S(1)} %copy-done), kind=kLoop, calls=%fused_computation.103 | loop fusion | bytes 4194304 | tf_op jit(solution)/shard_map/slice | solution.py:81
  33.4 5.6 %collective-permute-done = f32[64,640]{1,0:T(8,128)} collective-permute-done((f32[64,640]{1,0:T(8,128)}, f32[64,640]{1,0:T(8,128)}, u32[]{:S(2)}, u32[]{:S(2)}) %collective-permute-start) | collective-permute-done | bytes 163872 | tf_op jit(solution)/shard_map/ppermute | solution.py:47
  38.9 3.5 %collective-permute-start.1 = (f32[5,64,512]{2,1,0:T(8,128)S(1)}, f32[5,64,512]{2,1,0:T(8,128)S(1)}, u32[]{:S(2)}, u32[]{:S(2)}) collective-permute-start(f32[5,64,512]{2,1,0:T(8,128)S(1)} %pad_maximum_fusion), channel_id=1, source_target_pairs={{0,8},{8,0},{16,24},{24,16},{32,40},{40,32},{48,56},{56,48},{64,72... | collective-permute-start | bytes 1966088 | tf_op jit(solution)/shard_map/ppermute | solution.py:47
  44.3 10.0 %all-to-all-start.1 = ((f32[64,8,128]{2,1,0:T(8,128)}), f32[64,8,128]{2,1,0:T(8,128)S(1)}, u32[]{:S(2)}, u32[]{:S(2)}) async-start(f32[64,8,128]{2,1,0:T(8,128)} %bitcast.20), calls=%async_computation.1 | async-start | bytes 524288 | tf_op jit(solution)/shard_map/all_to_all | solution.py:20
  56.8 10.0 %all-to-all-done.1 = f32[64,8,128]{2,1,0:T(8,128)S(1)} async-done(((f32[64,8,128]{2,1,0:T(8,128)}), f32[64,8,128]{2,1,0:T(8,128)S(1)}, u32[]{:S(2)}, u32[]{:S(2)}) %all-to-all-start.1) | async-done | bytes 262176 | tf_op jit(solution)/shard_map/all_to_all | solution.py:20
  68.0 7.9 %all-to-all-start.2 = ((f32[8,128,128]{2,1,0:T(8,128)}), f32[8,128,128]{2,1,0:T(8,128)}, u32[]{:S(2)}, u32[]{:S(2)}) async-start(f32[8,128,128]{2,1,0:T(8,128)} %broadcast_in_dim.20), calls=%async_computation.2 | async-start | bytes 1048576 | tf_op jit(solution)/shard_map/all_to_all | solution.py:20
  80.9 4.9 %collective-permute-done.2 = f32[512,128]{1,0:T(8,128)} collective-permute-done((f32[512,128]{1,0:T(8,128)S(1)}, f32[512,128]{1,0:T(8,128)}, u32[]{:S(2)}, u32[]{:S(2)}) %collective-permute-start.2) | collective-permute-done | bytes 262176 | tf_op jit(solution)/shard_map/ppermute | solution.py:47
  90.1 3.9 %all-to-all-start.3 = ((f32[32,16,128]{2,1,0:T(8,128)}), f32[32,16,128]{2,1,0:T(8,128)S(1)}, u32[]{:S(2)}, u32[]{:S(2)}) async-start(f32[32,16,128]{2,1,0:T(8,128)} %bitcast.134), calls=%async_computation.3 | async-start | bytes 524288 | tf_op jit(solution)/shard_map/all_to_all | solution.py:20
  95.3 2.8 %collective-permute-start.3 = (f32[64,128]{1,0:T(8,128)S(1)}, f32[64,128]{1,0:T(8,128)}, u32[]{:S(2)}, u32[]{:S(2)}) collective-permute-start(f32[64,128]{1,0:T(8,128)S(1)} %constant_dynamic-slice_fusion.3), channel_id=1, source_target_pairs={{0,8},{8,0},{16,24},{24,16},{32,40},{40,32},{48,56},{56,48},{64,72... | collective-permute-start | bytes 98312 | tf_op jit(solution)/shard_map/ppermute | solution.py:47
  99.8 3.4 %collective-permute-done.3 = f32[64,128]{1,0:T(8,128)} collective-permute-done((f32[64,128]{1,0:T(8,128)S(1)}, f32[64,128]{1,0:T(8,128)}, u32[]{:S(2)}, u32[]{:S(2)}) %collective-permute-start.3) | collective-permute-done | bytes 32800 | tf_op jit(solution)/shard_map/ppermute | solution.py:47
  103.3 2.8 %all-to-all-done.3 = f32[32,16,128]{2,1,0:T(8,128)S(1)} async-done(((f32[32,16,128]{2,1,0:T(8,128)}), f32[32,16,128]{2,1,0:T(8,128)S(1)}, u32[]{:S(2)}, u32[]{:S(2)}) %all-to-all-start.3) | async-done | bytes 262176 | tf_op jit(solution)/shard_map/all_to_all | solution.py:20
  106.8 7.7 %all-to-all-start.4 = ((f32[32,16,128]{2,1,0:T(8,128)}), f32[32,16,128]{2,1,0:T(8,128)S(1)}, u32[]{:S(2)}, u32[]{:S(2)}) async-start(f32[32,16,128]{2,1,0:T(8,128)} %broadcast_in_dim.22), calls=%async_computation.4 | async-start | bytes 524288 | tf_op jit(solution)/shard_map/all_to_all | solution.py:20
  116.7 10.3 %all-to-all-done.4 = f32[32,16,128]{2,1,0:T(8,128)S(1)} async-done(((f32[32,16,128]{2,1,0:T(8,128)}), f32[32,16,128]{2,1,0:T(8,128)S(1)}, u32[]{:S(2)}, u32[]{:S(2)}) %all-to-all-start.4) | async-done | bytes 262176 | tf_op jit(solution)/shard_map/all_to_all | solution.py:20
  128.2 6.2 %all-to-all-start.5 = ((f32[8,128,128]{2,1,0:T(8,128)}), f32[8,128,128]{2,1,0:T(8,128)S(1)}, u32[]{:S(2)}, u32[]{:S(2)}) async-start(f32[8,128,128]{2,1,0:T(8,128)} %broadcast_in_dim.23), calls=%async_computation.5 | async-start | bytes 1048576 | tf_op jit(solution)/shard_map/all_to_all | solution.py:20
  134.4 2.8 %collective-permute-start.4 = (f32[512,128]{1,0:T(8,128)S(1)}, f32[512,128]{1,0:T(8,128)}, u32[]{:S(2)}, u32[]{:S(2)}) collective-permute-start(f32[512,128]{1,0:T(8,128)S(1)} %bitcast.127), channel_id=1, source_target_pairs={{0,8},{8,0},{16,24},{24,16},{32,40},{40,32},{48,56},{56,48},{64,72... | collective-permute-start | bytes 786440 | tf_op jit(solution)/shard_map/ppermute | solution.py:47
  139.7 4.5 %collective-permute-done.4 = f32[512,128]{1,0:T(8,128)} collective-permute-done((f32[512,128]{1,0:T(8,128)S(1)}, f32[512,128]{1,0:T(8,128)}, u32[]{:S(2)}, u32[]{:S(2)}) %collective-permute-start.4) | collective-permute-done | bytes 262176 | tf_op jit(solution)/shard_map/ppermute | solution.py:47
  146.3 4.9 %all-to-all-start.6 = ((f32[32,16,128]{2,1,0:T(8,128)}), f32[32,16,128]{2,1,0:T(8,128)}, u32[]{:S(2)}, u32[]{:S(2)}) async-start(f32[32,16,128]{2,1,0:T(8,128)} %fusion.27), calls=%async_computation.6 | async-start | bytes 524288 | tf_op jit(solution)/shard_map/all_to_all | solution.py:20
  153.6 2.7 %collective-permute-start.5 = (f32[64,128]{1,0:T(8,128)S(1)}, f32[64,128]{1,0:T(8,128)S(1)}, u32[]{:S(2)}, u32[]{:S(2)}) collective-permute-start(f32[64,128]{1,0:T(8,128)S(1)} %constant_dynamic-slice_fusion.2), channel_id=1, source_target_pairs={{0,8},{8,0},{16,24},{24,16},{32,40},{40,32},{48,56},{56,48},{64,72... | collective-permute-start | bytes 98312 | tf_op jit(solution)/shard_map/ppermute | solution.py:47
  156.3 4.8 %collective-permute-done.5 = f32[64,128]{1,0:T(8,128)S(1)} collective-permute-done((f32[64,128]{1,0:T(8,128)S(1)}, f32[64,128]{1,0:T(8,128)S(1)}, u32[]{:S(2)}, u32[]{:S(2)}) %collective-permute-start.5) | collective-permute-done | bytes 32800 | tf_op jit(solution)/shard_map/ppermute | solution.py:47
  165.1 7.0 %all-to-all-start.7 = ((f32[32,16,128]{2,1,0:T(8,128)}), f32[32,16,128]{2,1,0:T(8,128)S(1)}, u32[]{:S(2)}, u32[]{:S(2)}) async-start(f32[32,16,128]{2,1,0:T(8,128)} %broadcast_in_dim.24), calls=%async_computation.7 | async-start | bytes 524288 | tf_op jit(solution)/shard_map/all_to_all | solution.py:20
  172.0 2.8 %convolution_add_fusion.2 = f32[256,256]{1,0:T(8,128)} fusion(f32[256,256]{1,0:T(8,128)} %fusion.3, f32[256,512]{1,0:T(8,128)} %bitcast.130, f32[512,128]{1,0:T(8,128)S(1)} %get-tuple-element.94, f32[512,128]{1,0:T(8,128)S(1)} %get-tuple-element.93), kind=kOutput, calls=%fused_computation.8 | convolution fusion | flops 402849792 | bytes 1572864 | tf_op jit(solution)/shard_map/dot_general | solution.py:10
  174.9 8.8 %all-to-all-done.7 = f32[32,16,128]{2,1,0:T(8,128)S(1)} async-done(((f32[32,16,128]{2,1,0:T(8,128)}), f32[32,16,128]{2,1,0:T(8,128)S(1)}, u32[]{:S(2)}, u32[]{:S(2)}) %all-to-all-start.7) | async-done | bytes 262176 | tf_op jit(solution)/shard_map/all_to_all | solution.py:20
  184.8 8.0 %all-to-all-start.8 = ((f32[8,128,128]{2,1,0:T(8,128)}), f32[8,128,128]{2,1,0:T(8,128)S(1)}, u32[]{:S(2)}, u32[]{:S(2)}) async-start(f32[8,128,128]{2,1,0:T(8,128)} %broadcast_in_dim.25), calls=%async_computation.8 | async-start | bytes 1048576 | tf_op jit(solution)/shard_map/all_to_all | solution.py:20
  196.5 6.1 %collective-permute-done.6 = f32[512,128]{1,0:T(8,128)S(1)} collective-permute-done((f32[512,128]{1,0:T(8,128)S(1)}, f32[512,128]{1,0:T(8,128)S(1)}, u32[]{:S(2)}, u32[]{:S(2)}) %collective-permute-start.6) | collective-permute-done | bytes 262176 | tf_op jit(solution)/shard_map/ppermute | solution.py:47
  203.7 4.1 %all-to-all-start.9 = ((f32[32,16,128]{2,1,0:T(8,128)}), f32[32,16,128]{2,1,0:T(8,128)S(1)}, u32[]{:S(2)}, u32[]{:S(2)}) async-start(f32[32,16,128]{2,1,0:T(8,128)} %fusion.25), calls=%async_computation.9 | async-start | bytes 524288 | tf_op jit(solution)/shard_map/all_to_all | solution.py:20
  208.3 11.6 %all-to-all-done.9 = f32[32,16,128]{2,1,0:T(8,128)S(1)} async-done(((f32[32,16,128]{2,1,0:T(8,128)}), f32[32,16,128]{2,1,0:T(8,128)S(1)}, u32[]{:S(2)}, u32[]{:S(2)}) %all-to-all-start.9) | async-done | bytes 262176 | tf_op jit(solution)/shard_map/all_to_all | solution.py:20
  220.8 7.0 %all-to-all-start.10 = ((f32[64,16,128]{2,1,0:T(8,128)}), f32[64,16,128]{2,1,0:T(8,128)S(1)}, u32[]{:S(2)}, u32[]{:S(2)}) async-start(f32[64,16,128]{2,1,0:T(8,128)} %broadcast_in_dim.26), calls=%async_computation.10 | async-start | bytes 1048576 | tf_op jit(solution)/shard_map/all_to_all | solution.py:20
  229.7 13.9 %all-to-all-done.10 = f32[64,16,128]{2,1,0:T(8,128)S(1)} async-done(((f32[64,16,128]{2,1,0:T(8,128)}), f32[64,16,128]{2,1,0:T(8,128)S(1)}, u32[]{:S(2)}, u32[]{:S(2)}) %all-to-all-start.10) | async-done | bytes 524320 | tf_op jit(solution)/shard_map/all_to_all | solution.py:20
  245.6 8.5 %all-to-all-start.11 = ((f32[8,32,256]{2,1,0:T(8,128)}), f32[8,32,256]{2,1,0:T(8,128)S(1)}, u32[]{:S(2)}, u32[]{:S(2)}) async-start(f32[8,32,256]{2,1,0:T(8,128)} %bitcast.46), calls=%async_computation.11 | async-start | bytes 524288 | tf_op jit(solution)/shard_map/all_to_all | solution.py:20
  255.0 5.6 %all-to-all-done.11 = f32[8,32,256]{2,1,0:T(8,128)S(1)} async-done(((f32[8,32,256]{2,1,0:T(8,128)}), f32[8,32,256]{2,1,0:T(8,128)S(1)}, u32[]{:S(2)}, u32[]{:S(2)}) %all-to-all-start.11) | async-done | bytes 262176 | tf_op jit(solution)/shard_map/all_to_all | solution.py:20
  (113 shorter events, 55.3 us)
Async XLA Ops:
  0.6 21.7 %copy-start.5 = (f32[6,64,512]{2,1,0:T(8,128)S(1)}, f32[6,64,512]{2,1,0:T(8,128)}, u32[]{:S(2)}) copy-start(f32[6,64,512]{2,1,0:T(8,128)} %param.6) | copy-start | bytes 2359300
  0.6 25.9 %copy-start = (f32[4,64,4,512]{3,2,1,0:T(4,128)S(1)}, f32[4,64,4,512]{3,2,1,0:T(4,128)}, u32[]{:S(2)}) copy-start(f32[4,64,4,512]{3,2,1,0:T(4,128)} %param.7) | copy-start | bytes 6291460
  4.0 34.9 %all-to-all-start = ((f32[64,8,256]{2,1,0:T(8,128)}), f32[64,8,256]{2,1,0:T(8,128)}, u32[]{:S(2)}, u32[]{:S(2)}) async-start(f32[64,8,256]{2,1,0:T(8,128)} %fusion.17), calls=%async_computation | async-start | bytes 1048576 | tf_op jit(solution)/shard_map/all_to_all | solution.py:20
  23.6 5.7 %copy-start.8 = (f32[4,512,64]{1,2,0:T(8,128)S(1)}, f32[4,512,64]{1,2,0:T(8,128)}, u32[]{:S(2)}) copy-start(f32[4,512,64]{1,2,0:T(8,128)} %param.5) | copy-start | bytes 1572868
  23.6 15.3 %collective-permute-start = (f32[64,640]{1,0:T(8,128)}, f32[64,640]{1,0:T(8,128)}, u32[]{:S(2)}, u32[]{:S(2)}) collective-permute-start(f32[64,640]{1,0:T(8,128)} %pad_maximum_fusion.13), channel_id=1, source_target_pairs={{0,8},{8,0},{16,24},{24,16},{32,40},{40,32},{48,56},{56,48},{64,72... | collective-permute-start | bytes 491528 | tf_op jit(solution)/shard_map/ppermute | solution.py:47
  29.3 1.2 copy-start.4
  29.3 1.3 copy-start.3
  29.3 2.2 copy-start.2
  31.5 22.8 %copy-start.10 = (f32[1,64,256]{2,1,0:T(8,128)S(1)}, f32[1,64,256]{2,1,0:T(8,128)}, u32[]{:S(2)}) copy-start(f32[1,64,256]{2,1,0:T(8,128)} %copy-done.9) | copy-start | bytes 196612
  38.9 39.2 %collective-permute-start.1 = (f32[5,64,512]{2,1,0:T(8,128)S(1)}, f32[5,64,512]{2,1,0:T(8,128)S(1)}, u32[]{:S(2)}, u32[]{:S(2)}) collective-permute-start(f32[5,64,512]{2,1,0:T(8,128)S(1)} %pad_maximum_fusion), channel_id=1, source_target_pairs={{0,8},{8,0},{16,24},{24,16},{32,40},{40,32},{48,56},{56,48},{64,72... | collective-permute-start | bytes 1966088 | tf_op jit(solution)/shard_map/ppermute | solution.py:47
  44.3 22.4 %all-to-all-start.1 = ((f32[64,8,128]{2,1,0:T(8,128)}), f32[64,8,128]{2,1,0:T(8,128)S(1)}, u32[]{:S(2)}, u32[]{:S(2)}) async-start(f32[64,8,128]{2,1,0:T(8,128)} %bitcast.20), calls=%async_computation.1 | async-start | bytes 524288 | tf_op jit(solution)/shard_map/all_to_all | solution.py:20
  68.0 17.8 %all-to-all-start.2 = ((f32[8,128,128]{2,1,0:T(8,128)}), f32[8,128,128]{2,1,0:T(8,128)}, u32[]{:S(2)}, u32[]{:S(2)}) async-start(f32[8,128,128]{2,1,0:T(8,128)} %broadcast_in_dim.20), calls=%async_computation.2 | async-start | bytes 1048576 | tf_op jit(solution)/shard_map/all_to_all | solution.py:20
  75.8 9.9 %collective-permute-start.2 = (f32[512,128]{1,0:T(8,128)S(1)}, f32[512,128]{1,0:T(8,128)}, u32[]{:S(2)}, u32[]{:S(2)}) collective-permute-start(f32[512,128]{1,0:T(8,128)S(1)} %bitcast.123), channel_id=1, source_target_pairs={{0,8},{8,0},{16,24},{24,16},{32,40},{40,32},{48,56},{56,48},{64,72... | collective-permute-start | bytes 786440 | tf_op jit(solution)/shard_map/ppermute | solution.py:47
  78.2 0.9 copy-start.7
  80.9 17.2 %copy-start.1 = (f32[4,64,1,512]{3,1,0,2:T(8,128)S(1)}, f32[4,64,1,512]{3,1,0,2:T(8,128)}, u32[]{:S(2)}) copy-start(f32[4,64,1,512]{3,1,0,2:T(8,128)} %copy.48) | copy-start | bytes 1572868
  90.1 15.9 %all-to-all-start.3 = ((f32[32,16,128]{2,1,0:T(8,128)}), f32[32,16,128]{2,1,0:T(8,128)S(1)}, u32[]{:S(2)}, u32[]{:S(2)}) async-start(f32[32,16,128]{2,1,0:T(8,128)} %bitcast.134), calls=%async_computation.3 | async-start | bytes 524288 | tf_op jit(solution)/shard_map/all_to_all | solution.py:20
  95.3 7.9 %collective-permute-start.3 = (f32[64,128]{1,0:T(8,128)S(1)}, f32[64,128]{1,0:T(8,128)}, u32[]{:S(2)}, u32[]{:S(2)}) collective-permute-start(f32[64,128]{1,0:T(8,128)S(1)} %constant_dynamic-slice_fusion.3), channel_id=1, source_target_pairs={{0,8},{8,0},{16,24},{24,16},{32,40},{40,32},{48,56},{56,48},{64,72... | collective-permute-start | bytes 98312 | tf_op jit(solution)/shard_map/ppermute | solution.py:47
  106.8 20.1 %all-to-all-start.4 = ((f32[32,16,128]{2,1,0:T(8,128)}), f32[32,16,128]{2,1,0:T(8,128)S(1)}, u32[]{:S(2)}, u32[]{:S(2)}) async-start(f32[32,16,128]{2,1,0:T(8,128)} %broadcast_in_dim.22), calls=%async_computation.4 | async-start | bytes 524288 | tf_op jit(solution)/shard_map/all_to_all | solution.py:20
  128.2 16.1 %all-to-all-start.5 = ((f32[8,128,128]{2,1,0:T(8,128)}), f32[8,128,128]{2,1,0:T(8,128)S(1)}, u32[]{:S(2)}, u32[]{:S(2)}) async-start(f32[8,128,128]{2,1,0:T(8,128)} %broadcast_in_dim.23), calls=%async_computation.5 | async-start | bytes 1048576 | tf_op jit(solution)/shard_map/all_to_all | solution.py:20
  134.4 9.9 %collective-permute-start.4 = (f32[512,128]{1,0:T(8,128)S(1)}, f32[512,128]{1,0:T(8,128)}, u32[]{:S(2)}, u32[]{:S(2)}) collective-permute-start(f32[512,128]{1,0:T(8,128)S(1)} %bitcast.127), channel_id=1, source_target_pairs={{0,8},{8,0},{16,24},{24,16},{32,40},{40,32},{48,56},{56,48},{64,72... | collective-permute-start | bytes 786440 | tf_op jit(solution)/shard_map/ppermute | solution.py:47
  146.3 17.0 %all-to-all-start.6 = ((f32[32,16,128]{2,1,0:T(8,128)}), f32[32,16,128]{2,1,0:T(8,128)}, u32[]{:S(2)}, u32[]{:S(2)}) async-start(f32[32,16,128]{2,1,0:T(8,128)} %fusion.27), calls=%async_computation.6 | async-start | bytes 524288 | tf_op jit(solution)/shard_map/all_to_all | solution.py:20
  153.6 7.5 %collective-permute-start.5 = (f32[64,128]{1,0:T(8,128)S(1)}, f32[64,128]{1,0:T(8,128)S(1)}, u32[]{:S(2)}, u32[]{:S(2)}) collective-permute-start(f32[64,128]{1,0:T(8,128)S(1)} %constant_dynamic-slice_fusion.2), channel_id=1, source_target_pairs={{0,8},{8,0},{16,24},{24,16},{32,40},{40,32},{48,56},{56,48},{64,72... | collective-permute-start | bytes 98312 | tf_op jit(solution)/shard_map/ppermute | solution.py:47
  165.1 18.6 %all-to-all-start.7 = ((f32[32,16,128]{2,1,0:T(8,128)}), f32[32,16,128]{2,1,0:T(8,128)S(1)}, u32[]{:S(2)}, u32[]{:S(2)}) async-start(f32[32,16,128]{2,1,0:T(8,128)} %broadcast_in_dim.24), calls=%async_computation.7 | async-start | bytes 524288 | tf_op jit(solution)/shard_map/all_to_all | solution.py:20
  184.8 17.8 %all-to-all-start.8 = ((f32[8,128,128]{2,1,0:T(8,128)}), f32[8,128,128]{2,1,0:T(8,128)S(1)}, u32[]{:S(2)}, u32[]{:S(2)}) async-start(f32[8,128,128]{2,1,0:T(8,128)} %broadcast_in_dim.25), calls=%async_computation.8 | async-start | bytes 1048576 | tf_op jit(solution)/shard_map/all_to_all | solution.py:20
  192.8 9.8 %collective-permute-start.6 = (f32[512,128]{1,0:T(8,128)S(1)}, f32[512,128]{1,0:T(8,128)S(1)}, u32[]{:S(2)}, u32[]{:S(2)}) collective-permute-start(f32[512,128]{1,0:T(8,128)S(1)} %bitcast.125), channel_id=1, source_target_pairs={{0,8},{8,0},{16,24},{24,16},{32,40},{40,32},{48,56},{56,48},{64,72... | collective-permute-start | bytes 786440 | tf_op jit(solution)/shard_map/ppermute | solution.py:47
  202.6 5.2 %copy-start.11 = (f32[512,128]{1,0:T(8,128)}, f32[512,128]{1,0:T(8,128)S(1)}, u32[]{:S(2)}) copy-start(f32[512,128]{1,0:T(8,128)S(1)} %collective-permute-done.6) | copy-start | bytes 786436
  203.7 16.2 %all-to-all-start.9 = ((f32[32,16,128]{2,1,0:T(8,128)}), f32[32,16,128]{2,1,0:T(8,128)S(1)}, u32[]{:S(2)}, u32[]{:S(2)}) async-start(f32[32,16,128]{2,1,0:T(8,128)} %fusion.25), calls=%async_computation.9 | async-start | bytes 524288 | tf_op jit(solution)/shard_map/all_to_all | solution.py:20
  207.8 20.0 %slice-start = ((f32[8,64,256]{2,1,0:T(8,128)}), f32[4,64,256]{2,1,0:T(8,128)S(1)}, s32[]{:S(2)}) async-start(f32[8,64,256]{2,1,0:T(8,128)} %param.4), calls=%async_computation.12 | async-start | bytes 524288 | tf_op jit(solution)/shard_map/slice | solution.py:89
  208.3 19.8 %copy-start.12 = (f32[512,128]{1,0:T(8,128)S(1)}, f32[512,128]{1,0:T(8,128)}, u32[]{:S(2)}) copy-start(f32[512,128]{1,0:T(8,128)} %copy-done.11) | copy-start | bytes 786436
  220.8 7.6 %copy-start.6 = (f32[256,256]{1,0:T(8,128)S(1)}, f32[256,256]{1,0:T(8,128)}, u32[]{:S(2)}) copy-start(f32[256,256]{1,0:T(8,128)} %convolution_add_fusion.2) | copy-start | bytes 786436
  220.8 22.8 %all-to-all-start.10 = ((f32[64,16,128]{2,1,0:T(8,128)}), f32[64,16,128]{2,1,0:T(8,128)S(1)}, u32[]{:S(2)}, u32[]{:S(2)}) async-start(f32[64,16,128]{2,1,0:T(8,128)} %broadcast_in_dim.26), calls=%async_computation.10 | async-start | bytes 1048576 | tf_op jit(solution)/shard_map/all_to_all | solution.py:20
  245.6 15.0 %all-to-all-start.11 = ((f32[8,32,256]{2,1,0:T(8,128)}), f32[8,32,256]{2,1,0:T(8,128)S(1)}, u32[]{:S(2)}, u32[]{:S(2)}) async-start(f32[8,32,256]{2,1,0:T(8,128)} %bitcast.46), calls=%async_computation.11 | async-start | bytes 524288 | tf_op jit(solution)/shard_map/all_to_all | solution.py:20
  (1 other events, 0.6 us)
